TPU v7x, 32 devices: a whole 2x2x4 slice. The times are simulated.
32 devices in a mesh: atoms: 8 (over z, x), bands: 4 (over y, core).
Axes of the slice: x: 2, y: 2, z: 4, core: 2. Of those that a mesh axis runs over, the one named last changes fastest.
Arguments:
- eigvecs: bfloat16 [8192, 8192], P('atoms', 'bands'), may hold values from -0.59765625 to 0.59765625
- occupations: float32 [8192], P('bands'), may hold values from 0.2 to 2
- energies: float32 [8192], P('bands'), may hold values from -1 to 0.5
- neighbours: int32 [64, 16], P('atoms'), may hold values from 0 to 63, as said below
Outputs:
- density: float32 [64, 16, 128, 128], P('atoms', None, 'bands')
- energy_density: float32 [64, 16, 128, 128], P('atoms', None, 'bands')
Inputs may be any that keep to these rules, and one draw needn't show every extreme that they name: `neighbours`: every block named in the rows of one atoms domain lies in that domain or in one of the 2 domains on either side along the atoms axis, taken cyclically; from each of those 4 other domains the rows of one domain name exactly 2 distinct blocks.
All inputs are finite; a program needn't handle non-finite values.
Results may differ from a plain program's by a relative error of at most 0.014.
Values may be sent and summed in bfloat16 or wider, within the bound.
No kernel may reach another device: no remote copies, remote signals or barrier semaphores. Data moves between devices by JAX's collectives and lax.ppermute only.
A program may use at most 128 MiB of HBM per device.

v0:
```python
import jax
import jax.numpy as jnp
from jax import lax
from jax.sharding import PartitionSpec as P

CAP = 2
R = 2


def shifted(value, axis, steps):
    count = lax.axis_size(axis)
    pairs = [(source, (source + steps) % count) for source in range(count)]
    return lax.ppermute(value, axis, pairs)


def body(eigvecs, occupations, energies, neighbours):
    n_atoms = lax.axis_size("atoms")
    own_index = lax.axis_index("atoms")
    blocks_dev, neigh_count = neighbours.shape
    tile_rows = eigvecs.shape[0] // blocks_dev
    band_dev = eigvecs.shape[1]
    total_blocks = blocks_dev * n_atoms
    local_rows = eigvecs.reshape(blocks_dev, tile_rows, band_dev)
    flat_ids = neighbours.reshape(-1)
    owners = flat_ids // blocks_dev
    within = flat_ids % blocks_dev
    distance = (owners - own_index) % n_atoms
    slot_group = jnp.where(distance <= R, distance + R - 1, distance - n_atoms + R)
    offsets = list(range(-R, 0)) + list(range(1, R + 1))
    hits = flat_ids[:, None] == jnp.arange(total_blocks, dtype=jnp.int32)[None, :]
    needed = jnp.any(hits, axis=0).reshape(n_atoms, blocks_dev)
    needed = needed & (jnp.arange(n_atoms, dtype=jnp.int32)[:, None] != own_index)
    needed_int = needed.astype(jnp.int32)
    ranks = jnp.cumsum(needed_int, axis=1) - needed_int
    select = needed[:, :, None] & (
        ranks[:, :, None] == jnp.arange(CAP, dtype=jnp.int32)[None, None, :]
    )
    block_numbers = jnp.arange(blocks_dev, dtype=jnp.int32)[None, :, None]
    wanted = jnp.sum(select.astype(jnp.int32) * block_numbers, axis=1)

    def deliver(offset):
        target = (own_index + offset) % n_atoms
        request = lax.dynamic_index_in_dim(wanted, target, 0, keepdims=False)
        asked = shifted(request, "atoms", offset)
        return shifted(local_rows[asked], "atoms", -offset)

    arrived = jnp.concatenate([deliver(offset) for offset in offsets], 0)
    flat_ranks = ranks.reshape(-1)[flat_ids]
    remote_place = blocks_dev + slot_group * CAP + flat_ranks
    position = jnp.where(owners == own_index, within, remote_place)
    positions = position.reshape(blocks_dev, neigh_count)
    available = jnp.concatenate([local_rows, arrived], 0)
    weight_energy = occupations * energies
    scaled = jnp.stack([local_rows * occupations, local_rows * weight_energy], 1).astype(
        jnp.bfloat16
    )

    def one_block(pair):
        left, where_rows = pair
        right = available[where_rows]
        return jnp.einsum("sab,kcb->ksac", left, right, preferred_element_type=jnp.float32)

    partial_value = lax.map(one_block, (scaled, positions))
    summed = lax.psum_scatter(
        partial_value.astype(jnp.bfloat16), "bands", scatter_dimension=3, tiled=True
    ).astype(jnp.float32)
    return (summed[:, :, 0], summed[:, :, 1])


def solution(mesh):
    return jax.shard_map(
        body,
        mesh=mesh,
        in_specs=(P("atoms", "bands"), P("bands"), P("bands"), P("atoms", None)),
        out_specs=(P("atoms", None, "bands", None), P("atoms", None, "bands", None)),
        check_vma=False,
    )
```

profile of v0, /device:TPU:0, one launch (start us, length us, event | category | flops | bytes accessed | tf_op | source)
XLA Modules:
  0.0 322.8 jit_solution(6487311593379166113)
XLA Ops:
  8.9 5.1 %collective-permute-start = (s32[2]{0:T(128)S(1)}, s32[2]{0:T(128)S(1)}, u32[]{:S(2)}, u32[]{:S(2)}) collective-permute-start(s32[2]{0:T(128)S(1)} %get-tuple-element.33), channel_id=1, source_target_pairs={{0,24},{4,28},{8,0},{12,4},{16,8},{20,12},{24,16},{28,20},{1,25},{... | collective-permute-start | bytes 32 | tf_op jit(solution)/shard_map/ppermute | solution.py:13
  20.0 6.1 %fusion.10 = (bf16[8,1,128,2048]{3,2,1,0:T(8,128)(2,1)S(1)}, bf16[8,1,128,2048]{3,2,1,0:T(8,128)(2,1)}) fusion(bf16[8,1,128,2048]{3,2,1,0:T(8,128)(2,1)} %bitcast.42, f32[2048]{0:T(1024)} %param.7, f32[2048]{0:T(1024)S(1)} %mul.50), kind=kLoop, calls=%fused_computation.20 | loop fusion | flops 10485760 | bytes 12599296 | tf_op jit(solution)/shard_map/convert.1
  26.1 6.2 %pad_maximum_fusion = bf16[8,2,128,2048]{3,2,1,0:T(8,128)(2,1)} fusion(bf16[8,1,128,2048]{3,2,1,0:T(8,128)(2,1)} %get-tuple-element.49, bf16[8,1,128,2048]{3,2,1,0:T(8,128)(2,1)S(1)} %get-tuple-element.48), kind=kLoop, calls=%fused_computation.22 | loop fusion | flops 4194304 | bytes 16777216 | tf_op jit(solution)/shard_map/stack | solution.py:54
  54.1 9.2 %collective-permute-done.1 = bf16[2,128,2048]{2,1,0:T(8,128)(2,1)} collective-permute-done((bf16[2,128,2048]{2,1,0:T(8,128)(2,1)S(1)}, bf16[2,128,2048]{2,1,0:T(8,128)(2,1)}, u32[]{:S(2)}, u32[]{:S(2)}) %collective-permute-start.1) | collective-permute-done | bytes 1048608 | tf_op jit(solution)/shard_map/ppermute | solution.py:13
  64.5 22.1 %collective-permute-done.3 = bf16[2,128,2048]{2,1,0:T(8,128)(2,1)} collective-permute-done((bf16[2,128,2048]{2,1,0:T(8,128)(2,1)S(1)}, bf16[2,128,2048]{2,1,0:T(8,128)(2,1)}, u32[]{:S(2)}, u32[]{:S(2)}) %collective-permute-start.3) | collective-permute-done | bytes 1048608 | tf_op jit(solution)/shard_map/ppermute | solution.py:13
  90.1 15.9 %collective-permute-done.7 = bf16[2,128,2048]{2,1,0:T(8,128)(2,1)S(1)} collective-permute-done((bf16[2,128,2048]{2,1,0:T(8,128)(2,1)}, bf16[2,128,2048]{2,1,0:T(8,128)(2,1)S(1)}, u32[]{:S(2)}, u32[]{:S(2)}) %collective-permute-start.7) | collective-permute-done | bytes 1048608 | tf_op jit(solution)/shard_map/ppermute | solution.py:13
  109.4 127.7 %while.10 = (s32[]{:T(128)}, bf16[8,16,2,128,128]{4,3,1,0,2:T(8,128)(2,1)}, s32[8,16]{1,0:T(8,128)S(1)}, bf16[16,128,2048]{2,1,0:T(8,128)(2,1)}, bf16[8,2,128,2048]{3,2,1,0:T(8,128)(2,1)}, /*index=5*/s32[]{:T(128)}) while((s32[]{:T(128)}, bf16[8,16,2,128,128]{4,3,1,0,2:T(8,128)(2,1)}, s32[8,16]{1,0:T(8,128)S(1)}, ...), condition=%wide.region_4.5_spmd, body=%wide.region_3.4_spmd.sunk | while | flops 2147484672 | bytes 31462728 | solution.py:63
  109.4 8.0 %gather_fusion = bf16[16,128,2048]{2,1,0:T(8,128)(2,1)} fusion(bf16[16,128,2048]{2,1,0:T(8,128)(2,1)} %get-tuple-element.100, s32[1024]{0:T(1024)S(1)} %pad_clamp_fusion.7), kind=kCustom, calls=%fused_computation.clone.1 | custom fusion | bytes 16777280 | tf_op jit(solution)/shard_map/while/body/eval_jaxpr/gather | solution.py:60
  117.4 6.0 %fusion.27 = bf16[1,16,2,128,128]{3,4,2,1,0:T(8,128)(2,1)S(1)} fusion(bf16[16,128,2048]{2,1,0:T(8,128)(2,1)} %gather_fusion, bf16[8,2,128,2048]{3,2,1,0:T(8,128)(2,1)} %get-tuple-element.101, s32[]{:T(128)} %get-tuple-element.91), kind=kOutput, calls=%fused_computation.8.clone.1 | convolution fusion | flops 2147483648 | bytes 10486272 | tf_op jit(solution)/shard_map/while/body/eval_jaxpr/sab,kcb->ksac/dot_general | solution.py:61
  125.2 8.1 %gather_fusion = bf16[16,128,2048]{2,1,0:T(8,128)(2,1)} fusion(bf16[16,128,2048]{2,1,0:T(8,128)(2,1)} %get-tuple-element.100, s32[1024]{0:T(1024)S(1)} %pad_clamp_fusion.7), kind=kCustom, calls=%fused_computation.clone.1 | custom fusion | bytes 16777280 | tf_op jit(solution)/shard_map/while/body/eval_jaxpr/gather | solution.py:60
  133.3 6.0 %fusion.27 = bf16[1,16,2,128,128]{3,4,2,1,0:T(8,128)(2,1)S(1)} fusion(bf16[16,128,2048]{2,1,0:T(8,128)(2,1)} %gather_fusion, bf16[8,2,128,2048]{3,2,1,0:T(8,128)(2,1)} %get-tuple-element.101, s32[]{:T(128)} %get-tuple-element.91), kind=kOutput, calls=%fused_computation.8.clone.1 | convolution fusion | flops 2147483648 | bytes 10486272 | tf_op jit(solution)/shard_map/while/body/eval_jaxpr/sab,kcb->ksac/dot_general | solution.py:61
  141.2 8.1 %gather_fusion = bf16[16,128,2048]{2,1,0:T(8,128)(2,1)} fusion(bf16[16,128,2048]{2,1,0:T(8,128)(2,1)} %get-tuple-element.100, s32[1024]{0:T(1024)S(1)} %pad_clamp_fusion.7), kind=kCustom, calls=%fused_computation.clone.1 | custom fusion | bytes 16777280 | tf_op jit(solution)/shard_map/while/body/eval_jaxpr/gather | solution.py:60
  149.3 6.0 %fusion.27 = bf16[1,16,2,128,128]{3,4,2,1,0:T(8,128)(2,1)S(1)} fusion(bf16[16,128,2048]{2,1,0:T(8,128)(2,1)} %gather_fusion, bf16[8,2,128,2048]{3,2,1,0:T(8,128)(2,1)} %get-tuple-element.101, s32[]{:T(128)} %get-tuple-element.91), kind=kOutput, calls=%fused_computation.8.clone.1 | convolution fusion | flops 2147483648 | bytes 10486272 | tf_op jit(solution)/shard_map/while/body/eval_jaxpr/sab,kcb->ksac/dot_general | solution.py:61
  157.2 8.1 %gather_fusion = bf16[16,128,2048]{2,1,0:T(8,128)(2,1)} fusion(bf16[16,128,2048]{2,1,0:T(8,128)(2,1)} %get-tuple-element.100, s32[1024]{0:T(1024)S(1)} %pad_clamp_fusion.7), kind=kCustom, calls=%fused_computation.clone.1 | custom fusion | bytes 16777280 | tf_op jit(solution)/shard_map/while/body/eval_jaxpr/gather | solution.py:60
  165.3 6.0 %fusion.27 = bf16[1,16,2,128,128]{3,4,2,1,0:T(8,128)(2,1)S(1)} fusion(bf16[16,128,2048]{2,1,0:T(8,128)(2,1)} %gather_fusion, bf16[8,2,128,2048]{3,2,1,0:T(8,128)(2,1)} %get-tuple-element.101, s32[]{:T(128)} %get-tuple-element.91), kind=kOutput, calls=%fused_computation.8.clone.1 | convolution fusion | flops 2147483648 | bytes 10486272 | tf_op jit(solution)/shard_map/while/body/eval_jaxpr/sab,kcb->ksac/dot_general | solution.py:61
  173.2 8.1 %gather_fusion = bf16[16,128,2048]{2,1,0:T(8,128)(2,1)} fusion(bf16[16,128,2048]{2,1,0:T(8,128)(2,1)} %get-tuple-element.100, s32[1024]{0:T(1024)S(1)} %pad_clamp_fusion.7), kind=kCustom, calls=%fused_computation.clone.1 | custom fusion | bytes 16777280 | tf_op jit(solution)/shard_map/while/body/eval_jaxpr/gather | solution.py:60
  181.3 6.0 %fusion.27 = bf16[1,16,2,128,128]{3,4,2,1,0:T(8,128)(2,1)S(1)} fusion(bf16[16,128,2048]{2,1,0:T(8,128)(2,1)} %gather_fusion, bf16[8,2,128,2048]{3,2,1,0:T(8,128)(2,1)} %get-tuple-element.101, s32[]{:T(128)} %get-tuple-element.91), kind=kOutput, calls=%fused_computation.8.clone.1 | convolution fusion | flops 2147483648 | bytes 10486272 | tf_op jit(solution)/shard_map/while/body/eval_jaxpr/sab,kcb->ksac/dot_general | solution.py:61
  189.1 8.1 %gather_fusion = bf16[16,128,2048]{2,1,0:T(8,128)(2,1)} fusion(bf16[16,128,2048]{2,1,0:T(8,128)(2,1)} %get-tuple-element.100, s32[1024]{0:T(1024)S(1)} %pad_clamp_fusion.7), kind=kCustom, calls=%fused_computation.clone.1 | custom fusion | bytes 16777280 | tf_op jit(solution)/shard_map/while/body/eval_jaxpr/gather | solution.py:60
  197.2 6.0 %fusion.27 = bf16[1,16,2,128,128]{3,4,2,1,0:T(8,128)(2,1)S(1)} fusion(bf16[16,128,2048]{2,1,0:T(8,128)(2,1)} %gather_fusion, bf16[8,2,128,2048]{3,2,1,0:T(8,128)(2,1)} %get-tuple-element.101, s32[]{:T(128)} %get-tuple-element.91), kind=kOutput, calls=%fused_computation.8.clone.1 | convolution fusion | flops 2147483648 | bytes 10486272 | tf_op jit(solution)/shard_map/while/body/eval_jaxpr/sab,kcb->ksac/dot_general | solution.py:61
  205.1 8.1 %gather_fusion = bf16[16,128,2048]{2,1,0:T(8,128)(2,1)} fusion(bf16[16,128,2048]{2,1,0:T(8,128)(2,1)} %get-tuple-element.100, s32[1024]{0:T(1024)S(1)} %pad_clamp_fusion.7), kind=kCustom, calls=%fused_computation.clone.1 | custom fusion | bytes 16777280 | tf_op jit(solution)/shard_map/while/body/eval_jaxpr/gather | solution.py:60
  213.2 6.0 %fusion.27 = bf16[1,16,2,128,128]{3,4,2,1,0:T(8,128)(2,1)S(1)} fusion(bf16[16,128,2048]{2,1,0:T(8,128)(2,1)} %gather_fusion, bf16[8,2,128,2048]{3,2,1,0:T(8,128)(2,1)} %get-tuple-element.101, s32[]{:T(128)} %get-tuple-element.91), kind=kOutput, calls=%fused_computation.8.clone.1 | convolution fusion | flops 2147483648 | bytes 10486272 | tf_op jit(solution)/shard_map/while/body/eval_jaxpr/sab,kcb->ksac/dot_general | solution.py:61
  221.0 8.1 %gather_fusion = bf16[16,128,2048]{2,1,0:T(8,128)(2,1)} fusion(bf16[16,128,2048]{2,1,0:T(8,128)(2,1)} %get-tuple-element.100, s32[1024]{0:T(1024)S(1)} %pad_clamp_fusion.7), kind=kCustom, calls=%fused_computation.clone.1 | custom fusion | bytes 16777280 | tf_op jit(solution)/shard_map/while/body/eval_jaxpr/gather | solution.py:60
  229.2 6.0 %fusion.27 = bf16[1,16,2,128,128]{3,4,2,1,0:T(8,128)(2,1)S(1)} fusion(bf16[16,128,2048]{2,1,0:T(8,128)(2,1)} %gather_fusion, bf16[8,2,128,2048]{3,2,1,0:T(8,128)(2,1)} %get-tuple-element.101, s32[]{:T(128)} %get-tuple-element.91), kind=kOutput, calls=%fused_computation.8.clone.1 | convolution fusion | flops 2147483648 | bytes 10486272 | tf_op jit(solution)/shard_map/while/body/eval_jaxpr/sab,kcb->ksac/dot_general | solution.py:61
  237.0 74.0 %reduce-scatter.2.cloned.1.call-done = bf16[8,16,2,32,128]{4,3,1,0,2:T(8,128)(2,1)} async-done(((bf16[8,16,2,128,128]{4,3,1,0,2:T(8,128)(2,1)}), bf16[8,16,2,32,128]{4,3,1,0,2:T(8,128)(2,1)}) %reduce-scatter.2.cloned.1.call-update) | async-done | bytes 2097168 | tf_op jit(solution)/shard_map/reduce_scatter | solution.py:64
  (88 shorter events, 56.9 us)
Async XLA Ops:
  7.2 303.9 %reduce-scatter.2.cloned.1.call-start = ((), (), s32[]{:S(2)}) async-start(), calls=%async_computation.1 | async-start | bytes 10485760 | tf_op jit(solution)/shard_map/reduce_scatter | solution.py:64
  8.9 23.4 %collective-permute-start = (s32[2]{0:T(128)S(1)}, s32[2]{0:T(128)S(1)}, u32[]{:S(2)}, u32[]{:S(2)}) collective-permute-start(s32[2]{0:T(128)S(1)} %get-tuple-element.33), channel_id=1, source_target_pairs={{0,24},{4,28},{8,0},{12,4},{16,8},{20,12},{24,16},{28,20},{1,25},{... | collective-permute-start | bytes 32 | tf_op jit(solution)/shard_map/ppermute | solution.py:13
  14.0 18.3 %collective-permute-start.2 = (s32[2]{0:T(128)S(1)}, s32[2]{0:T(128)S(1)}, u32[]{:S(2)}, u32[]{:S(2)}) collective-permute-start(s32[2]{0:T(128)S(1)} %get-tuple-element.32), channel_id=1, source_target_pairs={{0,28},{4,0},{8,4},{12,8},{16,12},{20,16},{24,20},{28,24},{1,29},{... | collective-permute-start | bytes 32 | tf_op jit(solution)/shard_map/ppermute | solution.py:13
  15.4 24.2 %collective-permute-start.4 = (s32[2]{0:T(128)S(1)}, s32[2]{0:T(128)S(1)}, u32[]{:S(2)}, u32[]{:S(2)}) collective-permute-start(s32[2]{0:T(128)S(1)} %get-tuple-element.31), channel_id=1, source_target_pairs={{0,4},{4,8},{8,12},{12,16},{16,20},{20,24},{24,28},{28,0},{1,5},{5... | collective-permute-start | bytes 32 | tf_op jit(solution)/shard_map/ppermute | solution.py:13
  16.0 23.5 %collective-permute-start.6 = (s32[2]{0:T(128)S(1)}, s32[2]{0:T(128)S(1)}, u32[]{:S(2)}, u32[]{:S(2)}) collective-permute-start(s32[2]{0:T(128)S(1)} %get-tuple-element.30), channel_id=1, source_target_pairs={{0,8},{4,12},{8,16},{12,20},{16,24},{20,28},{24,0},{28,4},{1,9},{5... | collective-permute-start | bytes 32 | tf_op jit(solution)/shard_map/ppermute | solution.py:13
  26.1 19.6 %copy-start.1 = (s32[8,16]{1,0:T(8,128)S(1)}, s32[8,16]{1,0:T(8,128)}, u32[]{:S(2)}) copy-start(s32[8,16]{1,0:T(8,128)} %param.9) | copy-start | bytes 1540
  35.1 28.1 %collective-permute-start.1 = (bf16[2,128,2048]{2,1,0:T(8,128)(2,1)S(1)}, bf16[2,128,2048]{2,1,0:T(8,128)(2,1)}, u32[]{:S(2)}, u32[]{:S(2)}) collective-permute-start(bf16[2,128,2048]{2,1,0:T(8,128)(2,1)S(1)} %gather_fusion.2), channel_id=1, source_target_pairs={{0,8},{4,12},{8,16},{12,20},{16,24},{20,28},{24,0},{28,4},{1,9},{5... | collective-permute-start | bytes 3145736 | tf_op jit(solution)/shard_map/ppermute | solution.py:13
  38.0 48.6 %collective-permute-start.3 = (bf16[2,128,2048]{2,1,0:T(8,128)(2,1)S(1)}, bf16[2,128,2048]{2,1,0:T(8,128)(2,1)}, u32[]{:S(2)}, u32[]{:S(2)}) collective-permute-start(bf16[2,128,2048]{2,1,0:T(8,128)(2,1)S(1)} %gather_fusion.3), channel_id=1, source_target_pairs={{0,4},{4,8},{8,12},{12,16},{16,20},{20,24},{24,28},{28,0},{1,5},{5... | collective-permute-start | bytes 3145736 | tf_op jit(solution)/shard_map/ppermute | solution.py:13
  42.4 46.4 %collective-permute-start.5 = (bf16[2,128,2048]{2,1,0:T(8,128)(2,1)S(1)}, bf16[2,128,2048]{2,1,0:T(8,128)(2,1)}, u32[]{:S(2)}, u32[]{:S(2)}) collective-permute-start(bf16[2,128,2048]{2,1,0:T(8,128)(2,1)S(1)} %gather_fusion.4), channel_id=1, source_target_pairs={{0,28},{4,0},{8,4},{12,8},{16,12},{20,16},{24,20},{28,24},{1,29},{... | collective-permute-start | bytes 3145736 | tf_op jit(solution)/shard_map/ppermute | solution.py:13
  49.6 56.5 %collective-permute-start.7 = (bf16[2,128,2048]{2,1,0:T(8,128)(2,1)}, bf16[2,128,2048]{2,1,0:T(8,128)(2,1)S(1)}, u32[]{:S(2)}, u32[]{:S(2)}) collective-permute-start(bf16[2,128,2048]{2,1,0:T(8,128)(2,1)} %gather_fusion.5), channel_id=1, source_target_pairs={{0,24},{4,28},{8,0},{12,4},{16,8},{20,12},{24,16},{28,20},{1,25},{... | collective-permute-start | bytes 3145736 | tf_op jit(solution)/shard_map/ppermute | solution.py:13
  106.1 3.2 copy-start
Sparse Core Ops, SparseCore 0:
  237.2 73.8 reduce-scatter.1
where the time goes:
time: 324 us; the launch traced here: 323 us
  waiting for transfers between devices  122 us (38%)
  local copies, waits for them, and re-layouts  107 us (33%)
  matrix products  48 us (15%)
  other arithmetic  15.8 us (5%)
  starting transfers between devices  15 us (5%)
  between operations  14.3 us (4%)
    reduce_scatter x1, waiting for transfers between devices, body(): lax.psum_scatter(partial_value.astype(jnp.bfloat16), 'bands', scatter_dim...  74 us
    gather x8, local copies, waits for them, and re-layouts, one_block(): right = available[where_rows]  64.8 us
    ppermute x8, waiting for transfers between devices, shifted(): return lax.ppermute(value, axis, pairs)  48.1 us
    dot_general x8, matrix products, one_block(): jnp.einsum('sab,kcb->ksac', left, right, preferred_element_type=jnp.float32)  48 us
    ppermute x8, starting transfers between devices, shifted(): return lax.ppermute(value, axis, pairs)  15 us
    dynamic_update_slice x16, local copies, waits for them, and re-layouts, body(): partial_value = lax.map(one_block, (scaled, positions))  14.6 us
    gather x4, local copies, waits for them, and re-layouts, deliver(): return shifted(local_rows[asked], 'atoms', -offset)  12.2 us
    unnamed x8, local copies, waits for them, and re-layouts  9.58 us
  transfers between devices with their start and end apart: 9, of which 5 were waited for; matrix products, arithmetic and copies ran while one was open for 11% of the time, Pallas kernels for 0%

commit v1 on v0

v1 whole, which is shorter than its diff:
```python
import functools

import jax
import jax.numpy as jnp
from jax import lax
from jax.experimental import pallas as pl
from jax.experimental.pallas import tpu as pltpu
from jax.sharding import PartitionSpec as P

R = 2
VMEM_LIMIT = 48 * 1024 * 1024


def shifted(value, axis, steps):
    count = lax.axis_size(axis)
    pairs = [(source, (source + steps) % count) for source in range(count)]
    return lax.ppermute(value, axis, pairs)


def strip_target(group, chips, step, other_core):
    chip = lax.rem(lax.shift_right_logical(group, 1) + step, chips)
    return chip * 2 + ((group & 1) ^ other_core)


def to_strip_target(value, chips, step, other_core):
    pairs = [
        (group, (group // 2 + step) % chips * 2 + (group % 2 ^ other_core))
        for group in range(2 * chips)
    ]
    return lax.ppermute(value, "bands", pairs)


def pick_kernel(count, blocks, tile, place_ref, *refs):
    asks, (own, sib), outs = refs[:count], refs[count : count + 2], refs[count + 2 : -1]
    sems = refs[-1]
    first = place_ref[0] * blocks
    copies = []
    for index in range(count):
        ids = asks[index][...] - first
        mine = (ids >= 0) & (ids < blocks)
        lowest = jnp.min(jnp.where(mine, ids, blocks - 1))
        highest = jnp.max(jnp.where(mine, ids, 0))
        block = jnp.where(place_ref[1] == 0, lowest, highest)
        rows = pl.ds(pl.multiple_of(block * tile, tile), tile)
        for half, source in enumerate((own, sib)):
            copy = pltpu.make_async_copy(
                source.at[rows, :], outs[index].at[half], sems.at[index, half]
            )
            copy.start()
            copies.append(copy)
    for copy in copies:
        copy.wait()


def pick(place, asks, own, sib, tile):
    blocks, bands = asks[0].shape[0], own.shape[1]
    count = len(asks)
    return pl.pallas_call(
        functools.partial(pick_kernel, count, blocks, tile),
        out_shape=[jax.ShapeDtypeStruct((2, tile, bands), own.dtype)] * count,
        in_specs=[pl.BlockSpec(memory_space=pltpu.SMEM)]
        + [pl.BlockSpec(memory_space=pltpu.VMEM)] * count
        + [pl.BlockSpec(memory_space=pl.ANY)] * 2,
        out_specs=[pl.BlockSpec(memory_space=pl.ANY)] * count,
        scratch_shapes=[pltpu.SemaphoreType.DMA((count, 2))],
        name="pick_blocks",
        cost_estimate=pl.CostEstimate(
            flops=0, bytes_accessed=8 * count * tile * bands, transcendentals=0
        ),
    )(place, *asks, own, sib)


def tiles_kernel(n_right, n_strips, tile, place_ref, *refs):
    own, sib = refs[:2]
    rights = refs[2:4]
    weights = refs[4:6]
    outs = refs[6 : 6 + n_strips]
    scaled, total = refs[6 + n_strips :]
    strip = tile // n_strips
    n_left = own.shape[0] // tile

    @pl.when(pl.program_id(0) == 0)
    def _():
        for j in range(n_right):
            for half in range(2):
                block = rights[half][j * tile : (j + 1) * tile, :].astype(jnp.float32)
                for kind in range(2):
                    value = block * weights[half][kind : kind + 1, :]
                    scaled[j, half, kind * tile : (kind + 1) * tile, :] = value.astype(
                        scaled.dtype
                    )

    for j in range(n_right):
        contract = (((1,), (1,)), ((), ()))
        value = lax.dot_general(
            own[...], scaled[j, 0], contract, preferred_element_type=jnp.float32
        )
        value += lax.dot_general(
            sib[...], scaled[j, 1], contract, preferred_element_type=jnp.float32
        )
        total[...] = value
        for index in range(n_strips):
            start = place_ref[2 + index] * strip
            for i in range(n_left):
                rows = pl.ds(pl.multiple_of(i * tile + start, strip), strip)
                outs[index][j, i] = total[rows, :].astype(outs[index].dtype)


def tiles(place, own, sib, arrived, weights, n_strips, tile, step_blocks):
    rows, bands = own.shape
    n_right = rows // tile // 2 if arrived is None else 1
    blocks = rows // tile
    steps = blocks // step_blocks
    strip = tile // n_strips
    left = pl.BlockSpec((step_blocks * tile, bands), lambda i, place: (i, 0))
    if arrived is None:
        rights = [own, sib]
        right = pl.BlockSpec((n_right * tile, bands), lambda i, place: (place[1], 0))
        right_specs = [right, right]
    else:
        rights = [arrived, arrived]
        right_specs = [
            pl.BlockSpec((None, tile, bands), lambda i, place: (0, 0, 0)),
            pl.BlockSpec((None, tile, bands), lambda i, place: (1, 0, 0)),
        ]
    weight = pl.BlockSpec((2, bands), lambda i, place: (0, 0))
    return pl.pallas_call(
        functools.partial(tiles_kernel, n_right, n_strips, tile),
        out_shape=[
            jax.ShapeDtypeStruct((n_right, blocks, strip, 2 * tile), jnp.bfloat16)
        ]
        * n_strips,
        grid_spec=pltpu.PrefetchScalarGridSpec(
            num_scalar_prefetch=1,
            grid=(steps,),
            in_specs=[left, left] + right_specs + [weight, weight],
            out_specs=[
                pl.BlockSpec(
                    (n_right, step_blocks, strip, 2 * tile),
                    lambda i, place: (0, i, 0, 0),
                )
            ]
            * n_strips,
            scratch_shapes=[
                pltpu.VMEM((n_right, 2, 2 * tile, bands), jnp.bfloat16),
                pltpu.VMEM((step_blocks * tile, 2 * tile), jnp.float32),
            ],
        ),
        name="tiles",
        compiler_params=pltpu.CompilerParams(vmem_limit_bytes=VMEM_LIMIT),
        cost_estimate=pl.CostEstimate(
            flops=2 * rows * (n_right * 2 * tile) * 2 * bands,
            bytes_accessed=4 * rows * bands + 4 * n_right * tile * bands,
            transcendentals=0,
        ),
    )(place, own, sib, *rights, *weights)


def place_kernel(chips, sizes, tile, where_ref, *refs):
    n_chunks = len(sizes)
    per_core = sum(sizes)
    ins = refs[: 2 * chips * n_chunks]
    density, energy, pool = refs[2 * chips * n_chunks :]
    for other_core in range(2):
        first = 0
        for chunk in range(n_chunks):
            for j in range(sizes[chunk]):
                total = None
                for step in range(chips):
                    ref = ins[(step * 2 + other_core) * n_chunks + chunk]
                    value = ref[j, 0].astype(jnp.float32)
                    total = value if total is None else total + value
                pool[other_core * per_core + first + j] = total
            first += sizes[chunk]
    i = pl.program_id(0)
    for slot in range(density.shape[1]):
        where = where_ref[i, slot]
        density[0, slot] = pool[where, :, :tile]
        energy[0, slot] = pool[where, :, tile:]


def place_tiles(where, strips, chips, tile):
    sizes = [value.shape[0] for value in strips[0]]
    _, blocks, strip, width = strips[0][0].shape
    slots = where.shape[1]
    out = jax.ShapeDtypeStruct((blocks, slots, strip, tile), jnp.float32)
    flat = [value for group in strips for value in group]
    return pl.pallas_call(
        functools.partial(place_kernel, chips, sizes, tile),
        out_shape=[out, out],
        grid_spec=pltpu.PrefetchScalarGridSpec(
            num_scalar_prefetch=1,
            grid=(blocks,),
            in_specs=[
                pl.BlockSpec(
                    (value.shape[0], 1, strip, width), lambda i, where: (0, i, 0, 0)
                )
                for value in flat
            ],
            out_specs=[
                pl.BlockSpec((1, slots, strip, tile), lambda i, where: (i, 0, 0, 0))
            ]
            * 2,
            scratch_shapes=[pltpu.VMEM((2 * sum(sizes), strip, width), jnp.float32)],
        ),
        name="place_tiles",
        compiler_params=pltpu.CompilerParams(vmem_limit_bytes=VMEM_LIMIT),
        cost_estimate=pl.CostEstimate(
            flops=0,
            bytes_accessed=sum(2 * value.size for value in flat)
            + 8 * blocks * slots * strip * tile,
            transcendentals=0,
        ),
    )(where, *flat)


def body(eigvecs, occupations, energies, neighbours):
    n_atoms = lax.axis_size("atoms")
    n_bands = lax.axis_size("bands")
    chips = n_bands // 2
    own_index = lax.axis_index("atoms").astype(jnp.int32)
    group = lax.axis_index("bands").astype(jnp.int32)
    core = group & 1
    blocks = neighbours.shape[0]
    tile = eigvecs.shape[0] // blocks
    half_blocks = blocks // 2
    offsets = [-1, 1, 2, -2]

    asks = [shifted(neighbours, "atoms", offset) for offset in offsets]
    sib = to_strip_target(eigvecs, chips, 0, 1)
    own_weights = jnp.stack([occupations, occupations * energies], 0)
    sib_weights = to_strip_target(own_weights, chips, 0, 1)
    weights = (own_weights, sib_weights)

    targets = [
        strip_target(group, chips, step, other)
        for step in range(chips)
        for other in range(2)
    ]
    place = jnp.stack([own_index, core] + targets).astype(jnp.int32)

    near = pick(place, asks[:2], eigvecs, sib, tile)
    far = pick(place, asks[2:], eigvecs, sib, tile)
    arrived = [
        shifted(value, "atoms", -offset)
        for value, offset in zip(list(near) + list(far), offsets)
    ]

    def exchanged(parts):
        return [
            part if index == 0 else to_strip_target(part, chips, index // 2, index % 2)
            for index, part in enumerate(parts)
        ]

    chunks = [
        exchanged(
            tiles(place, eigvecs, sib, None, weights, n_bands, tile, 2)
        )
    ]
    for value in arrived:
        chunks.append(
            exchanged(
                tiles(place, eigvecs, sib, value, weights, n_bands, tile, 2)
            )
        )
    strips = [[chunk[index] for chunk in chunks] for index in range(n_bands)]

    owners = neighbours // blocks
    within = neighbours % blocks
    distance = (owners - own_index) % n_atoms
    spot = within % half_blocks
    side = within // half_blocks
    for index, offset in enumerate(offsets):
        from_it = distance == offset % n_atoms
        highest = jnp.max(jnp.where(from_it, within, -1))
        side = jnp.where(from_it, (within == highest).astype(jnp.int32), side)
        spot = jnp.where(from_it, half_blocks + index, spot)
    per_core = half_blocks + len(offsets)
    where = ((side + core) % 2) * per_core + spot
    density, energy = place_tiles(where.astype(jnp.int32), strips, chips, tile)
    return density, energy


def solution(mesh):
    return jax.shard_map(
        body,
        mesh=mesh,
        in_specs=(P("atoms", "bands"), P("bands"), P("bands"), P("atoms", None)),
        out_specs=(P("atoms", None, "bands", None), P("atoms", None, "bands", None)),
        check_vma=False,
    )
```

time: 324 us -> 275 us (0.85)
  Pallas kernels: 0 us -> 174 us
  local copies, waits for them, and re-layouts: 107 us -> 1.28 us
  waiting for transfers between devices: 122 us -> 65 us
  matrix products: 48 us -> 0 us
  starting transfers between devices: 15 us -> 29.7 us
  between operations: 14.3 us -> 0.8 us
  other arithmetic: 15.8 us -> 4 us
    pallas_call x0 -> x8, Pallas kernels: none -> 174 us  [the longest x2 131 us: pick(): pl.pallas_call(functools.partial(pick_kernel, count, blocks, tile), out_s...]
    gather x14 -> x0, local copies, waits for them, and re-layouts: 78.3 us -> none  [the longest x8 64.8 us: one_block(): right = available[where_rows]]
    reduce_scatter x1 -> x0, waiting for transfers between devices: 74 us -> none  [body(): lax.psum_scatter(partial_value.astype(jnp.bfloat16), 'bands', scatter_dim...]
    dot_general x8 -> x0, matrix products: 48 us -> none  [one_block(): jnp.einsum('sab,kcb->ksac', left, right, preferred_element_type=jnp.float32)]
    dynamic_update_slice x16 -> x0, local copies, waits for them, and re-layouts: 14.6 us -> none  [body(): partial_value = lax.map(one_block, (scaled, positions))]
    another operation x3 -> x1, other arithmetic: 12.4 us -> 0.02 us  [body(): own_weights = jnp.stack([occupations, occupations * energies], 0)]
    ppermute x0 -> x17, starting transfers between devices: none -> 11.1 us  [to_strip_target(): return lax.ppermute(value, 'bands', pairs)]
    ppermute x0 -> x17, waiting for transfers between devices: none -> 9.35 us  [to_strip_target(): return lax.ppermute(value, 'bands', pairs)]
  transfers between devices with their start and end apart: 9 -> 25, of which waited for: 5 -> 9; matrix products, arithmetic and copies ran while one was open for 11% -> 2% of each run, Pallas kernels for 0% -> 38%
where the time goes in v1:
time: 275 us
  Pallas kernels  174 us (63%)
  waiting for transfers between devices  65 us (24%)
  starting transfers between devices  29.7 us (11%)
  other arithmetic  4 us (1%)
    pallas_call x2, Pallas kernels, pick(): pl.pallas_call(functools.partial(pick_kernel, count, blocks, tile), out_s...  131 us
    ppermute x8, waiting for transfers between devices, shifted(): return lax.ppermute(value, axis, pairs)  55.6 us
    pallas_call x5, Pallas kernels, tiles(): pl.pallas_call(functools.partial(tiles_kernel, n_right, n_strips, tile),...  38.3 us
    ppermute x8, starting transfers between devices, shifted(): return lax.ppermute(value, axis, pairs)  18.6 us
    ppermute x17, starting transfers between devices, to_strip_target(): return lax.ppermute(value, 'bands', pairs)  11.1 us
    ppermute x17, waiting for transfers between devices, to_strip_target(): return lax.ppermute(value, 'bands', pairs)  9.35 us
  transfers between devices with their start and end apart: 25, of which 9 were waited for; matrix products, arithmetic and copies ran while one was open for 2% of the time, Pallas kernels for 38%

profile of v1, /device:TPU:0, one launch (start us, length us, event | category | flops | bytes accessed | tf_op | source)
XLA Modules:
  0.0 274.7 jit_solution(2150540730739616760)
XLA Ops:
  1.1 2.6 collective-permute-start.6
  3.8 2.1 collective-permute-start.7
  8.3 65.6 %pick_blocks.3 = (bf16[2,128,2048]{2,1,0:T(8,128)(2,1)}, bf16[2,128,2048]{2,1,0:T(8,128)(2,1)}) custom-call(s32[6]{0:T(128)} %stack.36.place_ref, s32[8,16]{1,0:T(8,128)} %copy-done.3, s32[8,16]{1,0:T(8,128)} %copy-done.4, bf16[1024,2048]{1,0:T(8,128)(2,1)} %refs_0_.9, bf16[1024,2048]{1,0:T(8,128)(2,1)} %collective-permute-done.refs_1_.refs_3_), custom_call_target="tpu_custom_call" | custom-call | bytes 4194304 | tf_op jit(solution)/shard_map/pick_blocks/pallas_call | solution.py:58
  73.9 5.0 %collective-permute-start.8 = (bf16[2,128,2048]{2,1,0:T(8,128)(2,1)}, bf16[2,128,2048]{2,1,0:T(8,128)(2,1)S(1)}, u32[]{:S(2)}, u32[]{:S(2)}) collective-permute-start(bf16[2,128,2048]{2,1,0:T(8,128)(2,1)} %get-tuple-element.31), channel_id=1, source_target_pairs={{0,24},{4,28},{8,0},{12,4},{16,8},{20,12},{24,16},{28,20},{1,25},{... | collective-permute-start | bytes 3145736 | tf_op jit(solution)/shard_map/ppermute | solution.py:17
  79.0 4.8 %collective-permute-start.2 = (s32[8,16]{1,0:T(8,128)S(1)}, s32[8,16]{1,0:T(8,128)S(1)}, u32[]{:S(2)}, u32[]{:S(2)}) collective-permute-start(s32[8,16]{1,0:T(8,128)S(1)} %copy-done.7), channel_id=1, source_target_pairs={{0,28},{4,0},{8,4},{12,8},{16,12},{20,16},{24,20},{28,24},{1,29},{... | collective-permute-start | bytes 1544 | tf_op jit(solution)/shard_map/ppermute | solution.py:17
  83.8 40.7 %collective-permute-done.2.refs_0_ = s32[8,16]{1,0:T(8,128)S(1)} collective-permute-done((s32[8,16]{1,0:T(8,128)S(1)}, s32[8,16]{1,0:T(8,128)S(1)}, u32[]{:S(2)}, u32[]{:S(2)}) %collective-permute-start.2) | collective-permute-done | bytes 544 | tf_op jit(solution)/shard_map/ppermute | solution.py:17
  124.5 1.7 collective-permute-done.3.refs_1_
  126.8 65.6 %pick_blocks.2 = (bf16[2,128,2048]{2,1,0:T(8,128)(2,1)}, bf16[2,128,2048]{2,1,0:T(8,128)(2,1)}) custom-call(s32[6]{0:T(128)} %stack.36.place_ref, s32[8,16]{1,0:T(8,128)} %copy-done.5, s32[8,16]{1,0:T(8,128)} %copy-done.6, bf16[1024,2048]{1,0:T(8,128)(2,1)} %refs_0_.9, bf16[1024,2048]{1,0:T(8,128)(2,1)} %collective-permute-done.refs_1_.refs_3_), custom_call_target="tpu_custom_call" | custom-call | bytes 4194304 | tf_op jit(solution)/shard_map/pick_blocks/pallas_call | solution.py:58
  192.4 4.0 %collective-permute-start.5 = (bf16[2,128,2048]{2,1,0:T(8,128)(2,1)}, bf16[2,128,2048]{2,1,0:T(8,128)(2,1)S(1)}, u32[]{:S(2)}, u32[]{:S(2)}) collective-permute-start(bf16[2,128,2048]{2,1,0:T(8,128)(2,1)} %get-tuple-element.29), channel_id=1, source_target_pairs={{0,28},{4,0},{8,4},{12,8},{16,12},{20,16},{24,20},{28,24},{1,29},{... | collective-permute-start | bytes 3145736 | tf_op jit(solution)/shard_map/ppermute | solution.py:17
  196.4 15.3 %tiles.5 = (bf16[4,8,32,256]{3,2,1,0:T(8,128)(2,1)S(1)}, bf16[4,8,32,256]{3,2,1,0:T(8,128)(2,1)S(1)}, bf16[4,8,32,256]{3,2,1,0:T(8,128)(2,1)S(1)}, bf16[4,8,32,256]{3,2,1,0:T(8,128)(2,1)S(1)}) custom-call(s32[6]{0:T(128)S(1)} %copy-done.1, bf16[1024,2048]{1,0:T(8,128)(2,1)} %refs_0_.9, bf16[1024,2048]{1,0:T(8,128)(2,1)} %collective-permute-done.refs_1_.refs_3_, ...), custom_call_target="tpu_custom_call" | custom-call | flops 8589934592 | bytes 12582912 | tf_op jit(solution)/shard_map/tiles/pallas_call | solution.py:127
  212.6 1.5 collective-permute-start.15
  214.5 5.8 %tiles.8 = (bf16[1,8,32,256]{3,2,1,0:T(8,128)(2,1)S(1)}, bf16[1,8,32,256]{3,2,1,0:T(8,128)(2,1)S(1)}, bf16[1,8,32,256]{3,2,1,0:T(8,128)(2,1)S(1)}, bf16[1,8,32,256]{3,2,1,0:T(8,128)(2,1)S(1)}) custom-call(s32[6]{0:T(128)S(1)} %copy-done.1, bf16[1024,2048]{1,0:T(8,128)(2,1)S(1)} %copy-done, bf16[1024,2048]{1,0:T(8,128)(2,1)} %collective-permute-done.refs_1_.refs_3_, ...), custom_call_target="tpu_custom_call" | custom-call | flops 2147483648 | bytes 9437184 | tf_op jit(solution)/shard_map/tiles/pallas_call | solution.py:127
  220.2 5.8 %tiles.9 = (bf16[1,8,32,256]{3,2,1,0:T(8,128)(2,1)S(1)}, bf16[1,8,32,256]{3,2,1,0:T(8,128)(2,1)S(1)}, bf16[1,8,32,256]{3,2,1,0:T(8,128)(2,1)S(1)}, bf16[1,8,32,256]{3,2,1,0:T(8,128)(2,1)S(1)}) custom-call(s32[6]{0:T(128)S(1)} %copy-done.1, bf16[1024,2048]{1,0:T(8,128)(2,1)S(1)} %copy-done, bf16[1024,2048]{1,0:T(8,128)(2,1)} %collective-permute-done.refs_1_.refs_3_, ...), custom_call_target="tpu_custom_call" | custom-call | flops 2147483648 | bytes 9437184 | tf_op jit(solution)/shard_map/tiles/pallas_call | solution.py:127
  226.3 12.8 %collective-permute-done.5.refs_2_.refs_3_ = bf16[2,128,2048]{2,1,0:T(8,128)(2,1)S(1)} collective-permute-done((bf16[2,128,2048]{2,1,0:T(8,128)(2,1)}, bf16[2,128,2048]{2,1,0:T(8,128)(2,1)S(1)}, u32[]{:S(2)}, u32[]{:S(2)}) %collective-permute-start.5) | collective-permute-done | bytes 1048608 | tf_op jit(solution)/shard_map/ppermute | solution.py:17
  239.2 5.8 %tiles.7 = (bf16[1,8,32,256]{3,2,1,0:T(8,128)(2,1)S(1)}, bf16[1,8,32,256]{3,2,1,0:T(8,128)(2,1)S(1)}, bf16[1,8,32,256]{3,2,1,0:T(8,128)(2,1)S(1)}, bf16[1,8,32,256]{3,2,1,0:T(8,128)(2,1)S(1)}) custom-call(s32[6]{0:T(128)S(1)} %copy-done.1, bf16[1024,2048]{1,0:T(8,128)(2,1)S(1)} %copy-done, bf16[1024,2048]{1,0:T(8,128)(2,1)} %collective-permute-done.refs_1_.refs_3_, ...), custom_call_target="tpu_custom_call" | custom-call | flops 2147483648 | bytes 9437184 | tf_op jit(solution)/shard_map/tiles/pallas_call | solution.py:127
  245.0 1.6 collective-permute-start.18
  248.8 5.8 %tiles.6 = (bf16[1,8,32,256]{3,2,1,0:T(8,128)(2,1)S(1)}, bf16[1,8,32,256]{3,2,1,0:T(8,128)(2,1)S(1)}, bf16[1,8,32,256]{3,2,1,0:T(8,128)(2,1)S(1)}, bf16[1,8,32,256]{3,2,1,0:T(8,128)(2,1)S(1)}) custom-call(s32[6]{0:T(128)S(1)} %copy-done.1, bf16[1024,2048]{1,0:T(8,128)(2,1)S(1)} %copy-done, bf16[1024,2048]{1,0:T(8,128)(2,1)} %collective-permute-done.refs_1_.refs_3_, ...), custom_call_target="tpu_custom_call" | custom-call | flops 2147483648 | bytes 9437184 | tf_op jit(solution)/shard_map/tiles/pallas_call | solution.py:127
  254.6 1.6 collective-permute-start.17
  257.1 1.9 collective-permute-done.24.refs_19_
  259.0 1.5 collective-permute-start.16
  260.9 2.5 fusion.9.where_ref
  264.6 3.6 %collective-permute-done.16.refs_11_ = bf16[1,8,32,256]{3,2,1,0:T(8,128)(2,1)S(1)} collective-permute-done((bf16[1,8,32,256]{3,2,1,0:T(8,128)(2,1)S(1)}, bf16[1,8,32,256]{3,2,1,0:T(8,128)(2,1)S(1)}, u32[]{:S(2)}, u32[]{:S(2)}) %collective-permute-start.16) | collective-permute-done | bytes 131104 | tf_op jit(solution)/shard_map/ppermute | solution.py:30
  268.2 2.0 collective-permute-done.21.refs_16_
  270.2 4.5 %place_tiles.1 = (f32[8,16,32,128]{3,2,1,0:T(8,128)}, f32[8,16,32,128]{3,2,1,0:T(8,128)}) custom-call(s32[8,16]{1,0:T(8,128)S(1)} %fusion.9.where_ref, bf16[4,8,32,256]{3,2,1,0:T(8,128)(2,1)S(1)} %get-tuple-element.26.refs_0_, bf16[1,8,32,256]{3,2,1,0:T(8,128)(2,1)S(1)} %get-tuple-element.28.refs_1_, bf16[1,8,32,256]{3,2,1,0:T(8,128)(2,1)S(1)} %get-tuple-element.30.refs_2_, ...), custom_call_target="tpu_custom_call" | custom-call | bytes 8388608 | tf_op jit(solution)/shard_map/place_tiles/pallas_call | solution.py:188
  (55 shorter events, 9.8 us)
Async XLA Ops:
  0.6 7.6 %collective-permute-start = (bf16[1024,2048]{1,0:T(8,128)(2,1)}, bf16[1024,2048]{1,0:T(8,128)(2,1)}, u32[]{:S(2)}, u32[]{:S(2)}) collective-permute-start(bf16[1024,2048]{1,0:T(8,128)(2,1)} %refs_0_.9), channel_id=1, source_target_pairs={{0,1},{1,0},{2,3},{3,2},{4,5},{5,4},{6,7},{7,6},{8,9},{9,8},{10,11... | collective-permute-start | bytes 12582920 | tf_op jit(solution)/shard_map/ppermute | solution.py:30
  1.1 6.5 %collective-permute-start.6 = (s32[8,16]{1,0:T(8,128)}, s32[8,16]{1,0:T(8,128)S(1)}, u32[]{:S(2)}, u32[]{:S(2)}) collective-permute-start(s32[8,16]{1,0:T(8,128)} %param.7), channel_id=1, source_target_pairs={{0,8},{4,12},{8,16},{12,20},{16,24},{20,28},{24,0},{28,4},{1,9},{5... | collective-permute-start | bytes 1544 | tf_op jit(solution)/shard_map/ppermute | solution.py:17
  73.9 138.7 %collective-permute-start.8 = (bf16[2,128,2048]{2,1,0:T(8,128)(2,1)}, bf16[2,128,2048]{2,1,0:T(8,128)(2,1)S(1)}, u32[]{:S(2)}, u32[]{:S(2)}) collective-permute-start(bf16[2,128,2048]{2,1,0:T(8,128)(2,1)} %get-tuple-element.31), channel_id=1, source_target_pairs={{0,24},{4,28},{8,0},{12,4},{16,8},{20,12},{24,16},{28,20},{1,25},{... | collective-permute-start | bytes 3145736 | tf_op jit(solution)/shard_map/ppermute | solution.py:17
  78.9 135.2 %collective-permute-start.9 = (bf16[2,128,2048]{2,1,0:T(8,128)(2,1)}, bf16[2,128,2048]{2,1,0:T(8,128)(2,1)S(1)}, u32[]{:S(2)}, u32[]{:S(2)}) collective-permute-start(bf16[2,128,2048]{2,1,0:T(8,128)(2,1)} %get-tuple-element.33), channel_id=1, source_target_pairs={{0,8},{4,12},{8,16},{12,20},{16,24},{20,28},{24,0},{28,4},{1,9},{5... | collective-permute-start | bytes 3145736 | tf_op jit(solution)/shard_map/ppermute | solution.py:17
  78.9 117.5 %collective-permute-start.1 = (f32[2,2048]{1,0:T(2,128)S(1)}, f32[2,2048]{1,0:T(2,128)S(1)}, u32[]{:S(2)}, u32[]{:S(2)}) collective-permute-start(f32[2,2048]{1,0:T(2,128)S(1)} %pad_maximum_fusion.refs_4_), channel_id=1, source_target_pairs={{0,1},{1,0},{2,3},{3,2},{4,5},{5,4},{6,7},{7,6},{8,9},{9,8},{10,11... | collective-permute-start | bytes 49160 | tf_op jit(solution)/shard_map/ppermute | solution.py:30
  79.0 45.5 %collective-permute-start.2 = (s32[8,16]{1,0:T(8,128)S(1)}, s32[8,16]{1,0:T(8,128)S(1)}, u32[]{:S(2)}, u32[]{:S(2)}) collective-permute-start(s32[8,16]{1,0:T(8,128)S(1)} %copy-done.7), channel_id=1, source_target_pairs={{0,28},{4,0},{8,4},{12,8},{16,12},{20,16},{24,20},{28,24},{1,29},{... | collective-permute-start | bytes 1544 | tf_op jit(solution)/shard_map/ppermute | solution.py:17
  83.8 42.4 %collective-permute-start.3 = (s32[8,16]{1,0:T(8,128)S(1)}, s32[8,16]{1,0:T(8,128)S(1)}, u32[]{:S(2)}, u32[]{:S(2)}) collective-permute-start(s32[8,16]{1,0:T(8,128)S(1)} %copy-done.7), channel_id=1, source_target_pairs={{0,4},{4,8},{8,12},{12,16},{16,20},{20,24},{24,28},{28,0},{1,5},{5... | collective-permute-start | bytes 1544 | tf_op jit(solution)/shard_map/ppermute | solution.py:17
  192.4 46.8 %collective-permute-start.5 = (bf16[2,128,2048]{2,1,0:T(8,128)(2,1)}, bf16[2,128,2048]{2,1,0:T(8,128)(2,1)S(1)}, u32[]{:S(2)}, u32[]{:S(2)}) collective-permute-start(bf16[2,128,2048]{2,1,0:T(8,128)(2,1)} %get-tuple-element.29), channel_id=1, source_target_pairs={{0,28},{4,0},{8,4},{12,8},{16,12},{20,16},{24,20},{28,24},{1,29},{... | collective-permute-start | bytes 3145736 | tf_op jit(solution)/shard_map/ppermute | solution.py:17
  196.4 50.6 %collective-permute-start.4 = (bf16[2,128,2048]{2,1,0:T(8,128)(2,1)}, bf16[2,128,2048]{2,1,0:T(8,128)(2,1)S(1)}, u32[]{:S(2)}, u32[]{:S(2)}) collective-permute-start(bf16[2,128,2048]{2,1,0:T(8,128)(2,1)} %get-tuple-element.27), channel_id=1, source_target_pairs={{0,4},{4,8},{8,12},{12,16},{16,20},{20,24},{24,28},{28,0},{1,5},{5... | collective-permute-start | bytes 3145736 | tf_op jit(solution)/shard_map/ppermute | solution.py:17
  211.8 14.2 %collective-permute-start.10 = (bf16[4,8,32,256]{3,2,1,0:T(8,128)(2,1)S(1)}, bf16[4,8,32,256]{3,2,1,0:T(8,128)(2,1)S(1)}, u32[]{:S(2)}, u32[]{:S(2)}) collective-permute-start(bf16[4,8,32,256]{3,2,1,0:T(8,128)(2,1)S(1)} %get-tuple-element.35), channel_id=1, source_target_pairs={{0,1},{1,0},{2,3},{3,2},{4,5},{5,4},{6,7},{7,6},{8,9},{9,8},{10,11... | collective-permute-start | bytes 1572872 | tf_op jit(solution)/shard_map/ppermute | solution.py:30
  212.6 32.4 %collective-permute-start.15 = (bf16[4,8,32,256]{3,2,1,0:T(8,128)(2,1)S(1)}, bf16[4,8,32,256]{3,2,1,0:T(8,128)(2,1)S(1)}, u32[]{:S(2)}, u32[]{:S(2)}) collective-permute-start(bf16[4,8,32,256]{3,2,1,0:T(8,128)(2,1)S(1)} %get-tuple-element.40), channel_id=1, source_target_pairs={{0,2},{1,3},{2,0},{3,1},{4,6},{5,7},{6,4},{7,5},{8,10},{9,11},{10,... | collective-permute-start | bytes 1572872 | tf_op jit(solution)/shard_map/ppermute | solution.py:30
  214.1 32.4 %collective-permute-start.20 = (bf16[4,8,32,256]{3,2,1,0:T(8,128)(2,1)S(1)}, bf16[4,8,32,256]{3,2,1,0:T(8,128)(2,1)S(1)}, u32[]{:S(2)}, u32[]{:S(2)}) collective-permute-start(bf16[4,8,32,256]{3,2,1,0:T(8,128)(2,1)S(1)} %get-tuple-element.45), channel_id=1, source_target_pairs={{0,3},{1,2},{2,1},{3,0},{4,7},{5,6},{6,5},{7,4},{8,11},{9,10},{10,... | collective-permute-start | bytes 1572872 | tf_op jit(solution)/shard_map/ppermute | solution.py:30
  226.0 22.2 %collective-permute-start.13 = (bf16[1,8,32,256]{3,2,1,0:T(8,128)(2,1)S(1)}, bf16[1,8,32,256]{3,2,1,0:T(8,128)(2,1)S(1)}, u32[]{:S(2)}, u32[]{:S(2)}) collective-permute-start(bf16[1,8,32,256]{3,2,1,0:T(8,128)(2,1)S(1)} %get-tuple-element.38), channel_id=1, source_target_pairs={{0,1},{1,0},{2,3},{3,2},{4,5},{5,4},{6,7},{7,6},{8,9},{9,8},{10,11... | collective-permute-start | bytes 393224 | tf_op jit(solution)/shard_map/ppermute | solution.py:30
  239.2 9.6 %collective-permute-start.14 = (bf16[1,8,32,256]{3,2,1,0:T(8,128)(2,1)S(1)}, bf16[1,8,32,256]{3,2,1,0:T(8,128)(2,1)S(1)}, u32[]{:S(2)}, u32[]{:S(2)}) collective-permute-start(bf16[1,8,32,256]{3,2,1,0:T(8,128)(2,1)S(1)} %get-tuple-element.39), channel_id=1, source_target_pairs={{0,1},{1,0},{2,3},{3,2},{4,5},{5,4},{6,7},{7,6},{8,9},{9,8},{10,11... | collective-permute-start | bytes 393224 | tf_op jit(solution)/shard_map/ppermute | solution.py:30
  245.0 9.6 %collective-permute-start.18 = (bf16[1,8,32,256]{3,2,1,0:T(8,128)(2,1)S(1)}, bf16[1,8,32,256]{3,2,1,0:T(8,128)(2,1)S(1)}, u32[]{:S(2)}, u32[]{:S(2)}) collective-permute-start(bf16[1,8,32,256]{3,2,1,0:T(8,128)(2,1)S(1)} %get-tuple-element.43), channel_id=1, source_target_pairs={{0,2},{1,3},{2,0},{3,1},{4,6},{5,7},{6,4},{7,5},{8,10},{9,11},{10,... | collective-permute-start | bytes 393224 | tf_op jit(solution)/shard_map/ppermute | solution.py:30
  246.6 9.6 %collective-permute-start.19 = (bf16[1,8,32,256]{3,2,1,0:T(8,128)(2,1)S(1)}, bf16[1,8,32,256]{3,2,1,0:T(8,128)(2,1)S(1)}, u32[]{:S(2)}, u32[]{:S(2)}) collective-permute-start(bf16[1,8,32,256]{3,2,1,0:T(8,128)(2,1)S(1)} %get-tuple-element.44), channel_id=1, source_target_pairs={{0,2},{1,3},{2,0},{3,1},{4,6},{5,7},{6,4},{7,5},{8,10},{9,11},{10,... | collective-permute-start | bytes 393224 | tf_op jit(solution)/shard_map/ppermute | solution.py:30
  247.1 9.5 %collective-permute-start.23 = (bf16[1,8,32,256]{3,2,1,0:T(8,128)(2,1)S(1)}, bf16[1,8,32,256]{3,2,1,0:T(8,128)(2,1)S(1)}, u32[]{:S(2)}, u32[]{:S(2)}) collective-permute-start(bf16[1,8,32,256]{3,2,1,0:T(8,128)(2,1)S(1)} %get-tuple-element.48), channel_id=1, source_target_pairs={{0,3},{1,2},{2,1},{3,0},{4,7},{5,6},{6,5},{7,4},{8,11},{9,10},{10,... | collective-permute-start | bytes 393224 | tf_op jit(solution)/shard_map/ppermute | solution.py:30
  248.2 10.8 %collective-permute-start.24 = (bf16[1,8,32,256]{3,2,1,0:T(8,128)(2,1)S(1)}, bf16[1,8,32,256]{3,2,1,0:T(8,128)(2,1)S(1)}, u32[]{:S(2)}, u32[]{:S(2)}) collective-permute-start(bf16[1,8,32,256]{3,2,1,0:T(8,128)(2,1)S(1)} %get-tuple-element.49), channel_id=1, source_target_pairs={{0,3},{1,2},{2,1},{3,0},{4,7},{5,6},{6,5},{7,4},{8,11},{9,10},{10,... | collective-permute-start | bytes 393224 | tf_op jit(solution)/shard_map/ppermute | solution.py:30
  248.8 11.7 %collective-permute-start.12 = (bf16[1,8,32,256]{3,2,1,0:T(8,128)(2,1)S(1)}, bf16[1,8,32,256]{3,2,1,0:T(8,128)(2,1)S(1)}, u32[]{:S(2)}, u32[]{:S(2)}) collective-permute-start(bf16[1,8,32,256]{3,2,1,0:T(8,128)(2,1)S(1)} %get-tuple-element.37), channel_id=1, source_target_pairs={{0,1},{1,0},{2,3},{3,2},{4,5},{5,4},{6,7},{7,6},{8,9},{9,8},{10,11... | collective-permute-start | bytes 393224 | tf_op jit(solution)/shard_map/ppermute | solution.py:30
  254.6 8.8 %collective-permute-start.17 = (bf16[1,8,32,256]{3,2,1,0:T(8,128)(2,1)S(1)}, bf16[1,8,32,256]{3,2,1,0:T(8,128)(2,1)S(1)}, u32[]{:S(2)}, u32[]{:S(2)}) collective-permute-start(bf16[1,8,32,256]{3,2,1,0:T(8,128)(2,1)S(1)} %get-tuple-element.42), channel_id=1, source_target_pairs={{0,2},{1,3},{2,0},{3,1},{4,6},{5,7},{6,4},{7,5},{8,10},{9,11},{10,... | collective-permute-start | bytes 393224 | tf_op jit(solution)/shard_map/ppermute | solution.py:30
  256.2 8.4 %collective-permute-start.22 = (bf16[1,8,32,256]{3,2,1,0:T(8,128)(2,1)S(1)}, bf16[1,8,32,256]{3,2,1,0:T(8,128)(2,1)S(1)}, u32[]{:S(2)}, u32[]{:S(2)}) collective-permute-start(bf16[1,8,32,256]{3,2,1,0:T(8,128)(2,1)S(1)} %get-tuple-element.47), channel_id=1, source_target_pairs={{0,3},{1,2},{2,1},{3,0},{4,7},{5,6},{6,5},{7,4},{8,11},{9,10},{10,... | collective-permute-start | bytes 393224 | tf_op jit(solution)/shard_map/ppermute | solution.py:30
  256.5 8.1 %collective-permute-start.11 = (bf16[1,8,32,256]{3,2,1,0:T(8,128)(2,1)S(1)}, bf16[1,8,32,256]{3,2,1,0:T(8,128)(2,1)S(1)}, u32[]{:S(2)}, u32[]{:S(2)}) collective-permute-start(bf16[1,8,32,256]{3,2,1,0:T(8,128)(2,1)S(1)} %get-tuple-element.36), channel_id=1, source_target_pairs={{0,1},{1,0},{2,3},{3,2},{4,5},{5,4},{6,7},{7,6},{8,9},{9,8},{10,11... | collective-permute-start | bytes 393224 | tf_op jit(solution)/shard_map/ppermute | solution.py:30
  259.0 9.2 %collective-permute-start.16 = (bf16[1,8,32,256]{3,2,1,0:T(8,128)(2,1)S(1)}, bf16[1,8,32,256]{3,2,1,0:T(8,128)(2,1)S(1)}, u32[]{:S(2)}, u32[]{:S(2)}) collective-permute-start(bf16[1,8,32,256]{3,2,1,0:T(8,128)(2,1)S(1)} %get-tuple-element.41), channel_id=1, source_target_pairs={{0,2},{1,3},{2,0},{3,1},{4,6},{5,7},{6,4},{7,5},{8,10},{9,11},{10,... | collective-permute-start | bytes 393224 | tf_op jit(solution)/shard_map/ppermute | solution.py:30
  260.5 9.7 %collective-permute-start.21 = (bf16[1,8,32,256]{3,2,1,0:T(8,128)(2,1)S(1)}, bf16[1,8,32,256]{3,2,1,0:T(8,128)(2,1)S(1)}, u32[]{:S(2)}, u32[]{:S(2)}) collective-permute-start(bf16[1,8,32,256]{3,2,1,0:T(8,128)(2,1)S(1)} %get-tuple-element.46), channel_id=1, source_target_pairs={{0,3},{1,2},{2,1},{3,0},{4,7},{5,6},{6,5},{7,4},{8,11},{9,10},{10,... | collective-permute-start | bytes 393224 | tf_op jit(solution)/shard_map/ppermute | solution.py:30
  (9 other events, 286.3 us)

commit v2 on v1

--- a/solution.py
+++ b/solution.py
@@ -8,7 +8,7 @@
 from jax.sharding import PartitionSpec as P
 
 R = 2
-VMEM_LIMIT = 48 * 1024 * 1024
+VMEM_LIMIT = 40 * 1024 * 1024
 
 
 def shifted(value, axis, steps):
@@ -61,99 +61,128 @@
         in_specs=[pl.BlockSpec(memory_space=pltpu.SMEM)]
         + [pl.BlockSpec(memory_space=pltpu.VMEM)] * count
         + [pl.BlockSpec(memory_space=pl.ANY)] * 2,
-        out_specs=[pl.BlockSpec(memory_space=pl.ANY)] * count,
+        out_specs=[pl.BlockSpec(memory_space=pltpu.VMEM)] * count,
         scratch_shapes=[pltpu.SemaphoreType.DMA((count, 2))],
         name="pick_blocks",
+        compiler_params=pltpu.CompilerParams(vmem_limit_bytes=VMEM_LIMIT),
         cost_estimate=pl.CostEstimate(
             flops=0, bytes_accessed=8 * count * tile * bands, transcendentals=0
         ),
     )(place, *asks, own, sib)
 
 
-def tiles_kernel(n_right, n_strips, tile, place_ref, *refs):
-    own, sib = refs[:2]
-    rights = refs[2:4]
-    weights = refs[4:6]
-    outs = refs[6 : 6 + n_strips]
-    scaled, total = refs[6 + n_strips :]
+def tiles_kernel(n_right, n_strips, tile, local, place_ref, *refs):
+    own, sib, own_weight, sib_weight = refs[:4]
+    refs = refs[4:]
+    arrived = None
+    if not local:
+        arrived, refs = refs[0], refs[1:]
+    outs, (scaled, total) = refs[:n_strips], refs[n_strips:]
     strip = tile // n_strips
     n_left = own.shape[0] // tile
-
-    @pl.when(pl.program_id(0) == 0)
+    step, n_steps = pl.program_id(0), pl.num_programs(0)
+
+    @pl.when(step == 0)
     def _():
+        total[...] = jnp.zeros_like(total)
+
+    def add(left, weight):
         for j in range(n_right):
-            for half in range(2):
-                block = rights[half][j * tile : (j + 1) * tile, :].astype(jnp.float32)
-                for kind in range(2):
-                    value = block * weights[half][kind : kind + 1, :]
-                    scaled[j, half, kind * tile : (kind + 1) * tile, :] = value.astype(
-                        scaled.dtype
-                    )
-
-    for j in range(n_right):
-        contract = (((1,), (1,)), ((), ()))
-        value = lax.dot_general(
-            own[...], scaled[j, 0], contract, preferred_element_type=jnp.float32
+            if local:
+                first = pl.multiple_of((place_ref[1] * n_right + j) * tile, tile)
+                block = left[pl.ds(first, tile), :]
+            else:
+                block = arrived[0]
+            block = block.astype(jnp.float32)
+            for kind in range(2):
+                rows = pl.ds((2 * j + kind) * tile, tile)
+                scaled[rows, :] = (block * weight[kind : kind + 1, :]).astype(scaled.dtype)
+        total[...] += lax.dot_general(
+            left[...],
+            scaled[...],
+            (((1,), (1,)), ((), ())),
+            preferred_element_type=jnp.float32,
         )
-        value += lax.dot_general(
-            sib[...], scaled[j, 1], contract, preferred_element_type=jnp.float32
-        )
-        total[...] = value
+
+    @pl.when(step < n_steps // 2)
+    def _():
+        add(own, own_weight)
+
+    @pl.when(step >= n_steps // 2)
+    def _():
+        add(sib, sib_weight)
+
+    @pl.when(step == n_steps - 1)
+    def _():
         for index in range(n_strips):
             start = place_ref[2 + index] * strip
             for i in range(n_left):
                 rows = pl.ds(pl.multiple_of(i * tile + start, strip), strip)
-                outs[index][j, i] = total[rows, :].astype(outs[index].dtype)
-
-
-def tiles(place, own, sib, arrived, weights, n_strips, tile, step_blocks):
+                for j in range(n_right):
+                    value = total[rows, 2 * tile * j : 2 * tile * (j + 1)]
+                    outs[index][j, i] = value.astype(outs[index].dtype)
+
+
+def tiles(place, own, sib, arrived, weights, n_strips, tile):
     rows, bands = own.shape
-    n_right = rows // tile // 2 if arrived is None else 1
+    local = arrived is None
     blocks = rows // tile
-    steps = blocks // step_blocks
+    n_right = blocks // 2 if local else 1
     strip = tile // n_strips
-    left = pl.BlockSpec((step_blocks * tile, bands), lambda i, place: (i, 0))
-    if arrived is None:
-        rights = [own, sib]
-        right = pl.BlockSpec((n_right * tile, bands), lambda i, place: (place[1], 0))
-        right_specs = [right, right]
-    else:
-        rights = [arrived, arrived]
-        right_specs = [
-            pl.BlockSpec((None, tile, bands), lambda i, place: (0, 0, 0)),
-            pl.BlockSpec((None, tile, bands), lambda i, place: (1, 0, 0)),
-        ]
-    weight = pl.BlockSpec((2, bands), lambda i, place: (0, 0))
+    depth = min(bands, 1024 if local else 512)
+    steps = bands // depth
+    width = n_right * 2 * tile
+
+    def first_half(s, place):
+        return 0, jnp.minimum(s, steps - 1)
+
+    def second_half(s, place):
+        return 0, jnp.maximum(s - steps, 0)
+
+    in_specs = [
+        pl.BlockSpec((rows, depth), first_half),
+        pl.BlockSpec((rows, depth), second_half),
+        pl.BlockSpec((2, depth), first_half),
+        pl.BlockSpec((2, depth), second_half),
+    ]
+    operands = [own, sib, *weights]
+    if not local:
+        in_specs.append(
+            pl.BlockSpec(
+                (1, tile, depth),
+                lambda s, place: (lax.div(s, steps), 0, lax.rem(s, steps)),
+            )
+        )
+        operands.append(arrived)
     return pl.pallas_call(
-        functools.partial(tiles_kernel, n_right, n_strips, tile),
+        functools.partial(tiles_kernel, n_right, n_strips, tile, local),
         out_shape=[
             jax.ShapeDtypeStruct((n_right, blocks, strip, 2 * tile), jnp.bfloat16)
         ]
         * n_strips,
         grid_spec=pltpu.PrefetchScalarGridSpec(
             num_scalar_prefetch=1,
-            grid=(steps,),
-            in_specs=[left, left] + right_specs + [weight, weight],
+            grid=(2 * steps,),
+            in_specs=in_specs,
             out_specs=[
                 pl.BlockSpec(
-                    (n_right, step_blocks, strip, 2 * tile),
-                    lambda i, place: (0, i, 0, 0),
+                    (n_right, blocks, strip, 2 * tile), lambda s, place: (0, 0, 0, 0)
                 )
             ]
             * n_strips,
             scratch_shapes=[
-                pltpu.VMEM((n_right, 2, 2 * tile, bands), jnp.bfloat16),
-                pltpu.VMEM((step_blocks * tile, 2 * tile), jnp.float32),
+                pltpu.VMEM((width, depth), jnp.bfloat16),
+                pltpu.VMEM((rows, width), jnp.float32),
             ],
         ),
         name="tiles",
         compiler_params=pltpu.CompilerParams(vmem_limit_bytes=VMEM_LIMIT),
         cost_estimate=pl.CostEstimate(
-            flops=2 * rows * (n_right * 2 * tile) * 2 * bands,
-            bytes_accessed=4 * rows * bands + 4 * n_right * tile * bands,
+            flops=2 * rows * width * 2 * bands,
+            bytes_accessed=4 * rows * bands + 4 * tile * bands,
             transcendentals=0,
         ),
-    )(place, own, sib, *rights, *weights)
+    )(place, *operands)
 
 
 def place_kernel(chips, sizes, tile, where_ref, *refs):
@@ -239,45 +268,48 @@
     ]
     place = jnp.stack([own_index, core] + targets).astype(jnp.int32)
 
-    near = pick(place, asks[:2], eigvecs, sib, tile)
-    far = pick(place, asks[2:], eigvecs, sib, tile)
+    picked = pick(place, asks, eigvecs, sib, tile)
     arrived = [
         shifted(value, "atoms", -offset)
-        for value, offset in zip(list(near) + list(far), offsets)
-    ]
-
-    def exchanged(parts):
-        return [
-            part if index == 0 else to_strip_target(part, chips, index // 2, index % 2)
-            for index, part in enumerate(parts)
-        ]
-
-    chunks = [
-        exchanged(
-            tiles(place, eigvecs, sib, None, weights, n_bands, tile, 2)
-        )
-    ]
-    for value in arrived:
-        chunks.append(
-            exchanged(
-                tiles(place, eigvecs, sib, value, weights, n_bands, tile, 2)
-            )
-        )
-    strips = [[chunk[index] for chunk in chunks] for index in range(n_bands)]
-
-    owners = neighbours // blocks
-    within = neighbours % blocks
-    distance = (owners - own_index) % n_atoms
-    spot = within % half_blocks
-    side = within // half_blocks
+        for value, offset in zip(picked[:3], offsets[:3])
+    ]
+    *arrived[:2], last = lax.optimization_barrier((*arrived[:2], picked[3]))
+    arrived.append(shifted(last, "atoms", -offsets[3]))
+
+    owners = lax.div(neighbours, blocks)
+    within = lax.rem(neighbours, blocks)
+    distance = lax.rem(owners - own_index + n_atoms, n_atoms)
+    spot = lax.rem(within, half_blocks)
+    side = lax.div(within, half_blocks)
     for index, offset in enumerate(offsets):
         from_it = distance == offset % n_atoms
         highest = jnp.max(jnp.where(from_it, within, -1))
         side = jnp.where(from_it, (within == highest).astype(jnp.int32), side)
         spot = jnp.where(from_it, half_blocks + index, spot)
     per_core = half_blocks + len(offsets)
-    where = ((side + core) % 2) * per_core + spot
-    density, energy = place_tiles(where.astype(jnp.int32), strips, chips, tile)
+    where = (side ^ core) * per_core + spot
+    where, place = lax.optimization_barrier((where.astype(jnp.int32), place))
+
+    def exchanged(parts):
+        return [
+            part if index == 0 else to_strip_target(part, chips, index // 2, index % 2)
+            for index, part in enumerate(parts)
+        ]
+
+    chunks = [
+        exchanged(
+            tiles(place, eigvecs, sib, None, weights, n_bands, tile)
+        )
+    ]
+    for value in arrived:
+        chunks.append(
+            exchanged(
+                tiles(place, eigvecs, sib, value, weights, n_bands, tile)
+            )
+        )
+    strips = [[chunk[index] for chunk in chunks] for index in range(n_bands)]
+
+    density, energy = place_tiles(where, strips, chips, tile)
     return density, energy
 
 

time: 275 us -> 134 us (0.49)
  Pallas kernels: 174 us -> 50.6 us
  waiting for transfers between devices: 65 us -> 49.5 us
  starting transfers between devices: 29.7 us -> 26.4 us
    pallas_call x2 -> x1, Pallas kernels: 131 us -> 2.72 us  [pick(): pl.pallas_call(functools.partial(pick_kernel, count, blocks, tile), out_s...]
    ppermute x8, waiting for transfers between devices: 55.6 us -> 40.2 us  [shifted(): return lax.ppermute(value, axis, pairs)]
    pallas_call x5, Pallas kernels: 38.3 us -> 43.5 us  [tiles(): pl.pallas_call(functools.partial(tiles_kernel, n_right, n_strips, tile, l...]
    ppermute x8, starting transfers between devices: 18.6 us -> 15.3 us  [shifted(): return lax.ppermute(value, axis, pairs)]
  transfers between devices with their start and end apart: 25 -> 25, of which waited for: 9 -> 7; matrix products, arithmetic and copies ran while one was open for 2% -> 3% of each run, Pallas kernels for 38% -> 33%
where the time goes in v2:
time: 134 us; the launch traced here: 133 us
  Pallas kernels  50.6 us (38%)
  waiting for transfers between devices  49.5 us (37%)
  starting transfers between devices  26.4 us (20%)
  other arithmetic  3.32 us (2%)
  local copies, waits for them, and re-layouts  2.28 us (2%)
    pallas_call x5, Pallas kernels, tiles(): pl.pallas_call(functools.partial(tiles_kernel, n_right, n_strips, tile, l...  43.5 us
    ppermute x8, waiting for transfers between devices, shifted(): return lax.ppermute(value, axis, pairs)  40.2 us
    ppermute x8, starting transfers between devices, shifted(): return lax.ppermute(value, axis, pairs)  15.3 us
    ppermute x17, starting transfers between devices, to_strip_target(): return lax.ppermute(value, 'bands', pairs)  11.1 us
    ppermute x17, waiting for transfers between devices, to_strip_target(): return lax.ppermute(value, 'bands', pairs)  9.27 us
    pallas_call x1, Pallas kernels, place_tiles(): pl.pallas_call(functools.partial(place_kernel, chips, sizes, tile), out_s...  4.46 us
    pallas_call x1, Pallas kernels, pick(): pl.pallas_call(functools.partial(pick_kernel, count, blocks, tile), out_s...  2.72 us
  transfers between devices with their start and end apart: 25, of which 7 were waited for; matrix products, arithmetic and copies ran while one was open for 3% of the time, Pallas kernels for 33%

profile of v2, /device:TPU:0, one launch (start us, length us, event | category | flops | bytes accessed | tf_op | source)
XLA Modules:
  0.0 132.9 jit_solution(13703574243637265282)
XLA Ops:
  1.1 5.6 %collective-permute-start.2 = (s32[8,16]{1,0:T(8,128)}, s32[8,16]{1,0:T(8,128)S(1)}, u32[]{:S(2)}, u32[]{:S(2)}) collective-permute-start(s32[8,16]{1,0:T(8,128)} %param.7), channel_id=1, source_target_pairs={{0,28},{4,0},{8,4},{12,8},{16,12},{20,16},{24,20},{28,24},{1,29},{... | collective-permute-start | bytes 1544 | tf_op jit(solution)/shard_map/ppermute | solution.py:17
  6.7 3.8 %collective-permute-start.5 = (s32[8,16]{1,0:T(8,128)}, s32[8,16]{1,0:T(8,128)S(1)}, u32[]{:S(2)}, u32[]{:S(2)}) collective-permute-start(s32[8,16]{1,0:T(8,128)} %param.7), channel_id=1, source_target_pairs={{0,24},{4,28},{8,0},{12,4},{16,8},{20,12},{24,16},{28,20},{1,25},{... | collective-permute-start | bytes 1544 | tf_op jit(solution)/shard_map/ppermute | solution.py:17
  10.7 2.6 %collective-permute-done.3.refs_1_ = s32[8,16]{1,0:T(8,128)S(1)} collective-permute-done((s32[8,16]{1,0:T(8,128)}, s32[8,16]{1,0:T(8,128)S(1)}, u32[]{:S(2)}, u32[]{:S(2)}) %collective-permute-start.3) | collective-permute-done | bytes 544 | tf_op jit(solution)/shard_map/ppermute | solution.py:17
  13.3 2.2 %copy-done = bf16[1024,2048]{1,0:T(8,128)(2,1)S(1)} copy-done((bf16[1024,2048]{1,0:T(8,128)(2,1)S(1)}, bf16[1024,2048]{1,0:T(8,128)(2,1)}, u32[]{:S(2)}) %copy-start) | copy-done | bytes 4194328
  15.5 2.7 %pick_blocks.1 = (bf16[2,128,2048]{2,1,0:T(8,128)(2,1)S(1)}, bf16[2,128,2048]{2,1,0:T(8,128)(2,1)S(1)}, bf16[2,128,2048]{2,1,0:T(8,128)(2,1)S(1)}, bf16[2,128,2048]{2,1,0:T(8,128)(2,1)S(1)}) custom-call(s32[6]{0:T(128)S(1)} %stack.36.place_ref, s32[8,16]{1,0:T(8,128)S(1)} %collective-permute-done.2.refs_0_, s32[8,16]{1,0:T(8,128)S(1)} %collective-permute-done.3.refs_1_, ...), custom_call_target="tpu_custom_call" | custom-call | bytes 8388608 | tf_op jit(solution)/shard_map/pick_blocks/pallas_call | solution.py:58
  18.9 4.1 %collective-permute-start.7 = (bf16[2,128,2048]{2,1,0:T(8,128)(2,1)S(1)}, bf16[2,128,2048]{2,1,0:T(8,128)(2,1)S(1)}, u32[]{:S(2)}, u32[]{:S(2)}) collective-permute-start(bf16[2,128,2048]{2,1,0:T(8,128)(2,1)S(1)} %get-tuple-element.35), channel_id=1, source_target_pairs={{0,28},{4,0},{8,4},{12,8},{16,12},{20,16},{24,20},{28,24},{1,29},{... | collective-permute-start | bytes 3145736 | tf_op jit(solution)/shard_map/ppermute | solution.py:17
  23.9 1.1 collective-permute-start.8
  25.0 2.5 %fusion.9.where_ref = s32[8,16]{1,0:T(8,128)S(1)} fusion(pred[8,16]{1,0:T(8,128)(4,1)S(1)} %get-tuple-element.67, pred[8,16]{1,0:T(8,128)(4,1)S(1)} %get-tuple-element.66, pred[8,16]{1,0:T(8,128)(4,1)S(1)} %get-tuple-element.65, pred[8,16]{1,0:T(8,128)(4,1)S(1)} %get-tuple-element.64, s32[]{:T(128)} %and.14, s32[]{:T(128)} %get-tuple-element.62, ...), kind=kLoop, calls=%fused_computation.18 | loop fusion | flops 4352 | bytes 1556 | tf_op jit(solution)/shard_map/add | solution.py:290
  27.5 35.4 %collective-permute-done.6.refs_4_ = bf16[2,128,2048]{2,1,0:T(8,128)(2,1)S(1)} collective-permute-done((bf16[2,128,2048]{2,1,0:T(8,128)(2,1)S(1)}, bf16[2,128,2048]{2,1,0:T(8,128)(2,1)S(1)}, u32[]{:S(2)}, u32[]{:S(2)}) %collective-permute-start.6) | collective-permute-done | bytes 1048608 | tf_op jit(solution)/shard_map/ppermute | solution.py:17
  62.9 2.2 %collective-permute-done.7.refs_4_ = bf16[2,128,2048]{2,1,0:T(8,128)(2,1)S(1)} collective-permute-done((bf16[2,128,2048]{2,1,0:T(8,128)(2,1)S(1)}, bf16[2,128,2048]{2,1,0:T(8,128)(2,1)S(1)}, u32[]{:S(2)}, u32[]{:S(2)}) %collective-permute-start.7) | collective-permute-done | bytes 1048608 | tf_op jit(solution)/shard_map/ppermute | solution.py:17
  65.1 12.4 %tiles.5 = (bf16[4,8,32,256]{3,2,1,0:T(8,128)(2,1)S(1)}, bf16[4,8,32,256]{3,2,1,0:T(8,128)(2,1)S(1)}, bf16[4,8,32,256]{3,2,1,0:T(8,128)(2,1)S(1)}, bf16[4,8,32,256]{3,2,1,0:T(8,128)(2,1)S(1)}) custom-call(s32[6]{0:T(128)S(1)} %stack.36.place_ref, bf16[1024,2048]{1,0:T(8,128)(2,1)S(1)} %copy-done, bf16[1024,2048]{1,0:T(8,128)(2,1)} %collective-permute-done.refs_1_.refs_5_, ...), custom_call_target="tpu_custom_call" | custom-call | flops 8589934592 | bytes 9437184 | tf_op jit(solution)/shard_map/tiles/pallas_call | solution.py:157
  77.6 1.6 %collective-permute-start.15 = (bf16[4,8,32,256]{3,2,1,0:T(8,128)(2,1)S(1)}, bf16[4,8,32,256]{3,2,1,0:T(8,128)(2,1)S(1)}, u32[]{:S(2)}, u32[]{:S(2)}) collective-permute-start(bf16[4,8,32,256]{3,2,1,0:T(8,128)(2,1)S(1)} %get-tuple-element.50), channel_id=1, source_target_pairs={{0,2},{1,3},{2,0},{3,1},{4,6},{5,7},{6,4},{7,5},{8,10},{9,11},{10,... | collective-permute-start | bytes 1572872 | tf_op jit(solution)/shard_map/ppermute | solution.py:30
  79.5 7.8 %tiles.8 = (bf16[1,8,32,256]{3,2,1,0:T(8,128)(2,1)S(1)}, bf16[1,8,32,256]{3,2,1,0:T(8,128)(2,1)S(1)}, bf16[1,8,32,256]{3,2,1,0:T(8,128)(2,1)S(1)}, bf16[1,8,32,256]{3,2,1,0:T(8,128)(2,1)S(1)}) custom-call(s32[6]{0:T(128)S(1)} %stack.36.place_ref, bf16[1024,2048]{1,0:T(8,128)(2,1)S(1)} %copy-done, bf16[1024,2048]{1,0:T(8,128)(2,1)} %collective-permute-done.refs_1_.refs_5_, ...), custom_call_target="tpu_custom_call" | custom-call | flops 2147483648 | bytes 9437184 | tf_op jit(solution)/shard_map/tiles/pallas_call | solution.py:157
  87.7 7.8 %tiles.7 = (bf16[1,8,32,256]{3,2,1,0:T(8,128)(2,1)S(1)}, bf16[1,8,32,256]{3,2,1,0:T(8,128)(2,1)S(1)}, bf16[1,8,32,256]{3,2,1,0:T(8,128)(2,1)S(1)}, bf16[1,8,32,256]{3,2,1,0:T(8,128)(2,1)S(1)}) custom-call(s32[6]{0:T(128)S(1)} %stack.36.place_ref, bf16[1024,2048]{1,0:T(8,128)(2,1)S(1)} %copy-done, bf16[1024,2048]{1,0:T(8,128)(2,1)} %collective-permute-done.refs_1_.refs_5_, ...), custom_call_target="tpu_custom_call" | custom-call | flops 2147483648 | bytes 9437184 | tf_op jit(solution)/shard_map/tiles/pallas_call | solution.py:157
  95.4 1.6 %collective-permute-start.18 = (bf16[1,8,32,256]{3,2,1,0:T(8,128)(2,1)S(1)}, bf16[1,8,32,256]{3,2,1,0:T(8,128)(2,1)S(1)}, u32[]{:S(2)}, u32[]{:S(2)}) collective-permute-start(bf16[1,8,32,256]{3,2,1,0:T(8,128)(2,1)S(1)} %get-tuple-element.53), channel_id=1, source_target_pairs={{0,2},{1,3},{2,0},{3,1},{4,6},{5,7},{6,4},{7,5},{8,10},{9,11},{10,... | collective-permute-start | bytes 393224 | tf_op jit(solution)/shard_map/ppermute | solution.py:30
  97.0 7.8 %tiles.6 = (bf16[1,8,32,256]{3,2,1,0:T(8,128)(2,1)S(1)}, bf16[1,8,32,256]{3,2,1,0:T(8,128)(2,1)S(1)}, bf16[1,8,32,256]{3,2,1,0:T(8,128)(2,1)S(1)}, bf16[1,8,32,256]{3,2,1,0:T(8,128)(2,1)S(1)}) custom-call(s32[6]{0:T(128)S(1)} %stack.36.place_ref, bf16[1024,2048]{1,0:T(8,128)(2,1)S(1)} %copy-done, bf16[1024,2048]{1,0:T(8,128)(2,1)} %collective-permute-done.refs_1_.refs_5_, ...), custom_call_target="tpu_custom_call" | custom-call | flops 2147483648 | bytes 9437184 | tf_op jit(solution)/shard_map/tiles/pallas_call | solution.py:157
  105.5 1.5 %collective-permute-start.17 = (bf16[1,8,32,256]{3,2,1,0:T(8,128)(2,1)S(1)}, bf16[1,8,32,256]{3,2,1,0:T(8,128)(2,1)S(1)}, u32[]{:S(2)}, u32[]{:S(2)}) collective-permute-start(bf16[1,8,32,256]{3,2,1,0:T(8,128)(2,1)S(1)} %get-tuple-element.52), channel_id=1, source_target_pairs={{0,2},{1,3},{2,0},{3,1},{4,6},{5,7},{6,4},{7,5},{8,10},{9,11},{10,... | collective-permute-start | bytes 393224 | tf_op jit(solution)/shard_map/ppermute | solution.py:30
  107.7 7.8 %tiles.9 = (bf16[1,8,32,256]{3,2,1,0:T(8,128)(2,1)S(1)}, bf16[1,8,32,256]{3,2,1,0:T(8,128)(2,1)S(1)}, bf16[1,8,32,256]{3,2,1,0:T(8,128)(2,1)S(1)}, bf16[1,8,32,256]{3,2,1,0:T(8,128)(2,1)S(1)}) custom-call(s32[6]{0:T(128)S(1)} %stack.36.place_ref, bf16[1024,2048]{1,0:T(8,128)(2,1)S(1)} %copy-done, bf16[1024,2048]{1,0:T(8,128)(2,1)} %collective-permute-done.refs_1_.refs_5_, ...), custom_call_target="tpu_custom_call" | custom-call | flops 2147483648 | bytes 9437184 | tf_op jit(solution)/shard_map/tiles/pallas_call | solution.py:157
  115.4 1.6 %collective-permute-start.16 = (bf16[1,8,32,256]{3,2,1,0:T(8,128)(2,1)S(1)}, bf16[1,8,32,256]{3,2,1,0:T(8,128)(2,1)S(1)}, u32[]{:S(2)}, u32[]{:S(2)}) collective-permute-start(bf16[1,8,32,256]{3,2,1,0:T(8,128)(2,1)S(1)} %get-tuple-element.51), channel_id=1, source_target_pairs={{0,2},{1,3},{2,0},{3,1},{4,6},{5,7},{6,4},{7,5},{8,10},{9,11},{10,... | collective-permute-start | bytes 393224 | tf_op jit(solution)/shard_map/ppermute | solution.py:30
  117.7 1.5 %collective-permute-start.19 = (bf16[1,8,32,256]{3,2,1,0:T(8,128)(2,1)S(1)}, bf16[1,8,32,256]{3,2,1,0:T(8,128)(2,1)S(1)}, u32[]{:S(2)}, u32[]{:S(2)}) collective-permute-start(bf16[1,8,32,256]{3,2,1,0:T(8,128)(2,1)S(1)} %get-tuple-element.54), channel_id=1, source_target_pairs={{0,2},{1,3},{2,0},{3,1},{4,6},{5,7},{6,4},{7,5},{8,10},{9,11},{10,... | collective-permute-start | bytes 393224 | tf_op jit(solution)/shard_map/ppermute | solution.py:30
  119.2 2.6 %collective-permute-done.16.refs_11_ = bf16[1,8,32,256]{3,2,1,0:T(8,128)(2,1)S(1)} collective-permute-done((bf16[1,8,32,256]{3,2,1,0:T(8,128)(2,1)S(1)}, bf16[1,8,32,256]{3,2,1,0:T(8,128)(2,1)S(1)}, u32[]{:S(2)}, u32[]{:S(2)}) %collective-permute-start.16) | collective-permute-done | bytes 131104 | tf_op jit(solution)/shard_map/ppermute | solution.py:30
  121.8 1.9 %collective-permute-done.21.refs_16_ = bf16[1,8,32,256]{3,2,1,0:T(8,128)(2,1)S(1)} collective-permute-done((bf16[1,8,32,256]{3,2,1,0:T(8,128)(2,1)S(1)}, bf16[1,8,32,256]{3,2,1,0:T(8,128)(2,1)S(1)}, u32[]{:S(2)}, u32[]{:S(2)}) %collective-permute-start.21) | collective-permute-done | bytes 131104 | tf_op jit(solution)/shard_map/ppermute | solution.py:30
  123.7 3.7 %collective-permute-done.19.refs_14_ = bf16[1,8,32,256]{3,2,1,0:T(8,128)(2,1)S(1)} collective-permute-done((bf16[1,8,32,256]{3,2,1,0:T(8,128)(2,1)S(1)}, bf16[1,8,32,256]{3,2,1,0:T(8,128)(2,1)S(1)}, u32[]{:S(2)}, u32[]{:S(2)}) %collective-permute-start.19) | collective-permute-done | bytes 131104 | tf_op jit(solution)/shard_map/ppermute | solution.py:30
  128.4 4.5 %place_tiles.1 = (f32[8,16,32,128]{3,2,1,0:T(8,128)}, f32[8,16,32,128]{3,2,1,0:T(8,128)}) custom-call(s32[8,16]{1,0:T(8,128)S(1)} %fusion.9.where_ref, bf16[4,8,32,256]{3,2,1,0:T(8,128)(2,1)S(1)} %get-tuple-element.33.refs_0_, bf16[1,8,32,256]{3,2,1,0:T(8,128)(2,1)S(1)} %get-tuple-element.38.refs_1_, bf16[1,8,32,256]{3,2,1,0:T(8,128)(2,1)S(1)} %get-tuple-element.40.refs_2_, ...), custom_call_target="tpu_custom_call" | custom-call | bytes 8388608 | tf_op jit(solution)/shard_map/place_tiles/pallas_call | solution.py:217
  (46 shorter events, 5.8 us)
Async XLA Ops:
  0.6 12.6 %collective-permute-start = (bf16[1024,2048]{1,0:T(8,128)(2,1)}, bf16[1024,2048]{1,0:T(8,128)(2,1)}, u32[]{:S(2)}, u32[]{:S(2)}) collective-permute-start(bf16[1024,2048]{1,0:T(8,128)(2,1)} %refs_0_.9), channel_id=1, source_target_pairs={{0,1},{1,0},{2,3},{3,2},{4,5},{5,4},{6,7},{7,6},{8,9},{9,8},{10,11... | collective-permute-start | bytes 12582920 | tf_op jit(solution)/shard_map/ppermute | solution.py:30
  1.1 9.5 %collective-permute-start.2 = (s32[8,16]{1,0:T(8,128)}, s32[8,16]{1,0:T(8,128)S(1)}, u32[]{:S(2)}, u32[]{:S(2)}) collective-permute-start(s32[8,16]{1,0:T(8,128)} %param.7), channel_id=1, source_target_pairs={{0,28},{4,0},{8,4},{12,8},{16,12},{20,16},{24,20},{28,24},{1,29},{... | collective-permute-start | bytes 1544 | tf_op jit(solution)/shard_map/ppermute | solution.py:17
  6.7 6.5 %collective-permute-start.3 = (s32[8,16]{1,0:T(8,128)}, s32[8,16]{1,0:T(8,128)S(1)}, u32[]{:S(2)}, u32[]{:S(2)}) collective-permute-start(s32[8,16]{1,0:T(8,128)} %param.7), channel_id=1, source_target_pairs={{0,4},{4,8},{8,12},{12,16},{16,20},{20,24},{24,28},{28,0},{1,5},{5... | collective-permute-start | bytes 1544 | tf_op jit(solution)/shard_map/ppermute | solution.py:17
  6.7 6.5 %collective-permute-start.4 = (s32[8,16]{1,0:T(8,128)}, s32[8,16]{1,0:T(8,128)S(1)}, u32[]{:S(2)}, u32[]{:S(2)}) collective-permute-start(s32[8,16]{1,0:T(8,128)} %param.7), channel_id=1, source_target_pairs={{0,8},{4,12},{8,16},{12,20},{16,24},{20,28},{24,0},{28,4},{1,9},{5... | collective-permute-start | bytes 1544 | tf_op jit(solution)/shard_map/ppermute | solution.py:17
  6.7 6.5 %collective-permute-start.5 = (s32[8,16]{1,0:T(8,128)}, s32[8,16]{1,0:T(8,128)S(1)}, u32[]{:S(2)}, u32[]{:S(2)}) collective-permute-start(s32[8,16]{1,0:T(8,128)} %param.7), channel_id=1, source_target_pairs={{0,24},{4,28},{8,0},{12,4},{16,8},{20,12},{24,16},{28,20},{1,25},{... | collective-permute-start | bytes 1544 | tf_op jit(solution)/shard_map/ppermute | solution.py:17
  18.2 44.7 %collective-permute-start.6 = (bf16[2,128,2048]{2,1,0:T(8,128)(2,1)S(1)}, bf16[2,128,2048]{2,1,0:T(8,128)(2,1)S(1)}, u32[]{:S(2)}, u32[]{:S(2)}) collective-permute-start(bf16[2,128,2048]{2,1,0:T(8,128)(2,1)S(1)} %get-tuple-element.34), channel_id=1, source_target_pairs={{0,4},{4,8},{8,12},{12,16},{16,20},{20,24},{24,28},{28,0},{1,5},{5... | collective-permute-start | bytes 3145736 | tf_op jit(solution)/shard_map/ppermute | solution.py:17
  18.9 46.3 %collective-permute-start.7 = (bf16[2,128,2048]{2,1,0:T(8,128)(2,1)S(1)}, bf16[2,128,2048]{2,1,0:T(8,128)(2,1)S(1)}, u32[]{:S(2)}, u32[]{:S(2)}) collective-permute-start(bf16[2,128,2048]{2,1,0:T(8,128)(2,1)S(1)} %get-tuple-element.35), channel_id=1, source_target_pairs={{0,28},{4,0},{8,4},{12,8},{16,12},{20,16},{24,20},{28,24},{1,29},{... | collective-permute-start | bytes 3145736 | tf_op jit(solution)/shard_map/ppermute | solution.py:17
  23.0 42.1 %collective-permute-start.1 = (f32[2,2048]{1,0:T(2,128)S(1)}, f32[2,2048]{1,0:T(2,128)S(1)}, u32[]{:S(2)}, u32[]{:S(2)}) collective-permute-start(f32[2,2048]{1,0:T(2,128)S(1)} %pad_maximum_fusion.refs_2_), channel_id=1, source_target_pairs={{0,1},{1,0},{2,3},{3,2},{4,5},{5,4},{6,7},{7,6},{8,9},{9,8},{10,11... | collective-permute-start | bytes 49160 | tf_op jit(solution)/shard_map/ppermute | solution.py:30
  23.9 55.6 %collective-permute-start.8 = (bf16[2,128,2048]{2,1,0:T(8,128)(2,1)S(1)}, bf16[2,128,2048]{2,1,0:T(8,128)(2,1)S(1)}, u32[]{:S(2)}, u32[]{:S(2)}) collective-permute-start(bf16[2,128,2048]{2,1,0:T(8,128)(2,1)S(1)} %get-tuple-element.41), channel_id=1, source_target_pairs={{0,24},{4,28},{8,0},{12,4},{16,8},{20,12},{24,16},{28,20},{1,25},{... | collective-permute-start | bytes 3145736 | tf_op jit(solution)/shard_map/ppermute | solution.py:17
  65.1 41.9 %collective-permute-start.9 = (bf16[2,128,2048]{2,1,0:T(8,128)(2,1)S(1)}, bf16[2,128,2048]{2,1,0:T(8,128)(2,1)S(1)}, u32[]{:S(2)}, u32[]{:S(2)}) collective-permute-start(bf16[2,128,2048]{2,1,0:T(8,128)(2,1)S(1)} %get-tuple-element.43), channel_id=1, source_target_pairs={{0,8},{4,12},{8,16},{12,20},{16,24},{20,28},{24,0},{28,4},{1,9},{5... | collective-permute-start | bytes 3145736 | tf_op jit(solution)/shard_map/ppermute | solution.py:17
  77.5 17.9 %collective-permute-start.10 = (bf16[4,8,32,256]{3,2,1,0:T(8,128)(2,1)S(1)}, bf16[4,8,32,256]{3,2,1,0:T(8,128)(2,1)S(1)}, u32[]{:S(2)}, u32[]{:S(2)}) collective-permute-start(bf16[4,8,32,256]{3,2,1,0:T(8,128)(2,1)S(1)} %get-tuple-element.45), channel_id=1, source_target_pairs={{0,1},{1,0},{2,3},{3,2},{4,5},{5,4},{6,7},{7,6},{8,9},{9,8},{10,11... | collective-permute-start | bytes 1572872 | tf_op jit(solution)/shard_map/ppermute | solution.py:30
  77.6 27.2 %collective-permute-start.15 = (bf16[4,8,32,256]{3,2,1,0:T(8,128)(2,1)S(1)}, bf16[4,8,32,256]{3,2,1,0:T(8,128)(2,1)S(1)}, u32[]{:S(2)}, u32[]{:S(2)}) collective-permute-start(bf16[4,8,32,256]{3,2,1,0:T(8,128)(2,1)S(1)} %get-tuple-element.50), channel_id=1, source_target_pairs={{0,2},{1,3},{2,0},{3,1},{4,6},{5,7},{6,4},{7,5},{8,10},{9,11},{10,... | collective-permute-start | bytes 1572872 | tf_op jit(solution)/shard_map/ppermute | solution.py:30
  79.2 25.7 %collective-permute-start.20 = (bf16[4,8,32,256]{3,2,1,0:T(8,128)(2,1)S(1)}, bf16[4,8,32,256]{3,2,1,0:T(8,128)(2,1)S(1)}, u32[]{:S(2)}, u32[]{:S(2)}) collective-permute-start(bf16[4,8,32,256]{3,2,1,0:T(8,128)(2,1)S(1)} %get-tuple-element.55), channel_id=1, source_target_pairs={{0,3},{1,2},{2,1},{3,0},{4,7},{5,6},{6,5},{7,4},{8,11},{9,10},{10,... | collective-permute-start | bytes 1572872 | tf_op jit(solution)/shard_map/ppermute | solution.py:30
  87.3 18.2 %collective-permute-start.13 = (bf16[1,8,32,256]{3,2,1,0:T(8,128)(2,1)S(1)}, bf16[1,8,32,256]{3,2,1,0:T(8,128)(2,1)S(1)}, u32[]{:S(2)}, u32[]{:S(2)}) collective-permute-start(bf16[1,8,32,256]{3,2,1,0:T(8,128)(2,1)S(1)} %get-tuple-element.48), channel_id=1, source_target_pairs={{0,1},{1,0},{2,3},{3,2},{4,5},{5,4},{6,7},{7,6},{8,9},{9,8},{10,11... | collective-permute-start | bytes 393224 | tf_op jit(solution)/shard_map/ppermute | solution.py:30
  95.4 11.6 %collective-permute-start.18 = (bf16[1,8,32,256]{3,2,1,0:T(8,128)(2,1)S(1)}, bf16[1,8,32,256]{3,2,1,0:T(8,128)(2,1)S(1)}, u32[]{:S(2)}, u32[]{:S(2)}) collective-permute-start(bf16[1,8,32,256]{3,2,1,0:T(8,128)(2,1)S(1)} %get-tuple-element.53), channel_id=1, source_target_pairs={{0,2},{1,3},{2,0},{3,1},{4,6},{5,7},{6,4},{7,5},{8,10},{9,11},{10,... | collective-permute-start | bytes 393224 | tf_op jit(solution)/shard_map/ppermute | solution.py:30
  104.8 10.6 %collective-permute-start.23 = (bf16[1,8,32,256]{3,2,1,0:T(8,128)(2,1)S(1)}, bf16[1,8,32,256]{3,2,1,0:T(8,128)(2,1)S(1)}, u32[]{:S(2)}, u32[]{:S(2)}) collective-permute-start(bf16[1,8,32,256]{3,2,1,0:T(8,128)(2,1)S(1)} %get-tuple-element.58), channel_id=1, source_target_pairs={{0,3},{1,2},{2,1},{3,0},{4,7},{5,6},{6,5},{7,4},{8,11},{9,10},{10,... | collective-permute-start | bytes 393224 | tf_op jit(solution)/shard_map/ppermute | solution.py:30
  104.9 12.1 %collective-permute-start.12 = (bf16[1,8,32,256]{3,2,1,0:T(8,128)(2,1)S(1)}, bf16[1,8,32,256]{3,2,1,0:T(8,128)(2,1)S(1)}, u32[]{:S(2)}, u32[]{:S(2)}) collective-permute-start(bf16[1,8,32,256]{3,2,1,0:T(8,128)(2,1)S(1)} %get-tuple-element.47), channel_id=1, source_target_pairs={{0,1},{1,0},{2,3},{3,2},{4,5},{5,4},{6,7},{7,6},{8,9},{9,8},{10,11... | collective-permute-start | bytes 393224 | tf_op jit(solution)/shard_map/ppermute | solution.py:30
  105.5 11.5 %collective-permute-start.17 = (bf16[1,8,32,256]{3,2,1,0:T(8,128)(2,1)S(1)}, bf16[1,8,32,256]{3,2,1,0:T(8,128)(2,1)S(1)}, u32[]{:S(2)}, u32[]{:S(2)}) collective-permute-start(bf16[1,8,32,256]{3,2,1,0:T(8,128)(2,1)S(1)} %get-tuple-element.52), channel_id=1, source_target_pairs={{0,2},{1,3},{2,0},{3,1},{4,6},{5,7},{6,4},{7,5},{8,10},{9,11},{10,... | collective-permute-start | bytes 393224 | tf_op jit(solution)/shard_map/ppermute | solution.py:30
  107.0 10.6 %collective-permute-start.22 = (bf16[1,8,32,256]{3,2,1,0:T(8,128)(2,1)S(1)}, bf16[1,8,32,256]{3,2,1,0:T(8,128)(2,1)S(1)}, u32[]{:S(2)}, u32[]{:S(2)}) collective-permute-start(bf16[1,8,32,256]{3,2,1,0:T(8,128)(2,1)S(1)} %get-tuple-element.57), channel_id=1, source_target_pairs={{0,3},{1,2},{2,1},{3,0},{4,7},{5,6},{6,5},{7,4},{8,11},{9,10},{10,... | collective-permute-start | bytes 393224 | tf_op jit(solution)/shard_map/ppermute | solution.py:30
  107.0 12.1 %collective-permute-start.11 = (bf16[1,8,32,256]{3,2,1,0:T(8,128)(2,1)S(1)}, bf16[1,8,32,256]{3,2,1,0:T(8,128)(2,1)S(1)}, u32[]{:S(2)}, u32[]{:S(2)}) collective-permute-start(bf16[1,8,32,256]{3,2,1,0:T(8,128)(2,1)S(1)} %get-tuple-element.46), channel_id=1, source_target_pairs={{0,1},{1,0},{2,3},{3,2},{4,5},{5,4},{6,7},{7,6},{8,9},{9,8},{10,11... | collective-permute-start | bytes 393224 | tf_op jit(solution)/shard_map/ppermute | solution.py:30
  117.0 6.7 %collective-permute-start.21 = (bf16[1,8,32,256]{3,2,1,0:T(8,128)(2,1)S(1)}, bf16[1,8,32,256]{3,2,1,0:T(8,128)(2,1)S(1)}, u32[]{:S(2)}, u32[]{:S(2)}) collective-permute-start(bf16[1,8,32,256]{3,2,1,0:T(8,128)(2,1)S(1)} %get-tuple-element.56), channel_id=1, source_target_pairs={{0,3},{1,2},{2,1},{3,0},{4,7},{5,6},{6,5},{7,4},{8,11},{9,10},{10,... | collective-permute-start | bytes 393224 | tf_op jit(solution)/shard_map/ppermute | solution.py:30
  117.0 6.7 %collective-permute-start.14 = (bf16[1,8,32,256]{3,2,1,0:T(8,128)(2,1)S(1)}, bf16[1,8,32,256]{3,2,1,0:T(8,128)(2,1)S(1)}, u32[]{:S(2)}, u32[]{:S(2)}) collective-permute-start(bf16[1,8,32,256]{3,2,1,0:T(8,128)(2,1)S(1)} %get-tuple-element.49), channel_id=1, source_target_pairs={{0,1},{1,0},{2,3},{3,2},{4,5},{5,4},{6,7},{7,6},{8,9},{9,8},{10,11... | collective-permute-start | bytes 393224 | tf_op jit(solution)/shard_map/ppermute | solution.py:30
  117.7 9.8 %collective-permute-start.19 = (bf16[1,8,32,256]{3,2,1,0:T(8,128)(2,1)S(1)}, bf16[1,8,32,256]{3,2,1,0:T(8,128)(2,1)S(1)}, u32[]{:S(2)}, u32[]{:S(2)}) collective-permute-start(bf16[1,8,32,256]{3,2,1,0:T(8,128)(2,1)S(1)} %get-tuple-element.54), channel_id=1, source_target_pairs={{0,2},{1,3},{2,0},{3,1},{4,6},{5,7},{6,4},{7,5},{8,10},{9,11},{10,... | collective-permute-start | bytes 393224 | tf_op jit(solution)/shard_map/ppermute | solution.py:30
  119.2 9.2 %collective-permute-start.24 = (bf16[1,8,32,256]{3,2,1,0:T(8,128)(2,1)S(1)}, bf16[1,8,32,256]{3,2,1,0:T(8,128)(2,1)S(1)}, u32[]{:S(2)}, u32[]{:S(2)}) collective-permute-start(bf16[1,8,32,256]{3,2,1,0:T(8,128)(2,1)S(1)} %get-tuple-element.59), channel_id=1, source_target_pairs={{0,3},{1,2},{2,1},{3,0},{4,7},{5,6},{6,5},{7,4},{8,11},{9,10},{10,... | collective-permute-start | bytes 393224 | tf_op jit(solution)/shard_map/ppermute | solution.py:30
  (5 other events, 36.1 us)

commit v3 on v2

--- a/solution.py
+++ b/solution.py
@@ -8,7 +8,8 @@
 from jax.sharding import PartitionSpec as P
 
 R = 2
-VMEM_LIMIT = 40 * 1024 * 1024
+VMEM_LIMIT = 24 * 1024 * 1024
+PICK_VMEM_LIMIT = 24 * 1024 * 1024
 
 
 def shifted(value, axis, steps):
@@ -48,141 +49,100 @@
             )
             copy.start()
             copies.append(copy)
+    if len(outs) > count:
+        copy = pltpu.make_async_copy(own, outs[count], sems.at[count, 0])
+        copy.start()
+        copies.append(copy)
     for copy in copies:
         copy.wait()
 
 
-def pick(place, asks, own, sib, tile):
+def pick(place, asks, own, sib, tile, keep_own):
     blocks, bands = asks[0].shape[0], own.shape[1]
     count = len(asks)
+    out_shape = [jax.ShapeDtypeStruct((2, tile, bands), own.dtype)] * count
+    if keep_own:
+        out_shape.append(jax.ShapeDtypeStruct(own.shape, own.dtype))
     return pl.pallas_call(
         functools.partial(pick_kernel, count, blocks, tile),
-        out_shape=[jax.ShapeDtypeStruct((2, tile, bands), own.dtype)] * count,
+        out_shape=out_shape,
         in_specs=[pl.BlockSpec(memory_space=pltpu.SMEM)]
         + [pl.BlockSpec(memory_space=pltpu.VMEM)] * count
         + [pl.BlockSpec(memory_space=pl.ANY)] * 2,
-        out_specs=[pl.BlockSpec(memory_space=pltpu.VMEM)] * count,
-        scratch_shapes=[pltpu.SemaphoreType.DMA((count, 2))],
+        out_specs=[pl.BlockSpec(memory_space=pltpu.VMEM)] * len(out_shape),
+        scratch_shapes=[pltpu.SemaphoreType.DMA((count + 1, 2))],
         name="pick_blocks",
-        compiler_params=pltpu.CompilerParams(vmem_limit_bytes=VMEM_LIMIT),
+        compiler_params=pltpu.CompilerParams(vmem_limit_bytes=PICK_VMEM_LIMIT),
         cost_estimate=pl.CostEstimate(
             flops=0, bytes_accessed=8 * count * tile * bands, transcendentals=0
         ),
     )(place, *asks, own, sib)
 
 
-def tiles_kernel(n_right, n_strips, tile, local, place_ref, *refs):
-    own, sib, own_weight, sib_weight = refs[:4]
-    refs = refs[4:]
-    arrived = None
-    if not local:
-        arrived, refs = refs[0], refs[1:]
+def tiles_kernel(n_arrived, n_right, n_strips, tile, place_ref, *refs):
+    lefts, weights = refs[:2], refs[2:4]
+    arrived, refs = refs[4 : 4 + n_arrived], refs[4 + n_arrived :]
     outs, (scaled, total) = refs[:n_strips], refs[n_strips:]
     strip = tile // n_strips
-    n_left = own.shape[0] // tile
-    step, n_steps = pl.program_id(0), pl.num_programs(0)
-
-    @pl.when(step == 0)
-    def _():
-        total[...] = jnp.zeros_like(total)
-
-    def add(left, weight):
-        for j in range(n_right):
-            if local:
-                first = pl.multiple_of((place_ref[1] * n_right + j) * tile, tile)
-                block = left[pl.ds(first, tile), :]
+    n_left = lefts[0].shape[0] // tile
+    for j in range(n_right):
+        slot = j % 2
+        for half in range(2):
+            if n_arrived:
+                block = arrived[j][half]
             else:
-                block = arrived[0]
+                first = pl.multiple_of((place_ref[0] * n_right + j) * tile, tile)
+                block = lefts[half][pl.ds(first, tile), :]
             block = block.astype(jnp.float32)
             for kind in range(2):
-                rows = pl.ds((2 * j + kind) * tile, tile)
-                scaled[rows, :] = (block * weight[kind : kind + 1, :]).astype(scaled.dtype)
-        total[...] += lax.dot_general(
-            left[...],
-            scaled[...],
-            (((1,), (1,)), ((), ())),
-            preferred_element_type=jnp.float32,
-        )
-
-    @pl.when(step < n_steps // 2)
-    def _():
-        add(own, own_weight)
-
-    @pl.when(step >= n_steps // 2)
-    def _():
-        add(sib, sib_weight)
-
-    @pl.when(step == n_steps - 1)
-    def _():
+                value = block * weights[half][kind : kind + 1, :]
+                rows = pl.ds(kind * tile, tile)
+                scaled[slot, half, rows, :] = value.astype(scaled.dtype)
+        for half in range(2):
+            value = lax.dot_general(
+                lefts[half][...],
+                scaled[slot, half],
+                (((1,), (1,)), ((), ())),
+                preferred_element_type=jnp.float32,
+            )
+            if half == 0:
+                total[slot] = value
+            else:
+                total[slot] += value
         for index in range(n_strips):
-            start = place_ref[2 + index] * strip
+            start = place_ref[1 + index] * strip
             for i in range(n_left):
                 rows = pl.ds(pl.multiple_of(i * tile + start, strip), strip)
-                for j in range(n_right):
-                    value = total[rows, 2 * tile * j : 2 * tile * (j + 1)]
-                    outs[index][j, i] = value.astype(outs[index].dtype)
+                outs[index][j, i] = total[slot, rows, :].astype(outs[index].dtype)
 
 
 def tiles(place, own, sib, arrived, weights, n_strips, tile):
     rows, bands = own.shape
-    local = arrived is None
     blocks = rows // tile
-    n_right = blocks // 2 if local else 1
+    n_right = len(arrived) if arrived else blocks // 2
     strip = tile // n_strips
-    depth = min(bands, 1024 if local else 512)
-    steps = bands // depth
-    width = n_right * 2 * tile
-
-    def first_half(s, place):
-        return 0, jnp.minimum(s, steps - 1)
-
-    def second_half(s, place):
-        return 0, jnp.maximum(s - steps, 0)
-
-    in_specs = [
-        pl.BlockSpec((rows, depth), first_half),
-        pl.BlockSpec((rows, depth), second_half),
-        pl.BlockSpec((2, depth), first_half),
-        pl.BlockSpec((2, depth), second_half),
-    ]
-    operands = [own, sib, *weights]
-    if not local:
-        in_specs.append(
-            pl.BlockSpec(
-                (1, tile, depth),
-                lambda s, place: (lax.div(s, steps), 0, lax.rem(s, steps)),
-            )
-        )
-        operands.append(arrived)
+    slots = min(n_right, 2)
+    vmem = pl.BlockSpec(memory_space=pltpu.VMEM)
     return pl.pallas_call(
-        functools.partial(tiles_kernel, n_right, n_strips, tile, local),
+        functools.partial(tiles_kernel, len(arrived), n_right, n_strips, tile),
         out_shape=[
             jax.ShapeDtypeStruct((n_right, blocks, strip, 2 * tile), jnp.bfloat16)
         ]
         * n_strips,
-        grid_spec=pltpu.PrefetchScalarGridSpec(
-            num_scalar_prefetch=1,
-            grid=(2 * steps,),
-            in_specs=in_specs,
-            out_specs=[
-                pl.BlockSpec(
-                    (n_right, blocks, strip, 2 * tile), lambda s, place: (0, 0, 0, 0)
-                )
-            ]
-            * n_strips,
-            scratch_shapes=[
-                pltpu.VMEM((width, depth), jnp.bfloat16),
-                pltpu.VMEM((rows, width), jnp.float32),
-            ],
-        ),
+        in_specs=[pl.BlockSpec(memory_space=pltpu.SMEM)] + [vmem] * (4 + len(arrived)),
+        out_specs=[vmem] * n_strips,
+        scratch_shapes=[
+            pltpu.VMEM((slots, 2, 2 * tile, bands), jnp.bfloat16),
+            pltpu.VMEM((slots, rows, 2 * tile), jnp.float32),
+        ],
         name="tiles",
         compiler_params=pltpu.CompilerParams(vmem_limit_bytes=VMEM_LIMIT),
         cost_estimate=pl.CostEstimate(
-            flops=2 * rows * width * 2 * bands,
-            bytes_accessed=4 * rows * bands + 4 * tile * bands,
+            flops=2 * rows * n_right * 2 * tile * 2 * bands,
+            bytes_accessed=4 * rows * bands + 4 * n_right * tile * bands,
             transcendentals=0,
         ),
-    )(place, *operands)
+    )(place, own, sib, *weights, *arrived)
 
 
 def place_kernel(chips, sizes, tile, where_ref, *refs):
@@ -266,15 +226,15 @@
         for step in range(chips)
         for other in range(2)
     ]
-    place = jnp.stack([own_index, core] + targets).astype(jnp.int32)
-
-    picked = pick(place, asks, eigvecs, sib, tile)
-    arrived = [
-        shifted(value, "atoms", -offset)
-        for value, offset in zip(picked[:3], offsets[:3])
-    ]
-    *arrived[:2], last = lax.optimization_barrier((*arrived[:2], picked[3]))
-    arrived.append(shifted(last, "atoms", -offsets[3]))
+    here = jnp.stack([own_index, core]).astype(jnp.int32)
+    place = jnp.stack([core] + targets).astype(jnp.int32)
+
+    near = list(pick(here, asks[:2], eigvecs, sib, tile, False))
+    here, near[0] = lax.optimization_barrier((here, near[0]))
+    far = list(pick(here, asks[2:], eigvecs, sib, tile, True))
+    own = far.pop()
+    near = [shifted(near[0], "atoms", -offsets[0]), shifted(near[1], "atoms", -offsets[1])]
+    third = shifted(far[0], "atoms", -offsets[2])
 
     owners = lax.div(neighbours, blocks)
     within = lax.rem(neighbours, blocks)
@@ -296,17 +256,19 @@
             for index, part in enumerate(parts)
         ]
 
-    chunks = [
-        exchanged(
-            tiles(place, eigvecs, sib, None, weights, n_bands, tile)
-        )
-    ]
-    for value in arrived:
-        chunks.append(
-            exchanged(
-                tiles(place, eigvecs, sib, value, weights, n_bands, tile)
-            )
-        )
+    def strips_of(*arrived):
+        return exchanged(tiles(place, own, sib, arrived, weights, n_bands, tile))
+
+    chunks = [strips_of()]
+    *near, source, chunks[0][:3] = lax.optimization_barrier(
+        (*near, far[1], chunks[0][:3])
+    )
+    fourth = shifted(source, "atoms", -offsets[3])
+    chunks.append(strips_of(*near))
+    third, chunks[1][0] = lax.optimization_barrier((third, chunks[1][0]))
+    chunks.append(strips_of(third))
+    fourth, chunks[1], chunks[2][:3] = lax.optimization_barrier((fourth, chunks[1], chunks[2][:3]))
+    chunks.append(strips_of(fourth))
     strips = [[chunk[index] for chunk in chunks] for index in range(n_bands)]
 
     density, energy = place_tiles(where, strips, chips, tile)

time: 134 us -> 124 us (0.925)
  Pallas kernels: 50.6 us -> 36.7 us
  waiting for transfers between devices: 49.5 us -> 52.6 us
  other arithmetic: 3.32 us -> 6.32 us
  starting transfers between devices: 26.4 us -> 24.9 us
    ppermute x17 -> x14, waiting for transfers between devices: 9.27 us -> 36.7 us  [to_strip_target(): return lax.ppermute(value, 'bands', pairs)]
    ppermute x8, waiting for transfers between devices: 40.2 us -> 15.9 us  [shifted(): return lax.ppermute(value, axis, pairs)]
    pallas_call x5 -> x4, Pallas kernels: 43.5 us -> 27.5 us  [tiles(): pl.pallas_call(functools.partial(tiles_kernel, len(arrived), n_right, n_s...]
    pallas_call x1 -> x2, Pallas kernels: 2.72 us -> 4.57 us  [pick(): pl.pallas_call(functools.partial(pick_kernel, count, blocks, tile), out_s...]
    ppermute x17 -> x14, starting transfers between devices: 11.1 us -> 10.1 us  [to_strip_target(): return lax.ppermute(value, 'bands', pairs)]
  transfers between devices with their start and end apart: 25 -> 22, of which waited for: 7 -> 11; matrix products, arithmetic and copies ran while one was open for 3% -> 5% of each run, Pallas kernels for 33% -> 26%
where the time goes in v3:
time: 124 us
  waiting for transfers between devices  52.6 us (42%)
  Pallas kernels  36.7 us (30%)
  starting transfers between devices  24.9 us (20%)
  other arithmetic  6.32 us (5%)
  local copies, waits for them, and re-layouts  2.27 us (2%)
    ppermute x14, waiting for transfers between devices, to_strip_target(): return lax.ppermute(value, 'bands', pairs)  36.7 us
    pallas_call x4, Pallas kernels, tiles(): pl.pallas_call(functools.partial(tiles_kernel, len(arrived), n_right, n_s...  27.5 us
    ppermute x8, waiting for transfers between devices, shifted(): return lax.ppermute(value, axis, pairs)  15.9 us
    ppermute x8, starting transfers between devices, shifted(): return lax.ppermute(value, axis, pairs)  14.8 us
    ppermute x14, starting transfers between devices, to_strip_target(): return lax.ppermute(value, 'bands', pairs)  10.1 us
    pallas_call x2, Pallas kernels, pick(): pl.pallas_call(functools.partial(pick_kernel, count, blocks, tile), out_s...  4.57 us
    pallas_call x1, Pallas kernels, place_tiles(): pl.pallas_call(functools.partial(place_kernel, chips, sizes, tile), out_s...  4.57 us
    add x1, other arithmetic, body(): where = (side ^ core) * per_core + spot  3.35 us
  transfers between devices with their start and end apart: 22, of which 11 were waited for; matrix products, arithmetic and copies ran while one was open for 5% of the time, Pallas kernels for 26%

profile of v3, /device:TPU:0, one launch (start us, length us, event | category | flops | bytes accessed | tf_op | source)
XLA Modules:
  0.0 123.5 jit_solution(15054576427200235519)
XLA Ops:
  1.1 5.6 %collective-permute-start = (s32[8,16]{1,0:T(8,128)}, s32[8,16]{1,0:T(8,128)S(1)}, u32[]{:S(2)}, u32[]{:S(2)}) collective-permute-start(s32[8,16]{1,0:T(8,128)} %param.7), channel_id=1, source_target_pairs={{0,28},{4,0},{8,4},{12,8},{16,12},{20,16},{24,20},{28,24},{1,29},{... | collective-permute-start | bytes 1544 | tf_op jit(solution)/shard_map/ppermute | solution.py:18
  10.8 3.3 %fusion.9.where_ref = s32[8,16]{1,0:T(8,128)S(1)} fusion(pred[8,16]{1,0:T(8,128)(4,1)S(1)} %get-tuple-element.91, pred[8,16]{1,0:T(8,128)(4,1)S(1)} %get-tuple-element.90, pred[8,16]{1,0:T(8,128)(4,1)S(1)} %get-tuple-element.89, pred[8,16]{1,0:T(8,128)(4,1)S(1)} %get-tuple-element.88, s32[]{:T(128)} %and.14, s32[]{:T(128)} %get-tuple-element.86, ...), kind=kLoop, calls=%fused_computation.18 | loop fusion | flops 4352 | bytes 1556 | tf_op jit(solution)/shard_map/add | solution.py:250
  15.3 2.2 %copy-done = bf16[1024,2048]{1,0:T(8,128)(2,1)S(1)} copy-done((bf16[1024,2048]{1,0:T(8,128)(2,1)S(1)}, bf16[1024,2048]{1,0:T(8,128)(2,1)}, u32[]{:S(2)}) %copy-start) | copy-done | bytes 4194328
  17.5 2.4 %pick_blocks.2 = (bf16[2,128,2048]{2,1,0:T(8,128)(2,1)S(1)}, bf16[2,128,2048]{2,1,0:T(8,128)(2,1)S(1)}) custom-call(s32[2]{0:T(128)S(1)} %pad_add_fusion.place_ref, s32[8,16]{1,0:T(8,128)S(1)} %collective-permute-done.refs_0_, s32[8,16]{1,0:T(8,128)S(1)} %collective-permute-done.1.refs_1_, bf16[1024,2048]{1,0:T(8,128)(2,1)S(1)} %copy-done, ...), custom_call_target="tpu_custom_call" | custom-call | bytes 4194304 | tf_op jit(solution)/shard_map/pick_blocks/pallas_call | solution.py:66
  19.9 3.3 %collective-permute-start.3 = (bf16[2,128,2048]{2,1,0:T(8,128)(2,1)S(1)}, bf16[2,128,2048]{2,1,0:T(8,128)(2,1)S(1)}, u32[]{:S(2)}, u32[]{:S(2)}) collective-permute-start(bf16[2,128,2048]{2,1,0:T(8,128)(2,1)S(1)} %get-tuple-element.45), channel_id=1, source_target_pairs={{0,4},{4,8},{8,12},{12,16},{16,20},{20,24},{24,28},{28,0},{1,5},{5... | collective-permute-start | bytes 3145736 | tf_op jit(solution)/shard_map/ppermute | solution.py:18
  23.2 3.3 %collective-permute-start.4 = (bf16[2,128,2048]{2,1,0:T(8,128)(2,1)S(1)}, bf16[2,128,2048]{2,1,0:T(8,128)(2,1)S(1)}, u32[]{:S(2)}, u32[]{:S(2)}) collective-permute-start(bf16[2,128,2048]{2,1,0:T(8,128)(2,1)S(1)} %get-tuple-element.46), channel_id=1, source_target_pairs={{0,28},{4,0},{8,4},{12,8},{16,12},{20,16},{24,20},{28,24},{1,29},{... | collective-permute-start | bytes 3145736 | tf_op jit(solution)/shard_map/ppermute | solution.py:18
  26.5 2.2 %pick_blocks.3 = (bf16[2,128,2048]{2,1,0:T(8,128)(2,1)S(1)}, bf16[2,128,2048]{2,1,0:T(8,128)(2,1)S(1)}, bf16[1024,2048]{1,0:T(8,128)(2,1)S(1)}) custom-call(s32[2]{0:T(128)S(1)} %pad_add_fusion.place_ref, s32[8,16]{1,0:T(8,128)S(1)} %collective-permute-done.5.refs_0_, s32[8,16]{1,0:T(8,128)S(1)} %collective-permute-done.6.refs_1_, ...), custom_call_target="tpu_custom_call" | custom-call | bytes 4194304 | tf_op jit(solution)/shard_map/pick_blocks/pallas_call | solution.py:66
  29.3 11.4 %tiles.4 = (bf16[4,8,32,256]{3,2,1,0:T(8,128)(2,1)S(1)}, bf16[4,8,32,256]{3,2,1,0:T(8,128)(2,1)S(1)}, bf16[4,8,32,256]{3,2,1,0:T(8,128)(2,1)S(1)}, bf16[4,8,32,256]{3,2,1,0:T(8,128)(2,1)S(1)}) custom-call(s32[5]{0:T(128)S(1)} %stack.39.place_ref, bf16[1024,2048]{1,0:T(8,128)(2,1)S(1)} %get-tuple-element.50.refs_0_, ...), custom_call_target="tpu_custom_call" | custom-call | flops 8589934592 | bytes 12582912 | tf_op jit(solution)/shard_map/tiles/pallas_call | solution.py:126
  40.8 1.6 %collective-permute-start.9 = (bf16[4,8,32,256]{3,2,1,0:T(8,128)(2,1)S(1)}, bf16[4,8,32,256]{3,2,1,0:T(8,128)(2,1)S(1)}, u32[]{:S(2)}, u32[]{:S(2)}) collective-permute-start(bf16[4,8,32,256]{3,2,1,0:T(8,128)(2,1)S(1)} %get-tuple-element.53), channel_id=1, source_target_pairs={{0,2},{1,3},{2,0},{3,1},{4,6},{5,7},{6,4},{7,5},{8,10},{9,11},{10,... | collective-permute-start | bytes 1572872 | tf_op jit(solution)/shard_map/ppermute | solution.py:31
  42.6 12.4 %collective-permute-done.9.refs_8_ = bf16[4,8,32,256]{3,2,1,0:T(8,128)(2,1)S(1)} collective-permute-done((bf16[4,8,32,256]{3,2,1,0:T(8,128)(2,1)S(1)}, bf16[4,8,32,256]{3,2,1,0:T(8,128)(2,1)S(1)}, u32[]{:S(2)}, u32[]{:S(2)}) %collective-permute-start.9) | collective-permute-done | bytes 524320 | tf_op jit(solution)/shard_map/ppermute | solution.py:31
  55.1 13.7 %collective-permute-done.3.refs_4_ = bf16[2,128,2048]{2,1,0:T(8,128)(2,1)S(1)} collective-permute-done((bf16[2,128,2048]{2,1,0:T(8,128)(2,1)S(1)}, bf16[2,128,2048]{2,1,0:T(8,128)(2,1)S(1)}, u32[]{:S(2)}, u32[]{:S(2)}) %collective-permute-start.3) | collective-permute-done | bytes 1048608 | tf_op jit(solution)/shard_map/ppermute | solution.py:18
  68.8 2.2 %collective-permute-done.4.refs_5_ = bf16[2,128,2048]{2,1,0:T(8,128)(2,1)S(1)} collective-permute-done((bf16[2,128,2048]{2,1,0:T(8,128)(2,1)S(1)}, bf16[2,128,2048]{2,1,0:T(8,128)(2,1)S(1)}, u32[]{:S(2)}, u32[]{:S(2)}) %collective-permute-start.4) | collective-permute-done | bytes 1048608 | tf_op jit(solution)/shard_map/ppermute | solution.py:18
  71.0 6.9 %tiles.5 = (bf16[2,8,32,256]{3,2,1,0:T(8,128)(2,1)S(1)}, bf16[2,8,32,256]{3,2,1,0:T(8,128)(2,1)S(1)}, bf16[2,8,32,256]{3,2,1,0:T(8,128)(2,1)S(1)}, bf16[2,8,32,256]{3,2,1,0:T(8,128)(2,1)S(1)}) custom-call(s32[5]{0:T(128)S(1)} %stack.39.place_ref, bf16[1024,2048]{1,0:T(8,128)(2,1)S(1)} %get-tuple-element.50.refs_0_, ...), custom_call_target="tpu_custom_call" | custom-call | flops 4294967296 | bytes 10485760 | tf_op jit(solution)/shard_map/tiles/pallas_call | solution.py:126
  77.9 4.6 %tiles.6 = (bf16[1,8,32,256]{3,2,1,0:T(8,128)(2,1)S(1)}, bf16[1,8,32,256]{3,2,1,0:T(8,128)(2,1)S(1)}, bf16[1,8,32,256]{3,2,1,0:T(8,128)(2,1)S(1)}, bf16[1,8,32,256]{3,2,1,0:T(8,128)(2,1)S(1)}) custom-call(s32[5]{0:T(128)S(1)} %stack.39.place_ref, bf16[1024,2048]{1,0:T(8,128)(2,1)S(1)} %get-tuple-element.50.refs_0_, ...), custom_call_target="tpu_custom_call" | custom-call | flops 2147483648 | bytes 9437184 | tf_op jit(solution)/shard_map/tiles/pallas_call | solution.py:126
  82.6 1.6 %collective-permute-start.16 = (bf16[1,8,32,256]{3,2,1,0:T(8,128)(2,1)S(1)}, bf16[1,8,32,256]{3,2,1,0:T(8,128)(2,1)S(1)}, u32[]{:S(2)}, u32[]{:S(2)}) collective-permute-start(bf16[1,8,32,256]{3,2,1,0:T(8,128)(2,1)S(1)} %get-tuple-element.67), channel_id=1, source_target_pairs={{0,2},{1,3},{2,0},{3,1},{4,6},{5,7},{6,4},{7,5},{8,10},{9,11},{10,... | collective-permute-start | bytes 393224 | tf_op jit(solution)/shard_map/ppermute | solution.py:31
  86.0 2.9 %collective-permute-done.16.refs_10_ = bf16[1,8,32,256]{3,2,1,0:T(8,128)(2,1)S(1)} collective-permute-done((bf16[1,8,32,256]{3,2,1,0:T(8,128)(2,1)S(1)}, bf16[1,8,32,256]{3,2,1,0:T(8,128)(2,1)S(1)}, u32[]{:S(2)}, u32[]{:S(2)}) %collective-permute-start.16) | collective-permute-done | bytes 131104 | tf_op jit(solution)/shard_map/ppermute | solution.py:31
  90.7 3.9 %collective-permute-done.13.refs_9_ = bf16[2,8,32,256]{3,2,1,0:T(8,128)(2,1)S(1)} collective-permute-done((bf16[2,8,32,256]{3,2,1,0:T(8,128)(2,1)S(1)}, bf16[2,8,32,256]{3,2,1,0:T(8,128)(2,1)S(1)}, u32[]{:S(2)}, u32[]{:S(2)}) %collective-permute-start.13) | collective-permute-done | bytes 262176 | tf_op jit(solution)/shard_map/ppermute | solution.py:31
  94.6 4.7 %collective-permute-done.14.refs_13_ = bf16[2,8,32,256]{3,2,1,0:T(8,128)(2,1)S(1)} collective-permute-done((bf16[2,8,32,256]{3,2,1,0:T(8,128)(2,1)S(1)}, bf16[2,8,32,256]{3,2,1,0:T(8,128)(2,1)S(1)}, u32[]{:S(2)}, u32[]{:S(2)}) %collective-permute-start.14) | collective-permute-done | bytes 262176 | tf_op jit(solution)/shard_map/ppermute | solution.py:31
  99.3 4.6 %tiles.7 = (bf16[1,8,32,256]{3,2,1,0:T(8,128)(2,1)S(1)}, bf16[1,8,32,256]{3,2,1,0:T(8,128)(2,1)S(1)}, bf16[1,8,32,256]{3,2,1,0:T(8,128)(2,1)S(1)}, bf16[1,8,32,256]{3,2,1,0:T(8,128)(2,1)S(1)}) custom-call(s32[5]{0:T(128)S(1)} %stack.39.place_ref, bf16[1024,2048]{1,0:T(8,128)(2,1)S(1)} %get-tuple-element.50.refs_0_, ...), custom_call_target="tpu_custom_call" | custom-call | flops 2147483648 | bytes 9437184 | tf_op jit(solution)/shard_map/tiles/pallas_call | solution.py:126
  106.5 4.0 %collective-permute-done.19.refs_12_ = bf16[4,8,32,256]{3,2,1,0:T(8,128)(2,1)S(1)} collective-permute-done((bf16[4,8,32,256]{3,2,1,0:T(8,128)(2,1)S(1)}, bf16[4,8,32,256]{3,2,1,0:T(8,128)(2,1)S(1)}, u32[]{:S(2)}, u32[]{:S(2)}) %collective-permute-start.19) | collective-permute-done | bytes 524320 | tf_op jit(solution)/shard_map/ppermute | solution.py:31
  110.5 2.8 %collective-permute-done.20.refs_14_ = bf16[1,8,32,256]{3,2,1,0:T(8,128)(2,1)S(1)} collective-permute-done((bf16[1,8,32,256]{3,2,1,0:T(8,128)(2,1)S(1)}, bf16[1,8,32,256]{3,2,1,0:T(8,128)(2,1)S(1)}, u32[]{:S(2)}, u32[]{:S(2)}) %collective-permute-start.20) | collective-permute-done | bytes 131104 | tf_op jit(solution)/shard_map/ppermute | solution.py:31
  113.3 3.7 %collective-permute-done.18.refs_11_ = bf16[1,8,32,256]{3,2,1,0:T(8,128)(2,1)S(1)} collective-permute-done((bf16[1,8,32,256]{3,2,1,0:T(8,128)(2,1)S(1)}, bf16[1,8,32,256]{3,2,1,0:T(8,128)(2,1)S(1)}, u32[]{:S(2)}, u32[]{:S(2)}) %collective-permute-start.18) | collective-permute-done | bytes 131104 | tf_op jit(solution)/shard_map/ppermute | solution.py:31
  117.0 1.9 %collective-permute-done.21.refs_15_ = bf16[1,8,32,256]{3,2,1,0:T(8,128)(2,1)S(1)} collective-permute-done((bf16[1,8,32,256]{3,2,1,0:T(8,128)(2,1)S(1)}, bf16[1,8,32,256]{3,2,1,0:T(8,128)(2,1)S(1)}, u32[]{:S(2)}, u32[]{:S(2)}) %collective-permute-start.21) | collective-permute-done | bytes 131104 | tf_op jit(solution)/shard_map/ppermute | solution.py:31
  118.9 4.6 %place_tiles.1 = (f32[8,16,32,128]{3,2,1,0:T(8,128)}, f32[8,16,32,128]{3,2,1,0:T(8,128)}) custom-call(s32[8,16]{1,0:T(8,128)S(1)} %fusion.9.where_ref, bf16[4,8,32,256]{3,2,1,0:T(8,128)(2,1)S(1)} %get-tuple-element.54.refs_0_, bf16[2,8,32,256]{3,2,1,0:T(8,128)(2,1)S(1)} %get-tuple-element.68.refs_1_, bf16[1,8,32,256]{3,2,1,0:T(8,128)(2,1)S(1)} %get-tuple-element.69.refs_2_, ...), custom_call_target="tpu_custom_call" | custom-call | bytes 8388608 | tf_op jit(solution)/shard_map/place_tiles/pallas_call | solution.py:177
  (37 shorter events, 12.9 us)
Async XLA Ops:
  0.6 14.6 %collective-permute-start.2 = (bf16[1024,2048]{1,0:T(8,128)(2,1)}, bf16[1024,2048]{1,0:T(8,128)(2,1)}, u32[]{:S(2)}, u32[]{:S(2)}) collective-permute-start(bf16[1024,2048]{1,0:T(8,128)(2,1)} %refs_2_.3), channel_id=1, source_target_pairs={{0,1},{1,0},{2,3},{3,2},{4,5},{5,4},{6,7},{7,6},{8,9},{9,8},{10,11... | collective-permute-start | bytes 12582920 | tf_op jit(solution)/shard_map/ppermute | solution.py:31
  1.1 13.2 %collective-permute-start = (s32[8,16]{1,0:T(8,128)}, s32[8,16]{1,0:T(8,128)S(1)}, u32[]{:S(2)}, u32[]{:S(2)}) collective-permute-start(s32[8,16]{1,0:T(8,128)} %param.7), channel_id=1, source_target_pairs={{0,28},{4,0},{8,4},{12,8},{16,12},{20,16},{24,20},{28,24},{1,29},{... | collective-permute-start | bytes 1544 | tf_op jit(solution)/shard_map/ppermute | solution.py:18
  6.7 8.5 %collective-permute-start.1 = (s32[8,16]{1,0:T(8,128)}, s32[8,16]{1,0:T(8,128)S(1)}, u32[]{:S(2)}, u32[]{:S(2)}) collective-permute-start(s32[8,16]{1,0:T(8,128)} %param.7), channel_id=1, source_target_pairs={{0,4},{4,8},{8,12},{12,16},{16,20},{20,24},{24,28},{28,0},{1,5},{5... | collective-permute-start | bytes 1544 | tf_op jit(solution)/shard_map/ppermute | solution.py:18
  6.7 19.8 %collective-permute-start.6 = (s32[8,16]{1,0:T(8,128)}, s32[8,16]{1,0:T(8,128)S(1)}, u32[]{:S(2)}, u32[]{:S(2)}) collective-permute-start(s32[8,16]{1,0:T(8,128)} %param.7), channel_id=1, source_target_pairs={{0,24},{4,28},{8,0},{12,4},{16,8},{20,12},{24,16},{28,20},{1,25},{... | collective-permute-start | bytes 1544 | tf_op jit(solution)/shard_map/ppermute | solution.py:18
  9.3 20.0 %collective-permute-start.7 = (f32[2,2048]{1,0:T(2,128)S(1)}, f32[2,2048]{1,0:T(2,128)S(1)}, u32[]{:S(2)}, u32[]{:S(2)}) collective-permute-start(f32[2,2048]{1,0:T(2,128)S(1)} %pad_maximum_fusion.refs_2_), channel_id=1, source_target_pairs={{0,1},{1,0},{2,3},{3,2},{4,5},{5,4},{6,7},{7,6},{8,9},{9,8},{10,11... | collective-permute-start | bytes 49160 | tf_op jit(solution)/shard_map/ppermute | solution.py:31
  14.3 12.2 %collective-permute-start.5 = (s32[8,16]{1,0:T(8,128)}, s32[8,16]{1,0:T(8,128)S(1)}, u32[]{:S(2)}, u32[]{:S(2)}) collective-permute-start(s32[8,16]{1,0:T(8,128)} %param.7), channel_id=1, source_target_pairs={{0,8},{4,12},{8,16},{12,20},{16,24},{20,28},{24,0},{28,4},{1,9},{5... | collective-permute-start | bytes 1544 | tf_op jit(solution)/shard_map/ppermute | solution.py:18
  15.3 2.2 %copy-start = (bf16[1024,2048]{1,0:T(8,128)(2,1)S(1)}, bf16[1024,2048]{1,0:T(8,128)(2,1)}, u32[]{:S(2)}) copy-start(bf16[1024,2048]{1,0:T(8,128)(2,1)} %refs_2_.3) | copy-start | bytes 12582916
  17.5 9.1 %copy-start.1 = (bf16[1024,2048]{1,0:T(8,128)(2,1)S(1)}, bf16[1024,2048]{1,0:T(8,128)(2,1)}, u32[]{:S(2)}) copy-start(bf16[1024,2048]{1,0:T(8,128)(2,1)} %refs_2_.3) | copy-start | bytes 12582916
  19.9 48.9 %collective-permute-start.3 = (bf16[2,128,2048]{2,1,0:T(8,128)(2,1)S(1)}, bf16[2,128,2048]{2,1,0:T(8,128)(2,1)S(1)}, u32[]{:S(2)}, u32[]{:S(2)}) collective-permute-start(bf16[2,128,2048]{2,1,0:T(8,128)(2,1)S(1)} %get-tuple-element.45), channel_id=1, source_target_pairs={{0,4},{4,8},{8,12},{12,16},{16,20},{20,24},{24,28},{28,0},{1,5},{5... | collective-permute-start | bytes 3145736 | tf_op jit(solution)/shard_map/ppermute | solution.py:18
  23.2 47.7 %collective-permute-start.4 = (bf16[2,128,2048]{2,1,0:T(8,128)(2,1)S(1)}, bf16[2,128,2048]{2,1,0:T(8,128)(2,1)S(1)}, u32[]{:S(2)}, u32[]{:S(2)}) collective-permute-start(bf16[2,128,2048]{2,1,0:T(8,128)(2,1)S(1)} %get-tuple-element.46), channel_id=1, source_target_pairs={{0,28},{4,0},{8,4},{12,8},{16,12},{20,16},{24,20},{28,24},{1,29},{... | collective-permute-start | bytes 3145736 | tf_op jit(solution)/shard_map/ppermute | solution.py:18
  28.7 49.2 %collective-permute-start.11 = (bf16[2,128,2048]{2,1,0:T(8,128)(2,1)S(1)}, bf16[2,128,2048]{2,1,0:T(8,128)(2,1)S(1)}, u32[]{:S(2)}, u32[]{:S(2)}) collective-permute-start(bf16[2,128,2048]{2,1,0:T(8,128)(2,1)S(1)} %get-tuple-element.56), channel_id=1, source_target_pairs={{0,24},{4,28},{8,0},{12,4},{16,8},{20,12},{24,16},{28,20},{1,25},{... | collective-permute-start | bytes 3145736 | tf_op jit(solution)/shard_map/ppermute | solution.py:18
  40.7 2.0 %collective-permute-start.8 = (bf16[4,8,32,256]{3,2,1,0:T(8,128)(2,1)S(1)}, bf16[4,8,32,256]{3,2,1,0:T(8,128)(2,1)S(1)}, u32[]{:S(2)}, u32[]{:S(2)}) collective-permute-start(bf16[4,8,32,256]{3,2,1,0:T(8,128)(2,1)S(1)} %get-tuple-element.52), channel_id=1, source_target_pairs={{0,1},{1,0},{2,3},{3,2},{4,5},{5,4},{6,7},{7,6},{8,9},{9,8},{10,11... | collective-permute-start | bytes 1572872 | tf_op jit(solution)/shard_map/ppermute | solution.py:31
  40.8 14.3 %collective-permute-start.9 = (bf16[4,8,32,256]{3,2,1,0:T(8,128)(2,1)S(1)}, bf16[4,8,32,256]{3,2,1,0:T(8,128)(2,1)S(1)}, u32[]{:S(2)}, u32[]{:S(2)}) collective-permute-start(bf16[4,8,32,256]{3,2,1,0:T(8,128)(2,1)S(1)} %get-tuple-element.53), channel_id=1, source_target_pairs={{0,2},{1,3},{2,0},{3,1},{4,6},{5,7},{6,4},{7,5},{8,10},{9,11},{10,... | collective-permute-start | bytes 1572872 | tf_op jit(solution)/shard_map/ppermute | solution.py:31
  71.0 28.3 %collective-permute-start.10 = (bf16[2,128,2048]{2,1,0:T(8,128)(2,1)S(1)}, bf16[2,128,2048]{2,1,0:T(8,128)(2,1)S(1)}, u32[]{:S(2)}, u32[]{:S(2)}) collective-permute-start(bf16[2,128,2048]{2,1,0:T(8,128)(2,1)S(1)} %get-tuple-element.55), channel_id=1, source_target_pairs={{0,8},{4,12},{8,16},{12,20},{16,24},{20,28},{24,0},{28,4},{1,9},{5... | collective-permute-start | bytes 3145736 | tf_op jit(solution)/shard_map/ppermute | solution.py:18
  82.5 2.3 %collective-permute-start.15 = (bf16[1,8,32,256]{3,2,1,0:T(8,128)(2,1)S(1)}, bf16[1,8,32,256]{3,2,1,0:T(8,128)(2,1)S(1)}, u32[]{:S(2)}, u32[]{:S(2)}) collective-permute-start(bf16[1,8,32,256]{3,2,1,0:T(8,128)(2,1)S(1)} %get-tuple-element.66), channel_id=1, source_target_pairs={{0,1},{1,0},{2,3},{3,2},{4,5},{5,4},{6,7},{7,6},{8,9},{9,8},{10,11... | collective-permute-start | bytes 393224 | tf_op jit(solution)/shard_map/ppermute | solution.py:31
  82.6 6.4 %collective-permute-start.16 = (bf16[1,8,32,256]{3,2,1,0:T(8,128)(2,1)S(1)}, bf16[1,8,32,256]{3,2,1,0:T(8,128)(2,1)S(1)}, u32[]{:S(2)}, u32[]{:S(2)}) collective-permute-start(bf16[1,8,32,256]{3,2,1,0:T(8,128)(2,1)S(1)} %get-tuple-element.67), channel_id=1, source_target_pairs={{0,2},{1,3},{2,0},{3,1},{4,6},{5,7},{6,4},{7,5},{8,10},{9,11},{10,... | collective-permute-start | bytes 393224 | tf_op jit(solution)/shard_map/ppermute | solution.py:31
  84.2 5.1 %collective-permute-start.12 = (bf16[2,8,32,256]{3,2,1,0:T(8,128)(2,1)S(1)}, bf16[2,8,32,256]{3,2,1,0:T(8,128)(2,1)S(1)}, u32[]{:S(2)}, u32[]{:S(2)}) collective-permute-start(bf16[2,8,32,256]{3,2,1,0:T(8,128)(2,1)S(1)} %get-tuple-element.61), channel_id=1, source_target_pairs={{0,1},{1,0},{2,3},{3,2},{4,5},{5,4},{6,7},{7,6},{8,9},{9,8},{10,11... | collective-permute-start | bytes 786440 | tf_op jit(solution)/shard_map/ppermute | solution.py:31
  84.3 10.2 %collective-permute-start.13 = (bf16[2,8,32,256]{3,2,1,0:T(8,128)(2,1)S(1)}, bf16[2,8,32,256]{3,2,1,0:T(8,128)(2,1)S(1)}, u32[]{:S(2)}, u32[]{:S(2)}) collective-permute-start(bf16[2,8,32,256]{3,2,1,0:T(8,128)(2,1)S(1)} %get-tuple-element.62), channel_id=1, source_target_pairs={{0,2},{1,3},{2,0},{3,1},{4,6},{5,7},{6,4},{7,5},{8,10},{9,11},{10,... | collective-permute-start | bytes 786440 | tf_op jit(solution)/shard_map/ppermute | solution.py:31
  84.9 14.4 %collective-permute-start.14 = (bf16[2,8,32,256]{3,2,1,0:T(8,128)(2,1)S(1)}, bf16[2,8,32,256]{3,2,1,0:T(8,128)(2,1)S(1)}, u32[]{:S(2)}, u32[]{:S(2)}) collective-permute-start(bf16[2,8,32,256]{3,2,1,0:T(8,128)(2,1)S(1)} %get-tuple-element.63), channel_id=1, source_target_pairs={{0,3},{1,2},{2,1},{3,0},{4,7},{5,6},{6,5},{7,4},{8,11},{9,10},{10,... | collective-permute-start | bytes 786440 | tf_op jit(solution)/shard_map/ppermute | solution.py:31
  89.0 21.6 %collective-permute-start.19 = (bf16[4,8,32,256]{3,2,1,0:T(8,128)(2,1)S(1)}, bf16[4,8,32,256]{3,2,1,0:T(8,128)(2,1)S(1)}, u32[]{:S(2)}, u32[]{:S(2)}) collective-permute-start(bf16[4,8,32,256]{3,2,1,0:T(8,128)(2,1)S(1)} %get-tuple-element.80), channel_id=1, source_target_pairs={{0,3},{1,2},{2,1},{3,0},{4,7},{5,6},{6,5},{7,4},{8,11},{9,10},{10,... | collective-permute-start | bytes 1572872 | tf_op jit(solution)/shard_map/ppermute | solution.py:31
  89.3 24.0 %collective-permute-start.20 = (bf16[1,8,32,256]{3,2,1,0:T(8,128)(2,1)S(1)}, bf16[1,8,32,256]{3,2,1,0:T(8,128)(2,1)S(1)}, u32[]{:S(2)}, u32[]{:S(2)}) collective-permute-start(bf16[1,8,32,256]{3,2,1,0:T(8,128)(2,1)S(1)} %get-tuple-element.82), channel_id=1, source_target_pairs={{0,3},{1,2},{2,1},{3,0},{4,7},{5,6},{6,5},{7,4},{8,11},{9,10},{10,... | collective-permute-start | bytes 393224 | tf_op jit(solution)/shard_map/ppermute | solution.py:31
  103.9 9.4 %collective-permute-start.17 = (bf16[1,8,32,256]{3,2,1,0:T(8,128)(2,1)S(1)}, bf16[1,8,32,256]{3,2,1,0:T(8,128)(2,1)S(1)}, u32[]{:S(2)}, u32[]{:S(2)}) collective-permute-start(bf16[1,8,32,256]{3,2,1,0:T(8,128)(2,1)S(1)} %get-tuple-element.75), channel_id=1, source_target_pairs={{0,1},{1,0},{2,3},{3,2},{4,5},{5,4},{6,7},{7,6},{8,9},{9,8},{10,11... | collective-permute-start | bytes 393224 | tf_op jit(solution)/shard_map/ppermute | solution.py:31
  105.0 12.0 %collective-permute-start.18 = (bf16[1,8,32,256]{3,2,1,0:T(8,128)(2,1)S(1)}, bf16[1,8,32,256]{3,2,1,0:T(8,128)(2,1)S(1)}, u32[]{:S(2)}, u32[]{:S(2)}) collective-permute-start(bf16[1,8,32,256]{3,2,1,0:T(8,128)(2,1)S(1)} %get-tuple-element.79), channel_id=1, source_target_pairs={{0,2},{1,3},{2,0},{3,1},{4,6},{5,7},{6,4},{7,5},{8,10},{9,11},{10,... | collective-permute-start | bytes 393224 | tf_op jit(solution)/shard_map/ppermute | solution.py:31
  106.5 12.4 %collective-permute-start.21 = (bf16[1,8,32,256]{3,2,1,0:T(8,128)(2,1)S(1)}, bf16[1,8,32,256]{3,2,1,0:T(8,128)(2,1)S(1)}, u32[]{:S(2)}, u32[]{:S(2)}) collective-permute-start(bf16[1,8,32,256]{3,2,1,0:T(8,128)(2,1)S(1)} %get-tuple-element.83), channel_id=1, source_target_pairs={{0,3},{1,2},{2,1},{3,0},{4,7},{5,6},{6,5},{7,4},{8,11},{9,10},{10,... | collective-permute-start | bytes 393224 | tf_op jit(solution)/shard_map/ppermute | solution.py:31

commit v4 on v3

--- a/solution.py
+++ b/solution.py
@@ -9,7 +9,7 @@
 
 R = 2
 VMEM_LIMIT = 24 * 1024 * 1024
-PICK_VMEM_LIMIT = 24 * 1024 * 1024
+SOON = pl.CostEstimate(flops=0, bytes_accessed=0, transcendentals=0)
 
 
 def shifted(value, axis, steps):
@@ -49,20 +49,14 @@
             )
             copy.start()
             copies.append(copy)
-    if len(outs) > count:
-        copy = pltpu.make_async_copy(own, outs[count], sems.at[count, 0])
-        copy.start()
-        copies.append(copy)
     for copy in copies:
         copy.wait()
 
 
-def pick(place, asks, own, sib, tile, keep_own):
+def pick(place, asks, own, sib, tile):
     blocks, bands = asks[0].shape[0], own.shape[1]
     count = len(asks)
     out_shape = [jax.ShapeDtypeStruct((2, tile, bands), own.dtype)] * count
-    if keep_own:
-        out_shape.append(jax.ShapeDtypeStruct(own.shape, own.dtype))
     return pl.pallas_call(
         functools.partial(pick_kernel, count, blocks, tile),
         out_shape=out_shape,
@@ -70,12 +64,10 @@
         + [pl.BlockSpec(memory_space=pltpu.VMEM)] * count
         + [pl.BlockSpec(memory_space=pl.ANY)] * 2,
         out_specs=[pl.BlockSpec(memory_space=pltpu.VMEM)] * len(out_shape),
-        scratch_shapes=[pltpu.SemaphoreType.DMA((count + 1, 2))],
+        scratch_shapes=[pltpu.SemaphoreType.DMA((count, 2))],
         name="pick_blocks",
-        compiler_params=pltpu.CompilerParams(vmem_limit_bytes=PICK_VMEM_LIMIT),
-        cost_estimate=pl.CostEstimate(
-            flops=0, bytes_accessed=8 * count * tile * bands, transcendentals=0
-        ),
+        compiler_params=pltpu.CompilerParams(vmem_limit_bytes=VMEM_LIMIT),
+        cost_estimate=SOON,
     )(place, *asks, own, sib)
 
 
@@ -137,46 +129,56 @@
         ],
         name="tiles",
         compiler_params=pltpu.CompilerParams(vmem_limit_bytes=VMEM_LIMIT),
-        cost_estimate=pl.CostEstimate(
-            flops=2 * rows * n_right * 2 * tile * 2 * bands,
-            bytes_accessed=4 * rows * bands + 4 * n_right * tile * bands,
-            transcendentals=0,
-        ),
+        cost_estimate=SOON,
     )(place, own, sib, *weights, *arrived)
 
 
-def place_kernel(chips, sizes, tile, where_ref, *refs):
+def strip_sum(ins, chips, n_chunks, other_core, chunk, j, i):
+    total = None
+    for step in range(chips):
+        value = ins[(step * 2 + other_core) * n_chunks + chunk][j, i].astype(jnp.float32)
+        total = value if total is None else total + value
+    return total
+
+
+def place_early_kernel(chips, sizes, per_core, tile, where_ref, *refs):
     n_chunks = len(sizes)
-    per_core = sum(sizes)
     ins = refs[: 2 * chips * n_chunks]
-    density, energy, pool = refs[2 * chips * n_chunks :]
+    density, energy, later, pool = refs[2 * chips * n_chunks :]
     for other_core in range(2):
-        first = 0
+        first = other_core * per_core
         for chunk in range(n_chunks):
             for j in range(sizes[chunk]):
-                total = None
-                for step in range(chips):
-                    ref = ins[(step * 2 + other_core) * n_chunks + chunk]
-                    value = ref[j, 0].astype(jnp.float32)
-                    total = value if total is None else total + value
-                pool[other_core * per_core + first + j] = total
+                pool[first + j] = strip_sum(ins, chips, n_chunks, other_core, chunk, j, 0)
             first += sizes[chunk]
     i = pl.program_id(0)
-    for slot in range(density.shape[1]):
+    slots = density.shape[1]
+
+    @pl.when(i == 0)
+    def _():
+        later[0] = 0
+
+    for slot in range(slots):
         where = where_ref[i, slot]
         density[0, slot] = pool[where, :, :tile]
         energy[0, slot] = pool[where, :, tile:]
 
-
-def place_tiles(where, strips, chips, tile):
+        @pl.when(lax.rem(where, per_core) == per_core - 1)
+        def _():
+            count = later[0] + 1
+            later[count] = i * slots + slot
+            later[0] = count
+
+
+def place_early(where, strips, chips, per_core, tile):
     sizes = [value.shape[0] for value in strips[0]]
     _, blocks, strip, width = strips[0][0].shape
     slots = where.shape[1]
     out = jax.ShapeDtypeStruct((blocks, slots, strip, tile), jnp.float32)
     flat = [value for group in strips for value in group]
     return pl.pallas_call(
-        functools.partial(place_kernel, chips, sizes, tile),
-        out_shape=[out, out],
+        functools.partial(place_early_kernel, chips, sizes, per_core, tile),
+        out_shape=[out, out, jax.ShapeDtypeStruct((blocks * slots + 1,), jnp.int32)],
         grid_spec=pltpu.PrefetchScalarGridSpec(
             num_scalar_prefetch=1,
             grid=(blocks,),
@@ -189,18 +191,71 @@
             out_specs=[
                 pl.BlockSpec((1, slots, strip, tile), lambda i, where: (i, 0, 0, 0))
             ]
-            * 2,
-            scratch_shapes=[pltpu.VMEM((2 * sum(sizes), strip, width), jnp.float32)],
+            * 2
+            + [pl.BlockSpec(memory_space=pltpu.SMEM)],
+            scratch_shapes=[pltpu.VMEM((2 * per_core, strip, width), jnp.float32)],
         ),
-        name="place_tiles",
+        name="place_early",
         compiler_params=pltpu.CompilerParams(vmem_limit_bytes=VMEM_LIMIT),
-        cost_estimate=pl.CostEstimate(
-            flops=0,
-            bytes_accessed=sum(2 * value.size for value in flat)
-            + 8 * blocks * slots * strip * tile,
-            transcendentals=0,
-        ),
+        cost_estimate=SOON,
     )(where, *flat)
+
+
+def place_late_kernel(chips, per_core, tile, where_ref, later, *refs):
+    ins, refs = refs[: 2 * chips], refs[2 * chips + 2 :]
+    density, energy, pool, sems = refs
+    blocks, slots = density.shape[:2]
+    for other_core in range(2):
+        for i in range(blocks):
+            total = strip_sum(ins, chips, 1, other_core, 0, 0, i)
+            pool[other_core, i, 0] = total[:, :tile]
+            pool[other_core, i, 1] = total[:, tile:]
+    count = later[0]
+
+    def copies(n):
+        entry = jnp.clip(later[n + 1], 0, blocks * slots - 1)
+        i, slot = lax.div(entry, slots), lax.rem(entry, slots)
+        other_core = jnp.clip(lax.div(where_ref[i, slot], per_core), 0, 1)
+        return [
+            pltpu.make_async_copy(
+                pool.at[other_core, i, kind], out.at[i, slot], sems.at[kind]
+            )
+            for kind, out in enumerate((density, energy))
+        ]
+
+    @pl.loop(0, count)
+    def _(n):
+        for copy in copies(n):
+            copy.start()
+
+    @pl.loop(0, count)
+    def _(n):
+        for copy in copies(n):
+            copy.wait()
+
+
+def place_late(where, later, strips, density, energy, chips, per_core, tile):
+    _, blocks, strip, _ = strips[0].shape
+    smem = pl.BlockSpec(memory_space=pltpu.SMEM)
+    anywhere = pl.BlockSpec(memory_space=pl.ANY)
+    out = jax.ShapeDtypeStruct(density.shape, density.dtype)
+    n_strips = len(strips)
+    return pl.pallas_call(
+        functools.partial(place_late_kernel, chips, per_core, tile),
+        out_shape=[out, out],
+        in_specs=[smem, smem]
+        + [pl.BlockSpec(memory_space=pltpu.VMEM)] * n_strips
+        + [anywhere] * 2,
+        out_specs=[anywhere] * 2,
+        scratch_shapes=[
+            pltpu.VMEM((2, blocks, 2, strip, tile), jnp.float32),
+            pltpu.SemaphoreType.DMA((2,)),
+        ],
+        input_output_aliases={2 + n_strips: 0, 3 + n_strips: 1},
+        name="place_late",
+        compiler_params=pltpu.CompilerParams(vmem_limit_bytes=VMEM_LIMIT),
+        cost_estimate=SOON,
+    )(where, later, *strips, density, energy)
 
 
 def body(eigvecs, occupations, energies, neighbours):
@@ -217,10 +272,6 @@
 
     asks = [shifted(neighbours, "atoms", offset) for offset in offsets]
     sib = to_strip_target(eigvecs, chips, 0, 1)
-    own_weights = jnp.stack([occupations, occupations * energies], 0)
-    sib_weights = to_strip_target(own_weights, chips, 0, 1)
-    weights = (own_weights, sib_weights)
-
     targets = [
         strip_target(group, chips, step, other)
         for step in range(chips)
@@ -229,12 +280,27 @@
     here = jnp.stack([own_index, core]).astype(jnp.int32)
     place = jnp.stack([core] + targets).astype(jnp.int32)
 
-    near = list(pick(here, asks[:2], eigvecs, sib, tile, False))
+    near = list(pick(here, asks[:2], eigvecs, sib, tile))
     here, near[0] = lax.optimization_barrier((here, near[0]))
-    far = list(pick(here, asks[2:], eigvecs, sib, tile, True))
-    own = far.pop()
+    far = list(pick(here, asks[2:], eigvecs, sib, tile))
+    occupations, far[0] = lax.optimization_barrier((occupations, far[0]))
     near = [shifted(near[0], "atoms", -offsets[0]), shifted(near[1], "atoms", -offsets[1])]
     third = shifted(far[0], "atoms", -offsets[2])
+    own_weights = jnp.stack([occupations, occupations * energies], 0)
+    sib_weights = to_strip_target(own_weights, chips, 0, 1)
+    weights = (own_weights, sib_weights)
+
+    def strips_of(*arrived):
+        parts = list(tiles(place, eigvecs, sib, arrived, weights, n_bands, tile))
+        parts[1] = to_strip_target(parts[1], chips, 0, 1)
+        for index in range(2, n_bands):
+            if index % 2:
+                parts[index], parts[1] = lax.optimization_barrier((parts[index], parts[1]))
+            parts[index] = to_strip_target(parts[index], chips, index // 2, index % 2)
+        return parts
+
+    chunks = [strips_of()]
+    neighbours, chunks[0][0] = lax.optimization_barrier((neighbours, chunks[0][0]))
 
     owners = lax.div(neighbours, blocks)
     within = lax.rem(neighbours, blocks)
@@ -247,32 +313,19 @@
         side = jnp.where(from_it, (within == highest).astype(jnp.int32), side)
         spot = jnp.where(from_it, half_blocks + index, spot)
     per_core = half_blocks + len(offsets)
-    where = (side ^ core) * per_core + spot
-    where, place = lax.optimization_barrier((where.astype(jnp.int32), place))
-
-    def exchanged(parts):
-        return [
-            part if index == 0 else to_strip_target(part, chips, index // 2, index % 2)
-            for index, part in enumerate(parts)
-        ]
-
-    def strips_of(*arrived):
-        return exchanged(tiles(place, own, sib, arrived, weights, n_bands, tile))
-
-    chunks = [strips_of()]
-    *near, source, chunks[0][:3] = lax.optimization_barrier(
-        (*near, far[1], chunks[0][:3])
+    where = ((side ^ core) * per_core + spot).astype(jnp.int32)
+
+    near, source, chunks[0][:3] = lax.optimization_barrier((near, far[1], chunks[0][:3]))
+    fourth = shifted(source, "atoms", -offsets[3])
+    chunks.append(strips_of(*near, third))
+    where, fourth, chunks[0], chunks[1][:3] = lax.optimization_barrier(
+        (where, fourth, chunks[0], chunks[1][:3])
     )
-    fourth = shifted(source, "atoms", -offsets[3])
-    chunks.append(strips_of(*near))
-    third, chunks[1][0] = lax.optimization_barrier((third, chunks[1][0]))
-    chunks.append(strips_of(third))
-    fourth, chunks[1], chunks[2][:3] = lax.optimization_barrier((fourth, chunks[1], chunks[2][:3]))
-    chunks.append(strips_of(fourth))
+    last = strips_of(fourth)
+    where, last[0] = lax.optimization_barrier((where, last[0]))
     strips = [[chunk[index] for chunk in chunks] for index in range(n_bands)]
-
-    density, energy = place_tiles(where, strips, chips, tile)
-    return density, energy
+    density, energy, later = place_early(where, strips, chips, per_core, tile)
+    return place_late(where, later, last, density, energy, chips, per_core, tile)
 
 
 def solution(mesh):

time: 124 us -> 131 us (1.056)
  waiting for transfers between devices: 52.6 us -> 56 us
  local copies, waits for them, and re-layouts: 2.27 us -> 5.46 us
  other arithmetic: 6.32 us -> 3.54 us
  starting transfers between devices: 24.9 us -> 26.8 us
    ppermute x8, waiting for transfers between devices: 15.9 us -> 24.3 us  [shifted(): return lax.ppermute(value, axis, pairs)]
    ppermute x14 -> x11, waiting for transfers between devices: 36.7 us -> 31.6 us  [to_strip_target(): return lax.ppermute(value, 'bands', pairs)]
    ppermute x8, starting transfers between devices: 14.8 us -> 18.7 us  [shifted(): return lax.ppermute(value, axis, pairs)]
    unnamed x4 -> x14, local copies, waits for them, and re-layouts: 2.19 us -> 5.38 us
    pallas_call x4 -> x3, Pallas kernels: 27.5 us -> 25.2 us  [tiles(): pl.pallas_call(functools.partial(tiles_kernel, len(arrived), n_right, n_s...]
    pallas_call x2, Pallas kernels: 4.57 us -> 6.56 us  [pick(): pl.pallas_call(functools.partial(pick_kernel, count, blocks, tile), out_s...]
    ppermute x14 -> x11, starting transfers between devices: 10.1 us -> 8.13 us  [to_strip_target(): return lax.ppermute(value, 'bands', pairs)]
    pallas_call x1 -> x2, Pallas kernels: 4.57 us -> 6.27 us  [the longest x1 4.63 us: place_early(): pl.pallas_call(functools.partial(place_early_kernel, chips, sizes, per_co...]
  transfers between devices with their start and end apart: 22 -> 19, of which waited for: 11 -> 9; matrix products, arithmetic and copies ran while one was open for 5% -> 3% of each run, Pallas kernels for 26% -> 25%
where the time goes in v4:
time: 131 us
  waiting for transfers between devices  56 us (43%)
  Pallas kernels  38 us (29%)
  starting transfers between devices  26.8 us (20%)
  local copies, waits for them, and re-layouts  5.46 us (4%)
  other arithmetic  3.54 us (3%)
    ppermute x11, waiting for transfers between devices, to_strip_target(): return lax.ppermute(value, 'bands', pairs)  31.6 us
    pallas_call x3, Pallas kernels, tiles(): pl.pallas_call(functools.partial(tiles_kernel, len(arrived), n_right, n_s...  25.2 us
    ppermute x8, waiting for transfers between devices, shifted(): return lax.ppermute(value, axis, pairs)  24.3 us
    ppermute x8, starting transfers between devices, shifted(): return lax.ppermute(value, axis, pairs)  18.7 us
    ppermute x11, starting transfers between devices, to_strip_target(): return lax.ppermute(value, 'bands', pairs)  8.13 us
    pallas_call x2, Pallas kernels, pick(): pl.pallas_call(functools.partial(pick_kernel, count, blocks, tile), out_s...  6.56 us
    unnamed x14, local copies, waits for them, and re-layouts  5.38 us
    pallas_call x1, Pallas kernels, place_early(): pl.pallas_call(functools.partial(place_early_kernel, chips, sizes, per_co...  4.63 us
  transfers between devices with their start and end apart: 19, of which 9 were waited for; matrix products, arithmetic and copies ran while one was open for 3% of the time, Pallas kernels for 25%

profile of v4, /device:TPU:0, one launch (start us, length us, event | category | flops | bytes accessed | tf_op | source)
XLA Modules:
  0.0 130.8 jit_solution(9439180679149918649)
XLA Ops:
  1.1 5.6 %collective-permute-start.1 = (s32[8,16]{1,0:T(8,128)}, s32[8,16]{1,0:T(8,128)S(1)}, u32[]{:S(2)}, u32[]{:S(2)}) collective-permute-start(s32[8,16]{1,0:T(8,128)} %param.7), channel_id=1, source_target_pairs={{0,28},{4,0},{8,4},{12,8},{16,12},{20,16},{24,20},{28,24},{1,29},{... | collective-permute-start | bytes 1544 | tf_op jit(solution)/shard_map/ppermute | solution.py:18
  6.8 1.5 %collective-permute-done.1.refs_0_ = s32[8,16]{1,0:T(8,128)S(1)} collective-permute-done((s32[8,16]{1,0:T(8,128)}, s32[8,16]{1,0:T(8,128)S(1)}, u32[]{:S(2)}, u32[]{:S(2)}) %collective-permute-start.1) | collective-permute-done | bytes 544 | tf_op jit(solution)/shard_map/ppermute | solution.py:18
  8.3 5.0 %collective-permute-done.2.refs_1_ = s32[8,16]{1,0:T(8,128)S(1)} collective-permute-done((s32[8,16]{1,0:T(8,128)}, s32[8,16]{1,0:T(8,128)S(1)}, u32[]{:S(2)}, u32[]{:S(2)}) %collective-permute-start.2) | collective-permute-done | bytes 544 | tf_op jit(solution)/shard_map/ppermute | solution.py:18
  13.3 2.2 %copy-done = bf16[1024,2048]{1,0:T(8,128)(2,1)S(1)} copy-done((bf16[1024,2048]{1,0:T(8,128)(2,1)S(1)}, bf16[1024,2048]{1,0:T(8,128)(2,1)}, u32[]{:S(2)}) %copy-start) | copy-done | bytes 4194328
  15.5 3.4 %pick_blocks.2 = (bf16[2,128,2048]{2,1,0:T(8,128)(2,1)}, bf16[2,128,2048]{2,1,0:T(8,128)(2,1)}) custom-call(s32[2]{0:T(128)S(1)} %pad_add_fusion.place_ref, s32[8,16]{1,0:T(8,128)S(1)} %collective-permute-done.1.refs_0_, s32[8,16]{1,0:T(8,128)S(1)} %collective-permute-done.2.refs_1_, bf16[1024,2048]{1,0:T(8,128)(2,1)S(1)} %copy-done, ...), custom_call_target="tpu_custom_call" | custom-call | tf_op jit(solution)/shard_map/pick_blocks/pallas_call | solution.py:60
  19.0 4.7 %collective-permute-start.7 = (bf16[2,128,2048]{2,1,0:T(8,128)(2,1)}, bf16[2,128,2048]{2,1,0:T(8,128)(2,1)S(1)}, u32[]{:S(2)}, u32[]{:S(2)}) collective-permute-start(bf16[2,128,2048]{2,1,0:T(8,128)(2,1)} %get-tuple-element.57), channel_id=1, source_target_pairs={{0,28},{4,0},{8,4},{12,8},{16,12},{20,16},{24,20},{28,24},{1,29},{... | collective-permute-start | bytes 3145736 | tf_op jit(solution)/shard_map/ppermute | solution.py:18
  23.7 3.8 %collective-permute-start.4 = (s32[8,16]{1,0:T(8,128)S(1)}, s32[8,16]{1,0:T(8,128)S(1)}, u32[]{:S(2)}, u32[]{:S(2)}) collective-permute-start(s32[8,16]{1,0:T(8,128)S(1)} %copy-done.5), channel_id=1, source_target_pairs={{0,24},{4,28},{8,0},{12,4},{16,8},{20,12},{24,16},{28,20},{1,25},{... | collective-permute-start | bytes 1544 | tf_op jit(solution)/shard_map/ppermute | solution.py:18
  27.5 17.9 %collective-permute-done.3.refs_0_ = s32[8,16]{1,0:T(8,128)S(1)} collective-permute-done((s32[8,16]{1,0:T(8,128)S(1)}, s32[8,16]{1,0:T(8,128)S(1)}, u32[]{:S(2)}, u32[]{:S(2)}) %collective-permute-start.3) | collective-permute-done | bytes 544 | tf_op jit(solution)/shard_map/ppermute | solution.py:18
  45.4 3.1 %pick_blocks.3 = (bf16[2,128,2048]{2,1,0:T(8,128)(2,1)}, bf16[2,128,2048]{2,1,0:T(8,128)(2,1)S(1)}) custom-call(s32[2]{0:T(128)S(1)} %pad_add_fusion.place_ref, s32[8,16]{1,0:T(8,128)S(1)} %collective-permute-done.3.refs_0_, s32[8,16]{1,0:T(8,128)S(1)} %collective-permute-done.4.refs_1_, bf16[1024,2048]{1,0:T(8,128)(2,1)S(1)} %copy-done, ...), custom_call_target="tpu_custom_call" | custom-call | tf_op jit(solution)/shard_map/pick_blocks/pallas_call | solution.py:60
  49.5 4.3 %collective-permute-start.12 = (bf16[2,128,2048]{2,1,0:T(8,128)(2,1)}, bf16[2,128,2048]{2,1,0:T(8,128)(2,1)S(1)}, u32[]{:S(2)}, u32[]{:S(2)}) collective-permute-start(bf16[2,128,2048]{2,1,0:T(8,128)(2,1)} %get-tuple-element.71), channel_id=1, source_target_pairs={{0,24},{4,28},{8,0},{12,4},{16,8},{20,12},{24,16},{28,20},{1,25},{... | collective-permute-start | bytes 3145736 | tf_op jit(solution)/shard_map/ppermute | solution.py:18
  55.1 2.2 %copy-done.1 = bf16[1024,2048]{1,0:T(8,128)(2,1)S(1)} copy-done((bf16[1024,2048]{1,0:T(8,128)(2,1)S(1)}, bf16[1024,2048]{1,0:T(8,128)(2,1)}, u32[]{:S(2)}) %copy-start.1) | copy-done | bytes 4194328
  57.3 11.5 %tiles.3 = (bf16[4,8,32,256]{3,2,1,0:T(8,128)(2,1)S(1)}, bf16[4,8,32,256]{3,2,1,0:T(8,128)(2,1)S(1)}, bf16[4,8,32,256]{3,2,1,0:T(8,128)(2,1)S(1)}, bf16[4,8,32,256]{3,2,1,0:T(8,128)(2,1)S(1)}) custom-call(s32[5]{0:T(128)S(1)} %stack.39.place_ref, bf16[1024,2048]{1,0:T(8,128)(2,1)S(1)} %copy-done.1, bf16[1024,2048]{1,0:T(8,128)(2,1)} %collective-permute-done.refs_3_.refs_1_, ...), custom_call_target="tpu_custom_call" | custom-call | tf_op jit(solution)/shard_map/tiles/pallas_call | solution.py:118
  69.0 1.5 %collective-permute-start.9 = (bf16[4,8,32,256]{3,2,1,0:T(8,128)(2,1)S(1)}, bf16[4,8,32,256]{3,2,1,0:T(8,128)(2,1)S(1)}, u32[]{:S(2)}, u32[]{:S(2)}) collective-permute-start(bf16[4,8,32,256]{3,2,1,0:T(8,128)(2,1)S(1)} %get-tuple-element.63), channel_id=1, source_target_pairs={{0,2},{1,3},{2,0},{3,1},{4,6},{5,7},{6,4},{7,5},{8,10},{9,11},{10,... | collective-permute-start | bytes 1572872 | tf_op jit(solution)/shard_map/ppermute | solution.py:31
  70.7 12.4 %collective-permute-done.9.refs_4_ = bf16[4,8,32,256]{3,2,1,0:T(8,128)(2,1)S(1)} collective-permute-done((bf16[4,8,32,256]{3,2,1,0:T(8,128)(2,1)S(1)}, bf16[4,8,32,256]{3,2,1,0:T(8,128)(2,1)S(1)}, u32[]{:S(2)}, u32[]{:S(2)}) %collective-permute-start.9) | collective-permute-done | bytes 524320 | tf_op jit(solution)/shard_map/ppermute | solution.py:31
  83.4 9.1 %tiles.4 = (bf16[3,8,32,256]{3,2,1,0:T(8,128)(2,1)S(1)}, bf16[3,8,32,256]{3,2,1,0:T(8,128)(2,1)S(1)}, bf16[3,8,32,256]{3,2,1,0:T(8,128)(2,1)S(1)}, bf16[3,8,32,256]{3,2,1,0:T(8,128)(2,1)S(1)}) custom-call(s32[5]{0:T(128)S(1)} %stack.39.place_ref, bf16[1024,2048]{1,0:T(8,128)(2,1)S(1)} %copy-done.1, bf16[1024,2048]{1,0:T(8,128)(2,1)} %collective-permute-done.refs_3_.refs_1_, ...), custom_call_target="tpu_custom_call" | custom-call | tf_op jit(solution)/shard_map/tiles/pallas_call | solution.py:118
  92.6 1.6 %collective-permute-start.11 = (bf16[4,8,32,256]{3,2,1,0:T(8,128)(2,1)S(1)}, bf16[4,8,32,256]{3,2,1,0:T(8,128)(2,1)S(1)}, u32[]{:S(2)}, u32[]{:S(2)}) collective-permute-start(bf16[4,8,32,256]{3,2,1,0:T(8,128)(2,1)S(1)} %get-tuple-element.68), channel_id=1, source_target_pairs={{0,3},{1,2},{2,1},{3,0},{4,7},{5,6},{6,5},{7,4},{8,11},{9,10},{10,... | collective-permute-start | bytes 1572872 | tf_op jit(solution)/shard_map/ppermute | solution.py:31
  96.4 2.7 %fusion.9.where_ref = s32[8,16]{1,0:T(8,128)S(1)} fusion(pred[8,16]{1,0:T(8,128)(4,1)S(1)} %get-tuple-element.105, pred[8,16]{1,0:T(8,128)(4,1)S(1)} %get-tuple-element.104, pred[8,16]{1,0:T(8,128)(4,1)S(1)} %get-tuple-element.103, pred[8,16]{1,0:T(8,128)(4,1)S(1)} %get-tuple-element.102, s32[]{:T(128)} %and.14, s32[]{:T(128)} %get-tuple-element.100, ...), kind=kLoop, calls=%fused_computation.18 | loop fusion | flops 4352 | bytes 1556 | tf_op jit(solution)/shard_map/add | solution.py:316
  99.1 7.4 %collective-permute-done.11.refs_6_ = bf16[4,8,32,256]{3,2,1,0:T(8,128)(2,1)S(1)} collective-permute-done((bf16[4,8,32,256]{3,2,1,0:T(8,128)(2,1)S(1)}, bf16[4,8,32,256]{3,2,1,0:T(8,128)(2,1)S(1)}, u32[]{:S(2)}, u32[]{:S(2)}) %collective-permute-start.11) | collective-permute-done | bytes 524320 | tf_op jit(solution)/shard_map/ppermute | solution.py:31
  106.5 9.4 %collective-permute-done.14.refs_5_ = bf16[3,8,32,256]{3,2,1,0:T(8,128)(2,1)S(1)} collective-permute-done((bf16[3,8,32,256]{3,2,1,0:T(8,128)(2,1)S(1)}, bf16[3,8,32,256]{3,2,1,0:T(8,128)(2,1)S(1)}, u32[]{:S(2)}, u32[]{:S(2)}) %collective-permute-start.14) | collective-permute-done | bytes 393248 | tf_op jit(solution)/shard_map/ppermute | solution.py:31
  115.9 4.6 %tiles.5 = (bf16[1,8,32,256]{3,2,1,0:T(8,128)(2,1)S(1)}, bf16[1,8,32,256]{3,2,1,0:T(8,128)(2,1)S(1)}, bf16[1,8,32,256]{3,2,1,0:T(8,128)(2,1)S(1)}, bf16[1,8,32,256]{3,2,1,0:T(8,128)(2,1)S(1)}) custom-call(s32[5]{0:T(128)S(1)} %stack.39.place_ref, bf16[1024,2048]{1,0:T(8,128)(2,1)S(1)} %copy-done.1, bf16[1024,2048]{1,0:T(8,128)(2,1)} %collective-permute-done.refs_3_.refs_1_, ...), custom_call_target="tpu_custom_call" | custom-call | tf_op jit(solution)/shard_map/tiles/pallas_call | solution.py:118
  120.6 1.6 %collective-permute-start.17 = (bf16[1,8,32,256]{3,2,1,0:T(8,128)(2,1)S(1)}, bf16[1,8,32,256]{3,2,1,0:T(8,128)(2,1)S(1)}, u32[]{:S(2)}, u32[]{:S(2)}) collective-permute-start(bf16[1,8,32,256]{3,2,1,0:T(8,128)(2,1)S(1)} %get-tuple-element.94), channel_id=1, source_target_pairs={{0,2},{1,3},{2,0},{3,1},{4,6},{5,7},{6,4},{7,5},{8,10},{9,11},{10,... | collective-permute-start | bytes 393224 | tf_op jit(solution)/shard_map/ppermute | solution.py:31
  123.2 4.6 %place_early.1 = (f32[8,16,32,128]{3,2,1,0:T(8,128)}, f32[8,16,32,128]{3,2,1,0:T(8,128)}, s32[129]{0:T(256)S(1)}) custom-call(s32[8,16]{1,0:T(8,128)S(1)} %fusion.9.where_ref, bf16[4,8,32,256]{3,2,1,0:T(8,128)(2,1)S(1)} %get-tuple-element.81.refs_0_, bf16[3,8,32,256]{3,2,1,0:T(8,128)(2,1)S(1)} %get-tuple-element.82.refs_1_, ...), custom_call_target="tpu_custom_call" | custom-call | tf_op jit(solution)/shard_map/place_early/pallas_call | solution.py:179
  127.8 1.1 collective-permute-done.18.refs_3_
  129.0 1.6 %place_late.1 = (f32[8,16,32,128]{3,2,1,0:T(8,128)}, f32[8,16,32,128]{3,2,1,0:T(8,128)}) custom-call(s32[8,16]{1,0:T(8,128)S(1)} %fusion.9.where_ref, s32[129]{0:T(256)S(1)} %get-tuple-element.89.later, bf16[1,8,32,256]{3,2,1,0:T(8,128)(2,1)S(1)} %get-tuple-element.90.refs_0_, ...), custom_call_target="tpu_custom_call", output_to_operand_aliasing={{0}: (6, {}), {1}: (7, {})} | custom-call | tf_op jit(solution)/shard_map/place_late/pallas_call | solution.py:243
  (41 shorter events, 7.0 us)
Async XLA Ops:
  0.6 12.6 %collective-permute-start = (bf16[1024,2048]{1,0:T(8,128)(2,1)}, bf16[1024,2048]{1,0:T(8,128)(2,1)}, u32[]{:S(2)}, u32[]{:S(2)}) collective-permute-start(bf16[1024,2048]{1,0:T(8,128)(2,1)} %refs_0_.5), channel_id=1, source_target_pairs={{0,1},{1,0},{2,3},{3,2},{4,5},{5,4},{6,7},{7,6},{8,9},{9,8},{10,11... | collective-permute-start | bytes 12582920 | tf_op jit(solution)/shard_map/ppermute | solution.py:31
  1.1 7.1 %collective-permute-start.1 = (s32[8,16]{1,0:T(8,128)}, s32[8,16]{1,0:T(8,128)S(1)}, u32[]{:S(2)}, u32[]{:S(2)}) collective-permute-start(s32[8,16]{1,0:T(8,128)} %param.7), channel_id=1, source_target_pairs={{0,28},{4,0},{8,4},{12,8},{16,12},{20,16},{24,20},{28,24},{1,29},{... | collective-permute-start | bytes 1544 | tf_op jit(solution)/shard_map/ppermute | solution.py:18
  6.7 6.5 %collective-permute-start.2 = (s32[8,16]{1,0:T(8,128)}, s32[8,16]{1,0:T(8,128)S(1)}, u32[]{:S(2)}, u32[]{:S(2)}) collective-permute-start(s32[8,16]{1,0:T(8,128)} %param.7), channel_id=1, source_target_pairs={{0,4},{4,8},{8,12},{12,16},{16,20},{20,24},{24,28},{28,0},{1,5},{5... | collective-permute-start | bytes 1544 | tf_op jit(solution)/shard_map/ppermute | solution.py:18
  13.3 2.2 %copy-start = (bf16[1024,2048]{1,0:T(8,128)(2,1)S(1)}, bf16[1024,2048]{1,0:T(8,128)(2,1)}, u32[]{:S(2)}) copy-start(bf16[1024,2048]{1,0:T(8,128)(2,1)} %refs_0_.5) | copy-start | bytes 12582916
  15.4 8.2 %copy-start.5 = (s32[8,16]{1,0:T(8,128)S(1)}, s32[8,16]{1,0:T(8,128)}, u32[]{:S(2)}) copy-start(s32[8,16]{1,0:T(8,128)} %param.7) | copy-start | bytes 1540
  18.9 64.2 %collective-permute-start.6 = (bf16[2,128,2048]{2,1,0:T(8,128)(2,1)}, bf16[2,128,2048]{2,1,0:T(8,128)(2,1)S(1)}, u32[]{:S(2)}, u32[]{:S(2)}) collective-permute-start(bf16[2,128,2048]{2,1,0:T(8,128)(2,1)} %get-tuple-element.56), channel_id=1, source_target_pairs={{0,4},{4,8},{8,12},{12,16},{16,20},{20,24},{24,28},{28,0},{1,5},{5... | collective-permute-start | bytes 3145736 | tf_op jit(solution)/shard_map/ppermute | solution.py:18
  19.0 34.8 %copy-start.4 = (f32[2048]{0:T(1024)S(1)}, f32[2048]{0:T(1024)}, u32[]{:S(2)}) copy-start(f32[2048]{0:T(1024)} %param.5) | copy-start | bytes 24580
  19.0 34.8 %copy-start.6 = (f32[2048]{0:T(1024)S(1)}, f32[2048]{0:T(1024)}, u32[]{:S(2)}) copy-start(f32[2048]{0:T(1024)} %param.6) | copy-start | bytes 24580
  19.0 64.2 %collective-permute-start.7 = (bf16[2,128,2048]{2,1,0:T(8,128)(2,1)}, bf16[2,128,2048]{2,1,0:T(8,128)(2,1)S(1)}, u32[]{:S(2)}, u32[]{:S(2)}) collective-permute-start(bf16[2,128,2048]{2,1,0:T(8,128)(2,1)} %get-tuple-element.57), channel_id=1, source_target_pairs={{0,28},{4,0},{8,4},{12,8},{16,12},{20,16},{24,20},{28,24},{1,29},{... | collective-permute-start | bytes 3145736 | tf_op jit(solution)/shard_map/ppermute | solution.py:18
  23.7 21.7 %collective-permute-start.3 = (s32[8,16]{1,0:T(8,128)S(1)}, s32[8,16]{1,0:T(8,128)S(1)}, u32[]{:S(2)}, u32[]{:S(2)}) collective-permute-start(s32[8,16]{1,0:T(8,128)S(1)} %copy-done.5), channel_id=1, source_target_pairs={{0,8},{4,12},{8,16},{12,20},{16,24},{20,28},{24,0},{28,4},{1,9},{5... | collective-permute-start | bytes 1544 | tf_op jit(solution)/shard_map/ppermute | solution.py:18
  23.7 21.7 %collective-permute-start.4 = (s32[8,16]{1,0:T(8,128)S(1)}, s32[8,16]{1,0:T(8,128)S(1)}, u32[]{:S(2)}, u32[]{:S(2)}) collective-permute-start(s32[8,16]{1,0:T(8,128)S(1)} %copy-done.5), channel_id=1, source_target_pairs={{0,24},{4,28},{8,0},{12,4},{16,8},{20,12},{24,16},{28,20},{1,25},{... | collective-permute-start | bytes 1544 | tf_op jit(solution)/shard_map/ppermute | solution.py:18
  49.5 33.9 %collective-permute-start.12 = (bf16[2,128,2048]{2,1,0:T(8,128)(2,1)}, bf16[2,128,2048]{2,1,0:T(8,128)(2,1)S(1)}, u32[]{:S(2)}, u32[]{:S(2)}) collective-permute-start(bf16[2,128,2048]{2,1,0:T(8,128)(2,1)} %get-tuple-element.71), channel_id=1, source_target_pairs={{0,24},{4,28},{8,0},{12,4},{16,8},{20,12},{24,16},{28,20},{1,25},{... | collective-permute-start | bytes 3145736 | tf_op jit(solution)/shard_map/ppermute | solution.py:18
  53.8 1.2 collective-permute-start.5
  57.2 25.9 %copy-start.3 = (bf16[2,128,2048]{2,1,0:T(8,128)(2,1)S(1)}, bf16[2,128,2048]{2,1,0:T(8,128)(2,1)}, u32[]{:S(2)}) copy-start(bf16[2,128,2048]{2,1,0:T(8,128)(2,1)} %copy-done.2) | copy-start | bytes 3145732
  68.7 2.0 %collective-permute-start.8 = (bf16[4,8,32,256]{3,2,1,0:T(8,128)(2,1)S(1)}, bf16[4,8,32,256]{3,2,1,0:T(8,128)(2,1)S(1)}, u32[]{:S(2)}, u32[]{:S(2)}) collective-permute-start(bf16[4,8,32,256]{3,2,1,0:T(8,128)(2,1)S(1)} %get-tuple-element.61), channel_id=1, source_target_pairs={{0,1},{1,0},{2,3},{3,2},{4,5},{5,4},{6,7},{7,6},{8,9},{9,8},{10,11... | collective-permute-start | bytes 1572872 | tf_op jit(solution)/shard_map/ppermute | solution.py:31
  69.0 14.2 %collective-permute-start.9 = (bf16[4,8,32,256]{3,2,1,0:T(8,128)(2,1)S(1)}, bf16[4,8,32,256]{3,2,1,0:T(8,128)(2,1)S(1)}, u32[]{:S(2)}, u32[]{:S(2)}) collective-permute-start(bf16[4,8,32,256]{3,2,1,0:T(8,128)(2,1)S(1)} %get-tuple-element.63), channel_id=1, source_target_pairs={{0,2},{1,3},{2,0},{3,1},{4,6},{5,7},{6,4},{7,5},{8,10},{9,11},{10,... | collective-permute-start | bytes 1572872 | tf_op jit(solution)/shard_map/ppermute | solution.py:31
  83.2 32.7 %collective-permute-start.10 = (bf16[2,128,2048]{2,1,0:T(8,128)(2,1)S(1)}, bf16[2,128,2048]{2,1,0:T(8,128)(2,1)S(1)}, u32[]{:S(2)}, u32[]{:S(2)}) collective-permute-start(bf16[2,128,2048]{2,1,0:T(8,128)(2,1)S(1)} %copy-done.3), channel_id=1, source_target_pairs={{0,8},{4,12},{8,16},{12,20},{16,24},{20,28},{24,0},{28,4},{1,9},{5... | collective-permute-start | bytes 3145736 | tf_op jit(solution)/shard_map/ppermute | solution.py:18
  92.5 3.0 %collective-permute-start.13 = (bf16[3,8,32,256]{3,2,1,0:T(8,128)(2,1)S(1)}, bf16[3,8,32,256]{3,2,1,0:T(8,128)(2,1)S(1)}, u32[]{:S(2)}, u32[]{:S(2)}) collective-permute-start(bf16[3,8,32,256]{3,2,1,0:T(8,128)(2,1)S(1)} %get-tuple-element.74), channel_id=1, source_target_pairs={{0,1},{1,0},{2,3},{3,2},{4,5},{5,4},{6,7},{7,6},{8,9},{9,8},{10,11... | collective-permute-start | bytes 1179656 | tf_op jit(solution)/shard_map/ppermute | solution.py:31
  92.6 13.9 %collective-permute-start.11 = (bf16[4,8,32,256]{3,2,1,0:T(8,128)(2,1)S(1)}, bf16[4,8,32,256]{3,2,1,0:T(8,128)(2,1)S(1)}, u32[]{:S(2)}, u32[]{:S(2)}) collective-permute-start(bf16[4,8,32,256]{3,2,1,0:T(8,128)(2,1)S(1)} %get-tuple-element.68), channel_id=1, source_target_pairs={{0,3},{1,2},{2,1},{3,0},{4,7},{5,6},{6,5},{7,4},{8,11},{9,10},{10,... | collective-permute-start | bytes 1572872 | tf_op jit(solution)/shard_map/ppermute | solution.py:31
  94.2 21.6 %collective-permute-start.14 = (bf16[3,8,32,256]{3,2,1,0:T(8,128)(2,1)S(1)}, bf16[3,8,32,256]{3,2,1,0:T(8,128)(2,1)S(1)}, u32[]{:S(2)}, u32[]{:S(2)}) collective-permute-start(bf16[3,8,32,256]{3,2,1,0:T(8,128)(2,1)S(1)} %get-tuple-element.76), channel_id=1, source_target_pairs={{0,2},{1,3},{2,0},{3,1},{4,6},{5,7},{6,4},{7,5},{8,10},{9,11},{10,... | collective-permute-start | bytes 1179656 | tf_op jit(solution)/shard_map/ppermute | solution.py:31
  95.5 27.7 %collective-permute-start.15 = (bf16[3,8,32,256]{3,2,1,0:T(8,128)(2,1)S(1)}, bf16[3,8,32,256]{3,2,1,0:T(8,128)(2,1)S(1)}, u32[]{:S(2)}, u32[]{:S(2)}) collective-permute-start(bf16[3,8,32,256]{3,2,1,0:T(8,128)(2,1)S(1)} %get-tuple-element.88), channel_id=1, source_target_pairs={{0,3},{1,2},{2,1},{3,0},{4,7},{5,6},{6,5},{7,4},{8,11},{9,10},{10,... | collective-permute-start | bytes 1179656 | tf_op jit(solution)/shard_map/ppermute | solution.py:31
  120.5 1.7 %collective-permute-start.16 = (bf16[1,8,32,256]{3,2,1,0:T(8,128)(2,1)S(1)}, bf16[1,8,32,256]{3,2,1,0:T(8,128)(2,1)S(1)}, u32[]{:S(2)}, u32[]{:S(2)}) collective-permute-start(bf16[1,8,32,256]{3,2,1,0:T(8,128)(2,1)S(1)} %get-tuple-element.92), channel_id=1, source_target_pairs={{0,1},{1,0},{2,3},{3,2},{4,5},{5,4},{6,7},{7,6},{8,9},{9,8},{10,11... | collective-permute-start | bytes 393224 | tf_op jit(solution)/shard_map/ppermute | solution.py:31
  120.6 7.2 %collective-permute-start.17 = (bf16[1,8,32,256]{3,2,1,0:T(8,128)(2,1)S(1)}, bf16[1,8,32,256]{3,2,1,0:T(8,128)(2,1)S(1)}, u32[]{:S(2)}, u32[]{:S(2)}) collective-permute-start(bf16[1,8,32,256]{3,2,1,0:T(8,128)(2,1)S(1)} %get-tuple-element.94), channel_id=1, source_target_pairs={{0,2},{1,3},{2,0},{3,1},{4,6},{5,7},{6,4},{7,5},{8,10},{9,11},{10,... | collective-permute-start | bytes 393224 | tf_op jit(solution)/shard_map/ppermute | solution.py:31
  122.2 6.8 %collective-permute-start.18 = (bf16[1,8,32,256]{3,2,1,0:T(8,128)(2,1)S(1)}, bf16[1,8,32,256]{3,2,1,0:T(8,128)(2,1)S(1)}, u32[]{:S(2)}, u32[]{:S(2)}) collective-permute-start(bf16[1,8,32,256]{3,2,1,0:T(8,128)(2,1)S(1)} %get-tuple-element.95), channel_id=1, source_target_pairs={{0,3},{1,2},{2,1},{3,0},{4,7},{5,6},{6,5},{7,4},{8,11},{9,10},{10,... | collective-permute-start | bytes 393224 | tf_op jit(solution)/shard_map/ppermute | solution.py:31
  (2 other events, 3.2 us)

commit v5 on v4

--- a/solution.py
+++ b/solution.py
@@ -280,12 +280,12 @@
     here = jnp.stack([own_index, core]).astype(jnp.int32)
     place = jnp.stack([core] + targets).astype(jnp.int32)
 
+    asks = lax.optimization_barrier(asks)
     near = list(pick(here, asks[:2], eigvecs, sib, tile))
     here, near[0] = lax.optimization_barrier((here, near[0]))
     far = list(pick(here, asks[2:], eigvecs, sib, tile))
     occupations, far[0] = lax.optimization_barrier((occupations, far[0]))
     near = [shifted(near[0], "atoms", -offsets[0]), shifted(near[1], "atoms", -offsets[1])]
-    third = shifted(far[0], "atoms", -offsets[2])
     own_weights = jnp.stack([occupations, occupations * energies], 0)
     sib_weights = to_strip_target(own_weights, chips, 0, 1)
     weights = (own_weights, sib_weights)
@@ -300,7 +300,10 @@
         return parts
 
     chunks = [strips_of()]
-    neighbours, chunks[0][0] = lax.optimization_barrier((neighbours, chunks[0][0]))
+    neighbours, chunks[0][0], far[0] = lax.optimization_barrier(
+        (neighbours, chunks[0][0], far[0])
+    )
+    third = shifted(far[0], "atoms", -offsets[2])
 
     owners = lax.div(neighbours, blocks)
     within = lax.rem(neighbours, blocks)
@@ -315,11 +318,16 @@
     per_core = half_blocks + len(offsets)
     where = ((side ^ core) * per_core + spot).astype(jnp.int32)
 
-    near, source, chunks[0][:3] = lax.optimization_barrier((near, far[1], chunks[0][:3]))
+    near, chunks[0][:3] = lax.optimization_barrier((near, chunks[0][:3]))
+    chunks.append(strips_of(*near))
+    source, chunks[1][0] = lax.optimization_barrier((far[1], chunks[1][0]))
     fourth = shifted(source, "atoms", -offsets[3])
-    chunks.append(strips_of(*near, third))
-    where, fourth, chunks[0], chunks[1][:3] = lax.optimization_barrier(
-        (where, fourth, chunks[0], chunks[1][:3])
+    third, chunks[0], chunks[1][:2] = lax.optimization_barrier(
+        (third, chunks[0], chunks[1][:2])
+    )
+    chunks.append(strips_of(third))
+    where, fourth, chunks[1], chunks[2][:3] = lax.optimization_barrier(
+        (where, fourth, chunks[1], chunks[2][:3])
     )
     last = strips_of(fourth)
     where, last[0] = lax.optimization_barrier((where, last[0]))

time: 131 us -> 119 us (0.908)
  waiting for transfers between devices: 56 us -> 45.2 us
  starting transfers between devices: 26.8 us -> 23.9 us
  Pallas kernels: 38 us -> 39.4 us
    ppermute x8, waiting for transfers between devices: 24.3 us -> 12.6 us  [shifted(): return lax.ppermute(value, axis, pairs)]
    ppermute x8, starting transfers between devices: 18.7 us -> 14.2 us  [shifted(): return lax.ppermute(value, axis, pairs)]
    pallas_call x3 -> x4, Pallas kernels: 25.2 us -> 27.6 us  [tiles(): pl.pallas_call(functools.partial(tiles_kernel, len(arrived), n_right, n_s...]
    ppermute x11 -> x14, starting transfers between devices: 8.13 us -> 9.73 us  [to_strip_target(): return lax.ppermute(value, 'bands', pairs)]
    ppermute x11 -> x14, waiting for transfers between devices: 31.6 us -> 32.6 us  [to_strip_target(): return lax.ppermute(value, 'bands', pairs)]
  transfers between devices with their start and end apart: 19 -> 22, of which waited for: 9 -> 11; matrix products, arithmetic and copies ran while one was open for 3% -> 3% of each run, Pallas kernels for 25% -> 25%
where the time goes in v5:
time: 119 us; the launch traced here: 118 us
  waiting for transfers between devices  45.2 us (38%)
  Pallas kernels  39.4 us (33%)
  starting transfers between devices  23.9 us (20%)
  local copies, waits for them, and re-layouts  5.48 us (5%)
  other arithmetic  3.39 us (3%)
    ppermute x14, waiting for transfers between devices, to_strip_target(): return lax.ppermute(value, 'bands', pairs)  32.6 us
    pallas_call x4, Pallas kernels, tiles(): pl.pallas_call(functools.partial(tiles_kernel, len(arrived), n_right, n_s...  27.6 us
    ppermute x8, starting transfers between devices, shifted(): return lax.ppermute(value, axis, pairs)  14.2 us
    ppermute x8, waiting for transfers between devices, shifted(): return lax.ppermute(value, axis, pairs)  12.6 us
    ppermute x14, starting transfers between devices, to_strip_target(): return lax.ppermute(value, 'bands', pairs)  9.73 us
    pallas_call x2, Pallas kernels, pick(): pl.pallas_call(functools.partial(pick_kernel, count, blocks, tile), out_s...  5.58 us
    unnamed x14, local copies, waits for them, and re-layouts  5.4 us
    pallas_call x1, Pallas kernels, place_early(): pl.pallas_call(functools.partial(place_early_kernel, chips, sizes, per_co...  4.59 us
  transfers between devices with their start and end apart: 22, of which 11 were waited for; matrix products, arithmetic and copies ran while one was open for 3% of the time, Pallas kernels for 25%

profile of v5, /device:TPU:0, one launch (start us, length us, event | category | flops | bytes accessed | tf_op | source)
XLA Modules:
  0.0 118.4 jit_solution(13748754983565352111)
XLA Ops:
  1.1 2.6 %collective-permute-start.3 = (s32[8,16]{1,0:T(8,128)}, s32[8,16]{1,0:T(8,128)S(1)}, u32[]{:S(2)}, u32[]{:S(2)}) collective-permute-start(s32[8,16]{1,0:T(8,128)} %param.7), channel_id=1, source_target_pairs={{0,8},{4,12},{8,16},{12,20},{16,24},{20,28},{24,0},{28,4},{1,9},{5... | collective-permute-start | bytes 1544 | tf_op jit(solution)/shard_map/ppermute | solution.py:18
  3.8 1.5 %collective-permute-start.2 = (s32[8,16]{1,0:T(8,128)}, s32[8,16]{1,0:T(8,128)S(1)}, u32[]{:S(2)}, u32[]{:S(2)}) collective-permute-start(s32[8,16]{1,0:T(8,128)} %param.7), channel_id=1, source_target_pairs={{0,4},{4,8},{8,12},{12,16},{16,20},{20,24},{24,28},{28,0},{1,5},{5... | collective-permute-start | bytes 1544 | tf_op jit(solution)/shard_map/ppermute | solution.py:18
  5.3 3.2 %collective-permute-start.1 = (s32[8,16]{1,0:T(8,128)}, s32[8,16]{1,0:T(8,128)S(1)}, u32[]{:S(2)}, u32[]{:S(2)}) collective-permute-start(s32[8,16]{1,0:T(8,128)} %param.7), channel_id=1, source_target_pairs={{0,28},{4,0},{8,4},{12,8},{16,12},{20,16},{24,20},{28,24},{1,29},{... | collective-permute-start | bytes 1544 | tf_op jit(solution)/shard_map/ppermute | solution.py:18
  10.3 2.0 %collective-permute-done.4.refs_1_ = s32[8,16]{1,0:T(8,128)S(1)} collective-permute-done((s32[8,16]{1,0:T(8,128)}, s32[8,16]{1,0:T(8,128)S(1)}, u32[]{:S(2)}, u32[]{:S(2)}) %collective-permute-start.4) | collective-permute-done | bytes 544 | tf_op jit(solution)/shard_map/ppermute | solution.py:18
  12.3 2.2 %copy-done = bf16[1024,2048]{1,0:T(8,128)(2,1)S(1)} copy-done((bf16[1024,2048]{1,0:T(8,128)(2,1)S(1)}, bf16[1024,2048]{1,0:T(8,128)(2,1)}, u32[]{:S(2)}) %copy-start) | copy-done | bytes 4194328
  14.5 3.4 %pick_blocks.2 = (bf16[2,128,2048]{2,1,0:T(8,128)(2,1)}, bf16[2,128,2048]{2,1,0:T(8,128)(2,1)}) custom-call(s32[2]{0:T(128)S(1)} %pad_add_fusion.place_ref, s32[8,16]{1,0:T(8,128)S(1)} %collective-permute-done.1.refs_0_, s32[8,16]{1,0:T(8,128)S(1)} %collective-permute-done.2.refs_1_, bf16[1024,2048]{1,0:T(8,128)(2,1)S(1)} %copy-done, ...), custom_call_target="tpu_custom_call" | custom-call | tf_op jit(solution)/shard_map/pick_blocks/pallas_call | solution.py:60
  18.1 4.7 %collective-permute-start.7 = (bf16[2,128,2048]{2,1,0:T(8,128)(2,1)}, bf16[2,128,2048]{2,1,0:T(8,128)(2,1)S(1)}, u32[]{:S(2)}, u32[]{:S(2)}) collective-permute-start(bf16[2,128,2048]{2,1,0:T(8,128)(2,1)} %get-tuple-element.82), channel_id=1, source_target_pairs={{0,28},{4,0},{8,4},{12,8},{16,12},{20,16},{24,20},{28,24},{1,29},{... | collective-permute-start | bytes 3145736 | tf_op jit(solution)/shard_map/ppermute | solution.py:18
  22.8 2.1 %pick_blocks.3 = (bf16[2,128,2048]{2,1,0:T(8,128)(2,1)S(1)}, bf16[2,128,2048]{2,1,0:T(8,128)(2,1)S(1)}) custom-call(s32[2]{0:T(128)S(1)} %pad_add_fusion.place_ref, s32[8,16]{1,0:T(8,128)S(1)} %collective-permute-done.3.refs_0_, s32[8,16]{1,0:T(8,128)S(1)} %collective-permute-done.4.refs_1_, bf16[1024,2048]{1,0:T(8,128)(2,1)S(1)} %copy-done, ...), custom_call_target="tpu_custom_call" | custom-call | tf_op jit(solution)/shard_map/pick_blocks/pallas_call | solution.py:60
  27.2 2.2 %copy-done.1 = bf16[1024,2048]{1,0:T(8,128)(2,1)S(1)} copy-done((bf16[1024,2048]{1,0:T(8,128)(2,1)S(1)}, bf16[1024,2048]{1,0:T(8,128)(2,1)}, u32[]{:S(2)}) %copy-start.1) | copy-done | bytes 4194328
  29.4 11.5 %tiles.4 = (bf16[4,8,32,256]{3,2,1,0:T(8,128)(2,1)S(1)}, bf16[4,8,32,256]{3,2,1,0:T(8,128)(2,1)S(1)}, bf16[4,8,32,256]{3,2,1,0:T(8,128)(2,1)S(1)}, bf16[4,8,32,256]{3,2,1,0:T(8,128)(2,1)S(1)}) custom-call(s32[5]{0:T(128)S(1)} %stack.39.place_ref, bf16[1024,2048]{1,0:T(8,128)(2,1)S(1)} %copy-done.1, bf16[1024,2048]{1,0:T(8,128)(2,1)} %collective-permute-done.refs_3_.refs_1_, ...), custom_call_target="tpu_custom_call" | custom-call | tf_op jit(solution)/shard_map/tiles/pallas_call | solution.py:118
  41.1 1.5 %collective-permute-start.9 = (bf16[4,8,32,256]{3,2,1,0:T(8,128)(2,1)S(1)}, bf16[4,8,32,256]{3,2,1,0:T(8,128)(2,1)S(1)}, u32[]{:S(2)}, u32[]{:S(2)}) collective-permute-start(bf16[4,8,32,256]{3,2,1,0:T(8,128)(2,1)S(1)} %get-tuple-element.87), channel_id=1, source_target_pairs={{0,2},{1,3},{2,0},{3,1},{4,6},{5,7},{6,4},{7,5},{8,10},{9,11},{10,... | collective-permute-start | bytes 1572872 | tf_op jit(solution)/shard_map/ppermute | solution.py:31
  43.1 12.2 %collective-permute-done.9.refs_6_ = bf16[4,8,32,256]{3,2,1,0:T(8,128)(2,1)S(1)} collective-permute-done((bf16[4,8,32,256]{3,2,1,0:T(8,128)(2,1)S(1)}, bf16[4,8,32,256]{3,2,1,0:T(8,128)(2,1)S(1)}, u32[]{:S(2)}, u32[]{:S(2)}) %collective-permute-start.9) | collective-permute-done | bytes 524320 | tf_op jit(solution)/shard_map/ppermute | solution.py:31
  55.3 7.0 %collective-permute-done.6.refs_4_ = bf16[2,128,2048]{2,1,0:T(8,128)(2,1)S(1)} collective-permute-done((bf16[2,128,2048]{2,1,0:T(8,128)(2,1)}, bf16[2,128,2048]{2,1,0:T(8,128)(2,1)S(1)}, u32[]{:S(2)}, u32[]{:S(2)}) %collective-permute-start.6) | collective-permute-done | bytes 1048608 | tf_op jit(solution)/shard_map/ppermute | solution.py:18
  62.3 2.1 %collective-permute-done.7.refs_5_ = bf16[2,128,2048]{2,1,0:T(8,128)(2,1)S(1)} collective-permute-done((bf16[2,128,2048]{2,1,0:T(8,128)(2,1)}, bf16[2,128,2048]{2,1,0:T(8,128)(2,1)S(1)}, u32[]{:S(2)}, u32[]{:S(2)}) %collective-permute-start.7) | collective-permute-done | bytes 1048608 | tf_op jit(solution)/shard_map/ppermute | solution.py:18
  64.4 6.9 %tiles.5 = (bf16[2,8,32,256]{3,2,1,0:T(8,128)(2,1)S(1)}, bf16[2,8,32,256]{3,2,1,0:T(8,128)(2,1)S(1)}, bf16[2,8,32,256]{3,2,1,0:T(8,128)(2,1)S(1)}, bf16[2,8,32,256]{3,2,1,0:T(8,128)(2,1)S(1)}) custom-call(s32[5]{0:T(128)S(1)} %stack.39.place_ref, bf16[1024,2048]{1,0:T(8,128)(2,1)S(1)} %copy-done.1, bf16[1024,2048]{1,0:T(8,128)(2,1)} %collective-permute-done.refs_3_.refs_1_, ...), custom_call_target="tpu_custom_call" | custom-call | tf_op jit(solution)/shard_map/tiles/pallas_call | solution.py:118
  76.7 10.1 %collective-permute-done.12.refs_9_ = bf16[4,8,32,256]{3,2,1,0:T(8,128)(2,1)S(1)} collective-permute-done((bf16[4,8,32,256]{3,2,1,0:T(8,128)(2,1)S(1)}, bf16[4,8,32,256]{3,2,1,0:T(8,128)(2,1)S(1)}, u32[]{:S(2)}, u32[]{:S(2)}) %collective-permute-start.12) | collective-permute-done | bytes 524320 | tf_op jit(solution)/shard_map/ppermute | solution.py:31
  86.8 4.6 %tiles.6 = (bf16[1,8,32,256]{3,2,1,0:T(8,128)(2,1)S(1)}, bf16[1,8,32,256]{3,2,1,0:T(8,128)(2,1)S(1)}, bf16[1,8,32,256]{3,2,1,0:T(8,128)(2,1)S(1)}, bf16[1,8,32,256]{3,2,1,0:T(8,128)(2,1)S(1)}) custom-call(s32[5]{0:T(128)S(1)} %stack.39.place_ref, bf16[1024,2048]{1,0:T(8,128)(2,1)S(1)} %copy-done.1, bf16[1024,2048]{1,0:T(8,128)(2,1)} %collective-permute-done.refs_3_.refs_1_, ...), custom_call_target="tpu_custom_call" | custom-call | tf_op jit(solution)/shard_map/tiles/pallas_call | solution.py:118
  91.8 1.4 %collective-permute-start.17 = (bf16[1,8,32,256]{3,2,1,0:T(8,128)(2,1)S(1)}, bf16[1,8,32,256]{3,2,1,0:T(8,128)(2,1)S(1)}, u32[]{:S(2)}, u32[]{:S(2)}) collective-permute-start(bf16[1,8,32,256]{3,2,1,0:T(8,128)(2,1)S(1)} %get-tuple-element.110), channel_id=1, source_target_pairs={{0,2},{1,3},{2,0},{3,1},{4,6},{5,7},{6,4},{7,5},{8,10},{9,11},{10,... | collective-permute-start | bytes 393224 | tf_op jit(solution)/shard_map/ppermute | solution.py:31
  93.2 2.6 %fusion.9.where_ref = s32[8,16]{1,0:T(8,128)S(1)} fusion(pred[8,16]{1,0:T(8,128)(4,1)S(1)} %get-tuple-element.143, pred[8,16]{1,0:T(8,128)(4,1)S(1)} %get-tuple-element.142, pred[8,16]{1,0:T(8,128)(4,1)S(1)} %get-tuple-element.141, pred[8,16]{1,0:T(8,128)(4,1)S(1)} %get-tuple-element.140, s32[]{:T(128)} %and.14, s32[]{:T(128)} %get-tuple-element.138, ...), kind=kLoop, calls=%fused_computation.18 | loop fusion | flops 4352 | bytes 1556 | tf_op jit(solution)/shard_map/add | solution.py:319
  95.8 5.2 %collective-permute-done.17.refs_8_ = bf16[1,8,32,256]{3,2,1,0:T(8,128)(2,1)S(1)} collective-permute-done((bf16[1,8,32,256]{3,2,1,0:T(8,128)(2,1)S(1)}, bf16[1,8,32,256]{3,2,1,0:T(8,128)(2,1)S(1)}, u32[]{:S(2)}, u32[]{:S(2)}) %collective-permute-start.17) | collective-permute-done | bytes 131104 | tf_op jit(solution)/shard_map/ppermute | solution.py:31
  100.9 4.6 %tiles.7 = (bf16[1,8,32,256]{3,2,1,0:T(8,128)(2,1)S(1)}, bf16[1,8,32,256]{3,2,1,0:T(8,128)(2,1)S(1)}, bf16[1,8,32,256]{3,2,1,0:T(8,128)(2,1)S(1)}, bf16[1,8,32,256]{3,2,1,0:T(8,128)(2,1)S(1)}) custom-call(s32[5]{0:T(128)S(1)} %stack.39.place_ref, bf16[1024,2048]{1,0:T(8,128)(2,1)S(1)} %copy-done.1, bf16[1024,2048]{1,0:T(8,128)(2,1)} %collective-permute-done.refs_3_.refs_1_, ...), custom_call_target="tpu_custom_call" | custom-call | tf_op jit(solution)/shard_map/tiles/pallas_call | solution.py:118
  108.6 2.3 %collective-permute-done.18.refs_11_ = bf16[1,8,32,256]{3,2,1,0:T(8,128)(2,1)S(1)} collective-permute-done((bf16[1,8,32,256]{3,2,1,0:T(8,128)(2,1)S(1)}, bf16[1,8,32,256]{3,2,1,0:T(8,128)(2,1)S(1)}, u32[]{:S(2)}, u32[]{:S(2)}) %collective-permute-start.18) | collective-permute-done | bytes 131104 | tf_op jit(solution)/shard_map/ppermute | solution.py:31
  110.9 4.6 %place_early.1 = (f32[8,16,32,128]{3,2,1,0:T(8,128)}, f32[8,16,32,128]{3,2,1,0:T(8,128)}, s32[129]{0:T(256)S(1)}) custom-call(s32[8,16]{1,0:T(8,128)S(1)} %fusion.9.where_ref, bf16[4,8,32,256]{3,2,1,0:T(8,128)(2,1)S(1)} %get-tuple-element.115.refs_0_, bf16[2,8,32,256]{3,2,1,0:T(8,128)(2,1)S(1)} %get-tuple-element.116.refs_1_, ...), custom_call_target="tpu_custom_call" | custom-call | tf_op jit(solution)/shard_map/place_early/pallas_call | solution.py:179
  116.6 1.6 %place_late.1 = (f32[8,16,32,128]{3,2,1,0:T(8,128)}, f32[8,16,32,128]{3,2,1,0:T(8,128)}) custom-call(s32[8,16]{1,0:T(8,128)S(1)} %fusion.9.where_ref, s32[129]{0:T(256)S(1)} %get-tuple-element.127.later, bf16[1,8,32,256]{3,2,1,0:T(8,128)(2,1)S(1)} %get-tuple-element.128.refs_0_, ...), custom_call_target="tpu_custom_call", output_to_operand_aliasing={{0}: (6, {}), {1}: (7, {})} | custom-call | tf_op jit(solution)/shard_map/place_late/pallas_call | solution.py:243
  (48 shorter events, 15.0 us)
Async XLA Ops:
  0.6 11.7 %collective-permute-start = (bf16[1024,2048]{1,0:T(8,128)(2,1)}, bf16[1024,2048]{1,0:T(8,128)(2,1)}, u32[]{:S(2)}, u32[]{:S(2)}) collective-permute-start(bf16[1024,2048]{1,0:T(8,128)(2,1)} %refs_0_.7), channel_id=1, source_target_pairs={{0,1},{1,0},{2,3},{3,2},{4,5},{5,4},{6,7},{7,6},{8,9},{9,8},{10,11... | collective-permute-start | bytes 12582920 | tf_op jit(solution)/shard_map/ppermute | solution.py:31
  1.1 7.8 %collective-permute-start.3 = (s32[8,16]{1,0:T(8,128)}, s32[8,16]{1,0:T(8,128)S(1)}, u32[]{:S(2)}, u32[]{:S(2)}) collective-permute-start(s32[8,16]{1,0:T(8,128)} %param.7), channel_id=1, source_target_pairs={{0,8},{4,12},{8,16},{12,20},{16,24},{20,28},{24,0},{28,4},{1,9},{5... | collective-permute-start | bytes 1544 | tf_op jit(solution)/shard_map/ppermute | solution.py:18
  3.8 6.5 %collective-permute-start.2 = (s32[8,16]{1,0:T(8,128)}, s32[8,16]{1,0:T(8,128)S(1)}, u32[]{:S(2)}, u32[]{:S(2)}) collective-permute-start(s32[8,16]{1,0:T(8,128)} %param.7), channel_id=1, source_target_pairs={{0,4},{4,8},{8,12},{12,16},{16,20},{20,24},{24,28},{28,0},{1,5},{5... | collective-permute-start | bytes 1544 | tf_op jit(solution)/shard_map/ppermute | solution.py:18
  5.3 5.0 %collective-permute-start.1 = (s32[8,16]{1,0:T(8,128)}, s32[8,16]{1,0:T(8,128)S(1)}, u32[]{:S(2)}, u32[]{:S(2)}) collective-permute-start(s32[8,16]{1,0:T(8,128)} %param.7), channel_id=1, source_target_pairs={{0,28},{4,0},{8,4},{12,8},{16,12},{20,16},{24,20},{28,24},{1,29},{... | collective-permute-start | bytes 1544 | tf_op jit(solution)/shard_map/ppermute | solution.py:18
  8.5 3.8 %collective-permute-start.4 = (s32[8,16]{1,0:T(8,128)}, s32[8,16]{1,0:T(8,128)S(1)}, u32[]{:S(2)}, u32[]{:S(2)}) collective-permute-start(s32[8,16]{1,0:T(8,128)} %param.7), channel_id=1, source_target_pairs={{0,24},{4,28},{8,0},{12,4},{16,8},{20,12},{24,16},{28,20},{1,25},{... | collective-permute-start | bytes 1544 | tf_op jit(solution)/shard_map/ppermute | solution.py:18
  18.0 44.4 %collective-permute-start.6 = (bf16[2,128,2048]{2,1,0:T(8,128)(2,1)}, bf16[2,128,2048]{2,1,0:T(8,128)(2,1)S(1)}, u32[]{:S(2)}, u32[]{:S(2)}) collective-permute-start(bf16[2,128,2048]{2,1,0:T(8,128)(2,1)} %get-tuple-element.81), channel_id=1, source_target_pairs={{0,4},{4,8},{8,12},{12,16},{16,20},{20,24},{24,28},{28,0},{1,5},{5... | collective-permute-start | bytes 3145736 | tf_op jit(solution)/shard_map/ppermute | solution.py:18
  18.1 46.4 %collective-permute-start.7 = (bf16[2,128,2048]{2,1,0:T(8,128)(2,1)}, bf16[2,128,2048]{2,1,0:T(8,128)(2,1)S(1)}, u32[]{:S(2)}, u32[]{:S(2)}) collective-permute-start(bf16[2,128,2048]{2,1,0:T(8,128)(2,1)} %get-tuple-element.82), channel_id=1, source_target_pairs={{0,28},{4,0},{8,4},{12,8},{16,12},{20,16},{24,20},{28,24},{1,29},{... | collective-permute-start | bytes 3145736 | tf_op jit(solution)/shard_map/ppermute | solution.py:18
  25.9 1.2 %collective-permute-start.5 = (f32[2,2048]{1,0:T(2,128)S(1)}, f32[2,2048]{1,0:T(2,128)S(1)}, u32[]{:S(2)}, u32[]{:S(2)}) collective-permute-start(f32[2,2048]{1,0:T(2,128)S(1)} %pad_maximum_fusion.refs_2_), channel_id=1, source_target_pairs={{0,1},{1,0},{2,3},{3,2},{4,5},{5,4},{6,7},{7,6},{8,9},{9,8},{10,11... | collective-permute-start | bytes 49160 | tf_op jit(solution)/shard_map/ppermute | solution.py:31
  29.4 13.2 %copy-start.3 = (bf16[2,128,2048]{2,1,0:T(8,128)(2,1)S(1)}, bf16[2,128,2048]{2,1,0:T(8,128)(2,1)}, u32[]{:S(2)}) copy-start(bf16[2,128,2048]{2,1,0:T(8,128)(2,1)} %copy-done.2) | copy-start | bytes 3145732
  40.9 2.2 %collective-permute-start.8 = (bf16[4,8,32,256]{3,2,1,0:T(8,128)(2,1)S(1)}, bf16[4,8,32,256]{3,2,1,0:T(8,128)(2,1)S(1)}, u32[]{:S(2)}, u32[]{:S(2)}) collective-permute-start(bf16[4,8,32,256]{3,2,1,0:T(8,128)(2,1)S(1)} %get-tuple-element.85), channel_id=1, source_target_pairs={{0,1},{1,0},{2,3},{3,2},{4,5},{5,4},{6,7},{7,6},{8,9},{9,8},{10,11... | collective-permute-start | bytes 1572872 | tf_op jit(solution)/shard_map/ppermute | solution.py:31
  41.1 14.2 %collective-permute-start.9 = (bf16[4,8,32,256]{3,2,1,0:T(8,128)(2,1)S(1)}, bf16[4,8,32,256]{3,2,1,0:T(8,128)(2,1)S(1)}, u32[]{:S(2)}, u32[]{:S(2)}) collective-permute-start(bf16[4,8,32,256]{3,2,1,0:T(8,128)(2,1)S(1)} %get-tuple-element.87), channel_id=1, source_target_pairs={{0,2},{1,3},{2,0},{3,1},{4,6},{5,7},{6,4},{7,5},{8,10},{9,11},{10,... | collective-permute-start | bytes 1572872 | tf_op jit(solution)/shard_map/ppermute | solution.py:31
  42.6 44.2 %collective-permute-start.11 = (bf16[2,128,2048]{2,1,0:T(8,128)(2,1)S(1)}, bf16[2,128,2048]{2,1,0:T(8,128)(2,1)S(1)}, u32[]{:S(2)}, u32[]{:S(2)}) collective-permute-start(bf16[2,128,2048]{2,1,0:T(8,128)(2,1)S(1)} %copy-done.3), channel_id=1, source_target_pairs={{0,24},{4,28},{8,0},{12,4},{16,8},{20,12},{24,16},{28,20},{1,25},{... | collective-permute-start | bytes 3145736 | tf_op jit(solution)/shard_map/ppermute | solution.py:18
  43.1 32.9 %copy-start.5 = (s32[8,16]{1,0:T(8,128)S(1)}, s32[8,16]{1,0:T(8,128)}, u32[]{:S(2)}) copy-start(s32[8,16]{1,0:T(8,128)} %param.7) | copy-start | bytes 1540
  71.3 29.6 %collective-permute-start.10 = (bf16[2,128,2048]{2,1,0:T(8,128)(2,1)S(1)}, bf16[2,128,2048]{2,1,0:T(8,128)(2,1)S(1)}, u32[]{:S(2)}, u32[]{:S(2)}) collective-permute-start(bf16[2,128,2048]{2,1,0:T(8,128)(2,1)S(1)} %get-tuple-element.91), channel_id=1, source_target_pairs={{0,8},{4,12},{8,16},{12,20},{16,24},{20,28},{24,0},{28,4},{1,9},{5... | collective-permute-start | bytes 3145736 | tf_op jit(solution)/shard_map/ppermute | solution.py:18
  72.7 14.2 %collective-permute-start.12 = (bf16[4,8,32,256]{3,2,1,0:T(8,128)(2,1)S(1)}, bf16[4,8,32,256]{3,2,1,0:T(8,128)(2,1)S(1)}, u32[]{:S(2)}, u32[]{:S(2)}) collective-permute-start(bf16[4,8,32,256]{3,2,1,0:T(8,128)(2,1)S(1)} %get-tuple-element.96), channel_id=1, source_target_pairs={{0,3},{1,2},{2,1},{3,0},{4,7},{5,6},{6,5},{7,4},{8,11},{9,10},{10,... | collective-permute-start | bytes 1572872 | tf_op jit(solution)/shard_map/ppermute | solution.py:31
  73.5 1.9 %collective-permute-start.13 = (bf16[2,8,32,256]{3,2,1,0:T(8,128)(2,1)S(1)}, bf16[2,8,32,256]{3,2,1,0:T(8,128)(2,1)S(1)}, u32[]{:S(2)}, u32[]{:S(2)}) collective-permute-start(bf16[2,8,32,256]{3,2,1,0:T(8,128)(2,1)S(1)} %get-tuple-element.99), channel_id=1, source_target_pairs={{0,1},{1,0},{2,3},{3,2},{4,5},{5,4},{6,7},{7,6},{8,9},{9,8},{10,11... | collective-permute-start | bytes 786440 | tf_op jit(solution)/shard_map/ppermute | solution.py:31
  74.3 21.5 %collective-permute-start.14 = (bf16[2,8,32,256]{3,2,1,0:T(8,128)(2,1)S(1)}, bf16[2,8,32,256]{3,2,1,0:T(8,128)(2,1)S(1)}, u32[]{:S(2)}, u32[]{:S(2)}) collective-permute-start(bf16[2,8,32,256]{3,2,1,0:T(8,128)(2,1)S(1)} %get-tuple-element.103), channel_id=1, source_target_pairs={{0,2},{1,3},{2,0},{3,1},{4,6},{5,7},{6,4},{7,5},{8,10},{9,11},{10,... | collective-permute-start | bytes 786440 | tf_op jit(solution)/shard_map/ppermute | solution.py:31
  75.5 25.5 %collective-permute-start.15 = (bf16[2,8,32,256]{3,2,1,0:T(8,128)(2,1)S(1)}, bf16[2,8,32,256]{3,2,1,0:T(8,128)(2,1)S(1)}, u32[]{:S(2)}, u32[]{:S(2)}) collective-permute-start(bf16[2,8,32,256]{3,2,1,0:T(8,128)(2,1)S(1)} %get-tuple-element.104), channel_id=1, source_target_pairs={{0,3},{1,2},{2,1},{3,0},{4,7},{5,6},{6,5},{7,4},{8,11},{9,10},{10,... | collective-permute-start | bytes 786440 | tf_op jit(solution)/shard_map/ppermute | solution.py:31
  91.4 4.3 %collective-permute-start.16 = (bf16[1,8,32,256]{3,2,1,0:T(8,128)(2,1)S(1)}, bf16[1,8,32,256]{3,2,1,0:T(8,128)(2,1)S(1)}, u32[]{:S(2)}, u32[]{:S(2)}) collective-permute-start(bf16[1,8,32,256]{3,2,1,0:T(8,128)(2,1)S(1)} %get-tuple-element.108), channel_id=1, source_target_pairs={{0,1},{1,0},{2,3},{3,2},{4,5},{5,4},{6,7},{7,6},{8,9},{9,8},{10,11... | collective-permute-start | bytes 393224 | tf_op jit(solution)/shard_map/ppermute | solution.py:31
  91.8 9.2 %collective-permute-start.17 = (bf16[1,8,32,256]{3,2,1,0:T(8,128)(2,1)S(1)}, bf16[1,8,32,256]{3,2,1,0:T(8,128)(2,1)S(1)}, u32[]{:S(2)}, u32[]{:S(2)}) collective-permute-start(bf16[1,8,32,256]{3,2,1,0:T(8,128)(2,1)S(1)} %get-tuple-element.110), channel_id=1, source_target_pairs={{0,2},{1,3},{2,0},{3,1},{4,6},{5,7},{6,4},{7,5},{8,10},{9,11},{10,... | collective-permute-start | bytes 393224 | tf_op jit(solution)/shard_map/ppermute | solution.py:31
  105.6 2.2 %collective-permute-start.19 = (bf16[1,8,32,256]{3,2,1,0:T(8,128)(2,1)S(1)}, bf16[1,8,32,256]{3,2,1,0:T(8,128)(2,1)S(1)}, u32[]{:S(2)}, u32[]{:S(2)}) collective-permute-start(bf16[1,8,32,256]{3,2,1,0:T(8,128)(2,1)S(1)} %get-tuple-element.130), channel_id=1, source_target_pairs={{0,1},{1,0},{2,3},{3,2},{4,5},{5,4},{6,7},{7,6},{8,9},{9,8},{10,11... | collective-permute-start | bytes 393224 | tf_op jit(solution)/shard_map/ppermute | solution.py:31
  105.7 5.3 %collective-permute-start.18 = (bf16[1,8,32,256]{3,2,1,0:T(8,128)(2,1)S(1)}, bf16[1,8,32,256]{3,2,1,0:T(8,128)(2,1)S(1)}, u32[]{:S(2)}, u32[]{:S(2)}) collective-permute-start(bf16[1,8,32,256]{3,2,1,0:T(8,128)(2,1)S(1)} %get-tuple-element.126), channel_id=1, source_target_pairs={{0,3},{1,2},{2,1},{3,0},{4,7},{5,6},{6,5},{7,4},{8,11},{9,10},{10,... | collective-permute-start | bytes 393224 | tf_op jit(solution)/shard_map/ppermute | solution.py:31
  107.1 8.4 %collective-permute-start.20 = (bf16[1,8,32,256]{3,2,1,0:T(8,128)(2,1)S(1)}, bf16[1,8,32,256]{3,2,1,0:T(8,128)(2,1)S(1)}, u32[]{:S(2)}, u32[]{:S(2)}) collective-permute-start(bf16[1,8,32,256]{3,2,1,0:T(8,128)(2,1)S(1)} %get-tuple-element.132), channel_id=1, source_target_pairs={{0,2},{1,3},{2,0},{3,1},{4,6},{5,7},{6,4},{7,5},{8,10},{9,11},{10,... | collective-permute-start | bytes 393224 | tf_op jit(solution)/shard_map/ppermute | solution.py:31
  107.8 8.8 %collective-permute-start.21 = (bf16[1,8,32,256]{3,2,1,0:T(8,128)(2,1)S(1)}, bf16[1,8,32,256]{3,2,1,0:T(8,128)(2,1)S(1)}, u32[]{:S(2)}, u32[]{:S(2)}) collective-permute-start(bf16[1,8,32,256]{3,2,1,0:T(8,128)(2,1)S(1)} %get-tuple-element.133), channel_id=1, source_target_pairs={{0,3},{1,2},{2,1},{3,0},{4,7},{5,6},{6,5},{7,4},{8,11},{9,10},{10,... | collective-permute-start | bytes 393224 | tf_op jit(solution)/shard_map/ppermute | solution.py:31
  (5 other events, 21.1 us)

commit v6 on v4

--- a/solution.py
+++ b/solution.py
@@ -10,6 +10,14 @@
 R = 2
 VMEM_LIMIT = 24 * 1024 * 1024
 SOON = pl.CostEstimate(flops=0, bytes_accessed=0, transcendentals=0)
+
+
+def in_hbm(value):
+    return pltpu.with_memory_space_constraint(value, pltpu.HBM)
+
+
+def in_vmem(value):
+    return pltpu.with_memory_space_constraint(value, pltpu.VMEM)
 
 
 def shifted(value, axis, steps):
@@ -56,25 +64,49 @@
 def pick(place, asks, own, sib, tile):
     blocks, bands = asks[0].shape[0], own.shape[1]
     count = len(asks)
-    out_shape = [jax.ShapeDtypeStruct((2, tile, bands), own.dtype)] * count
     return pl.pallas_call(
         functools.partial(pick_kernel, count, blocks, tile),
-        out_shape=out_shape,
+        out_shape=[pltpu.VMEM((2, tile, bands), own.dtype)] * count,
         in_specs=[pl.BlockSpec(memory_space=pltpu.SMEM)]
         + [pl.BlockSpec(memory_space=pltpu.VMEM)] * count
         + [pl.BlockSpec(memory_space=pl.ANY)] * 2,
-        out_specs=[pl.BlockSpec(memory_space=pltpu.VMEM)] * len(out_shape),
+        out_specs=[pl.BlockSpec(memory_space=pltpu.VMEM)] * count,
         scratch_shapes=[pltpu.SemaphoreType.DMA((count, 2))],
         name="pick_blocks",
         compiler_params=pltpu.CompilerParams(vmem_limit_bytes=VMEM_LIMIT),
         cost_estimate=SOON,
-    )(place, *asks, own, sib)
-
-
-def tiles_kernel(n_arrived, n_right, n_strips, tile, place_ref, *refs):
+    )(place, *asks, in_hbm(own), in_hbm(sib))
+
+
+def keep_kernel(own, sib, own_out, sib_out, sems):
+    copies = []
+    for half, (source, out) in enumerate(((own, own_out), (sib, sib_out))):
+        copies.append(pltpu.make_async_copy(source, out, sems.at[half]))
+    for copy in copies:
+        copy.start()
+    for copy in copies:
+        copy.wait()
+
+
+def keep(own, sib):
+    return pl.pallas_call(
+        keep_kernel,
+        out_shape=[pltpu.VMEM(own.shape, own.dtype)] * 2,
+        in_specs=[pl.BlockSpec(memory_space=pl.ANY)] * 2,
+        out_specs=[pl.BlockSpec(memory_space=pltpu.VMEM)] * 2,
+        scratch_shapes=[pltpu.SemaphoreType.DMA((2,))],
+        name="keep",
+        compiler_params=pltpu.CompilerParams(vmem_limit_bytes=VMEM_LIMIT),
+        cost_estimate=SOON,
+    )(in_hbm(own), in_hbm(sib))
+
+
+def tiles_kernel(n_arrived, n_right, n_strips, tile, paired, place_ref, *refs):
     lefts, weights = refs[:2], refs[2:4]
     arrived, refs = refs[4 : 4 + n_arrived], refs[4 + n_arrived :]
-    outs, (scaled, total) = refs[:n_strips], refs[n_strips:]
+    outs, (scaled, total) = refs[:-2], refs[-2:]
+    if paired:
+        outs = outs[:2] + tuple(out.at[index] for out in outs[2:] for index in range(2))
     strip = tile // n_strips
     n_left = lefts[0].shape[0] // tile
     for j in range(n_right):
@@ -108,21 +140,21 @@
                 outs[index][j, i] = total[slot, rows, :].astype(outs[index].dtype)
 
 
-def tiles(place, own, sib, arrived, weights, n_strips, tile):
+def tiles(place, own, sib, arrived, weights, n_strips, tile, paired):
     rows, bands = own.shape
     blocks = rows // tile
     n_right = len(arrived) if arrived else blocks // 2
     strip = tile // n_strips
     slots = min(n_right, 2)
     vmem = pl.BlockSpec(memory_space=pltpu.VMEM)
-    return pl.pallas_call(
-        functools.partial(tiles_kernel, len(arrived), n_right, n_strips, tile),
-        out_shape=[
-            jax.ShapeDtypeStruct((n_right, blocks, strip, 2 * tile), jnp.bfloat16)
-        ]
-        * n_strips,
+    out = jax.ShapeDtypeStruct((n_right, blocks, strip, 2 * tile), jnp.bfloat16)
+    pair = jax.ShapeDtypeStruct((2, *out.shape), out.dtype)
+    outs = [out, out] + [pair] * (n_strips // 2 - 1) if paired else [out] * n_strips
+    return pl.pallas_call(
+        functools.partial(tiles_kernel, len(arrived), n_right, n_strips, tile, paired),
+        out_shape=outs,
         in_specs=[pl.BlockSpec(memory_space=pltpu.SMEM)] + [vmem] * (4 + len(arrived)),
-        out_specs=[vmem] * n_strips,
+        out_specs=[vmem] * len(outs),
         scratch_shapes=[
             pltpu.VMEM((slots, 2, 2 * tile, bands), jnp.bfloat16),
             pltpu.VMEM((slots, rows, 2 * tile), jnp.float32),
@@ -130,7 +162,7 @@
         name="tiles",
         compiler_params=pltpu.CompilerParams(vmem_limit_bytes=VMEM_LIMIT),
         cost_estimate=SOON,
-    )(place, own, sib, *weights, *arrived)
+    )(place, in_vmem(own), in_vmem(sib), *weights, *arrived)
 
 
 def strip_sum(ins, chips, n_chunks, other_core, chunk, j, i):
@@ -268,10 +300,14 @@
     blocks = neighbours.shape[0]
     tile = eigvecs.shape[0] // blocks
     half_blocks = blocks // 2
-    offsets = [-1, 1, 2, -2]
-
-    asks = [shifted(neighbours, "atoms", offset) for offset in offsets]
+    offsets = [2, -1, 1, -2]
+
+    asks = [shifted(neighbours, "atoms", offset) for offset in offsets[:3]]
     sib = to_strip_target(eigvecs, chips, 0, 1)
+    own_weights = jnp.stack([occupations, occupations * energies], 0)
+    sib_weights = to_strip_target(own_weights, chips, 0, 1)
+    weights = (own_weights, sib_weights)
+
     targets = [
         strip_target(group, chips, step, other)
         for step in range(chips)
@@ -280,27 +316,34 @@
     here = jnp.stack([own_index, core]).astype(jnp.int32)
     place = jnp.stack([core] + targets).astype(jnp.int32)
 
-    near = list(pick(here, asks[:2], eigvecs, sib, tile))
-    here, near[0] = lax.optimization_barrier((here, near[0]))
-    far = list(pick(here, asks[2:], eigvecs, sib, tile))
-    occupations, far[0] = lax.optimization_barrier((occupations, far[0]))
-    near = [shifted(near[0], "atoms", -offsets[0]), shifted(near[1], "atoms", -offsets[1])]
-    third = shifted(far[0], "atoms", -offsets[2])
-    own_weights = jnp.stack([occupations, occupations * energies], 0)
-    sib_weights = to_strip_target(own_weights, chips, 0, 1)
-    weights = (own_weights, sib_weights)
-
-    def strips_of(*arrived):
-        parts = list(tiles(place, eigvecs, sib, arrived, weights, n_bands, tile))
-        parts[1] = to_strip_target(parts[1], chips, 0, 1)
-        for index in range(2, n_bands):
-            if index % 2:
-                parts[index], parts[1] = lax.optimization_barrier((parts[index], parts[1]))
-            parts[index] = to_strip_target(parts[index], chips, index // 2, index % 2)
+    asks = lax.optimization_barrier(asks)
+    picked = list(pick(here, asks, eigvecs, sib, tile))
+    late_neighbours, picked[0] = lax.optimization_barrier((neighbours, picked[0]))
+    arrived = [
+        shifted(value, "atoms", -offset) for value, offset in zip(picked, offsets)
+    ]
+    last_ask = shifted(late_neighbours, "atoms", offsets[3])
+    kept_eigvecs, picked[0] = lax.optimization_barrier((eigvecs, picked[0]))
+    own, kept_sib = keep(kept_eigvecs, sib)
+
+    def strips_of(arrived, paired):
+        parts = list(tiles(place, own, kept_sib, arrived, weights, n_bands, tile, paired))
+        for index in range(1, len(parts)):
+            step, other = (max(index - 1, 0), index == 1) if paired else (index // 2, index % 2)
+            parts[index] = to_strip_target(parts[index], chips, step, int(other))
         return parts
 
-    chunks = [strips_of()]
-    neighbours, chunks[0][0] = lax.optimization_barrier((neighbours, chunks[0][0]))
+    def passed_on(parts):
+        singles = parts[:2]
+        for pair in parts[2:]:
+            singles += [pair[0], to_strip_target(pair[1], chips, 0, 1)]
+        return singles
+
+    chunks = [strips_of((), True)]
+    neighbours, here, last_ask, chunks[0][0] = lax.optimization_barrier(
+        (neighbours, here, last_ask, chunks[0][0])
+    )
+    (last_picked,) = pick(here, [last_ask], eigvecs, sib, tile)
 
     owners = lax.div(neighbours, blocks)
     within = lax.rem(neighbours, blocks)
@@ -315,13 +358,14 @@
     per_core = half_blocks + len(offsets)
     where = ((side ^ core) * per_core + spot).astype(jnp.int32)
 
-    near, source, chunks[0][:3] = lax.optimization_barrier((near, far[1], chunks[0][:3]))
-    fourth = shifted(source, "atoms", -offsets[3])
-    chunks.append(strips_of(*near, third))
-    where, fourth, chunks[0], chunks[1][:3] = lax.optimization_barrier(
-        (where, fourth, chunks[0], chunks[1][:3])
+    arrived, last_picked, chunks[0] = lax.optimization_barrier(
+        (arrived, last_picked, chunks[0])
     )
-    last = strips_of(fourth)
+    fourth = shifted(last_picked, "atoms", -offsets[3])
+    chunks.append(strips_of(arrived, True))
+    where, fourth, chunks[1] = lax.optimization_barrier((where, fourth, chunks[1]))
+    last = strips_of((fourth,), False)
+    chunks = [passed_on(chunk) for chunk in chunks]
     where, last[0] = lax.optimization_barrier((where, last[0]))
     strips = [[chunk[index] for chunk in chunks] for index in range(n_bands)]
     density, energy, later = place_early(where, strips, chips, per_core, tile)

time: 131 us -> 106 us (0.81)
  waiting for transfers between devices: 56 us -> 46.1 us
  starting transfers between devices: 26.8 us -> 17.9 us
  local copies, waits for them, and re-layouts: 5.46 us -> 0.24 us
  Pallas kernels: 38 us -> 34.4 us
    ppermute x11, waiting for transfers between devices: 31.6 us -> 15.1 us  [to_strip_target(): return lax.ppermute(value, 'bands', pairs)]
    ppermute x8, starting transfers between devices: 18.7 us -> 11.3 us  [shifted(): return lax.ppermute(value, axis, pairs)]
    ppermute x8, waiting for transfers between devices: 24.3 us -> 31 us  [shifted(): return lax.ppermute(value, axis, pairs)]
    unnamed x14 -> x2, local copies, waits for them, and re-layouts: 5.38 us -> 0.01 us
    pallas_call x3, Pallas kernels: 25.2 us -> 20.1 us  [tiles(): pl.pallas_call(functools.partial(tiles_kernel, len(arrived), n_right, n_s...]
    pallas_call x0 -> x1, Pallas kernels: none -> 3.48 us  [keep(): pl.pallas_call(keep_kernel, out_shape=[pltpu.VMEM(own.shape, own.dtype)]...]
    pallas_call x2, Pallas kernels: 6.56 us -> 4.59 us  [pick(): pl.pallas_call(functools.partial(pick_kernel, count, blocks, tile), out_s...]
    ppermute x11, starting transfers between devices: 8.13 us -> 6.56 us  [to_strip_target(): return lax.ppermute(value, 'bands', pairs)]
  transfers between devices with their start and end apart: 19 -> 19, of which waited for: 9 -> 7; matrix products, arithmetic and copies ran while one was open for 3% -> 5% of each run, Pallas kernels for 25% -> 31%
where the time goes in v6:
time: 106 us; the launch traced here: 104 us
  waiting for transfers between devices  46.1 us (43%)
  Pallas kernels  34.4 us (32%)
  starting transfers between devices  17.9 us (17%)
  other arithmetic  4.85 us (5%)
    ppermute x8, waiting for transfers between devices, shifted(): return lax.ppermute(value, axis, pairs)  31 us
    pallas_call x3, Pallas kernels, tiles(): pl.pallas_call(functools.partial(tiles_kernel, len(arrived), n_right, n_s...  20.1 us
    ppermute x11, waiting for transfers between devices, to_strip_target(): return lax.ppermute(value, 'bands', pairs)  15.1 us
    ppermute x8, starting transfers between devices, shifted(): return lax.ppermute(value, axis, pairs)  11.3 us
    ppermute x11, starting transfers between devices, to_strip_target(): return lax.ppermute(value, 'bands', pairs)  6.56 us
    pallas_call x1, Pallas kernels, place_early(): pl.pallas_call(functools.partial(place_early_kernel, chips, sizes, per_co...  4.64 us
    pallas_call x2, Pallas kernels, pick(): pl.pallas_call(functools.partial(pick_kernel, count, blocks, tile), out_s...  4.59 us
    pallas_call x1, Pallas kernels, keep(): pl.pallas_call(keep_kernel, out_shape=[pltpu.VMEM(own.shape, own.dtype)]...  3.48 us
  transfers between devices with their start and end apart: 19, of which 7 were waited for; matrix products, arithmetic and copies ran while one was open for 5% of the time, Pallas kernels for 31%

profile of v6, /device:TPU:0, one launch (start us, length us, event | category | flops | bytes accessed | tf_op | source)
XLA Modules:
  0.0 104.5 jit_solution(9313072632769522317)
XLA Ops:
  1.1 2.6 %collective-permute-start.2 = (s32[8,16]{1,0:T(8,128)}, s32[8,16]{1,0:T(8,128)S(1)}, u32[]{:S(2)}, u32[]{:S(2)}) collective-permute-start(s32[8,16]{1,0:T(8,128)} %param.7), channel_id=1, source_target_pairs={{0,4},{4,8},{8,12},{12,16},{16,20},{20,24},{24,28},{28,0},{1,5},{5... | collective-permute-start | bytes 1544 | tf_op jit(solution)/shard_map/ppermute | solution.py:26
  3.7 3.1 %collective-permute-start.1 = (s32[8,16]{1,0:T(8,128)}, s32[8,16]{1,0:T(8,128)S(1)}, u32[]{:S(2)}, u32[]{:S(2)}) collective-permute-start(s32[8,16]{1,0:T(8,128)} %param.7), channel_id=1, source_target_pairs={{0,28},{4,0},{8,4},{12,8},{16,12},{20,16},{24,20},{28,24},{1,29},{... | collective-permute-start | bytes 1544 | tf_op jit(solution)/shard_map/ppermute | solution.py:26
  6.8 0.7 mul.16
  8.6 3.9 %collective-permute-done.refs_0_ = s32[8,16]{1,0:T(8,128)S(1)} collective-permute-done((s32[8,16]{1,0:T(8,128)}, s32[8,16]{1,0:T(8,128)S(1)}, u32[]{:S(2)}, u32[]{:S(2)}) %collective-permute-start) | collective-permute-done | bytes 544 | tf_op jit(solution)/shard_map/ppermute | solution.py:26
  12.4 2.6 %pick_blocks.2 = (bf16[2,128,2048]{2,1,0:T(8,128)(2,1)S(1)}, bf16[2,128,2048]{2,1,0:T(8,128)(2,1)S(1)}, bf16[2,128,2048]{2,1,0:T(8,128)(2,1)S(1)}) custom-call(s32[2]{0:T(128)S(1)} %pad_add_fusion.place_ref, s32[8,16]{1,0:T(8,128)S(1)} %collective-permute-done.refs_0_, s32[8,16]{1,0:T(8,128)S(1)} %collective-permute-done.1.refs_1_, ...), custom_call_target="tpu_custom_call" | custom-call | tf_op jit(solution)/shard_map/pick_blocks/pallas_call | solution.py:67
  15.1 0.9 collective-permute-start.6
  15.9 1.5 %collective-permute-start.7 = (bf16[2,128,2048]{2,1,0:T(8,128)(2,1)S(1)}, bf16[2,128,2048]{2,1,0:T(8,128)(2,1)S(1)}, u32[]{:S(2)}, u32[]{:S(2)}) collective-permute-start(bf16[2,128,2048]{2,1,0:T(8,128)(2,1)S(1)} %get-tuple-element.55), channel_id=1, source_target_pairs={{0,4},{4,8},{8,12},{12,16},{16,20},{20,24},{24,28},{28,0},{1,5},{5... | collective-permute-start | bytes 3145736 | tf_op jit(solution)/shard_map/ppermute | solution.py:26
  17.4 3.2 %collective-permute-start.8 = (bf16[2,128,2048]{2,1,0:T(8,128)(2,1)S(1)}, bf16[2,128,2048]{2,1,0:T(8,128)(2,1)S(1)}, u32[]{:S(2)}, u32[]{:S(2)}) collective-permute-start(bf16[2,128,2048]{2,1,0:T(8,128)(2,1)S(1)} %get-tuple-element.56), channel_id=1, source_target_pairs={{0,28},{4,0},{8,4},{12,8},{16,12},{20,16},{24,20},{28,24},{1,29},{... | collective-permute-start | bytes 3145736 | tf_op jit(solution)/shard_map/ppermute | solution.py:26
  20.7 3.5 %keep.1 = (bf16[1024,2048]{1,0:T(8,128)(2,1)S(1)}, bf16[1024,2048]{1,0:T(8,128)(2,1)S(1)}) custom-call(bf16[1024,2048]{1,0:T(8,128)(2,1)} %refs_1_.1, bf16[1024,2048]{1,0:T(8,128)(2,1)} %collective-permute-done.3.refs_4_.sib.refs_2_), custom_call_target="tpu_custom_call" | custom-call | tf_op jit(solution)/shard_map/keep/pallas_call | solution.py:92
  24.2 9.7 %tiles.3 = (bf16[4,8,32,256]{3,2,1,0:T(8,128)(2,1)S(1)}, bf16[4,8,32,256]{3,2,1,0:T(8,128)(2,1)S(1)}, bf16[2,4,8,32,256]{4,3,2,1,0:T(8,128)(2,1)S(1)}) custom-call(s32[5]{0:T(128)S(1)} %stack.41.place_ref, bf16[1024,2048]{1,0:T(8,128)(2,1)S(1)} %get-tuple-element.51.refs_0_, bf16[1024,2048]{1,0:T(8,128)(2,1)S(1)} %get-tuple-element.52.refs_1_, ...), custom_call_target="tpu_custom_call" | custom-call | tf_op jit(solution)/shard_map/tiles/pallas_call | solution.py:153
  33.9 1.6 %collective-permute-start.10 = (bf16[2,4,8,32,256]{4,3,2,1,0:T(8,128)(2,1)S(1)}, bf16[2,4,8,32,256]{4,3,2,1,0:T(8,128)(2,1)S(1)}, u32[]{:S(2)}, u32[]{:S(2)}) collective-permute-start(bf16[2,4,8,32,256]{4,3,2,1,0:T(8,128)(2,1)S(1)} %get-tuple-element.61), channel_id=1, source_target_pairs={{0,2},{1,3},{2,0},{3,1},{4,6},{5,7},{6,4},{7,5},{8,10},{9,11},{10,... | collective-permute-start | bytes 3145736 | tf_op jit(solution)/shard_map/ppermute | solution.py:39
  35.5 26.3 %collective-permute-done.4.refs_0_ = s32[8,16]{1,0:T(8,128)S(1)} collective-permute-done((s32[8,16]{1,0:T(8,128)S(1)}, s32[8,16]{1,0:T(8,128)S(1)}, u32[]{:S(2)}, u32[]{:S(2)}) %collective-permute-start.4) | collective-permute-done | bytes 544 | tf_op jit(solution)/shard_map/ppermute | solution.py:26
  61.8 2.0 %pick_blocks.3 = bf16[2,128,2048]{2,1,0:T(8,128)(2,1)S(1)} custom-call(s32[2]{0:T(128)S(1)} %pad_add_fusion.place_ref, s32[8,16]{1,0:T(8,128)S(1)} %collective-permute-done.4.refs_0_, bf16[1024,2048]{1,0:T(8,128)(2,1)} %refs_1_.1, bf16[1024,2048]{1,0:T(8,128)(2,1)} %collective-permute-done.3.refs_4_.sib.refs_2_), custom_call_target="tpu_custom_call" | custom-call | tf_op jit(solution)/shard_map/pick_blocks/pallas_call | solution.py:67
  63.8 0.8 collective-permute-done.8.refs_6_
  64.7 7.4 %tiles.4 = (bf16[3,8,32,256]{3,2,1,0:T(8,128)(2,1)S(1)}, bf16[3,8,32,256]{3,2,1,0:T(8,128)(2,1)S(1)}, bf16[2,3,8,32,256]{4,3,2,1,0:T(8,128)(2,1)S(1)}) custom-call(s32[5]{0:T(128)S(1)} %stack.41.place_ref, bf16[1024,2048]{1,0:T(8,128)(2,1)S(1)} %get-tuple-element.51.refs_0_, bf16[1024,2048]{1,0:T(8,128)(2,1)S(1)} %get-tuple-element.52.refs_1_, ...), custom_call_target="tpu_custom_call" | custom-call | tf_op jit(solution)/shard_map/tiles/pallas_call | solution.py:153
  72.1 1.6 %collective-permute-start.13 = (bf16[2,3,8,32,256]{4,3,2,1,0:T(8,128)(2,1)S(1)}, bf16[2,3,8,32,256]{4,3,2,1,0:T(8,128)(2,1)S(1)}, u32[]{:S(2)}, u32[]{:S(2)}) collective-permute-start(bf16[2,3,8,32,256]{4,3,2,1,0:T(8,128)(2,1)S(1)} %get-tuple-element.68), channel_id=1, source_target_pairs={{0,2},{1,3},{2,0},{3,1},{4,6},{5,7},{6,4},{7,5},{8,10},{9,11},{10,... | collective-permute-start | bytes 2359304 | tf_op jit(solution)/shard_map/ppermute | solution.py:39
  73.7 0.8 select_reduce_fusion.3
  74.4 2.6 %fusion.9.where_ref = s32[8,16]{1,0:T(8,128)S(1)} fusion(pred[8,16]{1,0:T(8,128)(4,1)S(1)} %get-tuple-element.93, pred[8,16]{1,0:T(8,128)(4,1)S(1)} %get-tuple-element.92, pred[8,16]{1,0:T(8,128)(4,1)S(1)} %get-tuple-element.91, pred[8,16]{1,0:T(8,128)(4,1)S(1)} %get-tuple-element.90, s32[]{:T(128)} %and.14, s32[]{:T(128)} %get-tuple-element.88, ...), kind=kLoop, calls=%fused_computation.22 | loop fusion | flops 4352 | bytes 1556 | tf_op jit(solution)/shard_map/add | solution.py:359
  77.7 13.8 %collective-permute-done.13 = bf16[2,3,8,32,256]{4,3,2,1,0:T(8,128)(2,1)S(1)} collective-permute-done((bf16[2,3,8,32,256]{4,3,2,1,0:T(8,128)(2,1)S(1)}, bf16[2,3,8,32,256]{4,3,2,1,0:T(8,128)(2,1)S(1)}, u32[]{:S(2)}, u32[]{:S(2)}) %collective-permute-start.13) | collective-permute-done | bytes 786464 | tf_op jit(solution)/shard_map/ppermute | solution.py:39
  91.8 3.0 %tiles.5 = (bf16[1,8,32,256]{3,2,1,0:T(8,128)(2,1)S(1)}, bf16[1,8,32,256]{3,2,1,0:T(8,128)(2,1)S(1)}, bf16[1,8,32,256]{3,2,1,0:T(8,128)(2,1)S(1)}, bf16[1,8,32,256]{3,2,1,0:T(8,128)(2,1)S(1)}) custom-call(s32[5]{0:T(128)S(1)} %stack.41.place_ref, bf16[1024,2048]{1,0:T(8,128)(2,1)S(1)} %get-tuple-element.51.refs_0_, ...), custom_call_target="tpu_custom_call" | custom-call | tf_op jit(solution)/shard_map/tiles/pallas_call | solution.py:153
  95.3 1.5 %collective-permute-start.17 = (bf16[1,8,32,256]{3,2,1,0:T(8,128)(2,1)S(1)}, bf16[1,8,32,256]{3,2,1,0:T(8,128)(2,1)S(1)}, u32[]{:S(2)}, u32[]{:S(2)}) collective-permute-start(bf16[1,8,32,256]{3,2,1,0:T(8,128)(2,1)S(1)} %get-tuple-element.82), channel_id=1, source_target_pairs={{0,2},{1,3},{2,0},{3,1},{4,6},{5,7},{6,4},{7,5},{8,10},{9,11},{10,... | collective-permute-start | bytes 393224 | tf_op jit(solution)/shard_map/ppermute | solution.py:39
  96.9 4.6 %place_early.1 = (f32[8,16,32,128]{3,2,1,0:T(8,128)}, f32[8,16,32,128]{3,2,1,0:T(8,128)}, s32[129]{0:T(256)S(1)}) custom-call(s32[8,16]{1,0:T(8,128)S(1)} %fusion.9.where_ref, bf16[4,8,32,256]{3,2,1,0:T(8,128)(2,1)S(1)} %get-tuple-element.73.refs_0_, bf16[3,8,32,256]{3,2,1,0:T(8,128)(2,1)S(1)} %get-tuple-element.74.refs_1_, ...), custom_call_target="tpu_custom_call" | custom-call | tf_op jit(solution)/shard_map/place_early/pallas_call | solution.py:211
  101.7 1.1 %collective-permute-done.18.refs_3_ = bf16[1,8,32,256]{3,2,1,0:T(8,128)(2,1)S(1)} collective-permute-done((bf16[1,8,32,256]{3,2,1,0:T(8,128)(2,1)S(1)}, bf16[1,8,32,256]{3,2,1,0:T(8,128)(2,1)S(1)}, u32[]{:S(2)}, u32[]{:S(2)}) %collective-permute-start.18) | collective-permute-done | bytes 131104 | tf_op jit(solution)/shard_map/ppermute | solution.py:39
  102.7 1.6 %place_late.1 = (f32[8,16,32,128]{3,2,1,0:T(8,128)}, f32[8,16,32,128]{3,2,1,0:T(8,128)}) custom-call(s32[8,16]{1,0:T(8,128)S(1)} %fusion.9.where_ref, s32[129]{0:T(256)S(1)} %get-tuple-element.79.later, bf16[1,8,32,256]{3,2,1,0:T(8,128)(2,1)S(1)} %get-tuple-element.80.refs_0_, ...), custom_call_target="tpu_custom_call", output_to_operand_aliasing={{0}: (6, {}), {1}: (7, {})} | custom-call | tf_op jit(solution)/shard_map/place_late/pallas_call | solution.py:275
  (32 shorter events, 3.3 us)
Async XLA Ops:
  0.6 11.8 %collective-permute-start.3 = (bf16[1024,2048]{1,0:T(8,128)(2,1)}, bf16[1024,2048]{1,0:T(8,128)(2,1)}, u32[]{:S(2)}, u32[]{:S(2)}) collective-permute-start(bf16[1024,2048]{1,0:T(8,128)(2,1)} %refs_1_.1), channel_id=1, source_target_pairs={{0,1},{1,0},{2,3},{3,2},{4,5},{5,4},{6,7},{7,6},{8,9},{9,8},{10,11... | collective-permute-start | bytes 12582920 | tf_op jit(solution)/shard_map/ppermute | solution.py:39
  1.1 7.4 %collective-permute-start.2 = (s32[8,16]{1,0:T(8,128)}, s32[8,16]{1,0:T(8,128)S(1)}, u32[]{:S(2)}, u32[]{:S(2)}) collective-permute-start(s32[8,16]{1,0:T(8,128)} %param.7), channel_id=1, source_target_pairs={{0,4},{4,8},{8,12},{12,16},{16,20},{20,24},{24,28},{28,0},{1,5},{5... | collective-permute-start | bytes 1544 | tf_op jit(solution)/shard_map/ppermute | solution.py:26
  3.7 4.9 %collective-permute-start.1 = (s32[8,16]{1,0:T(8,128)}, s32[8,16]{1,0:T(8,128)S(1)}, u32[]{:S(2)}, u32[]{:S(2)}) collective-permute-start(s32[8,16]{1,0:T(8,128)} %param.7), channel_id=1, source_target_pairs={{0,28},{4,0},{8,4},{12,8},{16,12},{20,16},{24,20},{28,24},{1,29},{... | collective-permute-start | bytes 1544 | tf_op jit(solution)/shard_map/ppermute | solution.py:26
  6.8 5.6 %collective-permute-start = (s32[8,16]{1,0:T(8,128)}, s32[8,16]{1,0:T(8,128)S(1)}, u32[]{:S(2)}, u32[]{:S(2)}) collective-permute-start(s32[8,16]{1,0:T(8,128)} %param.7), channel_id=1, source_target_pairs={{0,8},{4,12},{8,16},{12,20},{16,24},{20,28},{24,0},{28,4},{1,9},{5... | collective-permute-start | bytes 1544 | tf_op jit(solution)/shard_map/ppermute | solution.py:26
  8.3 15.9 %collective-permute-start.5 = (f32[2,2048]{1,0:T(2,128)S(1)}, f32[2,2048]{1,0:T(2,128)S(1)}, u32[]{:S(2)}, u32[]{:S(2)}) collective-permute-start(f32[2,2048]{1,0:T(2,128)S(1)} %pad_maximum_fusion.refs_2_), channel_id=1, source_target_pairs={{0,1},{1,0},{2,3},{3,2},{4,5},{5,4},{6,7},{7,6},{8,9},{9,8},{10,11... | collective-permute-start | bytes 49160 | tf_op jit(solution)/shard_map/ppermute | solution.py:39
  15.1 48.7 %collective-permute-start.6 = (bf16[2,128,2048]{2,1,0:T(8,128)(2,1)S(1)}, bf16[2,128,2048]{2,1,0:T(8,128)(2,1)S(1)}, u32[]{:S(2)}, u32[]{:S(2)}) collective-permute-start(bf16[2,128,2048]{2,1,0:T(8,128)(2,1)S(1)} %get-tuple-element.49), channel_id=1, source_target_pairs={{0,24},{4,28},{8,0},{12,4},{16,8},{20,12},{24,16},{28,20},{1,25},{... | collective-permute-start | bytes 3145736 | tf_op jit(solution)/shard_map/ppermute | solution.py:26
  15.9 47.9 %collective-permute-start.7 = (bf16[2,128,2048]{2,1,0:T(8,128)(2,1)S(1)}, bf16[2,128,2048]{2,1,0:T(8,128)(2,1)S(1)}, u32[]{:S(2)}, u32[]{:S(2)}) collective-permute-start(bf16[2,128,2048]{2,1,0:T(8,128)(2,1)S(1)} %get-tuple-element.55), channel_id=1, source_target_pairs={{0,4},{4,8},{8,12},{12,16},{16,20},{20,24},{24,28},{28,0},{1,5},{5... | collective-permute-start | bytes 3145736 | tf_op jit(solution)/shard_map/ppermute | solution.py:26
  17.4 47.1 %collective-permute-start.8 = (bf16[2,128,2048]{2,1,0:T(8,128)(2,1)S(1)}, bf16[2,128,2048]{2,1,0:T(8,128)(2,1)S(1)}, u32[]{:S(2)}, u32[]{:S(2)}) collective-permute-start(bf16[2,128,2048]{2,1,0:T(8,128)(2,1)S(1)} %get-tuple-element.56), channel_id=1, source_target_pairs={{0,28},{4,0},{8,4},{12,8},{16,12},{20,16},{24,20},{28,24},{1,29},{... | collective-permute-start | bytes 3145736 | tf_op jit(solution)/shard_map/ppermute | solution.py:26
  24.2 11.3 %copy-start = (s32[8,16]{1,0:T(8,128)S(1)}, s32[8,16]{1,0:T(8,128)}, u32[]{:S(2)}) copy-start(s32[8,16]{1,0:T(8,128)} %param.7) | copy-start | bytes 1540
  33.9 30.7 %collective-permute-start.10 = (bf16[2,4,8,32,256]{4,3,2,1,0:T(8,128)(2,1)S(1)}, bf16[2,4,8,32,256]{4,3,2,1,0:T(8,128)(2,1)S(1)}, u32[]{:S(2)}, u32[]{:S(2)}) collective-permute-start(bf16[2,4,8,32,256]{4,3,2,1,0:T(8,128)(2,1)S(1)} %get-tuple-element.61), channel_id=1, source_target_pairs={{0,2},{1,3},{2,0},{3,1},{4,6},{5,7},{6,4},{7,5},{8,10},{9,11},{10,... | collective-permute-start | bytes 3145736 | tf_op jit(solution)/shard_map/ppermute | solution.py:39
  35.5 26.3 %collective-permute-start.4 = (s32[8,16]{1,0:T(8,128)S(1)}, s32[8,16]{1,0:T(8,128)S(1)}, u32[]{:S(2)}, u32[]{:S(2)}) collective-permute-start(s32[8,16]{1,0:T(8,128)S(1)} %copy-done), channel_id=1, source_target_pairs={{0,24},{4,28},{8,0},{12,4},{16,8},{20,12},{24,16},{28,20},{1,25},{... | collective-permute-start | bytes 1544 | tf_op jit(solution)/shard_map/ppermute | solution.py:26
  61.8 2.0 %collective-permute-start.9 = (bf16[4,8,32,256]{3,2,1,0:T(8,128)(2,1)S(1)}, bf16[4,8,32,256]{3,2,1,0:T(8,128)(2,1)S(1)}, u32[]{:S(2)}, u32[]{:S(2)}) collective-permute-start(bf16[4,8,32,256]{3,2,1,0:T(8,128)(2,1)S(1)} %get-tuple-element.60), channel_id=1, source_target_pairs={{0,1},{1,0},{2,3},{3,2},{4,5},{5,4},{6,7},{7,6},{8,9},{9,8},{10,11... | collective-permute-start | bytes 1572872 | tf_op jit(solution)/shard_map/ppermute | solution.py:39
  64.6 27.0 %collective-permute-start.11 = (bf16[2,128,2048]{2,1,0:T(8,128)(2,1)S(1)}, bf16[2,128,2048]{2,1,0:T(8,128)(2,1)S(1)}, u32[]{:S(2)}, u32[]{:S(2)}) collective-permute-start(bf16[2,128,2048]{2,1,0:T(8,128)(2,1)S(1)} %pick_blocks.3), channel_id=1, source_target_pairs={{0,8},{4,12},{8,16},{12,20},{16,24},{20,28},{24,0},{28,4},{1,9},{5... | collective-permute-start | bytes 3145736 | tf_op jit(solution)/shard_map/ppermute | solution.py:26
  72.1 19.4 %collective-permute-start.13 = (bf16[2,3,8,32,256]{4,3,2,1,0:T(8,128)(2,1)S(1)}, bf16[2,3,8,32,256]{4,3,2,1,0:T(8,128)(2,1)S(1)}, u32[]{:S(2)}, u32[]{:S(2)}) collective-permute-start(bf16[2,3,8,32,256]{4,3,2,1,0:T(8,128)(2,1)S(1)} %get-tuple-element.68), channel_id=1, source_target_pairs={{0,2},{1,3},{2,0},{3,1},{4,6},{5,7},{6,4},{7,5},{8,10},{9,11},{10,... | collective-permute-start | bytes 2359304 | tf_op jit(solution)/shard_map/ppermute | solution.py:39
  74.4 3.3 %collective-permute-start.12 = (bf16[3,8,32,256]{3,2,1,0:T(8,128)(2,1)S(1)}, bf16[3,8,32,256]{3,2,1,0:T(8,128)(2,1)S(1)}, u32[]{:S(2)}, u32[]{:S(2)}) collective-permute-start(bf16[3,8,32,256]{3,2,1,0:T(8,128)(2,1)S(1)} %get-tuple-element.67), channel_id=1, source_target_pairs={{0,1},{1,0},{2,3},{3,2},{4,5},{5,4},{6,7},{7,6},{8,9},{9,8},{10,11... | collective-permute-start | bytes 1179656 | tf_op jit(solution)/shard_map/ppermute | solution.py:39
  77.1 19.7 %collective-permute-start.14 = (bf16[4,8,32,256]{3,2,1,0:T(8,128)(2,1)S(1)}, bf16[4,8,32,256]{3,2,1,0:T(8,128)(2,1)S(1)}, u32[]{:S(2)}, u32[]{:S(2)}) collective-permute-start(bf16[4,8,32,256]{3,2,1,0:T(8,128)(2,1)S(1)} %get-tuple-element.94), channel_id=1, source_target_pairs={{0,1},{1,0},{2,3},{3,2},{4,5},{5,4},{6,7},{7,6},{8,9},{9,8},{10,11... | collective-permute-start | bytes 1572872 | tf_op jit(solution)/shard_map/ppermute | solution.py:39
  91.7 5.1 %collective-permute-start.15 = (bf16[3,8,32,256]{3,2,1,0:T(8,128)(2,1)S(1)}, bf16[3,8,32,256]{3,2,1,0:T(8,128)(2,1)S(1)}, u32[]{:S(2)}, u32[]{:S(2)}) collective-permute-start(bf16[3,8,32,256]{3,2,1,0:T(8,128)(2,1)S(1)} %get-tuple-element.96), channel_id=1, source_target_pairs={{0,1},{1,0},{2,3},{3,2},{4,5},{5,4},{6,7},{7,6},{8,9},{9,8},{10,11... | collective-permute-start | bytes 1179656 | tf_op jit(solution)/shard_map/ppermute | solution.py:39
  94.8 6.7 %collective-permute-start.16 = (bf16[1,8,32,256]{3,2,1,0:T(8,128)(2,1)S(1)}, bf16[1,8,32,256]{3,2,1,0:T(8,128)(2,1)S(1)}, u32[]{:S(2)}, u32[]{:S(2)}) collective-permute-start(bf16[1,8,32,256]{3,2,1,0:T(8,128)(2,1)S(1)} %get-tuple-element.81), channel_id=1, source_target_pairs={{0,1},{1,0},{2,3},{3,2},{4,5},{5,4},{6,7},{7,6},{8,9},{9,8},{10,11... | collective-permute-start | bytes 393224 | tf_op jit(solution)/shard_map/ppermute | solution.py:39
  95.3 6.4 %collective-permute-start.17 = (bf16[1,8,32,256]{3,2,1,0:T(8,128)(2,1)S(1)}, bf16[1,8,32,256]{3,2,1,0:T(8,128)(2,1)S(1)}, u32[]{:S(2)}, u32[]{:S(2)}) collective-permute-start(bf16[1,8,32,256]{3,2,1,0:T(8,128)(2,1)S(1)} %get-tuple-element.82), channel_id=1, source_target_pairs={{0,2},{1,3},{2,0},{3,1},{4,6},{5,7},{6,4},{7,5},{8,10},{9,11},{10,... | collective-permute-start | bytes 393224 | tf_op jit(solution)/shard_map/ppermute | solution.py:39
  96.8 5.9 %collective-permute-start.18 = (bf16[1,8,32,256]{3,2,1,0:T(8,128)(2,1)S(1)}, bf16[1,8,32,256]{3,2,1,0:T(8,128)(2,1)S(1)}, u32[]{:S(2)}, u32[]{:S(2)}) collective-permute-start(bf16[1,8,32,256]{3,2,1,0:T(8,128)(2,1)S(1)} %get-tuple-element.83), channel_id=1, source_target_pairs={{0,3},{1,2},{2,1},{3,0},{4,7},{5,6},{6,5},{7,4},{8,11},{9,10},{10,... | collective-permute-start | bytes 393224 | tf_op jit(solution)/shard_map/ppermute | solution.py:39

commit v7 on v6

--- a/solution.py
+++ b/solution.py
@@ -47,9 +47,9 @@
     for index in range(count):
         ids = asks[index][...] - first
         mine = (ids >= 0) & (ids < blocks)
-        lowest = jnp.min(jnp.where(mine, ids, blocks - 1))
-        highest = jnp.max(jnp.where(mine, ids, 0))
-        block = jnp.where(place_ref[1] == 0, lowest, highest)
+        ids = jnp.where(place_ref[1] == 0, blocks - 1 - ids, ids)
+        block = jnp.max(jnp.where(mine, ids, 0))
+        block = jnp.where(place_ref[1] == 0, blocks - 1 - block, block)
         rows = pl.ds(pl.multiple_of(block * tile, tile), tile)
         for half, source in enumerate((own, sib)):
             copy = pltpu.make_async_copy(
@@ -302,11 +302,9 @@
     half_blocks = blocks // 2
     offsets = [2, -1, 1, -2]
 
-    asks = [shifted(neighbours, "atoms", offset) for offset in offsets[:3]]
+    asks = [shifted(neighbours, "atoms", offset) for offset in offsets]
     sib = to_strip_target(eigvecs, chips, 0, 1)
     own_weights = jnp.stack([occupations, occupations * energies], 0)
-    sib_weights = to_strip_target(own_weights, chips, 0, 1)
-    weights = (own_weights, sib_weights)
 
     targets = [
         strip_target(group, chips, step, other)
@@ -316,13 +314,12 @@
     here = jnp.stack([own_index, core]).astype(jnp.int32)
     place = jnp.stack([core] + targets).astype(jnp.int32)
 
-    asks = lax.optimization_barrier(asks)
-    picked = list(pick(here, asks, eigvecs, sib, tile))
-    late_neighbours, picked[0] = lax.optimization_barrier((neighbours, picked[0]))
+    asks, own_weights = lax.optimization_barrier((asks, own_weights))
+    weights = (own_weights, to_strip_target(own_weights, chips, 0, 1))
+    picked = list(pick(here, asks[:3], eigvecs, sib, tile))
     arrived = [
         shifted(value, "atoms", -offset) for value, offset in zip(picked, offsets)
     ]
-    last_ask = shifted(late_neighbours, "atoms", offsets[3])
     kept_eigvecs, picked[0] = lax.optimization_barrier((eigvecs, picked[0]))
     own, kept_sib = keep(kept_eigvecs, sib)
 
@@ -340,10 +337,10 @@
         return singles
 
     chunks = [strips_of((), True)]
-    neighbours, here, last_ask, chunks[0][0] = lax.optimization_barrier(
-        (neighbours, here, last_ask, chunks[0][0])
+    neighbours, here, chunks[0][0] = lax.optimization_barrier(
+        (neighbours, here, chunks[0][0])
     )
-    (last_picked,) = pick(here, [last_ask], eigvecs, sib, tile)
+    (last_picked,) = pick(here, asks[3:], eigvecs, sib, tile)
 
     owners = lax.div(neighbours, blocks)
     within = lax.rem(neighbours, blocks)
@@ -358,14 +355,23 @@
     per_core = half_blocks + len(offsets)
     where = ((side ^ core) * per_core + spot).astype(jnp.int32)
 
-    arrived, last_picked, chunks[0] = lax.optimization_barrier(
-        (arrived, last_picked, chunks[0])
+    arrived[0], last_picked, chunks[0][:2] = lax.optimization_barrier(
+        (arrived[0], last_picked, chunks[0][:2])
     )
     fourth = shifted(last_picked, "atoms", -offsets[3])
-    chunks.append(strips_of(arrived, True))
-    where, fourth, chunks[1] = lax.optimization_barrier((where, fourth, chunks[1]))
+    parts = list(tiles(place, own, kept_sib, arrived[:1], weights, n_bands, tile, True))
+    pairs = [
+        to_strip_target(pair, chips, step + 1, 0) for step, pair in enumerate(parts[2:])
+    ]
+    near, parts[:2], pairs, chunks = lax.optimization_barrier(
+        (arrived[1:], parts[:2], pairs, chunks)
+    )
+    chunks.append([parts[0], to_strip_target(parts[1], chips, 0, 1)] + pairs)
+    direct = strips_of(near, False)
+    chunks, direct[0] = lax.optimization_barrier((chunks, direct[0]))
+    chunks = [passed_on(chunk) for chunk in chunks] + [direct]
+    where, fourth, chunks = lax.optimization_barrier((where, fourth, chunks))
     last = strips_of((fourth,), False)
-    chunks = [passed_on(chunk) for chunk in chunks]
     where, last[0] = lax.optimization_barrier((where, last[0]))
     strips = [[chunk[index] for chunk in chunks] for index in range(n_bands)]
     density, energy, later = place_early(where, strips, chips, per_core, tile)

time: 106 us -> 110 us (1.038)
  starting transfers between devices: 17.9 us -> 27.1 us
  waiting for transfers between devices: 46.1 us -> 40.1 us
  Pallas kernels: 34.4 us -> 36.3 us
    ppermute x8, starting transfers between devices: 11.3 us -> 18.2 us  [shifted(): return lax.ppermute(value, axis, pairs)]
    ppermute x11 -> x14, waiting for transfers between devices: 15.1 us -> 10.2 us  [to_strip_target(): return lax.ppermute(value, 'bands', pairs)]
    ppermute x11 -> x14, starting transfers between devices: 6.56 us -> 8.91 us  [to_strip_target(): return lax.ppermute(value, 'bands', pairs)]
    ppermute x8, waiting for transfers between devices: 31 us -> 29.8 us  [shifted(): return lax.ppermute(value, axis, pairs)]
    pallas_call x3 -> x4, Pallas kernels: 20.1 us -> 20.9 us  [tiles(): pl.pallas_call(functools.partial(tiles_kernel, len(arrived), n_right, n_s...]
  transfers between devices with their start and end apart: 19 -> 22, of which waited for: 7 -> 9; matrix products, arithmetic and copies ran while one was open for 5% -> 5% of each run, Pallas kernels for 31% -> 26%
where the time goes in v7:
time: 110 us; the launch traced here: 109 us
  waiting for transfers between devices  40.1 us (36%)
  Pallas kernels  36.3 us (33%)
  starting transfers between devices  27.1 us (25%)
  other arithmetic  4.79 us (4%)
    ppermute x8, waiting for transfers between devices, shifted(): return lax.ppermute(value, axis, pairs)  29.8 us
    pallas_call x4, Pallas kernels, tiles(): pl.pallas_call(functools.partial(tiles_kernel, len(arrived), n_right, n_s...  20.9 us
    ppermute x8, starting transfers between devices, shifted(): return lax.ppermute(value, axis, pairs)  18.2 us
    ppermute x14, waiting for transfers between devices, to_strip_target(): return lax.ppermute(value, 'bands', pairs)  10.2 us
    ppermute x14, starting transfers between devices, to_strip_target(): return lax.ppermute(value, 'bands', pairs)  8.91 us
    pallas_call x2, Pallas kernels, pick(): pl.pallas_call(functools.partial(pick_kernel, count, blocks, tile), out_s...  5.56 us
    pallas_call x1, Pallas kernels, place_early(): pl.pallas_call(functools.partial(place_early_kernel, chips, sizes, per_co...  4.59 us
    pallas_call x1, Pallas kernels, keep(): pl.pallas_call(keep_kernel, out_shape=[pltpu.VMEM(own.shape, own.dtype)]...  3.48 us
  transfers between devices with their start and end apart: 22, of which 9 were waited for; matrix products, arithmetic and copies ran while one was open for 5% of the time, Pallas kernels for 26%

profile of v7, /device:TPU:0, one launch (start us, length us, event | category | flops | bytes accessed | tf_op | source)
XLA Modules:
  0.0 109.4 jit_solution(497899712078814903)
XLA Ops:
  1.1 2.6 %collective-permute-start.2 = (s32[8,16]{1,0:T(8,128)}, s32[8,16]{1,0:T(8,128)S(1)}, u32[]{:S(2)}, u32[]{:S(2)}) collective-permute-start(s32[8,16]{1,0:T(8,128)} %param.7), channel_id=1, source_target_pairs={{0,4},{4,8},{8,12},{12,16},{16,20},{20,24},{24,28},{28,0},{1,5},{5... | collective-permute-start | bytes 1544 | tf_op jit(solution)/shard_map/ppermute | solution.py:26
  3.7 3.1 %collective-permute-start.1 = (s32[8,16]{1,0:T(8,128)}, s32[8,16]{1,0:T(8,128)S(1)}, u32[]{:S(2)}, u32[]{:S(2)}) collective-permute-start(s32[8,16]{1,0:T(8,128)} %param.7), channel_id=1, source_target_pairs={{0,28},{4,0},{8,4},{12,8},{16,12},{20,16},{24,20},{28,24},{1,29},{... | collective-permute-start | bytes 1544 | tf_op jit(solution)/shard_map/ppermute | solution.py:26
  6.8 3.8 %collective-permute-start.3 = (s32[8,16]{1,0:T(8,128)}, s32[8,16]{1,0:T(8,128)S(1)}, u32[]{:S(2)}, u32[]{:S(2)}) collective-permute-start(s32[8,16]{1,0:T(8,128)} %param.7), channel_id=1, source_target_pairs={{0,24},{4,28},{8,0},{12,4},{16,8},{20,12},{24,16},{28,20},{1,25},{... | collective-permute-start | bytes 1544 | tf_op jit(solution)/shard_map/ppermute | solution.py:26
  12.4 3.6 %pick_blocks.2 = (bf16[2,128,2048]{2,1,0:T(8,128)(2,1)}, bf16[2,128,2048]{2,1,0:T(8,128)(2,1)S(1)}, bf16[2,128,2048]{2,1,0:T(8,128)(2,1)S(1)}) custom-call(s32[2]{0:T(128)S(1)} %pad_add_fusion.place_ref, s32[8,16]{1,0:T(8,128)S(1)} %collective-permute-done.refs_0_, s32[8,16]{1,0:T(8,128)S(1)} %collective-permute-done.1.refs_1_, ...), custom_call_target="tpu_custom_call" | custom-call | tf_op jit(solution)/shard_map/pick_blocks/pallas_call | solution.py:67
  16.1 3.9 %collective-permute-start.6 = (bf16[2,128,2048]{2,1,0:T(8,128)(2,1)}, bf16[2,128,2048]{2,1,0:T(8,128)(2,1)S(1)}, u32[]{:S(2)}, u32[]{:S(2)}) collective-permute-start(bf16[2,128,2048]{2,1,0:T(8,128)(2,1)} %get-tuple-element.71), channel_id=1, source_target_pairs={{0,24},{4,28},{8,0},{12,4},{16,8},{20,12},{24,16},{28,20},{1,25},{... | collective-permute-start | bytes 3145736 | tf_op jit(solution)/shard_map/ppermute | solution.py:26
  20.1 4.7 %collective-permute-start.10 = (bf16[2,128,2048]{2,1,0:T(8,128)(2,1)S(1)}, bf16[2,128,2048]{2,1,0:T(8,128)(2,1)S(1)}, u32[]{:S(2)}, u32[]{:S(2)}) collective-permute-start(bf16[2,128,2048]{2,1,0:T(8,128)(2,1)S(1)} %get-tuple-element.84), channel_id=1, source_target_pairs={{0,28},{4,0},{8,4},{12,8},{16,12},{20,16},{24,20},{28,24},{1,29},{... | collective-permute-start | bytes 3145736 | tf_op jit(solution)/shard_map/ppermute | solution.py:26
  24.8 3.5 %keep.1 = (bf16[1024,2048]{1,0:T(8,128)(2,1)S(1)}, bf16[1024,2048]{1,0:T(8,128)(2,1)S(1)}) custom-call(bf16[1024,2048]{1,0:T(8,128)(2,1)} %refs_1_.1, bf16[1024,2048]{1,0:T(8,128)(2,1)} %collective-permute-done.4.refs_4_.sib.refs_2_), custom_call_target="tpu_custom_call" | custom-call | tf_op jit(solution)/shard_map/keep/pallas_call | solution.py:92
  28.3 9.7 %tiles.4 = (bf16[4,8,32,256]{3,2,1,0:T(8,128)(2,1)S(1)}, bf16[4,8,32,256]{3,2,1,0:T(8,128)(2,1)S(1)}, bf16[2,4,8,32,256]{4,3,2,1,0:T(8,128)(2,1)S(1)}) custom-call(s32[5]{0:T(128)S(1)} %stack.41.place_ref, bf16[1024,2048]{1,0:T(8,128)(2,1)S(1)} %get-tuple-element.73.refs_0_, bf16[1024,2048]{1,0:T(8,128)(2,1)S(1)} %get-tuple-element.74.refs_1_, ...), custom_call_target="tpu_custom_call" | custom-call | tf_op jit(solution)/shard_map/tiles/pallas_call | solution.py:153
  38.1 1.7 %collective-permute-start.12 = (bf16[2,4,8,32,256]{4,3,2,1,0:T(8,128)(2,1)S(1)}, bf16[2,4,8,32,256]{4,3,2,1,0:T(8,128)(2,1)S(1)}, u32[]{:S(2)}, u32[]{:S(2)}) collective-permute-start(bf16[2,4,8,32,256]{4,3,2,1,0:T(8,128)(2,1)S(1)} %get-tuple-element.91), channel_id=1, source_target_pairs={{0,2},{1,3},{2,0},{3,1},{4,6},{5,7},{6,4},{7,5},{8,10},{9,11},{10,... | collective-permute-start | bytes 3145736 | tf_op jit(solution)/shard_map/ppermute | solution.py:39
  39.8 2.0 %pick_blocks.3 = bf16[2,128,2048]{2,1,0:T(8,128)(2,1)S(1)} custom-call(s32[2]{0:T(128)S(1)} %pad_add_fusion.place_ref, s32[8,16]{1,0:T(8,128)S(1)} %collective-permute-done.3.refs_0_, bf16[1024,2048]{1,0:T(8,128)(2,1)} %refs_1_.1, bf16[1024,2048]{1,0:T(8,128)(2,1)} %collective-permute-done.4.refs_4_.sib.refs_2_), custom_call_target="tpu_custom_call" | custom-call | tf_op jit(solution)/shard_map/pick_blocks/pallas_call | solution.py:67
  41.7 2.2 %collective-permute-done.6.refs_4_ = bf16[2,128,2048]{2,1,0:T(8,128)(2,1)S(1)} collective-permute-done((bf16[2,128,2048]{2,1,0:T(8,128)(2,1)}, bf16[2,128,2048]{2,1,0:T(8,128)(2,1)S(1)}, u32[]{:S(2)}, u32[]{:S(2)}) %collective-permute-start.6) | collective-permute-done | bytes 1048608 | tf_op jit(solution)/shard_map/ppermute | solution.py:26
  43.9 3.0 %tiles.5 = (bf16[1,8,32,256]{3,2,1,0:T(8,128)(2,1)S(1)}, bf16[1,8,32,256]{3,2,1,0:T(8,128)(2,1)S(1)}, bf16[2,1,8,32,256]{4,3,2,1,0:T(8,128)(2,1)S(1)}) custom-call(s32[5]{0:T(128)S(1)} %stack.41.place_ref, bf16[1024,2048]{1,0:T(8,128)(2,1)S(1)} %get-tuple-element.73.refs_0_, bf16[1024,2048]{1,0:T(8,128)(2,1)S(1)} %get-tuple-element.74.refs_1_, ...), custom_call_target="tpu_custom_call" | custom-call | tf_op jit(solution)/shard_map/tiles/pallas_call | solution.py:153
  46.9 1.7 %collective-permute-start.11 = (bf16[2,1,8,32,256]{4,3,2,1,0:T(8,128)(2,1)S(1)}, bf16[2,1,8,32,256]{4,3,2,1,0:T(8,128)(2,1)S(1)}, u32[]{:S(2)}, u32[]{:S(2)}) collective-permute-start(bf16[2,1,8,32,256]{4,3,2,1,0:T(8,128)(2,1)S(1)} %get-tuple-element.88), channel_id=1, source_target_pairs={{0,2},{1,3},{2,0},{3,1},{4,6},{5,7},{6,4},{7,5},{8,10},{9,11},{10,... | collective-permute-start | bytes 786440 | tf_op jit(solution)/shard_map/ppermute | solution.py:39
  48.6 17.3 %collective-permute-done.9.refs_4_ = bf16[2,128,2048]{2,1,0:T(8,128)(2,1)S(1)} collective-permute-done((bf16[2,128,2048]{2,1,0:T(8,128)(2,1)S(1)}, bf16[2,128,2048]{2,1,0:T(8,128)(2,1)S(1)}, u32[]{:S(2)}, u32[]{:S(2)}) %collective-permute-start.9) | collective-permute-done | bytes 1048608 | tf_op jit(solution)/shard_map/ppermute | solution.py:26
  65.9 2.2 %collective-permute-done.10.refs_5_ = bf16[2,128,2048]{2,1,0:T(8,128)(2,1)S(1)} collective-permute-done((bf16[2,128,2048]{2,1,0:T(8,128)(2,1)S(1)}, bf16[2,128,2048]{2,1,0:T(8,128)(2,1)S(1)}, u32[]{:S(2)}, u32[]{:S(2)}) %collective-permute-start.10) | collective-permute-done | bytes 1048608 | tf_op jit(solution)/shard_map/ppermute | solution.py:26
  68.8 5.2 %tiles.6 = (bf16[2,8,32,256]{3,2,1,0:T(8,128)(2,1)S(1)}, bf16[2,8,32,256]{3,2,1,0:T(8,128)(2,1)S(1)}, bf16[2,8,32,256]{3,2,1,0:T(8,128)(2,1)S(1)}, bf16[2,8,32,256]{3,2,1,0:T(8,128)(2,1)S(1)}) custom-call(s32[5]{0:T(128)S(1)} %stack.41.place_ref, bf16[1024,2048]{1,0:T(8,128)(2,1)S(1)} %get-tuple-element.73.refs_0_, ...), custom_call_target="tpu_custom_call" | custom-call | tf_op jit(solution)/shard_map/tiles/pallas_call | solution.py:153
  78.0 2.5 %fusion.9.where_ref = s32[8,16]{1,0:T(8,128)S(1)} fusion(pred[8,16]{1,0:T(8,128)(4,1)S(1)} %get-tuple-element.141, pred[8,16]{1,0:T(8,128)(4,1)S(1)} %get-tuple-element.140, pred[8,16]{1,0:T(8,128)(4,1)S(1)} %get-tuple-element.139, pred[8,16]{1,0:T(8,128)(4,1)S(1)} %get-tuple-element.138, s32[]{:T(128)} %and.14, s32[]{:T(128)} %get-tuple-element.136, ...), kind=kLoop, calls=%fused_computation.22 | loop fusion | flops 4352 | bytes 1556 | tf_op jit(solution)/shard_map/add | solution.py:356
  80.5 3.9 %collective-permute-done.17.refs_8_ = bf16[2,8,32,256]{3,2,1,0:T(8,128)(2,1)S(1)} collective-permute-done((bf16[2,8,32,256]{3,2,1,0:T(8,128)(2,1)S(1)}, bf16[2,8,32,256]{3,2,1,0:T(8,128)(2,1)S(1)}, u32[]{:S(2)}, u32[]{:S(2)}) %collective-permute-start.17) | collective-permute-done | bytes 262176 | tf_op jit(solution)/shard_map/ppermute | solution.py:39
  84.4 3.9 %collective-permute-done.18.refs_11_ = bf16[2,8,32,256]{3,2,1,0:T(8,128)(2,1)S(1)} collective-permute-done((bf16[2,8,32,256]{3,2,1,0:T(8,128)(2,1)S(1)}, bf16[2,8,32,256]{3,2,1,0:T(8,128)(2,1)S(1)}, u32[]{:S(2)}, u32[]{:S(2)}) %collective-permute-start.18) | collective-permute-done | bytes 262176 | tf_op jit(solution)/shard_map/ppermute | solution.py:39
  88.3 7.8 %collective-permute-done.8.refs_4_ = bf16[2,128,2048]{2,1,0:T(8,128)(2,1)S(1)} collective-permute-done((bf16[2,128,2048]{2,1,0:T(8,128)(2,1)S(1)}, bf16[2,128,2048]{2,1,0:T(8,128)(2,1)S(1)}, u32[]{:S(2)}, u32[]{:S(2)}) %collective-permute-start.8) | collective-permute-done | bytes 1048608 | tf_op jit(solution)/shard_map/ppermute | solution.py:26
  96.1 3.0 %tiles.7 = (bf16[1,8,32,256]{3,2,1,0:T(8,128)(2,1)S(1)}, bf16[1,8,32,256]{3,2,1,0:T(8,128)(2,1)S(1)}, bf16[1,8,32,256]{3,2,1,0:T(8,128)(2,1)S(1)}, bf16[1,8,32,256]{3,2,1,0:T(8,128)(2,1)S(1)}) custom-call(s32[5]{0:T(128)S(1)} %stack.41.place_ref, bf16[1024,2048]{1,0:T(8,128)(2,1)S(1)} %get-tuple-element.73.refs_0_, ...), custom_call_target="tpu_custom_call" | custom-call | tf_op jit(solution)/shard_map/tiles/pallas_call | solution.py:153
  101.0 4.6 %place_early.1 = (f32[8,16,32,128]{3,2,1,0:T(8,128)}, f32[8,16,32,128]{3,2,1,0:T(8,128)}, s32[129]{0:T(256)S(1)}) custom-call(s32[8,16]{1,0:T(8,128)S(1)} %fusion.9.where_ref, bf16[4,8,32,256]{3,2,1,0:T(8,128)(2,1)S(1)} %get-tuple-element.115.refs_0_, bf16[1,8,32,256]{3,2,1,0:T(8,128)(2,1)S(1)} %get-tuple-element.116.refs_1_, ...), custom_call_target="tpu_custom_call" | custom-call | tf_op jit(solution)/shard_map/place_early/pallas_call | solution.py:211
  105.7 1.8 %collective-permute-done.21.refs_3_ = bf16[1,8,32,256]{3,2,1,0:T(8,128)(2,1)S(1)} collective-permute-done((bf16[1,8,32,256]{3,2,1,0:T(8,128)(2,1)S(1)}, bf16[1,8,32,256]{3,2,1,0:T(8,128)(2,1)S(1)}, u32[]{:S(2)}, u32[]{:S(2)}) %collective-permute-start.21) | collective-permute-done | bytes 131104 | tf_op jit(solution)/shard_map/ppermute | solution.py:39
  107.5 1.8 %place_late.1 = (f32[8,16,32,128]{3,2,1,0:T(8,128)}, f32[8,16,32,128]{3,2,1,0:T(8,128)}) custom-call(s32[8,16]{1,0:T(8,128)S(1)} %fusion.9.where_ref, s32[129]{0:T(256)S(1)} %get-tuple-element.127.later, bf16[1,8,32,256]{3,2,1,0:T(8,128)(2,1)S(1)} %get-tuple-element.128.refs_0_, ...), custom_call_target="tpu_custom_call", output_to_operand_aliasing={{0}: (6, {}), {1}: (7, {})} | custom-call | tf_op jit(solution)/shard_map/place_late/pallas_call | solution.py:275
  (39 shorter events, 8.8 us)
Async XLA Ops:
  0.6 11.8 %collective-permute-start.4 = (bf16[1024,2048]{1,0:T(8,128)(2,1)}, bf16[1024,2048]{1,0:T(8,128)(2,1)}, u32[]{:S(2)}, u32[]{:S(2)}) collective-permute-start(bf16[1024,2048]{1,0:T(8,128)(2,1)} %refs_1_.1), channel_id=1, source_target_pairs={{0,1},{1,0},{2,3},{3,2},{4,5},{5,4},{6,7},{7,6},{8,9},{9,8},{10,11... | collective-permute-start | bytes 12582920 | tf_op jit(solution)/shard_map/ppermute | solution.py:39
  1.1 11.0 %collective-permute-start.2 = (s32[8,16]{1,0:T(8,128)}, s32[8,16]{1,0:T(8,128)S(1)}, u32[]{:S(2)}, u32[]{:S(2)}) collective-permute-start(s32[8,16]{1,0:T(8,128)} %param.7), channel_id=1, source_target_pairs={{0,4},{4,8},{8,12},{12,16},{16,20},{20,24},{24,28},{28,0},{1,5},{5... | collective-permute-start | bytes 1544 | tf_op jit(solution)/shard_map/ppermute | solution.py:26
  3.7 8.5 %collective-permute-start.1 = (s32[8,16]{1,0:T(8,128)}, s32[8,16]{1,0:T(8,128)S(1)}, u32[]{:S(2)}, u32[]{:S(2)}) collective-permute-start(s32[8,16]{1,0:T(8,128)} %param.7), channel_id=1, source_target_pairs={{0,28},{4,0},{8,4},{12,8},{16,12},{20,16},{24,20},{28,24},{1,29},{... | collective-permute-start | bytes 1544 | tf_op jit(solution)/shard_map/ppermute | solution.py:26
  6.8 5.6 %collective-permute-start = (s32[8,16]{1,0:T(8,128)}, s32[8,16]{1,0:T(8,128)S(1)}, u32[]{:S(2)}, u32[]{:S(2)}) collective-permute-start(s32[8,16]{1,0:T(8,128)} %param.7), channel_id=1, source_target_pairs={{0,8},{4,12},{8,16},{12,20},{16,24},{20,28},{24,0},{28,4},{1,9},{5... | collective-permute-start | bytes 1544 | tf_op jit(solution)/shard_map/ppermute | solution.py:26
  6.8 5.6 %collective-permute-start.3 = (s32[8,16]{1,0:T(8,128)}, s32[8,16]{1,0:T(8,128)S(1)}, u32[]{:S(2)}, u32[]{:S(2)}) collective-permute-start(s32[8,16]{1,0:T(8,128)} %param.7), channel_id=1, source_target_pairs={{0,24},{4,28},{8,0},{12,4},{16,8},{20,12},{24,16},{28,20},{1,25},{... | collective-permute-start | bytes 1544 | tf_op jit(solution)/shard_map/ppermute | solution.py:26
  16.1 27.9 %collective-permute-start.6 = (bf16[2,128,2048]{2,1,0:T(8,128)(2,1)}, bf16[2,128,2048]{2,1,0:T(8,128)(2,1)S(1)}, u32[]{:S(2)}, u32[]{:S(2)}) collective-permute-start(bf16[2,128,2048]{2,1,0:T(8,128)(2,1)} %get-tuple-element.71), channel_id=1, source_target_pairs={{0,24},{4,28},{8,0},{12,4},{16,8},{20,12},{24,16},{28,20},{1,25},{... | collective-permute-start | bytes 3145736 | tf_op jit(solution)/shard_map/ppermute | solution.py:26
  20.0 8.3 %collective-permute-start.5 = (f32[2,2048]{1,0:T(2,128)S(1)}, f32[2,2048]{1,0:T(2,128)S(1)}, u32[]{:S(2)}, u32[]{:S(2)}) collective-permute-start(f32[2,2048]{1,0:T(2,128)S(1)} %pad_maximum_fusion.refs_2_), channel_id=1, source_target_pairs={{0,1},{1,0},{2,3},{3,2},{4,5},{5,4},{6,7},{7,6},{8,9},{9,8},{10,11... | collective-permute-start | bytes 49160 | tf_op jit(solution)/shard_map/ppermute | solution.py:39
  20.1 45.8 %collective-permute-start.9 = (bf16[2,128,2048]{2,1,0:T(8,128)(2,1)S(1)}, bf16[2,128,2048]{2,1,0:T(8,128)(2,1)S(1)}, u32[]{:S(2)}, u32[]{:S(2)}) collective-permute-start(bf16[2,128,2048]{2,1,0:T(8,128)(2,1)S(1)} %get-tuple-element.83), channel_id=1, source_target_pairs={{0,4},{4,8},{8,12},{12,16},{16,20},{20,24},{24,28},{28,0},{1,5},{5... | collective-permute-start | bytes 3145736 | tf_op jit(solution)/shard_map/ppermute | solution.py:26
  20.1 48.1 %collective-permute-start.10 = (bf16[2,128,2048]{2,1,0:T(8,128)(2,1)S(1)}, bf16[2,128,2048]{2,1,0:T(8,128)(2,1)S(1)}, u32[]{:S(2)}, u32[]{:S(2)}) collective-permute-start(bf16[2,128,2048]{2,1,0:T(8,128)(2,1)S(1)} %get-tuple-element.84), channel_id=1, source_target_pairs={{0,28},{4,0},{8,4},{12,8},{16,12},{20,16},{24,20},{28,24},{1,29},{... | collective-permute-start | bytes 3145736 | tf_op jit(solution)/shard_map/ppermute | solution.py:26
  38.1 30.1 %collective-permute-start.12 = (bf16[2,4,8,32,256]{4,3,2,1,0:T(8,128)(2,1)S(1)}, bf16[2,4,8,32,256]{4,3,2,1,0:T(8,128)(2,1)S(1)}, u32[]{:S(2)}, u32[]{:S(2)}) collective-permute-start(bf16[2,4,8,32,256]{4,3,2,1,0:T(8,128)(2,1)S(1)} %get-tuple-element.91), channel_id=1, source_target_pairs={{0,2},{1,3},{2,0},{3,1},{4,6},{5,7},{6,4},{7,5},{8,10},{9,11},{10,... | collective-permute-start | bytes 3145736 | tf_op jit(solution)/shard_map/ppermute | solution.py:39
  39.8 2.0 %collective-permute-start.7 = (bf16[4,8,32,256]{3,2,1,0:T(8,128)(2,1)S(1)}, bf16[4,8,32,256]{3,2,1,0:T(8,128)(2,1)S(1)}, u32[]{:S(2)}, u32[]{:S(2)}) collective-permute-start(bf16[4,8,32,256]{3,2,1,0:T(8,128)(2,1)S(1)} %get-tuple-element.81), channel_id=1, source_target_pairs={{0,1},{1,0},{2,3},{3,2},{4,5},{5,4},{6,7},{7,6},{8,9},{9,8},{10,11... | collective-permute-start | bytes 1572872 | tf_op jit(solution)/shard_map/ppermute | solution.py:39
  46.9 21.8 %collective-permute-start.11 = (bf16[2,1,8,32,256]{4,3,2,1,0:T(8,128)(2,1)S(1)}, bf16[2,1,8,32,256]{4,3,2,1,0:T(8,128)(2,1)S(1)}, u32[]{:S(2)}, u32[]{:S(2)}) collective-permute-start(bf16[2,1,8,32,256]{4,3,2,1,0:T(8,128)(2,1)S(1)} %get-tuple-element.88), channel_id=1, source_target_pairs={{0,2},{1,3},{2,0},{3,1},{4,6},{5,7},{6,4},{7,5},{8,10},{9,11},{10,... | collective-permute-start | bytes 786440 | tf_op jit(solution)/shard_map/ppermute | solution.py:39
  68.8 8.4 %copy-start = (s32[8,16]{1,0:T(8,128)S(1)}, s32[8,16]{1,0:T(8,128)}, u32[]{:S(2)}) copy-start(s32[8,16]{1,0:T(8,128)} %param.7) | copy-start | bytes 1540
  68.8 5.3 %collective-permute-start.13 = (bf16[1,8,32,256]{3,2,1,0:T(8,128)(2,1)S(1)}, bf16[1,8,32,256]{3,2,1,0:T(8,128)(2,1)S(1)}, u32[]{:S(2)}, u32[]{:S(2)}) collective-permute-start(bf16[1,8,32,256]{3,2,1,0:T(8,128)(2,1)S(1)} %get-tuple-element.96), channel_id=1, source_target_pairs={{0,1},{1,0},{2,3},{3,2},{4,5},{5,4},{6,7},{7,6},{8,9},{9,8},{10,11... | collective-permute-start | bytes 393224 | tf_op jit(solution)/shard_map/ppermute | solution.py:39
  68.8 27.4 %collective-permute-start.8 = (bf16[2,128,2048]{2,1,0:T(8,128)(2,1)S(1)}, bf16[2,128,2048]{2,1,0:T(8,128)(2,1)S(1)}, u32[]{:S(2)}, u32[]{:S(2)}) collective-permute-start(bf16[2,128,2048]{2,1,0:T(8,128)(2,1)S(1)} %pick_blocks.3), channel_id=1, source_target_pairs={{0,8},{4,12},{8,16},{12,20},{16,24},{20,28},{24,0},{28,4},{1,9},{5... | collective-permute-start | bytes 3145736 | tf_op jit(solution)/shard_map/ppermute | solution.py:26
  74.1 2.8 %collective-permute-start.15 = (bf16[1,8,32,256]{3,2,1,0:T(8,128)(2,1)S(1)}, bf16[1,8,32,256]{3,2,1,0:T(8,128)(2,1)S(1)}, u32[]{:S(2)}, u32[]{:S(2)}) collective-permute-start(bf16[1,8,32,256]{3,2,1,0:T(8,128)(2,1)S(1)} %get-tuple-element.144), channel_id=1, source_target_pairs={{0,1},{1,0},{2,3},{3,2},{4,5},{5,4},{6,7},{7,6},{8,9},{9,8},{10,11... | collective-permute-start | bytes 393224 | tf_op jit(solution)/shard_map/ppermute | solution.py:39
  74.7 13.6 %collective-permute-start.14 = (bf16[4,8,32,256]{3,2,1,0:T(8,128)(2,1)S(1)}, bf16[4,8,32,256]{3,2,1,0:T(8,128)(2,1)S(1)}, u32[]{:S(2)}, u32[]{:S(2)}) collective-permute-start(bf16[4,8,32,256]{3,2,1,0:T(8,128)(2,1)S(1)} %get-tuple-element.142), channel_id=1, source_target_pairs={{0,1},{1,0},{2,3},{3,2},{4,5},{5,4},{6,7},{7,6},{8,9},{9,8},{10,11... | collective-permute-start | bytes 1572872 | tf_op jit(solution)/shard_map/ppermute | solution.py:39
  74.8 5.7 %collective-permute-start.16 = (bf16[2,8,32,256]{3,2,1,0:T(8,128)(2,1)S(1)}, bf16[2,8,32,256]{3,2,1,0:T(8,128)(2,1)S(1)}, u32[]{:S(2)}, u32[]{:S(2)}) collective-permute-start(bf16[2,8,32,256]{3,2,1,0:T(8,128)(2,1)S(1)} %get-tuple-element.108), channel_id=1, source_target_pairs={{0,1},{1,0},{2,3},{3,2},{4,5},{5,4},{6,7},{7,6},{8,9},{9,8},{10,11... | collective-permute-start | bytes 786440 | tf_op jit(solution)/shard_map/ppermute | solution.py:39
  75.3 9.2 %collective-permute-start.17 = (bf16[2,8,32,256]{3,2,1,0:T(8,128)(2,1)S(1)}, bf16[2,8,32,256]{3,2,1,0:T(8,128)(2,1)S(1)}, u32[]{:S(2)}, u32[]{:S(2)}) collective-permute-start(bf16[2,8,32,256]{3,2,1,0:T(8,128)(2,1)S(1)} %get-tuple-element.109), channel_id=1, source_target_pairs={{0,2},{1,3},{2,0},{3,1},{4,6},{5,7},{6,4},{7,5},{8,10},{9,11},{10,... | collective-permute-start | bytes 786440 | tf_op jit(solution)/shard_map/ppermute | solution.py:39
  76.9 11.4 %collective-permute-start.18 = (bf16[2,8,32,256]{3,2,1,0:T(8,128)(2,1)S(1)}, bf16[2,8,32,256]{3,2,1,0:T(8,128)(2,1)S(1)}, u32[]{:S(2)}, u32[]{:S(2)}) collective-permute-start(bf16[2,8,32,256]{3,2,1,0:T(8,128)(2,1)S(1)} %get-tuple-element.110), channel_id=1, source_target_pairs={{0,3},{1,2},{2,1},{3,0},{4,7},{5,6},{6,5},{7,4},{8,11},{9,10},{10,... | collective-permute-start | bytes 786440 | tf_op jit(solution)/shard_map/ppermute | solution.py:39
  99.1 6.5 %collective-permute-start.19 = (bf16[1,8,32,256]{3,2,1,0:T(8,128)(2,1)S(1)}, bf16[1,8,32,256]{3,2,1,0:T(8,128)(2,1)S(1)}, u32[]{:S(2)}, u32[]{:S(2)}) collective-permute-start(bf16[1,8,32,256]{3,2,1,0:T(8,128)(2,1)S(1)} %get-tuple-element.129), channel_id=1, source_target_pairs={{0,1},{1,0},{2,3},{3,2},{4,5},{5,4},{6,7},{7,6},{8,9},{9,8},{10,11... | collective-permute-start | bytes 393224 | tf_op jit(solution)/shard_map/ppermute | solution.py:39
  99.2 6.5 %collective-permute-start.20 = (bf16[1,8,32,256]{3,2,1,0:T(8,128)(2,1)S(1)}, bf16[1,8,32,256]{3,2,1,0:T(8,128)(2,1)S(1)}, u32[]{:S(2)}, u32[]{:S(2)}) collective-permute-start(bf16[1,8,32,256]{3,2,1,0:T(8,128)(2,1)S(1)} %get-tuple-element.130), channel_id=1, source_target_pairs={{0,2},{1,3},{2,0},{3,1},{4,6},{5,7},{6,4},{7,5},{8,10},{9,11},{10,... | collective-permute-start | bytes 393224 | tf_op jit(solution)/shard_map/ppermute | solution.py:39
  100.9 6.6 %collective-permute-start.21 = (bf16[1,8,32,256]{3,2,1,0:T(8,128)(2,1)S(1)}, bf16[1,8,32,256]{3,2,1,0:T(8,128)(2,1)S(1)}, u32[]{:S(2)}, u32[]{:S(2)}) collective-permute-start(bf16[1,8,32,256]{3,2,1,0:T(8,128)(2,1)S(1)} %get-tuple-element.131), channel_id=1, source_target_pairs={{0,3},{1,2},{2,1},{3,0},{4,7},{5,6},{6,5},{7,4},{8,11},{9,10},{10,... | collective-permute-start | bytes 393224 | tf_op jit(solution)/shard_map/ppermute | solution.py:39

commit v8 on v7

v8 whole, which is shorter than its diff:
```python
import functools

import jax
import jax.numpy as jnp
from jax import lax
from jax.experimental import pallas as pl
from jax.experimental.pallas import tpu as pltpu
from jax.sharding import PartitionSpec as P

R = 2
VMEM_LIMIT = 24 * 1024 * 1024
SOON = pl.CostEstimate(flops=0, bytes_accessed=0, transcendentals=0)


def in_hbm(value):
    return pltpu.with_memory_space_constraint(value, pltpu.HBM)


def in_vmem(value):
    return pltpu.with_memory_space_constraint(value, pltpu.VMEM)


def shifted(value, axis, steps):
    count = lax.axis_size(axis)
    pairs = [(source, (source + steps) % count) for source in range(count)]
    return lax.ppermute(value, axis, pairs)


def strip_target(group, chips, step, other_core):
    chip = lax.rem(lax.shift_right_logical(group, 1) + step, chips)
    return chip * 2 + ((group & 1) ^ other_core)


def to_strip_target(value, chips, step, other_core):
    pairs = [
        (group, (group // 2 + step) % chips * 2 + (group % 2 ^ other_core))
        for group in range(2 * chips)
    ]
    return lax.ppermute(value, "bands", pairs)


def pick_kernel(count, blocks, tile, parts, place_ref, *refs):
    asks, (own, sib), outs = refs[:count], refs[count : count + 2], refs[count + 2 : -1]
    sems = refs[-1]
    first = place_ref[0] * blocks
    copies = []
    for index in range(count):
        ids = asks[index][...] - first
        mine = (ids >= 0) & (ids < blocks)
        lowest = jnp.min(jnp.where(mine, ids, blocks - 1))
        highest = jnp.max(jnp.where(mine, ids, 0))
        block = jnp.where(place_ref[1] == 0, lowest, highest)
        for part in range(parts):
            height = tile // parts
            start = pl.multiple_of(block * tile + part * height, height)
            out = outs[index * parts + part]
            for half, source in enumerate((own, sib)):
                copy = pltpu.make_async_copy(
                    source.at[pl.ds(start, height), :],
                    out.at[half],
                    sems.at[index * parts + part, half],
                )
                copy.start()
                copies.append(copy)
    for copy in copies:
        copy.wait()


def pick(place, asks, own, sib, tile, parts):
    blocks, bands = asks[0].shape[0], own.shape[1]
    count = len(asks)
    n_outs = count * parts
    return pl.pallas_call(
        functools.partial(pick_kernel, count, blocks, tile, parts),
        out_shape=[pltpu.VMEM((2, tile // parts, bands), own.dtype)] * n_outs,
        in_specs=[pl.BlockSpec(memory_space=pltpu.SMEM)]
        + [pl.BlockSpec(memory_space=pltpu.VMEM)] * count
        + [pl.BlockSpec(memory_space=pl.ANY)] * 2,
        out_specs=[pl.BlockSpec(memory_space=pltpu.VMEM)] * n_outs,
        scratch_shapes=[pltpu.SemaphoreType.DMA((n_outs, 2))],
        name="pick_blocks",
        compiler_params=pltpu.CompilerParams(vmem_limit_bytes=VMEM_LIMIT),
        cost_estimate=SOON,
    )(place, *asks, in_hbm(own), in_hbm(sib))


def keep_kernel(own, sib, own_out, sib_out, sems):
    copies = []
    for half, (source, out) in enumerate(((own, own_out), (sib, sib_out))):
        copies.append(pltpu.make_async_copy(source, out, sems.at[half]))
    for copy in copies:
        copy.start()
    for copy in copies:
        copy.wait()


def keep(own, sib):
    return pl.pallas_call(
        keep_kernel,
        out_shape=[pltpu.VMEM(own.shape, own.dtype)] * 2,
        in_specs=[pl.BlockSpec(memory_space=pl.ANY)] * 2,
        out_specs=[pl.BlockSpec(memory_space=pltpu.VMEM)] * 2,
        scratch_shapes=[pltpu.SemaphoreType.DMA((2,))],
        name="keep",
        compiler_params=pltpu.CompilerParams(vmem_limit_bytes=VMEM_LIMIT),
        cost_estimate=SOON,
    )(in_hbm(own), in_hbm(sib))


def tiles_kernel(heights, n_arrived, n_strips, tile, paired, place_ref, *refs):
    lefts, weights = refs[:2], refs[2:4]
    arrived, refs = refs[4 : 4 + n_arrived], refs[4 + n_arrived :]
    outs, (scaled, total) = refs[:-2], refs[-2:]
    if paired:
        outs = outs[:2] + tuple(out.at[index] for out in outs[2:] for index in range(2))
    strip = tile // n_strips
    n_left = lefts[0].shape[0] // tile
    unit = 0
    for j, height in enumerate(heights):
        slot = j % 2
        for half in range(2):
            if n_arrived:
                block = arrived[j][half]
            else:
                first = pl.multiple_of((place_ref[0] * len(heights) + j) * tile, tile)
                block = lefts[half][pl.ds(first, tile), :]
            block = block.astype(jnp.float32)
            for kind in range(2):
                value = block * weights[half][kind : kind + 1, :]
                rows = pl.ds(kind * height, height)
                scaled[slot, half, rows, :] = value.astype(scaled.dtype)
        width = 2 * height
        for half in range(2):
            value = lax.dot_general(
                lefts[half][...],
                scaled[slot, half, :width, :],
                (((1,), (1,)), ((), ())),
                preferred_element_type=jnp.float32,
            )
            if half == 0:
                total[slot, :, :width] = value
            else:
                total[slot, :, :width] += value
        for lane in range(0, width, tile):
            for index in range(n_strips):
                start = place_ref[1 + index] * strip
                for i in range(n_left):
                    rows = pl.ds(pl.multiple_of(i * tile + start, strip), strip)
                    value = total[slot, rows, lane : lane + tile]
                    outs[index][unit, i] = value.astype(outs[index].dtype)
            unit += 1


def tiles(place, own, sib, arrived, weights, n_strips, tile, paired):
    rows, bands = own.shape
    blocks = rows // tile
    heights = [value.shape[1] for value in arrived] or [tile] * (blocks // 2)
    strip = tile // n_strips
    slots = min(len(heights), 2)
    vmem = pl.BlockSpec(memory_space=pltpu.VMEM)
    units = sum(2 * height // tile for height in heights)
    out = jax.ShapeDtypeStruct((units, blocks, strip, tile), jnp.bfloat16)
    pair = jax.ShapeDtypeStruct((2, *out.shape), out.dtype)
    outs = [out, out] + [pair] * (n_strips // 2 - 1) if paired else [out] * n_strips
    return pl.pallas_call(
        functools.partial(tiles_kernel, heights, len(arrived), n_strips, tile, paired),
        out_shape=outs,
        in_specs=[pl.BlockSpec(memory_space=pltpu.SMEM)] + [vmem] * (4 + len(arrived)),
        out_specs=[vmem] * len(outs),
        scratch_shapes=[
            pltpu.VMEM((slots, 2, 2 * max(heights), bands), jnp.bfloat16),
            pltpu.VMEM((slots, rows, 2 * max(heights)), jnp.float32),
        ],
        name="tiles",
        compiler_params=pltpu.CompilerParams(vmem_limit_bytes=VMEM_LIMIT),
        cost_estimate=SOON,
    )(place, in_vmem(own), in_vmem(sib), *weights, *arrived)


def strip_sum(ins, chips, n_chunks, other_core, chunk, unit, i):
    total = None
    for step in range(chips):
        ref = ins[(step * 2 + other_core) * n_chunks + chunk]
        value = ref[unit, i].astype(jnp.float32)
        total = value if total is None else total + value
    return total


def place_early_kernel(chips, sizes, per_core, where_ref, *refs):
    n_chunks = len(sizes)
    ins = refs[: 2 * chips * n_chunks]
    density, energy, later, pool = refs[2 * chips * n_chunks :]
    for other_core in range(2):
        first = other_core * per_core
        for chunk in range(n_chunks):
            for unit in range(2 * sizes[chunk]):
                pool[first + unit // 2, unit % 2] = strip_sum(
                    ins, chips, n_chunks, other_core, chunk, unit, 0
                )
            first += sizes[chunk]
    i = pl.program_id(0)
    slots = density.shape[1]

    @pl.when(i == 0)
    def _():
        later[0] = 0

    for slot in range(slots):
        where = where_ref[i, slot]
        density[0, slot] = pool[where, 0]
        energy[0, slot] = pool[where, 1]

        @pl.when(lax.rem(where, per_core) == per_core - 1)
        def _():
            count = later[0] + 1
            later[count] = i * slots + slot
            later[0] = count


def place_early(where, strips, sizes, chips, per_core):
    _, blocks, strip, tile = strips[0][0].shape
    slots = where.shape[1]
    out = jax.ShapeDtypeStruct((blocks, slots, strip, tile), jnp.float32)
    flat = [value for group in strips for value in group]
    return pl.pallas_call(
        functools.partial(place_early_kernel, chips, sizes, per_core),
        out_shape=[out, out, jax.ShapeDtypeStruct((blocks * slots + 1,), jnp.int32)],
        grid_spec=pltpu.PrefetchScalarGridSpec(
            num_scalar_prefetch=1,
            grid=(blocks,),
            in_specs=[
                pl.BlockSpec(
                    (value.shape[0], 1, strip, tile), lambda i, where: (0, i, 0, 0)
                )
                for value in flat
            ],
            out_specs=[
                pl.BlockSpec((1, slots, strip, tile), lambda i, where: (i, 0, 0, 0))
            ]
            * 2
            + [pl.BlockSpec(memory_space=pltpu.SMEM)],
            scratch_shapes=[pltpu.VMEM((2 * per_core, 2, strip, tile), jnp.float32)],
        ),
        name="place_early",
        compiler_params=pltpu.CompilerParams(vmem_limit_bytes=VMEM_LIMIT),
        cost_estimate=SOON,
    )(where, *flat)


def place_late_kernel(chips, per_core, where_ref, later, *refs):
    lower, upper = refs[: 2 * chips], refs[2 * chips : 4 * chips]
    density, energy, pool, sems = refs[4 * chips + 2 :]
    blocks, slots = density.shape[:2]
    cut = density.shape[3] // 2
    unit = lower[0].shape[0] - 1
    for other_core in range(2):
        for i in range(blocks):
            low = strip_sum(lower, chips, 1, other_core, 0, unit, i)
            high = strip_sum(upper, chips, 1, other_core, 0, 0, i)
            pool[other_core, i, 0] = jnp.concatenate([low[:, :cut], high[:, :cut]], 1)
            pool[other_core, i, 1] = jnp.concatenate([low[:, cut:], high[:, cut:]], 1)
    count = later[0]

    def copies(n):
        entry = jnp.clip(later[n + 1], 0, blocks * slots - 1)
        i, slot = lax.div(entry, slots), lax.rem(entry, slots)
        other_core = jnp.clip(lax.div(where_ref[i, slot], per_core), 0, 1)
        return [
            pltpu.make_async_copy(
                pool.at[other_core, i, kind], out.at[i, slot], sems.at[kind]
            )
            for kind, out in enumerate((density, energy))
        ]

    @pl.loop(0, count)
    def _(n):
        for copy in copies(n):
            copy.start()

    @pl.loop(0, count)
    def _(n):
        for copy in copies(n):
            copy.wait()


def place_late(where, later, lower, upper, density, energy, chips, per_core):
    blocks, _, strip, tile = density.shape
    smem = pl.BlockSpec(memory_space=pltpu.SMEM)
    anywhere = pl.BlockSpec(memory_space=pl.ANY)
    out = jax.ShapeDtypeStruct(density.shape, density.dtype)
    strips = [*lower, *upper]
    return pl.pallas_call(
        functools.partial(place_late_kernel, chips, per_core),
        out_shape=[out, out],
        in_specs=[smem, smem]
        + [pl.BlockSpec(memory_space=pltpu.VMEM)] * len(strips)
        + [anywhere] * 2,
        out_specs=[anywhere] * 2,
        scratch_shapes=[
            pltpu.VMEM((2, blocks, 2, strip, tile), jnp.float32),
            pltpu.SemaphoreType.DMA((2,)),
        ],
        input_output_aliases={2 + len(strips): 0, 3 + len(strips): 1},
        name="place_late",
        compiler_params=pltpu.CompilerParams(vmem_limit_bytes=VMEM_LIMIT),
        cost_estimate=SOON,
    )(where, later, *strips, density, energy)


def body(eigvecs, occupations, energies, neighbours):
    n_atoms = lax.axis_size("atoms")
    n_bands = lax.axis_size("bands")
    chips = n_bands // 2
    own_index = lax.axis_index("atoms").astype(jnp.int32)
    group = lax.axis_index("bands").astype(jnp.int32)
    core = group & 1
    blocks = neighbours.shape[0]
    tile = eigvecs.shape[0] // blocks
    half_blocks = blocks // 2
    offsets = [-1, 1, 2, -2]

    asks = [shifted(neighbours, "atoms", offset) for offset in offsets]
    sib = to_strip_target(eigvecs, chips, 0, 1)
    own_weights = jnp.stack([occupations, occupations * energies], 0)

    targets = [
        strip_target(group, chips, step, other)
        for step in range(chips)
        for other in range(2)
    ]
    here = jnp.stack([own_index, core]).astype(jnp.int32)
    place = jnp.stack([core] + targets).astype(jnp.int32)

    asks, own_weights = lax.optimization_barrier((asks, own_weights))
    weights = (own_weights, to_strip_target(own_weights, chips, 0, 1))
    picked = list(pick(here, asks[:3], eigvecs, sib, tile, 1))
    arrived = [
        shifted(value, "atoms", -offset) for value, offset in zip(picked, offsets)
    ]
    kept_eigvecs, picked[0] = lax.optimization_barrier((eigvecs, picked[0]))
    own, kept_sib = keep(kept_eigvecs, sib)

    def strips_of(arrived, paired):
        parts = list(tiles(place, own, kept_sib, arrived, weights, n_bands, tile, paired))
        for index in range(1, len(parts)):
            step, other = (max(index - 1, 0), index == 1) if paired else (index // 2, index % 2)
            parts[index] = to_strip_target(parts[index], chips, step, int(other))
        return parts

    def passed_on(parts):
        singles = parts[:2]
        for pair in parts[2:]:
            singles += [pair[0], to_strip_target(pair[1], chips, 0, 1)]
        return singles

    chunks = [strips_of((), True)]
    neighbours, here, chunks[0][0] = lax.optimization_barrier(
        (neighbours, here, chunks[0][0])
    )
    halves = list(pick(here, asks[3:], eigvecs, sib, tile, 2))

    owners = lax.div(neighbours, blocks)
    within = lax.rem(neighbours, blocks)
    distance = lax.rem(owners - own_index + n_atoms, n_atoms)
    spot = lax.rem(within, half_blocks)
    side = lax.div(within, half_blocks)
    for index, offset in enumerate(offsets):
        from_it = distance == offset % n_atoms
        highest = jnp.max(jnp.where(from_it, within, -1))
        side = jnp.where(from_it, (within == highest).astype(jnp.int32), side)
        spot = jnp.where(from_it, half_blocks + index, spot)
    per_core = half_blocks + len(offsets)
    where = ((side ^ core) * per_core + spot).astype(jnp.int32)

    *near, third = arrived
    third, halves, chunks[0][:1] = lax.optimization_barrier((third, halves, chunks[0][:1]))
    lower = shifted(halves[0], "atoms", -offsets[3])
    parts = list(tiles(place, own, kept_sib, [third], weights, n_bands, tile, True))
    pairs = [
        to_strip_target(pair, chips, step + 1, 0) for step, pair in enumerate(parts[2:])
    ]
    near, lower, halves[1], parts[:2], pairs, chunks = lax.optimization_barrier(
        (near, lower, halves[1], parts[:2], pairs, chunks)
    )
    upper = shifted(halves[1], "atoms", -offsets[3])
    chunks.append([parts[0], to_strip_target(parts[1], chips, 0, 1)] + pairs)
    direct = strips_of([*near, lower], False)
    chunks, direct[0] = lax.optimization_barrier((chunks, direct[0]))
    chunks = [passed_on(chunk) for chunk in chunks] + [direct]
    where, upper, chunks = lax.optimization_barrier((where, upper, chunks))
    last = strips_of([upper], False)
    where, last[0] = lax.optimization_barrier((where, last[0]))
    local, far, direct = chunks
    strips = list(zip(local, direct, far))
    sizes = [half_blocks, 2, 1]
    density, energy, later = place_early(where, strips, sizes, chips, per_core)
    return place_late(where, later, direct, last, density, energy, chips, per_core)


def solution(mesh):
    return jax.shard_map(
        body,
        mesh=mesh,
        in_specs=(P("atoms", "bands"), P("bands"), P("bands"), P("atoms", None)),
        out_specs=(P("atoms", None, "bands", None), P("atoms", None, "bands", None)),
        check_vma=False,
    )
```

time: 110 us -> 113 us (1.027)
  waiting for transfers between devices: 40.1 us -> 43.1 us
  Pallas kernels: 36.3 us -> 38.9 us
  starting transfers between devices: 27.1 us -> 24.6 us
    pallas_call x7, Pallas kernels: 28.2 us -> 30.7 us  [the longest x4 23.1 us: tiles(): pl.pallas_call(functools.partial(tiles_kernel, heights, len(arrived), n_s...]
    ppermute x8 -> x9, starting transfers between devices: 18.2 us -> 16 us  [shifted(): return lax.ppermute(value, axis, pairs)]
    ppermute x8 -> x9, waiting for transfers between devices: 29.8 us -> 32 us  [shifted(): return lax.ppermute(value, axis, pairs)]
  transfers between devices with their start and end apart: 22 -> 23, of which waited for: 9 -> 6; matrix products, arithmetic and copies ran while one was open for 5% -> 4% of each run, Pallas kernels for 26% -> 27%
where the time goes in v8:
time: 113 us
  waiting for transfers between devices  43.1 us (38%)
  Pallas kernels  38.9 us (34%)
  starting transfers between devices  24.6 us (22%)
  other arithmetic  4.87 us (4%)
    ppermute x9, waiting for transfers between devices, shifted(): return lax.ppermute(value, axis, pairs)  32 us
    pallas_call x4, Pallas kernels, tiles(): pl.pallas_call(functools.partial(tiles_kernel, heights, len(arrived), n_s...  23.1 us
    ppermute x9, starting transfers between devices, shifted(): return lax.ppermute(value, axis, pairs)  16 us
    ppermute x14, waiting for transfers between devices, to_strip_target(): return lax.ppermute(value, 'bands', pairs)  11.1 us
    ppermute x14, starting transfers between devices, to_strip_target(): return lax.ppermute(value, 'bands', pairs)  8.58 us
    pallas_call x2, Pallas kernels, pick(): pl.pallas_call(functools.partial(pick_kernel, count, blocks, tile, parts)...  5.74 us
    pallas_call x1, Pallas kernels, place_early(): pl.pallas_call(functools.partial(place_early_kernel, chips, sizes, per_co...  4.74 us
    pallas_call x1, Pallas kernels, keep(): pl.pallas_call(keep_kernel, out_shape=[pltpu.VMEM(own.shape, own.dtype)]...  3.48 us
  transfers between devices with their start and end apart: 23, of which 6 were waited for; matrix products, arithmetic and copies ran while one was open for 4% of the time, Pallas kernels for 27%

profile of v8, /device:TPU:0, one launch (start us, length us, event | category | flops | bytes accessed | tf_op | source)
XLA Modules:
  0.0 112.5 jit_solution(3250483552927996476)
XLA Ops:
  1.1 2.6 %collective-permute-start.2 = (s32[8,16]{1,0:T(8,128)}, s32[8,16]{1,0:T(8,128)S(1)}, u32[]{:S(2)}, u32[]{:S(2)}) collective-permute-start(s32[8,16]{1,0:T(8,128)} %param.7), channel_id=1, source_target_pairs={{0,8},{4,12},{8,16},{12,20},{16,24},{20,28},{24,0},{28,4},{1,9},{5... | collective-permute-start | bytes 1544 | tf_op jit(solution)/shard_map/ppermute | solution.py:26
  5.3 3.2 %collective-permute-start = (s32[8,16]{1,0:T(8,128)}, s32[8,16]{1,0:T(8,128)S(1)}, u32[]{:S(2)}, u32[]{:S(2)}) collective-permute-start(s32[8,16]{1,0:T(8,128)} %param.7), channel_id=1, source_target_pairs={{0,28},{4,0},{8,4},{12,8},{16,12},{20,16},{24,20},{28,24},{1,29},{... | collective-permute-start | bytes 1544 | tf_op jit(solution)/shard_map/ppermute | solution.py:26
  10.3 2.0 %collective-permute-done.3.refs_0_ = s32[8,16]{1,0:T(8,128)S(1)} collective-permute-done((s32[8,16]{1,0:T(8,128)}, s32[8,16]{1,0:T(8,128)S(1)}, u32[]{:S(2)}, u32[]{:S(2)}) %collective-permute-start.3) | collective-permute-done | bytes 544 | tf_op jit(solution)/shard_map/ppermute | solution.py:26
  12.3 3.8 %pick_blocks.2 = (bf16[2,128,2048]{2,1,0:T(8,128)(2,1)S(1)}, bf16[2,128,2048]{2,1,0:T(8,128)(2,1)S(1)}, bf16[2,128,2048]{2,1,0:T(8,128)(2,1)}) custom-call(s32[2]{0:T(128)S(1)} %pad_add_fusion.place_ref, s32[8,16]{1,0:T(8,128)S(1)} %collective-permute-done.refs_0_, s32[8,16]{1,0:T(8,128)S(1)} %collective-permute-done.1.refs_1_, ...), custom_call_target="tpu_custom_call" | custom-call | tf_op jit(solution)/shard_map/pick_blocks/pallas_call | solution.py:73
  16.1 2.0 %collective-permute-start.8 = (bf16[2,128,2048]{2,1,0:T(8,128)(2,1)}, bf16[2,128,2048]{2,1,0:T(8,128)(2,1)S(1)}, u32[]{:S(2)}, u32[]{:S(2)}) collective-permute-start(bf16[2,128,2048]{2,1,0:T(8,128)(2,1)} %get-tuple-element.83), channel_id=1, source_target_pairs={{0,24},{4,28},{8,0},{12,4},{16,8},{20,12},{24,16},{28,20},{1,25},{... | collective-permute-start | bytes 3145736 | tf_op jit(solution)/shard_map/ppermute | solution.py:26
  19.3 3.6 %collective-permute-start.7 = (bf16[2,128,2048]{2,1,0:T(8,128)(2,1)S(1)}, bf16[2,128,2048]{2,1,0:T(8,128)(2,1)S(1)}, u32[]{:S(2)}, u32[]{:S(2)}) collective-permute-start(bf16[2,128,2048]{2,1,0:T(8,128)(2,1)S(1)} %get-tuple-element.82), channel_id=1, source_target_pairs={{0,28},{4,0},{8,4},{12,8},{16,12},{20,16},{24,20},{28,24},{1,29},{... | collective-permute-start | bytes 3145736 | tf_op jit(solution)/shard_map/ppermute | solution.py:26
  22.9 3.5 %keep.1 = (bf16[1024,2048]{1,0:T(8,128)(2,1)S(1)}, bf16[1024,2048]{1,0:T(8,128)(2,1)S(1)}) custom-call(bf16[1024,2048]{1,0:T(8,128)(2,1)} %refs_1_.1, bf16[1024,2048]{1,0:T(8,128)(2,1)} %collective-permute-done.4.refs_4_.sib.refs_2_), custom_call_target="tpu_custom_call" | custom-call | tf_op jit(solution)/shard_map/keep/pallas_call | solution.py:98
  26.4 9.8 %tiles.4 = (bf16[8,8,32,128]{3,2,1,0:T(8,128)(2,1)S(1)}, bf16[8,8,32,128]{3,2,1,0:T(8,128)(2,1)S(1)}, bf16[2,8,8,32,128]{4,3,2,1,0:T(8,128)(2,1)S(1)}) custom-call(s32[5]{0:T(128)S(1)} %stack.41.place_ref, bf16[1024,2048]{1,0:T(8,128)(2,1)S(1)} %get-tuple-element.77.refs_0_, bf16[1024,2048]{1,0:T(8,128)(2,1)S(1)} %get-tuple-element.78.refs_1_, ...), custom_call_target="tpu_custom_call" | custom-call | tf_op jit(solution)/shard_map/tiles/pallas_call | solution.py:165
  36.2 1.7 %collective-permute-start.12 = (bf16[2,8,8,32,128]{4,3,2,1,0:T(8,128)(2,1)S(1)}, bf16[2,8,8,32,128]{4,3,2,1,0:T(8,128)(2,1)S(1)}, u32[]{:S(2)}, u32[]{:S(2)}) collective-permute-start(bf16[2,8,8,32,128]{4,3,2,1,0:T(8,128)(2,1)S(1)} %get-tuple-element.97), channel_id=1, source_target_pairs={{0,2},{1,3},{2,0},{3,1},{4,6},{5,7},{6,4},{7,5},{8,10},{9,11},{10,... | collective-permute-start | bytes 3145736 | tf_op jit(solution)/shard_map/ppermute | solution.py:39
  37.9 2.0 %pick_blocks.3 = (bf16[2,64,2048]{2,1,0:T(8,128)(2,1)S(1)}, bf16[2,64,2048]{2,1,0:T(8,128)(2,1)S(1)}) custom-call(s32[2]{0:T(128)S(1)} %pad_add_fusion.place_ref, s32[8,16]{1,0:T(8,128)S(1)} %collective-permute-done.3.refs_0_, bf16[1024,2048]{1,0:T(8,128)(2,1)} %refs_1_.1, bf16[1024,2048]{1,0:T(8,128)(2,1)} %collective-permute-done.4.refs_4_.sib.refs_2_), custom_call_target="tpu_custom_call" | custom-call | tf_op jit(solution)/shard_map/pick_blocks/pallas_call | solution.py:73
  39.9 2.6 %collective-permute-done.8.refs_4_ = bf16[2,128,2048]{2,1,0:T(8,128)(2,1)S(1)} collective-permute-done((bf16[2,128,2048]{2,1,0:T(8,128)(2,1)}, bf16[2,128,2048]{2,1,0:T(8,128)(2,1)S(1)}, u32[]{:S(2)}, u32[]{:S(2)}) %collective-permute-start.8) | collective-permute-done | bytes 1048608 | tf_op jit(solution)/shard_map/ppermute | solution.py:26
  42.5 3.0 %tiles.5 = (bf16[2,8,32,128]{3,2,1,0:T(8,128)(2,1)S(1)}, bf16[2,8,32,128]{3,2,1,0:T(8,128)(2,1)S(1)}, bf16[2,2,8,32,128]{4,3,2,1,0:T(8,128)(2,1)S(1)}) custom-call(s32[5]{0:T(128)S(1)} %stack.41.place_ref, bf16[1024,2048]{1,0:T(8,128)(2,1)S(1)} %get-tuple-element.77.refs_0_, bf16[1024,2048]{1,0:T(8,128)(2,1)S(1)} %get-tuple-element.78.refs_1_, ...), custom_call_target="tpu_custom_call" | custom-call | tf_op jit(solution)/shard_map/tiles/pallas_call | solution.py:165
  45.5 1.6 %collective-permute-start.10 = (bf16[2,2,8,32,128]{4,3,2,1,0:T(8,128)(2,1)S(1)}, bf16[2,2,8,32,128]{4,3,2,1,0:T(8,128)(2,1)S(1)}, u32[]{:S(2)}, u32[]{:S(2)}) collective-permute-start(bf16[2,2,8,32,128]{4,3,2,1,0:T(8,128)(2,1)S(1)} %get-tuple-element.94), channel_id=1, source_target_pairs={{0,2},{1,3},{2,0},{3,1},{4,6},{5,7},{6,4},{7,5},{8,10},{9,11},{10,... | collective-permute-start | bytes 786440 | tf_op jit(solution)/shard_map/ppermute | solution.py:39
  47.1 20.0 %collective-permute-done.7.refs_5_ = bf16[2,128,2048]{2,1,0:T(8,128)(2,1)S(1)} collective-permute-done((bf16[2,128,2048]{2,1,0:T(8,128)(2,1)S(1)}, bf16[2,128,2048]{2,1,0:T(8,128)(2,1)S(1)}, u32[]{:S(2)}, u32[]{:S(2)}) %collective-permute-start.7) | collective-permute-done | bytes 1048608 | tf_op jit(solution)/shard_map/ppermute | solution.py:26
  67.1 7.4 %collective-permute-done.9.refs_6_ = bf16[2,64,2048]{2,1,0:T(8,128)(2,1)S(1)} collective-permute-done((bf16[2,64,2048]{2,1,0:T(8,128)(2,1)S(1)}, bf16[2,64,2048]{2,1,0:T(8,128)(2,1)S(1)}, u32[]{:S(2)}, u32[]{:S(2)}) %collective-permute-start.9) | collective-permute-done | bytes 524320 | tf_op jit(solution)/shard_map/ppermute | solution.py:26
  74.5 1.6 %collective-permute-start.13 = (bf16[2,64,2048]{2,1,0:T(8,128)(2,1)S(1)}, bf16[2,64,2048]{2,1,0:T(8,128)(2,1)S(1)}, u32[]{:S(2)}, u32[]{:S(2)}) collective-permute-start(bf16[2,64,2048]{2,1,0:T(8,128)(2,1)S(1)} %get-tuple-element.98), channel_id=1, source_target_pairs={{0,8},{4,12},{8,16},{12,20},{16,24},{20,28},{24,0},{28,4},{1,9},{5... | collective-permute-start | bytes 1572872 | tf_op jit(solution)/shard_map/ppermute | solution.py:26
  76.1 7.4 %tiles.6 = (bf16[5,8,32,128]{3,2,1,0:T(8,128)(2,1)S(1)}, bf16[5,8,32,128]{3,2,1,0:T(8,128)(2,1)S(1)}, bf16[5,8,32,128]{3,2,1,0:T(8,128)(2,1)S(1)}, bf16[5,8,32,128]{3,2,1,0:T(8,128)(2,1)S(1)}) custom-call(s32[5]{0:T(128)S(1)} %stack.41.place_ref, bf16[1024,2048]{1,0:T(8,128)(2,1)S(1)} %get-tuple-element.77.refs_0_, ...), custom_call_target="tpu_custom_call" | custom-call | tf_op jit(solution)/shard_map/tiles/pallas_call | solution.py:165
  87.1 2.6 %fusion.9.where_ref = s32[8,16]{1,0:T(8,128)S(1)} fusion(pred[8,16]{1,0:T(8,128)(4,1)S(1)} %get-tuple-element.149, pred[8,16]{1,0:T(8,128)(4,1)S(1)} %get-tuple-element.148, pred[8,16]{1,0:T(8,128)(4,1)S(1)} %get-tuple-element.147, pred[8,16]{1,0:T(8,128)(4,1)S(1)} %get-tuple-element.146, s32[]{:T(128)} %and.14, s32[]{:T(128)} %get-tuple-element.144, ...), kind=kLoop, calls=%fused_computation.22 | loop fusion | flops 4352 | bytes 1556 | tf_op jit(solution)/shard_map/add | solution.py:373
  89.7 5.3 %collective-permute-done.18.refs_7_.refs_2_ = bf16[5,8,32,128]{3,2,1,0:T(8,128)(2,1)S(1)} collective-permute-done((bf16[5,8,32,128]{3,2,1,0:T(8,128)(2,1)S(1)}, bf16[5,8,32,128]{3,2,1,0:T(8,128)(2,1)S(1)}, u32[]{:S(2)}, u32[]{:S(2)}) %collective-permute-start.18) | collective-permute-done | bytes 327712 | tf_op jit(solution)/shard_map/ppermute | solution.py:39
  95.0 5.7 %collective-permute-done.19.refs_10_.refs_3_ = bf16[5,8,32,128]{3,2,1,0:T(8,128)(2,1)S(1)} collective-permute-done((bf16[5,8,32,128]{3,2,1,0:T(8,128)(2,1)S(1)}, bf16[5,8,32,128]{3,2,1,0:T(8,128)(2,1)S(1)}, u32[]{:S(2)}, u32[]{:S(2)}) %collective-permute-start.19) | collective-permute-done | bytes 327712 | tf_op jit(solution)/shard_map/ppermute | solution.py:39
  100.8 2.9 %tiles.7 = (bf16[1,8,32,128]{3,2,1,0:T(8,128)(2,1)S(1)}, bf16[1,8,32,128]{3,2,1,0:T(8,128)(2,1)S(1)}, bf16[1,8,32,128]{3,2,1,0:T(8,128)(2,1)S(1)}, bf16[1,8,32,128]{3,2,1,0:T(8,128)(2,1)S(1)}) custom-call(s32[5]{0:T(128)S(1)} %stack.41.place_ref, bf16[1024,2048]{1,0:T(8,128)(2,1)S(1)} %get-tuple-element.77.refs_0_, ...), custom_call_target="tpu_custom_call" | custom-call | tf_op jit(solution)/shard_map/tiles/pallas_call | solution.py:165
  104.2 1.5 %collective-permute-start.21 = (bf16[1,8,32,128]{3,2,1,0:T(8,128)(2,1)S(1)}, bf16[1,8,32,128]{3,2,1,0:T(8,128)(2,1)S(1)}, u32[]{:S(2)}, u32[]{:S(2)}) collective-permute-start(bf16[1,8,32,128]{3,2,1,0:T(8,128)(2,1)S(1)} %get-tuple-element.138), channel_id=1, source_target_pairs={{0,2},{1,3},{2,0},{3,1},{4,6},{5,7},{6,4},{7,5},{8,10},{9,11},{10,... | collective-permute-start | bytes 196616 | tf_op jit(solution)/shard_map/ppermute | solution.py:39
  105.7 4.7 %place_early.1 = (f32[8,16,32,128]{3,2,1,0:T(8,128)}, f32[8,16,32,128]{3,2,1,0:T(8,128)}, s32[129]{0:T(256)S(1)}) custom-call(s32[8,16]{1,0:T(8,128)S(1)} %fusion.9.where_ref, bf16[8,8,32,128]{3,2,1,0:T(8,128)(2,1)S(1)} %get-tuple-element.123.refs_0_, bf16[5,8,32,128]{3,2,1,0:T(8,128)(2,1)S(1)} %get-tuple-element.124.refs_1_.refs_0_, ...), custom_call_target="tpu_custom_call" | custom-call | tf_op jit(solution)/shard_map/place_early/pallas_call | solution.py:225
  110.5 1.9 %place_late.1 = (f32[8,16,32,128]{3,2,1,0:T(8,128)}, f32[8,16,32,128]{3,2,1,0:T(8,128)}) custom-call(s32[8,16]{1,0:T(8,128)S(1)} %fusion.9.where_ref, s32[129]{0:T(256)S(1)} %get-tuple-element.135.later, bf16[5,8,32,128]{3,2,1,0:T(8,128)(2,1)S(1)} %get-tuple-element.124.refs_1_.refs_0_, ...), custom_call_target="tpu_custom_call", output_to_operand_aliasing={{0}: (10, {}), {1}: (11, {})} | custom-call | tf_op jit(solution)/shard_map/place_late/pallas_call | solution.py:292
  (41 shorter events, 9.2 us)
Async XLA Ops:
  0.6 11.7 %collective-permute-start.4 = (bf16[1024,2048]{1,0:T(8,128)(2,1)}, bf16[1024,2048]{1,0:T(8,128)(2,1)}, u32[]{:S(2)}, u32[]{:S(2)}) collective-permute-start(bf16[1024,2048]{1,0:T(8,128)(2,1)} %refs_1_.1), channel_id=1, source_target_pairs={{0,1},{1,0},{2,3},{3,2},{4,5},{5,4},{6,7},{7,6},{8,9},{9,8},{10,11... | collective-permute-start | bytes 12582920 | tf_op jit(solution)/shard_map/ppermute | solution.py:39
  1.1 9.2 %collective-permute-start.2 = (s32[8,16]{1,0:T(8,128)}, s32[8,16]{1,0:T(8,128)S(1)}, u32[]{:S(2)}, u32[]{:S(2)}) collective-permute-start(s32[8,16]{1,0:T(8,128)} %param.7), channel_id=1, source_target_pairs={{0,8},{4,12},{8,16},{12,20},{16,24},{20,28},{24,0},{28,4},{1,9},{5... | collective-permute-start | bytes 1544 | tf_op jit(solution)/shard_map/ppermute | solution.py:26
  3.8 6.6 %collective-permute-start.1 = (s32[8,16]{1,0:T(8,128)}, s32[8,16]{1,0:T(8,128)S(1)}, u32[]{:S(2)}, u32[]{:S(2)}) collective-permute-start(s32[8,16]{1,0:T(8,128)} %param.7), channel_id=1, source_target_pairs={{0,4},{4,8},{8,12},{12,16},{16,20},{20,24},{24,28},{28,0},{1,5},{5... | collective-permute-start | bytes 1544 | tf_op jit(solution)/shard_map/ppermute | solution.py:26
  5.3 5.1 %collective-permute-start = (s32[8,16]{1,0:T(8,128)}, s32[8,16]{1,0:T(8,128)S(1)}, u32[]{:S(2)}, u32[]{:S(2)}) collective-permute-start(s32[8,16]{1,0:T(8,128)} %param.7), channel_id=1, source_target_pairs={{0,28},{4,0},{8,4},{12,8},{16,12},{20,16},{24,20},{28,24},{1,29},{... | collective-permute-start | bytes 1544 | tf_op jit(solution)/shard_map/ppermute | solution.py:26
  8.5 3.8 %collective-permute-start.3 = (s32[8,16]{1,0:T(8,128)}, s32[8,16]{1,0:T(8,128)S(1)}, u32[]{:S(2)}, u32[]{:S(2)}) collective-permute-start(s32[8,16]{1,0:T(8,128)} %param.7), channel_id=1, source_target_pairs={{0,24},{4,28},{8,0},{12,4},{16,8},{20,12},{24,16},{28,20},{1,25},{... | collective-permute-start | bytes 1544 | tf_op jit(solution)/shard_map/ppermute | solution.py:26
  16.1 26.4 %collective-permute-start.8 = (bf16[2,128,2048]{2,1,0:T(8,128)(2,1)}, bf16[2,128,2048]{2,1,0:T(8,128)(2,1)S(1)}, u32[]{:S(2)}, u32[]{:S(2)}) collective-permute-start(bf16[2,128,2048]{2,1,0:T(8,128)(2,1)} %get-tuple-element.83), channel_id=1, source_target_pairs={{0,24},{4,28},{8,0},{12,4},{16,8},{20,12},{24,16},{28,20},{1,25},{... | collective-permute-start | bytes 3145736 | tf_op jit(solution)/shard_map/ppermute | solution.py:26
  18.1 8.3 %collective-permute-start.5 = (f32[2,2048]{1,0:T(2,128)S(1)}, f32[2,2048]{1,0:T(2,128)S(1)}, u32[]{:S(2)}, u32[]{:S(2)}) collective-permute-start(f32[2,2048]{1,0:T(2,128)S(1)} %pad_maximum_fusion.refs_2_), channel_id=1, source_target_pairs={{0,1},{1,0},{2,3},{3,2},{4,5},{5,4},{6,7},{7,6},{8,9},{9,8},{10,11... | collective-permute-start | bytes 49160 | tf_op jit(solution)/shard_map/ppermute | solution.py:39
  18.2 48.9 %collective-permute-start.6 = (bf16[2,128,2048]{2,1,0:T(8,128)(2,1)S(1)}, bf16[2,128,2048]{2,1,0:T(8,128)(2,1)S(1)}, u32[]{:S(2)}, u32[]{:S(2)}) collective-permute-start(bf16[2,128,2048]{2,1,0:T(8,128)(2,1)S(1)} %get-tuple-element.75), channel_id=1, source_target_pairs={{0,4},{4,8},{8,12},{12,16},{16,20},{20,24},{24,28},{28,0},{1,5},{5... | collective-permute-start | bytes 3145736 | tf_op jit(solution)/shard_map/ppermute | solution.py:26
  19.3 47.8 %collective-permute-start.7 = (bf16[2,128,2048]{2,1,0:T(8,128)(2,1)S(1)}, bf16[2,128,2048]{2,1,0:T(8,128)(2,1)S(1)}, u32[]{:S(2)}, u32[]{:S(2)}) collective-permute-start(bf16[2,128,2048]{2,1,0:T(8,128)(2,1)S(1)} %get-tuple-element.82), channel_id=1, source_target_pairs={{0,28},{4,0},{8,4},{12,8},{16,12},{20,16},{24,20},{28,24},{1,29},{... | collective-permute-start | bytes 3145736 | tf_op jit(solution)/shard_map/ppermute | solution.py:26
  36.2 30.9 %collective-permute-start.12 = (bf16[2,8,8,32,128]{4,3,2,1,0:T(8,128)(2,1)S(1)}, bf16[2,8,8,32,128]{4,3,2,1,0:T(8,128)(2,1)S(1)}, u32[]{:S(2)}, u32[]{:S(2)}) collective-permute-start(bf16[2,8,8,32,128]{4,3,2,1,0:T(8,128)(2,1)S(1)} %get-tuple-element.97), channel_id=1, source_target_pairs={{0,2},{1,3},{2,0},{3,1},{4,6},{5,7},{6,4},{7,5},{8,10},{9,11},{10,... | collective-permute-start | bytes 3145736 | tf_op jit(solution)/shard_map/ppermute | solution.py:39
  37.9 7.5 %collective-permute-start.11 = (bf16[8,8,32,128]{3,2,1,0:T(8,128)(2,1)S(1)}, bf16[8,8,32,128]{3,2,1,0:T(8,128)(2,1)S(1)}, u32[]{:S(2)}, u32[]{:S(2)}) collective-permute-start(bf16[8,8,32,128]{3,2,1,0:T(8,128)(2,1)S(1)} %get-tuple-element.96), channel_id=1, source_target_pairs={{0,1},{1,0},{2,3},{3,2},{4,5},{5,4},{6,7},{7,6},{8,9},{9,8},{10,11... | collective-permute-start | bytes 1572872 | tf_op jit(solution)/shard_map/ppermute | solution.py:39
  42.5 32.0 %collective-permute-start.9 = (bf16[2,64,2048]{2,1,0:T(8,128)(2,1)S(1)}, bf16[2,64,2048]{2,1,0:T(8,128)(2,1)S(1)}, u32[]{:S(2)}, u32[]{:S(2)}) collective-permute-start(bf16[2,64,2048]{2,1,0:T(8,128)(2,1)S(1)} %get-tuple-element.89), channel_id=1, source_target_pairs={{0,8},{4,12},{8,16},{12,20},{16,24},{20,28},{24,0},{28,4},{1,9},{5... | collective-permute-start | bytes 1572872 | tf_op jit(solution)/shard_map/ppermute | solution.py:26
  45.5 21.6 %collective-permute-start.10 = (bf16[2,2,8,32,128]{4,3,2,1,0:T(8,128)(2,1)S(1)}, bf16[2,2,8,32,128]{4,3,2,1,0:T(8,128)(2,1)S(1)}, u32[]{:S(2)}, u32[]{:S(2)}) collective-permute-start(bf16[2,2,8,32,128]{4,3,2,1,0:T(8,128)(2,1)S(1)} %get-tuple-element.94), channel_id=1, source_target_pairs={{0,2},{1,3},{2,0},{3,1},{4,6},{5,7},{6,4},{7,5},{8,10},{9,11},{10,... | collective-permute-start | bytes 786440 | tf_op jit(solution)/shard_map/ppermute | solution.py:39
  74.5 11.8 %copy-start = (s32[8,16]{1,0:T(8,128)S(1)}, s32[8,16]{1,0:T(8,128)}, u32[]{:S(2)}) copy-start(s32[8,16]{1,0:T(8,128)} %param.7) | copy-start | bytes 1540
  74.5 9.0 %collective-permute-start.14 = (bf16[2,8,32,128]{3,2,1,0:T(8,128)(2,1)S(1)}, bf16[2,8,32,128]{3,2,1,0:T(8,128)(2,1)S(1)}, u32[]{:S(2)}, u32[]{:S(2)}) collective-permute-start(bf16[2,8,32,128]{3,2,1,0:T(8,128)(2,1)S(1)} %get-tuple-element.103), channel_id=1, source_target_pairs={{0,1},{1,0},{2,3},{3,2},{4,5},{5,4},{6,7},{7,6},{8,9},{9,8},{10,11... | collective-permute-start | bytes 393224 | tf_op jit(solution)/shard_map/ppermute | solution.py:39
  74.5 26.3 %collective-permute-start.13 = (bf16[2,64,2048]{2,1,0:T(8,128)(2,1)S(1)}, bf16[2,64,2048]{2,1,0:T(8,128)(2,1)S(1)}, u32[]{:S(2)}, u32[]{:S(2)}) collective-permute-start(bf16[2,64,2048]{2,1,0:T(8,128)(2,1)S(1)} %get-tuple-element.98), channel_id=1, source_target_pairs={{0,8},{4,12},{8,16},{12,20},{16,24},{20,28},{24,0},{28,4},{1,9},{5... | collective-permute-start | bytes 1572872 | tf_op jit(solution)/shard_map/ppermute | solution.py:26
  83.6 2.5 %collective-permute-start.16 = (bf16[2,8,32,128]{3,2,1,0:T(8,128)(2,1)S(1)}, bf16[2,8,32,128]{3,2,1,0:T(8,128)(2,1)S(1)}, u32[]{:S(2)}, u32[]{:S(2)}) collective-permute-start(bf16[2,8,32,128]{3,2,1,0:T(8,128)(2,1)S(1)} %get-tuple-element.152), channel_id=1, source_target_pairs={{0,1},{1,0},{2,3},{3,2},{4,5},{5,4},{6,7},{7,6},{8,9},{9,8},{10,11... | collective-permute-start | bytes 393224 | tf_op jit(solution)/shard_map/ppermute | solution.py:39
  83.9 16.9 %collective-permute-start.15 = (bf16[8,8,32,128]{3,2,1,0:T(8,128)(2,1)S(1)}, bf16[8,8,32,128]{3,2,1,0:T(8,128)(2,1)S(1)}, u32[]{:S(2)}, u32[]{:S(2)}) collective-permute-start(bf16[8,8,32,128]{3,2,1,0:T(8,128)(2,1)S(1)} %get-tuple-element.150), channel_id=1, source_target_pairs={{0,1},{1,0},{2,3},{3,2},{4,5},{5,4},{6,7},{7,6},{8,9},{9,8},{10,11... | collective-permute-start | bytes 1572872 | tf_op jit(solution)/shard_map/ppermute | solution.py:39
  84.3 5.4 %collective-permute-start.17 = (bf16[5,8,32,128]{3,2,1,0:T(8,128)(2,1)S(1)}, bf16[5,8,32,128]{3,2,1,0:T(8,128)(2,1)S(1)}, u32[]{:S(2)}, u32[]{:S(2)}) collective-permute-start(bf16[5,8,32,128]{3,2,1,0:T(8,128)(2,1)S(1)} %get-tuple-element.116), channel_id=1, source_target_pairs={{0,1},{1,0},{2,3},{3,2},{4,5},{5,4},{6,7},{7,6},{8,9},{9,8},{10,11... | collective-permute-start | bytes 983048 | tf_op jit(solution)/shard_map/ppermute | solution.py:39
  84.5 10.5 %collective-permute-start.18 = (bf16[5,8,32,128]{3,2,1,0:T(8,128)(2,1)S(1)}, bf16[5,8,32,128]{3,2,1,0:T(8,128)(2,1)S(1)}, u32[]{:S(2)}, u32[]{:S(2)}) collective-permute-start(bf16[5,8,32,128]{3,2,1,0:T(8,128)(2,1)S(1)} %get-tuple-element.117), channel_id=1, source_target_pairs={{0,2},{1,3},{2,0},{3,1},{4,6},{5,7},{6,4},{7,5},{8,10},{9,11},{10,... | collective-permute-start | bytes 983048 | tf_op jit(solution)/shard_map/ppermute | solution.py:39
  86.0 14.8 %collective-permute-start.19 = (bf16[5,8,32,128]{3,2,1,0:T(8,128)(2,1)S(1)}, bf16[5,8,32,128]{3,2,1,0:T(8,128)(2,1)S(1)}, u32[]{:S(2)}, u32[]{:S(2)}) collective-permute-start(bf16[5,8,32,128]{3,2,1,0:T(8,128)(2,1)S(1)} %get-tuple-element.118), channel_id=1, source_target_pairs={{0,3},{1,2},{2,1},{3,0},{4,7},{5,6},{6,5},{7,4},{8,11},{9,10},{10,... | collective-permute-start | bytes 983048 | tf_op jit(solution)/shard_map/ppermute | solution.py:39
  103.7 6.8 %collective-permute-start.20 = (bf16[1,8,32,128]{3,2,1,0:T(8,128)(2,1)S(1)}, bf16[1,8,32,128]{3,2,1,0:T(8,128)(2,1)S(1)}, u32[]{:S(2)}, u32[]{:S(2)}) collective-permute-start(bf16[1,8,32,128]{3,2,1,0:T(8,128)(2,1)S(1)} %get-tuple-element.137), channel_id=1, source_target_pairs={{0,1},{1,0},{2,3},{3,2},{4,5},{5,4},{6,7},{7,6},{8,9},{9,8},{10,11... | collective-permute-start | bytes 196616 | tf_op jit(solution)/shard_map/ppermute | solution.py:39
  104.2 6.3 %collective-permute-start.21 = (bf16[1,8,32,128]{3,2,1,0:T(8,128)(2,1)S(1)}, bf16[1,8,32,128]{3,2,1,0:T(8,128)(2,1)S(1)}, u32[]{:S(2)}, u32[]{:S(2)}) collective-permute-start(bf16[1,8,32,128]{3,2,1,0:T(8,128)(2,1)S(1)} %get-tuple-element.138), channel_id=1, source_target_pairs={{0,2},{1,3},{2,0},{3,1},{4,6},{5,7},{6,4},{7,5},{8,10},{9,11},{10,... | collective-permute-start | bytes 196616 | tf_op jit(solution)/shard_map/ppermute | solution.py:39
  105.7 4.8 %collective-permute-start.22 = (bf16[1,8,32,128]{3,2,1,0:T(8,128)(2,1)S(1)}, bf16[1,8,32,128]{3,2,1,0:T(8,128)(2,1)S(1)}, u32[]{:S(2)}, u32[]{:S(2)}) collective-permute-start(bf16[1,8,32,128]{3,2,1,0:T(8,128)(2,1)S(1)} %get-tuple-element.139), channel_id=1, source_target_pairs={{0,3},{1,2},{2,1},{3,0},{4,7},{5,6},{6,5},{7,4},{8,11},{9,10},{10,... | collective-permute-start | bytes 196616 | tf_op jit(solution)/shard_map/ppermute | solution.py:39

commit v9 on v8

--- a/solution.py
+++ b/solution.py
@@ -379,22 +379,24 @@
     pairs = [
         to_strip_target(pair, chips, step + 1, 0) for step, pair in enumerate(parts[2:])
     ]
-    near, lower, halves[1], parts[:2], pairs, chunks = lax.optimization_barrier(
-        (near, lower, halves[1], parts[:2], pairs, chunks)
-    )
+    near, parts[:2], pairs, chunks, halves = lax.optimization_barrier((near, parts[:2], pairs, chunks, halves))
     upper = shifted(halves[1], "atoms", -offsets[3])
     chunks.append([parts[0], to_strip_target(parts[1], chips, 0, 1)] + pairs)
-    direct = strips_of([*near, lower], False)
-    chunks, direct[0] = lax.optimization_barrier((chunks, direct[0]))
-    chunks = [passed_on(chunk) for chunk in chunks] + [direct]
-    where, upper, chunks = lax.optimization_barrier((where, upper, chunks))
+    chunks = [passed_on(chunk) for chunk in chunks]
+    direct = strips_of(near, False)
+    lower, direct[:2] = lax.optimization_barrier((lower, direct[:2]))
+    lower = strips_of([lower], False)
+    where, upper, lower[:2], chunks, direct = lax.optimization_barrier(
+        (where, upper, lower[:2], chunks, direct)
+    )
+    chunks.append(direct)
     last = strips_of([upper], False)
     where, last[0] = lax.optimization_barrier((where, last[0]))
     local, far, direct = chunks
     strips = list(zip(local, direct, far))
     sizes = [half_blocks, 2, 1]
     density, energy, later = place_early(where, strips, sizes, chips, per_core)
-    return place_late(where, later, direct, last, density, energy, chips, per_core)
+    return place_late(where, later, lower, last, density, energy, chips, per_core)
 
 
 def solution(mesh):

time: 113 us -> 102 us (0.903)
  waiting for transfers between devices: 43.1 us -> 27.9 us
  starting transfers between devices: 24.6 us -> 28 us
    ppermute x14 -> x17, waiting for transfers between devices: 11.1 us -> 0.99 us  [to_strip_target(): return lax.ppermute(value, 'bands', pairs)]
    ppermute x9, waiting for transfers between devices: 32 us -> 26.9 us  [shifted(): return lax.ppermute(value, axis, pairs)]
    ppermute x14 -> x17, starting transfers between devices: 8.58 us -> 12.8 us  [to_strip_target(): return lax.ppermute(value, 'bands', pairs)]
    pallas_call x4 -> x5, Pallas kernels: 23.1 us -> 23.8 us  [tiles(): pl.pallas_call(functools.partial(tiles_kernel, heights, len(arrived), n_s...]
  transfers between devices with their start and end apart: 23 -> 26, of which waited for: 6 -> 5; matrix products, arithmetic and copies ran while one was open for 4% -> 5% of each run, Pallas kernels for 27% -> 34%
where the time goes in v9:
time: 102 us; the launch traced here: 101 us
  Pallas kernels  39.4 us (39%)
  starting transfers between devices  28 us (27%)
  waiting for transfers between devices  27.9 us (27%)
  other arithmetic  4.93 us (5%)
    ppermute x9, waiting for transfers between devices, shifted(): return lax.ppermute(value, axis, pairs)  26.9 us
    pallas_call x5, Pallas kernels, tiles(): pl.pallas_call(functools.partial(tiles_kernel, heights, len(arrived), n_s...  23.8 us
    ppermute x9, starting transfers between devices, shifted(): return lax.ppermute(value, axis, pairs)  15.2 us
    ppermute x17, starting transfers between devices, to_strip_target(): return lax.ppermute(value, 'bands', pairs)  12.8 us
    pallas_call x2, Pallas kernels, pick(): pl.pallas_call(functools.partial(pick_kernel, count, blocks, tile, parts)...  5.58 us
    pallas_call x1, Pallas kernels, place_early(): pl.pallas_call(functools.partial(place_early_kernel, chips, sizes, per_co...  4.71 us
    pallas_call x1, Pallas kernels, keep(): pl.pallas_call(keep_kernel, out_shape=[pltpu.VMEM(own.shape, own.dtype)]...  3.48 us
    add x1, other arithmetic, body(): where = ((side ^ core) * per_core + spot).astype(jnp.int32)  2.65 us
  transfers between devices with their start and end apart: 26, of which 5 were waited for; matrix products, arithmetic and copies ran while one was open for 5% of the time, Pallas kernels for 34%

profile of v9, /device:TPU:0, one launch (start us, length us, event | category | flops | bytes accessed | tf_op | source)
XLA Modules:
  0.0 101.4 jit_solution(10739652418629531503)
XLA Ops:
  1.1 2.6 %collective-permute-start.2 = (s32[8,16]{1,0:T(8,128)}, s32[8,16]{1,0:T(8,128)S(1)}, u32[]{:S(2)}, u32[]{:S(2)}) collective-permute-start(s32[8,16]{1,0:T(8,128)} %param.7), channel_id=1, source_target_pairs={{0,8},{4,12},{8,16},{12,20},{16,24},{20,28},{24,0},{28,4},{1,9},{5... | collective-permute-start | bytes 1544 | tf_op jit(solution)/shard_map/ppermute | solution.py:26
  5.3 3.2 %collective-permute-start = (s32[8,16]{1,0:T(8,128)}, s32[8,16]{1,0:T(8,128)S(1)}, u32[]{:S(2)}, u32[]{:S(2)}) collective-permute-start(s32[8,16]{1,0:T(8,128)} %param.7), channel_id=1, source_target_pairs={{0,28},{4,0},{8,4},{12,8},{16,12},{20,16},{24,20},{28,24},{1,29},{... | collective-permute-start | bytes 1544 | tf_op jit(solution)/shard_map/ppermute | solution.py:26
  10.3 2.0 %collective-permute-done.3.refs_0_ = s32[8,16]{1,0:T(8,128)S(1)} collective-permute-done((s32[8,16]{1,0:T(8,128)}, s32[8,16]{1,0:T(8,128)S(1)}, u32[]{:S(2)}, u32[]{:S(2)}) %collective-permute-start.3) | collective-permute-done | bytes 544 | tf_op jit(solution)/shard_map/ppermute | solution.py:26
  12.3 3.6 %pick_blocks.2 = (bf16[2,128,2048]{2,1,0:T(8,128)(2,1)S(1)}, bf16[2,128,2048]{2,1,0:T(8,128)(2,1)S(1)}, bf16[2,128,2048]{2,1,0:T(8,128)(2,1)}) custom-call(s32[2]{0:T(128)S(1)} %pad_add_fusion.place_ref, s32[8,16]{1,0:T(8,128)S(1)} %collective-permute-done.refs_0_, s32[8,16]{1,0:T(8,128)S(1)} %collective-permute-done.1.refs_1_, ...), custom_call_target="tpu_custom_call" | custom-call | tf_op jit(solution)/shard_map/pick_blocks/pallas_call | solution.py:73
  16.0 2.2 %collective-permute-start.8 = (bf16[2,128,2048]{2,1,0:T(8,128)(2,1)}, bf16[2,128,2048]{2,1,0:T(8,128)(2,1)S(1)}, u32[]{:S(2)}, u32[]{:S(2)}) collective-permute-start(bf16[2,128,2048]{2,1,0:T(8,128)(2,1)} %get-tuple-element.84), channel_id=1, source_target_pairs={{0,24},{4,28},{8,0},{12,4},{16,8},{20,12},{24,16},{28,20},{1,25},{... | collective-permute-start | bytes 3145736 | tf_op jit(solution)/shard_map/ppermute | solution.py:26
  19.3 3.6 %collective-permute-start.7 = (bf16[2,128,2048]{2,1,0:T(8,128)(2,1)S(1)}, bf16[2,128,2048]{2,1,0:T(8,128)(2,1)S(1)}, u32[]{:S(2)}, u32[]{:S(2)}) collective-permute-start(bf16[2,128,2048]{2,1,0:T(8,128)(2,1)S(1)} %get-tuple-element.83), channel_id=1, source_target_pairs={{0,28},{4,0},{8,4},{12,8},{16,12},{20,16},{24,20},{28,24},{1,29},{... | collective-permute-start | bytes 3145736 | tf_op jit(solution)/shard_map/ppermute | solution.py:26
  23.0 3.5 %keep.1 = (bf16[1024,2048]{1,0:T(8,128)(2,1)S(1)}, bf16[1024,2048]{1,0:T(8,128)(2,1)S(1)}) custom-call(bf16[1024,2048]{1,0:T(8,128)(2,1)} %refs_1_.1, bf16[1024,2048]{1,0:T(8,128)(2,1)} %collective-permute-done.4.refs_4_.sib.refs_2_), custom_call_target="tpu_custom_call" | custom-call | tf_op jit(solution)/shard_map/keep/pallas_call | solution.py:98
  26.5 9.8 %tiles.5 = (bf16[8,8,32,128]{3,2,1,0:T(8,128)(2,1)S(1)}, bf16[8,8,32,128]{3,2,1,0:T(8,128)(2,1)S(1)}, bf16[2,8,8,32,128]{4,3,2,1,0:T(8,128)(2,1)S(1)}) custom-call(s32[5]{0:T(128)S(1)} %stack.41.place_ref, bf16[1024,2048]{1,0:T(8,128)(2,1)S(1)} %get-tuple-element.78.refs_0_, bf16[1024,2048]{1,0:T(8,128)(2,1)S(1)} %get-tuple-element.79.refs_1_, ...), custom_call_target="tpu_custom_call" | custom-call | tf_op jit(solution)/shard_map/tiles/pallas_call | solution.py:165
  36.3 1.7 %collective-permute-start.11 = (bf16[2,8,8,32,128]{4,3,2,1,0:T(8,128)(2,1)S(1)}, bf16[2,8,8,32,128]{4,3,2,1,0:T(8,128)(2,1)S(1)}, u32[]{:S(2)}, u32[]{:S(2)}) collective-permute-start(bf16[2,8,8,32,128]{4,3,2,1,0:T(8,128)(2,1)S(1)} %get-tuple-element.96), channel_id=1, source_target_pairs={{0,2},{1,3},{2,0},{3,1},{4,6},{5,7},{6,4},{7,5},{8,10},{9,11},{10,... | collective-permute-start | bytes 3145736 | tf_op jit(solution)/shard_map/ppermute | solution.py:39
  38.0 2.0 %pick_blocks.3 = (bf16[2,64,2048]{2,1,0:T(8,128)(2,1)S(1)}, bf16[2,64,2048]{2,1,0:T(8,128)(2,1)S(1)}) custom-call(s32[2]{0:T(128)S(1)} %pad_add_fusion.place_ref, s32[8,16]{1,0:T(8,128)S(1)} %collective-permute-done.3.refs_0_, bf16[1024,2048]{1,0:T(8,128)(2,1)} %refs_1_.1, bf16[1024,2048]{1,0:T(8,128)(2,1)} %collective-permute-done.4.refs_4_.sib.refs_2_), custom_call_target="tpu_custom_call" | custom-call | tf_op jit(solution)/shard_map/pick_blocks/pallas_call | solution.py:73
  40.0 2.3 %collective-permute-done.8.refs_4_ = bf16[2,128,2048]{2,1,0:T(8,128)(2,1)S(1)} collective-permute-done((bf16[2,128,2048]{2,1,0:T(8,128)(2,1)}, bf16[2,128,2048]{2,1,0:T(8,128)(2,1)S(1)}, u32[]{:S(2)}, u32[]{:S(2)}) %collective-permute-start.8) | collective-permute-done | bytes 1048608 | tf_op jit(solution)/shard_map/ppermute | solution.py:26
  42.3 3.0 %tiles.6 = (bf16[2,8,32,128]{3,2,1,0:T(8,128)(2,1)S(1)}, bf16[2,8,32,128]{3,2,1,0:T(8,128)(2,1)S(1)}, bf16[2,2,8,32,128]{4,3,2,1,0:T(8,128)(2,1)S(1)}) custom-call(s32[5]{0:T(128)S(1)} %stack.41.place_ref, bf16[1024,2048]{1,0:T(8,128)(2,1)S(1)} %get-tuple-element.78.refs_0_, bf16[1024,2048]{1,0:T(8,128)(2,1)S(1)} %get-tuple-element.79.refs_1_, ...), custom_call_target="tpu_custom_call" | custom-call | tf_op jit(solution)/shard_map/tiles/pallas_call | solution.py:165
  45.3 1.6 %collective-permute-start.9 = (bf16[2,2,8,32,128]{4,3,2,1,0:T(8,128)(2,1)S(1)}, bf16[2,2,8,32,128]{4,3,2,1,0:T(8,128)(2,1)S(1)}, u32[]{:S(2)}, u32[]{:S(2)}) collective-permute-start(bf16[2,2,8,32,128]{4,3,2,1,0:T(8,128)(2,1)S(1)} %get-tuple-element.93), channel_id=1, source_target_pairs={{0,2},{1,3},{2,0},{3,1},{4,6},{5,7},{6,4},{7,5},{8,10},{9,11},{10,... | collective-permute-start | bytes 786440 | tf_op jit(solution)/shard_map/ppermute | solution.py:39
  46.9 20.2 %collective-permute-done.7.refs_5_ = bf16[2,128,2048]{2,1,0:T(8,128)(2,1)S(1)} collective-permute-done((bf16[2,128,2048]{2,1,0:T(8,128)(2,1)S(1)}, bf16[2,128,2048]{2,1,0:T(8,128)(2,1)S(1)}, u32[]{:S(2)}, u32[]{:S(2)}) %collective-permute-start.7) | collective-permute-done | bytes 1048608 | tf_op jit(solution)/shard_map/ppermute | solution.py:26
  67.8 5.3 %tiles.7 = (bf16[4,8,32,128]{3,2,1,0:T(8,128)(2,1)S(1)}, bf16[4,8,32,128]{3,2,1,0:T(8,128)(2,1)S(1)}, bf16[4,8,32,128]{3,2,1,0:T(8,128)(2,1)S(1)}, bf16[4,8,32,128]{3,2,1,0:T(8,128)(2,1)S(1)}) custom-call(s32[5]{0:T(128)S(1)} %stack.41.place_ref, bf16[1024,2048]{1,0:T(8,128)(2,1)S(1)} %get-tuple-element.78.refs_0_, ...), custom_call_target="tpu_custom_call" | custom-call | tf_op jit(solution)/shard_map/tiles/pallas_call | solution.py:165
  73.9 2.3 %collective-permute-done.13.refs_4_ = bf16[2,64,2048]{2,1,0:T(8,128)(2,1)S(1)} collective-permute-done((bf16[2,64,2048]{2,1,0:T(8,128)(2,1)S(1)}, bf16[2,64,2048]{2,1,0:T(8,128)(2,1)S(1)}, u32[]{:S(2)}, u32[]{:S(2)}) %collective-permute-start.13) | collective-permute-done | bytes 524320 | tf_op jit(solution)/shard_map/ppermute | solution.py:26
  76.3 1.6 %collective-permute-start.19 = (bf16[4,8,32,128]{3,2,1,0:T(8,128)(2,1)S(1)}, bf16[4,8,32,128]{3,2,1,0:T(8,128)(2,1)S(1)}, u32[]{:S(2)}, u32[]{:S(2)}) collective-permute-start(bf16[4,8,32,128]{3,2,1,0:T(8,128)(2,1)S(1)} %get-tuple-element.115), channel_id=1, source_target_pairs={{0,2},{1,3},{2,0},{3,1},{4,6},{5,7},{6,4},{7,5},{8,10},{9,11},{10,... | collective-permute-start | bytes 786440 | tf_op jit(solution)/shard_map/ppermute | solution.py:39
  78.6 2.9 %tiles.8 = (bf16[1,8,32,128]{3,2,1,0:T(8,128)(2,1)S(1)}, bf16[1,8,32,128]{3,2,1,0:T(8,128)(2,1)S(1)}, bf16[1,8,32,128]{3,2,1,0:T(8,128)(2,1)S(1)}, bf16[1,8,32,128]{3,2,1,0:T(8,128)(2,1)S(1)}) custom-call(s32[5]{0:T(128)S(1)} %stack.41.place_ref, bf16[1024,2048]{1,0:T(8,128)(2,1)S(1)} %get-tuple-element.78.refs_0_, ...), custom_call_target="tpu_custom_call" | custom-call | tf_op jit(solution)/shard_map/tiles/pallas_call | solution.py:165
  82.2 2.7 %fusion.9.where_ref = s32[8,16]{1,0:T(8,128)S(1)} fusion(pred[8,16]{1,0:T(8,128)(4,1)S(1)} %get-tuple-element.151, pred[8,16]{1,0:T(8,128)(4,1)S(1)} %get-tuple-element.150, pred[8,16]{1,0:T(8,128)(4,1)S(1)} %get-tuple-element.149, pred[8,16]{1,0:T(8,128)(4,1)S(1)} %get-tuple-element.148, s32[]{:T(128)} %and.14, s32[]{:T(128)} %get-tuple-element.146, ...), kind=kLoop, calls=%fused_computation.22 | loop fusion | flops 4352 | bytes 1556 | tf_op jit(solution)/shard_map/add | solution.py:373
  84.8 2.1 %collective-permute-start.21 = (bf16[1,8,32,128]{3,2,1,0:T(8,128)(2,1)S(1)}, bf16[1,8,32,128]{3,2,1,0:T(8,128)(2,1)S(1)}, u32[]{:S(2)}, u32[]{:S(2)}) collective-permute-start(bf16[1,8,32,128]{3,2,1,0:T(8,128)(2,1)S(1)} %get-tuple-element.136), channel_id=1, source_target_pairs={{0,2},{1,3},{2,0},{3,1},{4,6},{5,7},{6,4},{7,5},{8,10},{9,11},{10,... | collective-permute-start | bytes 196616 | tf_op jit(solution)/shard_map/ppermute | solution.py:39
  87.9 1.9 %collective-permute-start.22 = (bf16[1,8,32,128]{3,2,1,0:T(8,128)(2,1)S(1)}, bf16[1,8,32,128]{3,2,1,0:T(8,128)(2,1)S(1)}, u32[]{:S(2)}, u32[]{:S(2)}) collective-permute-start(bf16[1,8,32,128]{3,2,1,0:T(8,128)(2,1)S(1)} %get-tuple-element.137), channel_id=1, source_target_pairs={{0,3},{1,2},{2,1},{3,0},{4,7},{5,6},{6,5},{7,4},{8,11},{9,10},{10,... | collective-permute-start | bytes 196616 | tf_op jit(solution)/shard_map/ppermute | solution.py:39
  89.9 2.9 %tiles.9 = (bf16[1,8,32,128]{3,2,1,0:T(8,128)(2,1)S(1)}, bf16[1,8,32,128]{3,2,1,0:T(8,128)(2,1)S(1)}, bf16[1,8,32,128]{3,2,1,0:T(8,128)(2,1)S(1)}, bf16[1,8,32,128]{3,2,1,0:T(8,128)(2,1)S(1)}) custom-call(s32[5]{0:T(128)S(1)} %stack.41.place_ref, bf16[1024,2048]{1,0:T(8,128)(2,1)S(1)} %get-tuple-element.78.refs_0_, ...), custom_call_target="tpu_custom_call" | custom-call | tf_op jit(solution)/shard_map/tiles/pallas_call | solution.py:165
  94.7 4.7 %place_early.1 = (f32[8,16,32,128]{3,2,1,0:T(8,128)}, f32[8,16,32,128]{3,2,1,0:T(8,128)}, s32[129]{0:T(256)S(1)}) custom-call(s32[8,16]{1,0:T(8,128)S(1)} %fusion.9.where_ref, bf16[8,8,32,128]{3,2,1,0:T(8,128)(2,1)S(1)} %get-tuple-element.121.refs_0_, bf16[4,8,32,128]{3,2,1,0:T(8,128)(2,1)S(1)} %get-tuple-element.122.refs_1_, ...), custom_call_target="tpu_custom_call" | custom-call | tf_op jit(solution)/shard_map/place_early/pallas_call | solution.py:225
  99.5 1.8 %place_late.1 = (f32[8,16,32,128]{3,2,1,0:T(8,128)}, f32[8,16,32,128]{3,2,1,0:T(8,128)}) custom-call(s32[8,16]{1,0:T(8,128)S(1)} %fusion.9.where_ref, s32[129]{0:T(256)S(1)} %get-tuple-element.133.later, bf16[1,8,32,128]{3,2,1,0:T(8,128)(2,1)S(1)} %get-tuple-element.134.refs_0_, ...), custom_call_target="tpu_custom_call", output_to_operand_aliasing={{0}: (10, {}), {1}: (11, {})} | custom-call | tf_op jit(solution)/shard_map/place_late/pallas_call | solution.py:292
  (48 shorter events, 10.8 us)
Async XLA Ops:
  0.6 11.7 %collective-permute-start.4 = (bf16[1024,2048]{1,0:T(8,128)(2,1)}, bf16[1024,2048]{1,0:T(8,128)(2,1)}, u32[]{:S(2)}, u32[]{:S(2)}) collective-permute-start(bf16[1024,2048]{1,0:T(8,128)(2,1)} %refs_1_.1), channel_id=1, source_target_pairs={{0,1},{1,0},{2,3},{3,2},{4,5},{5,4},{6,7},{7,6},{8,9},{9,8},{10,11... | collective-permute-start | bytes 12582920 | tf_op jit(solution)/shard_map/ppermute | solution.py:39
  1.1 9.2 %collective-permute-start.2 = (s32[8,16]{1,0:T(8,128)}, s32[8,16]{1,0:T(8,128)S(1)}, u32[]{:S(2)}, u32[]{:S(2)}) collective-permute-start(s32[8,16]{1,0:T(8,128)} %param.7), channel_id=1, source_target_pairs={{0,8},{4,12},{8,16},{12,20},{16,24},{20,28},{24,0},{28,4},{1,9},{5... | collective-permute-start | bytes 1544 | tf_op jit(solution)/shard_map/ppermute | solution.py:26
  3.8 6.6 %collective-permute-start.1 = (s32[8,16]{1,0:T(8,128)}, s32[8,16]{1,0:T(8,128)S(1)}, u32[]{:S(2)}, u32[]{:S(2)}) collective-permute-start(s32[8,16]{1,0:T(8,128)} %param.7), channel_id=1, source_target_pairs={{0,4},{4,8},{8,12},{12,16},{16,20},{20,24},{24,28},{28,0},{1,5},{5... | collective-permute-start | bytes 1544 | tf_op jit(solution)/shard_map/ppermute | solution.py:26
  5.3 5.1 %collective-permute-start = (s32[8,16]{1,0:T(8,128)}, s32[8,16]{1,0:T(8,128)S(1)}, u32[]{:S(2)}, u32[]{:S(2)}) collective-permute-start(s32[8,16]{1,0:T(8,128)} %param.7), channel_id=1, source_target_pairs={{0,28},{4,0},{8,4},{12,8},{16,12},{20,16},{24,20},{28,24},{1,29},{... | collective-permute-start | bytes 1544 | tf_op jit(solution)/shard_map/ppermute | solution.py:26
  16.0 26.4 %collective-permute-start.8 = (bf16[2,128,2048]{2,1,0:T(8,128)(2,1)}, bf16[2,128,2048]{2,1,0:T(8,128)(2,1)S(1)}, u32[]{:S(2)}, u32[]{:S(2)}) collective-permute-start(bf16[2,128,2048]{2,1,0:T(8,128)(2,1)} %get-tuple-element.84), channel_id=1, source_target_pairs={{0,24},{4,28},{8,0},{12,4},{16,8},{20,12},{24,16},{28,20},{1,25},{... | collective-permute-start | bytes 3145736 | tf_op jit(solution)/shard_map/ppermute | solution.py:26
  18.2 8.3 %collective-permute-start.5 = (f32[2,2048]{1,0:T(2,128)S(1)}, f32[2,2048]{1,0:T(2,128)S(1)}, u32[]{:S(2)}, u32[]{:S(2)}) collective-permute-start(f32[2,2048]{1,0:T(2,128)S(1)} %pad_maximum_fusion.refs_2_), channel_id=1, source_target_pairs={{0,1},{1,0},{2,3},{3,2},{4,5},{5,4},{6,7},{7,6},{8,9},{9,8},{10,11... | collective-permute-start | bytes 49160 | tf_op jit(solution)/shard_map/ppermute | solution.py:39
  18.3 48.9 %collective-permute-start.6 = (bf16[2,128,2048]{2,1,0:T(8,128)(2,1)S(1)}, bf16[2,128,2048]{2,1,0:T(8,128)(2,1)S(1)}, u32[]{:S(2)}, u32[]{:S(2)}) collective-permute-start(bf16[2,128,2048]{2,1,0:T(8,128)(2,1)S(1)} %get-tuple-element.76), channel_id=1, source_target_pairs={{0,4},{4,8},{8,12},{12,16},{16,20},{20,24},{24,28},{28,0},{1,5},{5... | collective-permute-start | bytes 3145736 | tf_op jit(solution)/shard_map/ppermute | solution.py:26
  19.3 47.8 %collective-permute-start.7 = (bf16[2,128,2048]{2,1,0:T(8,128)(2,1)S(1)}, bf16[2,128,2048]{2,1,0:T(8,128)(2,1)S(1)}, u32[]{:S(2)}, u32[]{:S(2)}) collective-permute-start(bf16[2,128,2048]{2,1,0:T(8,128)(2,1)S(1)} %get-tuple-element.83), channel_id=1, source_target_pairs={{0,28},{4,0},{8,4},{12,8},{16,12},{20,16},{24,20},{28,24},{1,29},{... | collective-permute-start | bytes 3145736 | tf_op jit(solution)/shard_map/ppermute | solution.py:26
  36.3 30.8 %collective-permute-start.11 = (bf16[2,8,8,32,128]{4,3,2,1,0:T(8,128)(2,1)S(1)}, bf16[2,8,8,32,128]{4,3,2,1,0:T(8,128)(2,1)S(1)}, u32[]{:S(2)}, u32[]{:S(2)}) collective-permute-start(bf16[2,8,8,32,128]{4,3,2,1,0:T(8,128)(2,1)S(1)} %get-tuple-element.96), channel_id=1, source_target_pairs={{0,2},{1,3},{2,0},{3,1},{4,6},{5,7},{6,4},{7,5},{8,10},{9,11},{10,... | collective-permute-start | bytes 3145736 | tf_op jit(solution)/shard_map/ppermute | solution.py:39
  38.0 8.9 %collective-permute-start.10 = (bf16[8,8,32,128]{3,2,1,0:T(8,128)(2,1)S(1)}, bf16[8,8,32,128]{3,2,1,0:T(8,128)(2,1)S(1)}, u32[]{:S(2)}, u32[]{:S(2)}) collective-permute-start(bf16[8,8,32,128]{3,2,1,0:T(8,128)(2,1)S(1)} %get-tuple-element.95), channel_id=1, source_target_pairs={{0,1},{1,0},{2,3},{3,2},{4,5},{5,4},{6,7},{7,6},{8,9},{9,8},{10,11... | collective-permute-start | bytes 1572872 | tf_op jit(solution)/shard_map/ppermute | solution.py:39
  45.3 21.8 %collective-permute-start.9 = (bf16[2,2,8,32,128]{4,3,2,1,0:T(8,128)(2,1)S(1)}, bf16[2,2,8,32,128]{4,3,2,1,0:T(8,128)(2,1)S(1)}, u32[]{:S(2)}, u32[]{:S(2)}) collective-permute-start(bf16[2,2,8,32,128]{4,3,2,1,0:T(8,128)(2,1)S(1)} %get-tuple-element.93), channel_id=1, source_target_pairs={{0,2},{1,3},{2,0},{3,1},{4,6},{5,7},{6,4},{7,5},{8,10},{9,11},{10,... | collective-permute-start | bytes 786440 | tf_op jit(solution)/shard_map/ppermute | solution.py:39
  46.9 29.4 %collective-permute-start.13 = (bf16[2,64,2048]{2,1,0:T(8,128)(2,1)S(1)}, bf16[2,64,2048]{2,1,0:T(8,128)(2,1)S(1)}, u32[]{:S(2)}, u32[]{:S(2)}) collective-permute-start(bf16[2,64,2048]{2,1,0:T(8,128)(2,1)S(1)} %get-tuple-element.97), channel_id=1, source_target_pairs={{0,8},{4,12},{8,16},{12,20},{16,24},{20,28},{24,0},{28,4},{1,9},{5... | collective-permute-start | bytes 1572872 | tf_op jit(solution)/shard_map/ppermute | solution.py:26
  67.1 6.7 %collective-permute-start.17 = (bf16[2,8,32,128]{3,2,1,0:T(8,128)(2,1)S(1)}, bf16[2,8,32,128]{3,2,1,0:T(8,128)(2,1)S(1)}, u32[]{:S(2)}, u32[]{:S(2)}) collective-permute-start(bf16[2,8,32,128]{3,2,1,0:T(8,128)(2,1)S(1)} %get-tuple-element.111), channel_id=1, source_target_pairs={{0,1},{1,0},{2,3},{3,2},{4,5},{5,4},{6,7},{7,6},{8,9},{9,8},{10,11... | collective-permute-start | bytes 393224 | tf_op jit(solution)/shard_map/ppermute | solution.py:39
  67.2 22.6 %collective-permute-start.12 = (bf16[2,64,2048]{2,1,0:T(8,128)(2,1)S(1)}, bf16[2,64,2048]{2,1,0:T(8,128)(2,1)S(1)}, u32[]{:S(2)}, u32[]{:S(2)}) collective-permute-start(bf16[2,64,2048]{2,1,0:T(8,128)(2,1)S(1)} %get-tuple-element.99), channel_id=1, source_target_pairs={{0,8},{4,12},{8,16},{12,20},{16,24},{20,28},{24,0},{28,4},{1,9},{5... | collective-permute-start | bytes 1572872 | tf_op jit(solution)/shard_map/ppermute | solution.py:26
  73.3 16.6 %collective-permute-start.16 = (bf16[8,8,32,128]{3,2,1,0:T(8,128)(2,1)S(1)}, bf16[8,8,32,128]{3,2,1,0:T(8,128)(2,1)S(1)}, u32[]{:S(2)}, u32[]{:S(2)}) collective-permute-start(bf16[8,8,32,128]{3,2,1,0:T(8,128)(2,1)S(1)} %get-tuple-element.152), channel_id=1, source_target_pairs={{0,1},{1,0},{2,3},{3,2},{4,5},{5,4},{6,7},{7,6},{8,9},{9,8},{10,11... | collective-permute-start | bytes 1572872 | tf_op jit(solution)/shard_map/ppermute | solution.py:39
  73.9 7.7 %collective-permute-start.18 = (bf16[2,8,32,128]{3,2,1,0:T(8,128)(2,1)S(1)}, bf16[2,8,32,128]{3,2,1,0:T(8,128)(2,1)S(1)}, u32[]{:S(2)}, u32[]{:S(2)}) collective-permute-start(bf16[2,8,32,128]{3,2,1,0:T(8,128)(2,1)S(1)} %get-tuple-element.154), channel_id=1, source_target_pairs={{0,1},{1,0},{2,3},{3,2},{4,5},{5,4},{6,7},{7,6},{8,9},{9,8},{10,11... | collective-permute-start | bytes 393224 | tf_op jit(solution)/shard_map/ppermute | solution.py:39
  76.3 8.5 %collective-permute-start.19 = (bf16[4,8,32,128]{3,2,1,0:T(8,128)(2,1)S(1)}, bf16[4,8,32,128]{3,2,1,0:T(8,128)(2,1)S(1)}, u32[]{:S(2)}, u32[]{:S(2)}) collective-permute-start(bf16[4,8,32,128]{3,2,1,0:T(8,128)(2,1)S(1)} %get-tuple-element.115), channel_id=1, source_target_pairs={{0,2},{1,3},{2,0},{3,1},{4,6},{5,7},{6,4},{7,5},{8,10},{9,11},{10,... | collective-permute-start | bytes 786440 | tf_op jit(solution)/shard_map/ppermute | solution.py:39
  77.9 10.1 %collective-permute-start.20 = (bf16[4,8,32,128]{3,2,1,0:T(8,128)(2,1)S(1)}, bf16[4,8,32,128]{3,2,1,0:T(8,128)(2,1)S(1)}, u32[]{:S(2)}, u32[]{:S(2)}) collective-permute-start(bf16[4,8,32,128]{3,2,1,0:T(8,128)(2,1)S(1)} %get-tuple-element.116), channel_id=1, source_target_pairs={{0,3},{1,2},{2,1},{3,0},{4,7},{5,6},{6,5},{7,4},{8,11},{9,10},{10,... | collective-permute-start | bytes 786440 | tf_op jit(solution)/shard_map/ppermute | solution.py:39
  81.6 8.3 %collective-permute-start.15 = (bf16[1,8,32,128]{3,2,1,0:T(8,128)(2,1)S(1)}, bf16[1,8,32,128]{3,2,1,0:T(8,128)(2,1)S(1)}, u32[]{:S(2)}, u32[]{:S(2)}) collective-permute-start(bf16[1,8,32,128]{3,2,1,0:T(8,128)(2,1)S(1)} %get-tuple-element.106), channel_id=1, source_target_pairs={{0,1},{1,0},{2,3},{3,2},{4,5},{5,4},{6,7},{7,6},{8,9},{9,8},{10,11... | collective-permute-start | bytes 196616 | tf_op jit(solution)/shard_map/ppermute | solution.py:39
  84.8 14.6 %collective-permute-start.21 = (bf16[1,8,32,128]{3,2,1,0:T(8,128)(2,1)S(1)}, bf16[1,8,32,128]{3,2,1,0:T(8,128)(2,1)S(1)}, u32[]{:S(2)}, u32[]{:S(2)}) collective-permute-start(bf16[1,8,32,128]{3,2,1,0:T(8,128)(2,1)S(1)} %get-tuple-element.136), channel_id=1, source_target_pairs={{0,2},{1,3},{2,0},{3,1},{4,6},{5,7},{6,4},{7,5},{8,10},{9,11},{10,... | collective-permute-start | bytes 196616 | tf_op jit(solution)/shard_map/ppermute | solution.py:39
  87.9 11.5 %collective-permute-start.22 = (bf16[1,8,32,128]{3,2,1,0:T(8,128)(2,1)S(1)}, bf16[1,8,32,128]{3,2,1,0:T(8,128)(2,1)S(1)}, u32[]{:S(2)}, u32[]{:S(2)}) collective-permute-start(bf16[1,8,32,128]{3,2,1,0:T(8,128)(2,1)S(1)} %get-tuple-element.137), channel_id=1, source_target_pairs={{0,3},{1,2},{2,1},{3,0},{4,7},{5,6},{6,5},{7,4},{8,11},{9,10},{10,... | collective-permute-start | bytes 196616 | tf_op jit(solution)/shard_map/ppermute | solution.py:39
  92.8 6.7 %collective-permute-start.23 = (bf16[1,8,32,128]{3,2,1,0:T(8,128)(2,1)S(1)}, bf16[1,8,32,128]{3,2,1,0:T(8,128)(2,1)S(1)}, u32[]{:S(2)}, u32[]{:S(2)}) collective-permute-start(bf16[1,8,32,128]{3,2,1,0:T(8,128)(2,1)S(1)} %get-tuple-element.139), channel_id=1, source_target_pairs={{0,1},{1,0},{2,3},{3,2},{4,5},{5,4},{6,7},{7,6},{8,9},{9,8},{10,11... | collective-permute-start | bytes 196616 | tf_op jit(solution)/shard_map/ppermute | solution.py:39
  92.8 6.6 %collective-permute-start.24 = (bf16[1,8,32,128]{3,2,1,0:T(8,128)(2,1)S(1)}, bf16[1,8,32,128]{3,2,1,0:T(8,128)(2,1)S(1)}, u32[]{:S(2)}, u32[]{:S(2)}) collective-permute-start(bf16[1,8,32,128]{3,2,1,0:T(8,128)(2,1)S(1)} %get-tuple-element.140), channel_id=1, source_target_pairs={{0,2},{1,3},{2,0},{3,1},{4,6},{5,7},{6,4},{7,5},{8,10},{9,11},{10,... | collective-permute-start | bytes 196616 | tf_op jit(solution)/shard_map/ppermute | solution.py:39
  93.5 6.0 %collective-permute-start.25 = (bf16[1,8,32,128]{3,2,1,0:T(8,128)(2,1)S(1)}, bf16[1,8,32,128]{3,2,1,0:T(8,128)(2,1)S(1)}, u32[]{:S(2)}, u32[]{:S(2)}) collective-permute-start(bf16[1,8,32,128]{3,2,1,0:T(8,128)(2,1)S(1)} %get-tuple-element.141), channel_id=1, source_target_pairs={{0,3},{1,2},{2,1},{3,0},{4,7},{5,6},{6,5},{7,4},{8,11},{9,10},{10,... | collective-permute-start | bytes 196616 | tf_op jit(solution)/shard_map/ppermute | solution.py:39
  (3 other events, 19.3 us)

commit v10 on v9

--- a/solution.py
+++ b/solution.py
@@ -189,32 +189,52 @@
 def place_early_kernel(chips, sizes, per_core, where_ref, *refs):
     n_chunks = len(sizes)
     ins = refs[: 2 * chips * n_chunks]
-    density, energy, later, pool = refs[2 * chips * n_chunks :]
-    for other_core in range(2):
-        first = other_core * per_core
-        for chunk in range(n_chunks):
-            for unit in range(2 * sizes[chunk]):
-                pool[first + unit // 2, unit % 2] = strip_sum(
-                    ins, chips, n_chunks, other_core, chunk, unit, 0
-                )
-            first += sizes[chunk]
-    i = pl.program_id(0)
-    slots = density.shape[1]
-
-    @pl.when(i == 0)
-    def _():
-        later[0] = 0
-
-    for slot in range(slots):
-        where = where_ref[i, slot]
-        density[0, slot] = pool[where, 0]
-        energy[0, slot] = pool[where, 1]
-
-        @pl.when(lax.rem(where, per_core) == per_core - 1)
+    density, energy, later, pool, tiles_out, sems = refs[2 * chips * n_chunks :]
+    blocks, slots = density.shape[:2]
+    later[0] = 0
+
+    def copies(i, buffer):
+        return [
+            pltpu.make_async_copy(
+                tiles_out.at[buffer, kind], out.at[i], sems.at[buffer, kind]
+            )
+            for kind, out in enumerate((density, energy))
+        ]
+
+    @pl.loop(0, blocks)
+    def _(i):
+        buffer = lax.rem(i, 2)
+        for other_core in range(2):
+            first = other_core * per_core
+            for chunk in range(n_chunks):
+                for unit in range(2 * sizes[chunk]):
+                    pool[first + unit // 2, unit % 2] = strip_sum(
+                        ins, chips, n_chunks, other_core, chunk, unit, i
+                    )
+                first += sizes[chunk]
+
+        @pl.when(i >= 2)
         def _():
-            count = later[0] + 1
-            later[count] = i * slots + slot
-            later[0] = count
+            for copy in copies(i - 2, buffer):
+                copy.wait()
+
+        for slot in range(slots):
+            where = where_ref[i, slot]
+            for kind in range(2):
+                tiles_out[buffer, kind, slot] = pool[where, kind]
+
+            @pl.when(lax.rem(where, per_core) == per_core - 1)
+            def _():
+                count = later[0] + 1
+                later[count] = i * slots + slot
+                later[0] = count
+
+        for copy in copies(i, buffer):
+            copy.start()
+
+    for i in range(max(blocks - 2, 0), blocks):
+        for copy in copies(i, i % 2):
+            copy.wait()
 
 
 def place_early(where, strips, sizes, chips, per_core):
@@ -222,25 +242,17 @@
     slots = where.shape[1]
     out = jax.ShapeDtypeStruct((blocks, slots, strip, tile), jnp.float32)
     flat = [value for group in strips for value in group]
+    smem = pl.BlockSpec(memory_space=pltpu.SMEM)
     return pl.pallas_call(
         functools.partial(place_early_kernel, chips, sizes, per_core),
         out_shape=[out, out, jax.ShapeDtypeStruct((blocks * slots + 1,), jnp.int32)],
-        grid_spec=pltpu.PrefetchScalarGridSpec(
-            num_scalar_prefetch=1,
-            grid=(blocks,),
-            in_specs=[
-                pl.BlockSpec(
-                    (value.shape[0], 1, strip, tile), lambda i, where: (0, i, 0, 0)
-                )
-                for value in flat
-            ],
-            out_specs=[
-                pl.BlockSpec((1, slots, strip, tile), lambda i, where: (i, 0, 0, 0))
-            ]
-            * 2
-            + [pl.BlockSpec(memory_space=pltpu.SMEM)],
-            scratch_shapes=[pltpu.VMEM((2 * per_core, 2, strip, tile), jnp.float32)],
-        ),
+        in_specs=[smem] + [pl.BlockSpec(memory_space=pltpu.VMEM)] * len(flat),
+        out_specs=[pl.BlockSpec(memory_space=pl.ANY)] * 2 + [smem],
+        scratch_shapes=[
+            pltpu.VMEM((2 * per_core, 2, strip, tile), jnp.float32),
+            pltpu.VMEM((2, 2, slots, strip, tile), jnp.float32),
+            pltpu.SemaphoreType.DMA((2, 2)),
+        ],
         name="place_early",
         compiler_params=pltpu.CompilerParams(vmem_limit_bytes=VMEM_LIMIT),
         cost_estimate=SOON,
@@ -379,19 +391,26 @@
     pairs = [
         to_strip_target(pair, chips, step + 1, 0) for step, pair in enumerate(parts[2:])
     ]
-    near, parts[:2], pairs, chunks, halves = lax.optimization_barrier((near, parts[:2], pairs, chunks, halves))
+    near, where, parts[:2], pairs, chunks, halves = lax.optimization_barrier(
+        (near, where, parts[:2], pairs, chunks, halves)
+    )
     upper = shifted(halves[1], "atoms", -offsets[3])
     chunks.append([parts[0], to_strip_target(parts[1], chips, 0, 1)] + pairs)
     chunks = [passed_on(chunk) for chunk in chunks]
     direct = strips_of(near, False)
-    lower, direct[:2] = lax.optimization_barrier((lower, direct[:2]))
-    lower = strips_of([lower], False)
-    where, upper, lower[:2], chunks, direct = lax.optimization_barrier(
-        (where, upper, lower[:2], chunks, direct)
+    lower, direct[:2], chunks = lax.optimization_barrier((lower, direct[:2], chunks))
+    lower = list(tiles(place, own, kept_sib, [lower], weights, n_bands, tile, False))
+    lower_sib = lower[1]
+    for index in range(2, n_bands):
+        lower[index] = to_strip_target(lower[index], chips, index // 2, index % 2)
+    where, upper, lower[0], direct = lax.optimization_barrier(
+        (where, upper, lower[0], direct)
     )
     chunks.append(direct)
     last = strips_of([upper], False)
     where, last[0] = lax.optimization_barrier((where, last[0]))
+    lower[1] = to_strip_target(lower_sib, chips, 0, 1)
+    where, lower = lax.optimization_barrier((where, lower))
     local, far, direct = chunks
     strips = list(zip(local, direct, far))
     sizes = [half_blocks, 2, 1]

time: 102 us -> 101 us (level)
  starting transfers between devices: 28 us -> 26.2 us
    ppermute x17, waiting for transfers between devices: 0.99 us -> 6.09 us  [to_strip_target(): return lax.ppermute(value, 'bands', pairs)]
    ppermute x9, waiting for transfers between devices: 26.9 us -> 21.9 us  [shifted(): return lax.ppermute(value, axis, pairs)]
    ppermute x17, starting transfers between devices: 12.8 us -> 11 us  [to_strip_target(): return lax.ppermute(value, 'bands', pairs)]
  transfers between devices with their start and end apart: 26 -> 26, of which waited for: 5 -> 6; matrix products, arithmetic and copies ran while one was open for 5% -> 5% of each run, Pallas kernels for 34% -> 34%
where the time goes in v10:
time: 101 us; the launch traced here: 100 us
  Pallas kernels  39.7 us (39%)
  waiting for transfers between devices  27.9 us (28%)
  starting transfers between devices  26.2 us (26%)
  other arithmetic  4.92 us (5%)
  between operations  1.01 us (1%)
    pallas_call x5, Pallas kernels, tiles(): pl.pallas_call(functools.partial(tiles_kernel, heights, len(arrived), n_s...  23.8 us
    ppermute x9, waiting for transfers between devices, shifted(): return lax.ppermute(value, axis, pairs)  21.9 us
    ppermute x9, starting transfers between devices, shifted(): return lax.ppermute(value, axis, pairs)  15.2 us
    ppermute x17, starting transfers between devices, to_strip_target(): return lax.ppermute(value, 'bands', pairs)  11 us
    ppermute x17, waiting for transfers between devices, to_strip_target(): return lax.ppermute(value, 'bands', pairs)  6.09 us
    pallas_call x2, Pallas kernels, pick(): pl.pallas_call(functools.partial(pick_kernel, count, blocks, tile, parts)...  5.59 us
    pallas_call x1, Pallas kernels, place_early(): pl.pallas_call(functools.partial(place_early_kernel, chips, sizes, per_co...  4.89 us
    pallas_call x1, Pallas kernels, keep(): pl.pallas_call(keep_kernel, out_shape=[pltpu.VMEM(own.shape, own.dtype)]...  3.48 us
  transfers between devices with their start and end apart: 26, of which 6 were waited for; matrix products, arithmetic and copies ran while one was open for 5% of the time, Pallas kernels for 34%

profile of v10, /device:TPU:0, one launch (start us, length us, event | category | flops | bytes accessed | tf_op | source)
XLA Modules:
  0.0 100.0 jit_solution(7661932951134818903)
XLA Ops:
  1.1 2.6 %collective-permute-start.2 = (s32[8,16]{1,0:T(8,128)}, s32[8,16]{1,0:T(8,128)S(1)}, u32[]{:S(2)}, u32[]{:S(2)}) collective-permute-start(s32[8,16]{1,0:T(8,128)} %param.7), channel_id=1, source_target_pairs={{0,8},{4,12},{8,16},{12,20},{16,24},{20,28},{24,0},{28,4},{1,9},{5... | collective-permute-start | bytes 1544 | tf_op jit(solution)/shard_map/ppermute | solution.py:26
  5.3 3.2 %collective-permute-start = (s32[8,16]{1,0:T(8,128)}, s32[8,16]{1,0:T(8,128)S(1)}, u32[]{:S(2)}, u32[]{:S(2)}) collective-permute-start(s32[8,16]{1,0:T(8,128)} %param.7), channel_id=1, source_target_pairs={{0,28},{4,0},{8,4},{12,8},{16,12},{20,16},{24,20},{28,24},{1,29},{... | collective-permute-start | bytes 1544 | tf_op jit(solution)/shard_map/ppermute | solution.py:26
  10.3 2.0 %collective-permute-done.3.refs_0_ = s32[8,16]{1,0:T(8,128)S(1)} collective-permute-done((s32[8,16]{1,0:T(8,128)}, s32[8,16]{1,0:T(8,128)S(1)}, u32[]{:S(2)}, u32[]{:S(2)}) %collective-permute-start.3) | collective-permute-done | bytes 544 | tf_op jit(solution)/shard_map/ppermute | solution.py:26
  12.3 3.6 %pick_blocks.2 = (bf16[2,128,2048]{2,1,0:T(8,128)(2,1)S(1)}, bf16[2,128,2048]{2,1,0:T(8,128)(2,1)S(1)}, bf16[2,128,2048]{2,1,0:T(8,128)(2,1)}) custom-call(s32[2]{0:T(128)S(1)} %pad_add_fusion.place_ref, s32[8,16]{1,0:T(8,128)S(1)} %collective-permute-done.refs_0_, s32[8,16]{1,0:T(8,128)S(1)} %collective-permute-done.1.refs_1_, ...), custom_call_target="tpu_custom_call" | custom-call | tf_op jit(solution)/shard_map/pick_blocks/pallas_call | solution.py:73
  16.0 2.2 %collective-permute-start.8 = (bf16[2,128,2048]{2,1,0:T(8,128)(2,1)}, bf16[2,128,2048]{2,1,0:T(8,128)(2,1)S(1)}, u32[]{:S(2)}, u32[]{:S(2)}) collective-permute-start(bf16[2,128,2048]{2,1,0:T(8,128)(2,1)} %get-tuple-element.89), channel_id=1, source_target_pairs={{0,24},{4,28},{8,0},{12,4},{16,8},{20,12},{24,16},{28,20},{1,25},{... | collective-permute-start | bytes 3145736 | tf_op jit(solution)/shard_map/ppermute | solution.py:26
  19.3 3.6 %collective-permute-start.6 = (bf16[2,128,2048]{2,1,0:T(8,128)(2,1)S(1)}, bf16[2,128,2048]{2,1,0:T(8,128)(2,1)S(1)}, u32[]{:S(2)}, u32[]{:S(2)}) collective-permute-start(bf16[2,128,2048]{2,1,0:T(8,128)(2,1)S(1)} %get-tuple-element.82), channel_id=1, source_target_pairs={{0,28},{4,0},{8,4},{12,8},{16,12},{20,16},{24,20},{28,24},{1,29},{... | collective-permute-start | bytes 3145736 | tf_op jit(solution)/shard_map/ppermute | solution.py:26
  22.9 3.5 %keep.1 = (bf16[1024,2048]{1,0:T(8,128)(2,1)S(1)}, bf16[1024,2048]{1,0:T(8,128)(2,1)S(1)}) custom-call(bf16[1024,2048]{1,0:T(8,128)(2,1)} %refs_1_.1, bf16[1024,2048]{1,0:T(8,128)(2,1)} %collective-permute-done.4.refs_4_.sib.refs_2_), custom_call_target="tpu_custom_call" | custom-call | tf_op jit(solution)/shard_map/keep/pallas_call | solution.py:98
  26.4 9.8 %tiles.5 = (bf16[8,8,32,128]{3,2,1,0:T(8,128)(2,1)S(1)}, bf16[8,8,32,128]{3,2,1,0:T(8,128)(2,1)S(1)}, bf16[2,8,8,32,128]{4,3,2,1,0:T(8,128)(2,1)S(1)}) custom-call(s32[5]{0:T(128)S(1)} %stack.44.place_ref, bf16[1024,2048]{1,0:T(8,128)(2,1)S(1)} %get-tuple-element.84.refs_0_, bf16[1024,2048]{1,0:T(8,128)(2,1)S(1)} %get-tuple-element.85.refs_1_, ...), custom_call_target="tpu_custom_call" | custom-call | tf_op jit(solution)/shard_map/tiles/pallas_call | solution.py:165
  36.2 1.7 %collective-permute-start.11 = (bf16[2,8,8,32,128]{4,3,2,1,0:T(8,128)(2,1)S(1)}, bf16[2,8,8,32,128]{4,3,2,1,0:T(8,128)(2,1)S(1)}, u32[]{:S(2)}, u32[]{:S(2)}) collective-permute-start(bf16[2,8,8,32,128]{4,3,2,1,0:T(8,128)(2,1)S(1)} %get-tuple-element.101), channel_id=1, source_target_pairs={{0,2},{1,3},{2,0},{3,1},{4,6},{5,7},{6,4},{7,5},{8,10},{9,11},{10,... | collective-permute-start | bytes 3145736 | tf_op jit(solution)/shard_map/ppermute | solution.py:39
  38.0 2.0 %pick_blocks.3 = (bf16[2,64,2048]{2,1,0:T(8,128)(2,1)S(1)}, bf16[2,64,2048]{2,1,0:T(8,128)(2,1)S(1)}) custom-call(s32[2]{0:T(128)S(1)} %pad_add_fusion.place_ref, s32[8,16]{1,0:T(8,128)S(1)} %collective-permute-done.3.refs_0_, bf16[1024,2048]{1,0:T(8,128)(2,1)} %refs_1_.1, bf16[1024,2048]{1,0:T(8,128)(2,1)} %collective-permute-done.4.refs_4_.sib.refs_2_), custom_call_target="tpu_custom_call" | custom-call | tf_op jit(solution)/shard_map/pick_blocks/pallas_call | solution.py:73
  39.9 2.4 %collective-permute-done.8.refs_4_ = bf16[2,128,2048]{2,1,0:T(8,128)(2,1)S(1)} collective-permute-done((bf16[2,128,2048]{2,1,0:T(8,128)(2,1)}, bf16[2,128,2048]{2,1,0:T(8,128)(2,1)S(1)}, u32[]{:S(2)}, u32[]{:S(2)}) %collective-permute-start.8) | collective-permute-done | bytes 1048608 | tf_op jit(solution)/shard_map/ppermute | solution.py:26
  42.3 3.0 %tiles.6 = (bf16[2,8,32,128]{3,2,1,0:T(8,128)(2,1)S(1)}, bf16[2,8,32,128]{3,2,1,0:T(8,128)(2,1)S(1)}, bf16[2,2,8,32,128]{4,3,2,1,0:T(8,128)(2,1)S(1)}) custom-call(s32[5]{0:T(128)S(1)} %stack.44.place_ref, bf16[1024,2048]{1,0:T(8,128)(2,1)S(1)} %get-tuple-element.84.refs_0_, bf16[1024,2048]{1,0:T(8,128)(2,1)S(1)} %get-tuple-element.85.refs_1_, ...), custom_call_target="tpu_custom_call" | custom-call | tf_op jit(solution)/shard_map/tiles/pallas_call | solution.py:165
  45.3 1.6 %collective-permute-start.9 = (bf16[2,2,8,32,128]{4,3,2,1,0:T(8,128)(2,1)S(1)}, bf16[2,2,8,32,128]{4,3,2,1,0:T(8,128)(2,1)S(1)}, u32[]{:S(2)}, u32[]{:S(2)}) collective-permute-start(bf16[2,2,8,32,128]{4,3,2,1,0:T(8,128)(2,1)S(1)} %get-tuple-element.98), channel_id=1, source_target_pairs={{0,2},{1,3},{2,0},{3,1},{4,6},{5,7},{6,4},{7,5},{8,10},{9,11},{10,... | collective-permute-start | bytes 786440 | tf_op jit(solution)/shard_map/ppermute | solution.py:39
  47.7 2.7 %fusion.9.where_ref = s32[8,16]{1,0:T(8,128)S(1)} fusion(pred[8,16]{1,0:T(8,128)(4,1)S(1)} %get-tuple-element.161, pred[8,16]{1,0:T(8,128)(4,1)S(1)} %get-tuple-element.160, pred[8,16]{1,0:T(8,128)(4,1)S(1)} %get-tuple-element.159, pred[8,16]{1,0:T(8,128)(4,1)S(1)} %get-tuple-element.158, s32[]{:T(128)} %and.14, s32[]{:T(128)} %get-tuple-element.156, ...), kind=kLoop, calls=%fused_computation.22 | loop fusion | flops 4352 | bytes 1556 | tf_op jit(solution)/shard_map/add | solution.py:385
  50.4 16.7 %collective-permute-done.6.refs_5_ = bf16[2,128,2048]{2,1,0:T(8,128)(2,1)S(1)} collective-permute-done((bf16[2,128,2048]{2,1,0:T(8,128)(2,1)S(1)}, bf16[2,128,2048]{2,1,0:T(8,128)(2,1)S(1)}, u32[]{:S(2)}, u32[]{:S(2)}) %collective-permute-start.6) | collective-permute-done | bytes 1048608 | tf_op jit(solution)/shard_map/ppermute | solution.py:26
  68.5 5.3 %tiles.7 = (bf16[4,8,32,128]{3,2,1,0:T(8,128)(2,1)S(1)}, bf16[4,8,32,128]{3,2,1,0:T(8,128)(2,1)S(1)}, bf16[4,8,32,128]{3,2,1,0:T(8,128)(2,1)S(1)}, bf16[4,8,32,128]{3,2,1,0:T(8,128)(2,1)S(1)}) custom-call(s32[5]{0:T(128)S(1)} %stack.44.place_ref, bf16[1024,2048]{1,0:T(8,128)(2,1)S(1)} %get-tuple-element.84.refs_0_, ...), custom_call_target="tpu_custom_call" | custom-call | tf_op jit(solution)/shard_map/tiles/pallas_call | solution.py:165
  73.9 1.6 %collective-permute-start.18 = (bf16[4,8,32,128]{3,2,1,0:T(8,128)(2,1)S(1)}, bf16[4,8,32,128]{3,2,1,0:T(8,128)(2,1)S(1)}, u32[]{:S(2)}, u32[]{:S(2)}) collective-permute-start(bf16[4,8,32,128]{3,2,1,0:T(8,128)(2,1)S(1)} %get-tuple-element.120), channel_id=1, source_target_pairs={{0,2},{1,3},{2,0},{3,1},{4,6},{5,7},{6,4},{7,5},{8,10},{9,11},{10,... | collective-permute-start | bytes 786440 | tf_op jit(solution)/shard_map/ppermute | solution.py:39
  76.3 2.9 %tiles.8 = (bf16[1,8,32,128]{3,2,1,0:T(8,128)(2,1)S(1)}, bf16[1,8,32,128]{3,2,1,0:T(8,128)(2,1)S(1)}, bf16[1,8,32,128]{3,2,1,0:T(8,128)(2,1)S(1)}, bf16[1,8,32,128]{3,2,1,0:T(8,128)(2,1)S(1)}) custom-call(s32[5]{0:T(128)S(1)} %stack.44.place_ref, bf16[1024,2048]{1,0:T(8,128)(2,1)S(1)} %get-tuple-element.84.refs_0_, ...), custom_call_target="tpu_custom_call" | custom-call | tf_op jit(solution)/shard_map/tiles/pallas_call | solution.py:165
  79.2 1.7 %collective-permute-start.20 = (bf16[1,8,32,128]{3,2,1,0:T(8,128)(2,1)S(1)}, bf16[1,8,32,128]{3,2,1,0:T(8,128)(2,1)S(1)}, u32[]{:S(2)}, u32[]{:S(2)}) collective-permute-start(bf16[1,8,32,128]{3,2,1,0:T(8,128)(2,1)S(1)} %get-tuple-element.127), channel_id=1, source_target_pairs={{0,1},{1,0},{2,3},{3,2},{4,5},{5,4},{6,7},{7,6},{8,9},{9,8},{10,11... | collective-permute-start | bytes 196616 | tf_op jit(solution)/shard_map/ppermute | solution.py:39
  81.4 1.7 %collective-permute-done.18.refs_7_ = bf16[4,8,32,128]{3,2,1,0:T(8,128)(2,1)S(1)} collective-permute-done((bf16[4,8,32,128]{3,2,1,0:T(8,128)(2,1)S(1)}, bf16[4,8,32,128]{3,2,1,0:T(8,128)(2,1)S(1)}, u32[]{:S(2)}, u32[]{:S(2)}) %collective-permute-start.18) | collective-permute-done | bytes 262176 | tf_op jit(solution)/shard_map/ppermute | solution.py:39
  83.4 4.4 %collective-permute-done.19.refs_10_ = bf16[4,8,32,128]{3,2,1,0:T(8,128)(2,1)S(1)} collective-permute-done((bf16[4,8,32,128]{3,2,1,0:T(8,128)(2,1)S(1)}, bf16[4,8,32,128]{3,2,1,0:T(8,128)(2,1)S(1)}, u32[]{:S(2)}, u32[]{:S(2)}) %collective-permute-start.19) | collective-permute-done | bytes 262176 | tf_op jit(solution)/shard_map/ppermute | solution.py:39
  87.8 2.9 %tiles.9 = (bf16[1,8,32,128]{3,2,1,0:T(8,128)(2,1)S(1)}, bf16[1,8,32,128]{3,2,1,0:T(8,128)(2,1)S(1)}, bf16[1,8,32,128]{3,2,1,0:T(8,128)(2,1)S(1)}, bf16[1,8,32,128]{3,2,1,0:T(8,128)(2,1)S(1)}) custom-call(s32[5]{0:T(128)S(1)} %stack.44.place_ref, bf16[1024,2048]{1,0:T(8,128)(2,1)S(1)} %get-tuple-element.84.refs_0_, ...), custom_call_target="tpu_custom_call" | custom-call | tf_op jit(solution)/shard_map/tiles/pallas_call | solution.py:165
  93.0 4.9 %place_early.1 = (f32[8,16,32,128]{3,2,1,0:T(8,128)}, f32[8,16,32,128]{3,2,1,0:T(8,128)}, s32[129]{0:T(256)S(1)}) custom-call(s32[8,16]{1,0:T(8,128)S(1)} %fusion.9.where_ref, bf16[8,8,32,128]{3,2,1,0:T(8,128)(2,1)S(1)} %get-tuple-element.131.refs_0_, bf16[4,8,32,128]{3,2,1,0:T(8,128)(2,1)S(1)} %get-tuple-element.132.refs_1_, ...), custom_call_target="tpu_custom_call" | custom-call | tf_op jit(solution)/shard_map/place_early/pallas_call | solution.py:246
  98.0 1.9 %place_late.1 = (f32[8,16,32,128]{3,2,1,0:T(8,128)}, f32[8,16,32,128]{3,2,1,0:T(8,128)}) custom-call(s32[8,16]{1,0:T(8,128)S(1)} %fusion.9.where_ref, s32[129]{0:T(256)S(1)} %get-tuple-element.143.later, bf16[1,8,32,128]{3,2,1,0:T(8,128)(2,1)S(1)} %get-tuple-element.144.refs_0_, ...), custom_call_target="tpu_custom_call", output_to_operand_aliasing={{0}: (10, {}), {1}: (11, {})} | custom-call | tf_op jit(solution)/shard_map/place_late/pallas_call | solution.py:304
  (48 shorter events, 11.3 us)
Async XLA Ops:
  0.6 11.7 %collective-permute-start.4 = (bf16[1024,2048]{1,0:T(8,128)(2,1)}, bf16[1024,2048]{1,0:T(8,128)(2,1)}, u32[]{:S(2)}, u32[]{:S(2)}) collective-permute-start(bf16[1024,2048]{1,0:T(8,128)(2,1)} %refs_1_.1), channel_id=1, source_target_pairs={{0,1},{1,0},{2,3},{3,2},{4,5},{5,4},{6,7},{7,6},{8,9},{9,8},{10,11... | collective-permute-start | bytes 12582920 | tf_op jit(solution)/shard_map/ppermute | solution.py:39
  1.1 9.2 %collective-permute-start.2 = (s32[8,16]{1,0:T(8,128)}, s32[8,16]{1,0:T(8,128)S(1)}, u32[]{:S(2)}, u32[]{:S(2)}) collective-permute-start(s32[8,16]{1,0:T(8,128)} %param.7), channel_id=1, source_target_pairs={{0,8},{4,12},{8,16},{12,20},{16,24},{20,28},{24,0},{28,4},{1,9},{5... | collective-permute-start | bytes 1544 | tf_op jit(solution)/shard_map/ppermute | solution.py:26
  3.8 6.6 %collective-permute-start.1 = (s32[8,16]{1,0:T(8,128)}, s32[8,16]{1,0:T(8,128)S(1)}, u32[]{:S(2)}, u32[]{:S(2)}) collective-permute-start(s32[8,16]{1,0:T(8,128)} %param.7), channel_id=1, source_target_pairs={{0,4},{4,8},{8,12},{12,16},{16,20},{20,24},{24,28},{28,0},{1,5},{5... | collective-permute-start | bytes 1544 | tf_op jit(solution)/shard_map/ppermute | solution.py:26
  5.3 5.1 %collective-permute-start = (s32[8,16]{1,0:T(8,128)}, s32[8,16]{1,0:T(8,128)S(1)}, u32[]{:S(2)}, u32[]{:S(2)}) collective-permute-start(s32[8,16]{1,0:T(8,128)} %param.7), channel_id=1, source_target_pairs={{0,28},{4,0},{8,4},{12,8},{16,12},{20,16},{24,20},{28,24},{1,29},{... | collective-permute-start | bytes 1544 | tf_op jit(solution)/shard_map/ppermute | solution.py:26
  16.0 26.4 %collective-permute-start.8 = (bf16[2,128,2048]{2,1,0:T(8,128)(2,1)}, bf16[2,128,2048]{2,1,0:T(8,128)(2,1)S(1)}, u32[]{:S(2)}, u32[]{:S(2)}) collective-permute-start(bf16[2,128,2048]{2,1,0:T(8,128)(2,1)} %get-tuple-element.89), channel_id=1, source_target_pairs={{0,24},{4,28},{8,0},{12,4},{16,8},{20,12},{24,16},{28,20},{1,25},{... | collective-permute-start | bytes 3145736 | tf_op jit(solution)/shard_map/ppermute | solution.py:26
  18.1 8.3 %collective-permute-start.7 = (f32[2,2048]{1,0:T(2,128)S(1)}, f32[2,2048]{1,0:T(2,128)S(1)}, u32[]{:S(2)}, u32[]{:S(2)}) collective-permute-start(f32[2,2048]{1,0:T(2,128)S(1)} %pad_maximum_fusion.refs_2_), channel_id=1, source_target_pairs={{0,1},{1,0},{2,3},{3,2},{4,5},{5,4},{6,7},{7,6},{8,9},{9,8},{10,11... | collective-permute-start | bytes 49160 | tf_op jit(solution)/shard_map/ppermute | solution.py:39
  18.2 48.9 %collective-permute-start.5 = (bf16[2,128,2048]{2,1,0:T(8,128)(2,1)S(1)}, bf16[2,128,2048]{2,1,0:T(8,128)(2,1)S(1)}, u32[]{:S(2)}, u32[]{:S(2)}) collective-permute-start(bf16[2,128,2048]{2,1,0:T(8,128)(2,1)S(1)} %get-tuple-element.81), channel_id=1, source_target_pairs={{0,4},{4,8},{8,12},{12,16},{16,20},{20,24},{24,28},{28,0},{1,5},{5... | collective-permute-start | bytes 3145736 | tf_op jit(solution)/shard_map/ppermute | solution.py:26
  19.3 47.8 %collective-permute-start.6 = (bf16[2,128,2048]{2,1,0:T(8,128)(2,1)S(1)}, bf16[2,128,2048]{2,1,0:T(8,128)(2,1)S(1)}, u32[]{:S(2)}, u32[]{:S(2)}) collective-permute-start(bf16[2,128,2048]{2,1,0:T(8,128)(2,1)S(1)} %get-tuple-element.82), channel_id=1, source_target_pairs={{0,28},{4,0},{8,4},{12,8},{16,12},{20,16},{24,20},{28,24},{1,29},{... | collective-permute-start | bytes 3145736 | tf_op jit(solution)/shard_map/ppermute | solution.py:26
  36.2 30.9 %collective-permute-start.11 = (bf16[2,8,8,32,128]{4,3,2,1,0:T(8,128)(2,1)S(1)}, bf16[2,8,8,32,128]{4,3,2,1,0:T(8,128)(2,1)S(1)}, u32[]{:S(2)}, u32[]{:S(2)}) collective-permute-start(bf16[2,8,8,32,128]{4,3,2,1,0:T(8,128)(2,1)S(1)} %get-tuple-element.101), channel_id=1, source_target_pairs={{0,2},{1,3},{2,0},{3,1},{4,6},{5,7},{6,4},{7,5},{8,10},{9,11},{10,... | collective-permute-start | bytes 3145736 | tf_op jit(solution)/shard_map/ppermute | solution.py:39
  38.0 12.4 %collective-permute-start.10 = (bf16[8,8,32,128]{3,2,1,0:T(8,128)(2,1)S(1)}, bf16[8,8,32,128]{3,2,1,0:T(8,128)(2,1)S(1)}, u32[]{:S(2)}, u32[]{:S(2)}) collective-permute-start(bf16[8,8,32,128]{3,2,1,0:T(8,128)(2,1)S(1)} %get-tuple-element.100), channel_id=1, source_target_pairs={{0,1},{1,0},{2,3},{3,2},{4,5},{5,4},{6,7},{7,6},{8,9},{9,8},{10,11... | collective-permute-start | bytes 1572872 | tf_op jit(solution)/shard_map/ppermute | solution.py:39
  45.3 21.8 %collective-permute-start.9 = (bf16[2,2,8,32,128]{4,3,2,1,0:T(8,128)(2,1)S(1)}, bf16[2,2,8,32,128]{4,3,2,1,0:T(8,128)(2,1)S(1)}, u32[]{:S(2)}, u32[]{:S(2)}) collective-permute-start(bf16[2,2,8,32,128]{4,3,2,1,0:T(8,128)(2,1)S(1)} %get-tuple-element.98), channel_id=1, source_target_pairs={{0,2},{1,3},{2,0},{3,1},{4,6},{5,7},{6,4},{7,5},{8,10},{9,11},{10,... | collective-permute-start | bytes 786440 | tf_op jit(solution)/shard_map/ppermute | solution.py:39
  50.4 25.9 %collective-permute-start.13 = (bf16[2,64,2048]{2,1,0:T(8,128)(2,1)S(1)}, bf16[2,64,2048]{2,1,0:T(8,128)(2,1)S(1)}, u32[]{:S(2)}, u32[]{:S(2)}) collective-permute-start(bf16[2,64,2048]{2,1,0:T(8,128)(2,1)S(1)} %get-tuple-element.102), channel_id=1, source_target_pairs={{0,8},{4,12},{8,16},{12,20},{16,24},{20,28},{24,0},{28,4},{1,9},{5... | collective-permute-start | bytes 1572872 | tf_op jit(solution)/shard_map/ppermute | solution.py:26
  67.1 6.7 %collective-permute-start.16 = (bf16[2,8,32,128]{3,2,1,0:T(8,128)(2,1)S(1)}, bf16[2,8,32,128]{3,2,1,0:T(8,128)(2,1)S(1)}, u32[]{:S(2)}, u32[]{:S(2)}) collective-permute-start(bf16[2,8,32,128]{3,2,1,0:T(8,128)(2,1)S(1)} %get-tuple-element.114), channel_id=1, source_target_pairs={{0,1},{1,0},{2,3},{3,2},{4,5},{5,4},{6,7},{7,6},{8,9},{9,8},{10,11... | collective-permute-start | bytes 393224 | tf_op jit(solution)/shard_map/ppermute | solution.py:39
  67.2 20.6 %collective-permute-start.12 = (bf16[2,64,2048]{2,1,0:T(8,128)(2,1)S(1)}, bf16[2,64,2048]{2,1,0:T(8,128)(2,1)S(1)}, u32[]{:S(2)}, u32[]{:S(2)}) collective-permute-start(bf16[2,64,2048]{2,1,0:T(8,128)(2,1)S(1)} %get-tuple-element.105), channel_id=1, source_target_pairs={{0,8},{4,12},{8,16},{12,20},{16,24},{20,28},{24,0},{28,4},{1,9},{5... | collective-permute-start | bytes 1572872 | tf_op jit(solution)/shard_map/ppermute | solution.py:26
  67.9 8.4 %collective-permute-start.15 = (bf16[8,8,32,128]{3,2,1,0:T(8,128)(2,1)S(1)}, bf16[8,8,32,128]{3,2,1,0:T(8,128)(2,1)S(1)}, u32[]{:S(2)}, u32[]{:S(2)}) collective-permute-start(bf16[8,8,32,128]{3,2,1,0:T(8,128)(2,1)S(1)} %get-tuple-element.162), channel_id=1, source_target_pairs={{0,1},{1,0},{2,3},{3,2},{4,5},{5,4},{6,7},{7,6},{8,9},{9,8},{10,11... | collective-permute-start | bytes 1572872 | tf_op jit(solution)/shard_map/ppermute | solution.py:39
  68.0 5.9 %collective-permute-start.17 = (bf16[2,8,32,128]{3,2,1,0:T(8,128)(2,1)S(1)}, bf16[2,8,32,128]{3,2,1,0:T(8,128)(2,1)S(1)}, u32[]{:S(2)}, u32[]{:S(2)}) collective-permute-start(bf16[2,8,32,128]{3,2,1,0:T(8,128)(2,1)S(1)} %get-tuple-element.164), channel_id=1, source_target_pairs={{0,1},{1,0},{2,3},{3,2},{4,5},{5,4},{6,7},{7,6},{8,9},{9,8},{10,11... | collective-permute-start | bytes 393224 | tf_op jit(solution)/shard_map/ppermute | solution.py:39
  73.9 9.2 %collective-permute-start.18 = (bf16[4,8,32,128]{3,2,1,0:T(8,128)(2,1)S(1)}, bf16[4,8,32,128]{3,2,1,0:T(8,128)(2,1)S(1)}, u32[]{:S(2)}, u32[]{:S(2)}) collective-permute-start(bf16[4,8,32,128]{3,2,1,0:T(8,128)(2,1)S(1)} %get-tuple-element.120), channel_id=1, source_target_pairs={{0,2},{1,3},{2,0},{3,1},{4,6},{5,7},{6,4},{7,5},{8,10},{9,11},{10,... | collective-permute-start | bytes 786440 | tf_op jit(solution)/shard_map/ppermute | solution.py:39
  76.3 11.5 %collective-permute-start.19 = (bf16[4,8,32,128]{3,2,1,0:T(8,128)(2,1)S(1)}, bf16[4,8,32,128]{3,2,1,0:T(8,128)(2,1)S(1)}, u32[]{:S(2)}, u32[]{:S(2)}) collective-permute-start(bf16[4,8,32,128]{3,2,1,0:T(8,128)(2,1)S(1)} %get-tuple-element.121), channel_id=1, source_target_pairs={{0,3},{1,2},{2,1},{3,0},{4,7},{5,6},{6,5},{7,4},{8,11},{9,10},{10,... | collective-permute-start | bytes 786440 | tf_op jit(solution)/shard_map/ppermute | solution.py:39
  79.2 13.8 %collective-permute-start.20 = (bf16[1,8,32,128]{3,2,1,0:T(8,128)(2,1)S(1)}, bf16[1,8,32,128]{3,2,1,0:T(8,128)(2,1)S(1)}, u32[]{:S(2)}, u32[]{:S(2)}) collective-permute-start(bf16[1,8,32,128]{3,2,1,0:T(8,128)(2,1)S(1)} %get-tuple-element.127), channel_id=1, source_target_pairs={{0,1},{1,0},{2,3},{3,2},{4,5},{5,4},{6,7},{7,6},{8,9},{9,8},{10,11... | collective-permute-start | bytes 196616 | tf_op jit(solution)/shard_map/ppermute | solution.py:39
  80.9 12.1 %collective-permute-start.21 = (bf16[1,8,32,128]{3,2,1,0:T(8,128)(2,1)S(1)}, bf16[1,8,32,128]{3,2,1,0:T(8,128)(2,1)S(1)}, u32[]{:S(2)}, u32[]{:S(2)}) collective-permute-start(bf16[1,8,32,128]{3,2,1,0:T(8,128)(2,1)S(1)} %get-tuple-element.128), channel_id=1, source_target_pairs={{0,2},{1,3},{2,0},{3,1},{4,6},{5,7},{6,4},{7,5},{8,10},{9,11},{10,... | collective-permute-start | bytes 196616 | tf_op jit(solution)/shard_map/ppermute | solution.py:39
  83.1 9.9 %collective-permute-start.22 = (bf16[1,8,32,128]{3,2,1,0:T(8,128)(2,1)S(1)}, bf16[1,8,32,128]{3,2,1,0:T(8,128)(2,1)S(1)}, u32[]{:S(2)}, u32[]{:S(2)}) collective-permute-start(bf16[1,8,32,128]{3,2,1,0:T(8,128)(2,1)S(1)} %get-tuple-element.129), channel_id=1, source_target_pairs={{0,3},{1,2},{2,1},{3,0},{4,7},{5,6},{6,5},{7,4},{8,11},{9,10},{10,... | collective-permute-start | bytes 196616 | tf_op jit(solution)/shard_map/ppermute | solution.py:39
  90.7 7.3 %collective-permute-start.23 = (bf16[1,8,32,128]{3,2,1,0:T(8,128)(2,1)S(1)}, bf16[1,8,32,128]{3,2,1,0:T(8,128)(2,1)S(1)}, u32[]{:S(2)}, u32[]{:S(2)}) collective-permute-start(bf16[1,8,32,128]{3,2,1,0:T(8,128)(2,1)S(1)} %get-tuple-element.149), channel_id=1, source_target_pairs={{0,1},{1,0},{2,3},{3,2},{4,5},{5,4},{6,7},{7,6},{8,9},{9,8},{10,11... | collective-permute-start | bytes 196616 | tf_op jit(solution)/shard_map/ppermute | solution.py:39
  91.5 6.5 %collective-permute-start.24 = (bf16[1,8,32,128]{3,2,1,0:T(8,128)(2,1)S(1)}, bf16[1,8,32,128]{3,2,1,0:T(8,128)(2,1)S(1)}, u32[]{:S(2)}, u32[]{:S(2)}) collective-permute-start(bf16[1,8,32,128]{3,2,1,0:T(8,128)(2,1)S(1)} %get-tuple-element.150), channel_id=1, source_target_pairs={{0,2},{1,3},{2,0},{3,1},{4,6},{5,7},{6,4},{7,5},{8,10},{9,11},{10,... | collective-permute-start | bytes 196616 | tf_op jit(solution)/shard_map/ppermute | solution.py:39
  93.0 4.9 %collective-permute-start.25 = (bf16[1,8,32,128]{3,2,1,0:T(8,128)(2,1)S(1)}, bf16[1,8,32,128]{3,2,1,0:T(8,128)(2,1)S(1)}, u32[]{:S(2)}, u32[]{:S(2)}) collective-permute-start(bf16[1,8,32,128]{3,2,1,0:T(8,128)(2,1)S(1)} %get-tuple-element.151), channel_id=1, source_target_pairs={{0,3},{1,2},{2,1},{3,0},{4,7},{5,6},{6,5},{7,4},{8,11},{9,10},{10,... | collective-permute-start | bytes 196616 | tf_op jit(solution)/shard_map/ppermute | solution.py:39
  (3 other events, 10.9 us)

commit v11 on v10

--- a/solution.py
+++ b/solution.py
@@ -186,12 +186,34 @@
     return total
 
 
+def list_kernel(per_core, where_ref, later):
+    blocks, slots = where_ref.shape
+
+    def step(entry, count):
+        where = where_ref[lax.div(entry, slots), lax.rem(entry, slots)]
+        later[count + 1] = entry
+        return count + (lax.rem(where, per_core) == per_core - 1).astype(jnp.int32)
+
+    later[0] = lax.fori_loop(0, blocks * slots, step, 0)
+
+
+def list_open(where, per_core):
+    smem = pl.BlockSpec(memory_space=pltpu.SMEM)
+    return pl.pallas_call(
+        functools.partial(list_kernel, per_core),
+        out_shape=jax.ShapeDtypeStruct((where.size + 1,), jnp.int32),
+        in_specs=[smem],
+        out_specs=smem,
+        name="list_open",
+        cost_estimate=SOON,
+    )(where)
+
+
 def place_early_kernel(chips, sizes, per_core, where_ref, *refs):
     n_chunks = len(sizes)
     ins = refs[: 2 * chips * n_chunks]
-    density, energy, later, pool, tiles_out, sems = refs[2 * chips * n_chunks :]
+    density, energy, pool, tiles_out, sems = refs[2 * chips * n_chunks :]
     blocks, slots = density.shape[:2]
-    later[0] = 0
 
     def copies(i, buffer):
         return [
@@ -223,12 +245,6 @@
             for kind in range(2):
                 tiles_out[buffer, kind, slot] = pool[where, kind]
 
-            @pl.when(lax.rem(where, per_core) == per_core - 1)
-            def _():
-                count = later[0] + 1
-                later[count] = i * slots + slot
-                later[0] = count
-
         for copy in copies(i, buffer):
             copy.start()
 
@@ -245,9 +261,9 @@
     smem = pl.BlockSpec(memory_space=pltpu.SMEM)
     return pl.pallas_call(
         functools.partial(place_early_kernel, chips, sizes, per_core),
-        out_shape=[out, out, jax.ShapeDtypeStruct((blocks * slots + 1,), jnp.int32)],
+        out_shape=[out, out],
         in_specs=[smem] + [pl.BlockSpec(memory_space=pltpu.VMEM)] * len(flat),
-        out_specs=[pl.BlockSpec(memory_space=pl.ANY)] * 2 + [smem],
+        out_specs=[pl.BlockSpec(memory_space=pl.ANY)] * 2,
         scratch_shapes=[
             pltpu.VMEM((2 * per_core, 2, strip, tile), jnp.float32),
             pltpu.VMEM((2, 2, slots, strip, tile), jnp.float32),
@@ -345,7 +361,9 @@
 
     asks, own_weights = lax.optimization_barrier((asks, own_weights))
     weights = (own_weights, to_strip_target(own_weights, chips, 0, 1))
-    picked = list(pick(here, asks[:3], eigvecs, sib, tile, 1))
+    picked = list(pick(here, asks[2:3], eigvecs, sib, tile, 1))
+    here, picked[0] = lax.optimization_barrier((here, picked[0]))
+    picked = list(pick(here, asks[:2], eigvecs, sib, tile, 1)) + picked
     arrived = [
         shifted(value, "atoms", -offset) for value, offset in zip(picked, offsets)
     ]
@@ -391,8 +409,9 @@
     pairs = [
         to_strip_target(pair, chips, step + 1, 0) for step, pair in enumerate(parts[2:])
     ]
-    near, where, parts[:2], pairs, chunks, halves = lax.optimization_barrier(
-        (near, where, parts[:2], pairs, chunks, halves)
+    later = list_open(where, per_core)
+    near, where, later, parts[:2], pairs, chunks, halves = lax.optimization_barrier(
+        (near, where, later, parts[:2], pairs, chunks, halves)
     )
     upper = shifted(halves[1], "atoms", -offsets[3])
     chunks.append([parts[0], to_strip_target(parts[1], chips, 0, 1)] + pairs)
@@ -403,8 +422,8 @@
     lower_sib = lower[1]
     for index in range(2, n_bands):
         lower[index] = to_strip_target(lower[index], chips, index // 2, index % 2)
-    where, upper, lower[0], direct = lax.optimization_barrier(
-        (where, upper, lower[0], direct)
+    where, upper, lower[0], direct[:3] = lax.optimization_barrier(
+        (where, upper, lower[0], direct[:3])
     )
     chunks.append(direct)
     last = strips_of([upper], False)
@@ -414,7 +433,7 @@
     local, far, direct = chunks
     strips = list(zip(local, direct, far))
     sizes = [half_blocks, 2, 1]
-    density, energy, later = place_early(where, strips, sizes, chips, per_core)
+    density, energy = place_early(where, strips, sizes, chips, per_core)
     return place_late(where, later, lower, last, density, energy, chips, per_core)
 
 

time: 101 us -> 108 us (1.069)
  Pallas kernels: 39.7 us -> 46.1 us
  local copies, waits for them, and re-layouts: 0.2 us -> 6.57 us
  waiting for transfers between devices: 27.9 us -> 22.8 us
  starting transfers between devices: 26.2 us -> 24.6 us
    unnamed x2 -> x24, local copies, waits for them, and re-layouts: 0.01 us -> 5.2 us
    ppermute x9, waiting for transfers between devices: 21.9 us -> 17.4 us  [shifted(): return lax.ppermute(value, axis, pairs)]
    pallas_call x0 -> x1, Pallas kernels: none -> 3.04 us  [list_open(): pl.pallas_call(functools.partial(list_kernel, per_core), out_shape=jax.Sh...]
    pallas_call x2 -> x3, Pallas kernels: 5.59 us -> 7.56 us  [pick(): pl.pallas_call(functools.partial(pick_kernel, count, blocks, tile, parts)...]
    pallas_call x5, Pallas kernels: 23.8 us -> 25.6 us  [tiles(): pl.pallas_call(functools.partial(tiles_kernel, heights, len(arrived), n_s...]
    squeeze x2, local copies, waits for them, and re-layouts: 0.11 us -> 1.29 us  [passed_on(): singles += [pair[0], to_strip_target(pair[1], chips, 0, 1)]]
    ppermute x17, starting transfers between devices: 11 us -> 9.89 us  [to_strip_target(): return lax.ppermute(value, 'bands', pairs)]
  transfers between devices with their start and end apart: 26 -> 26, of which waited for: 6 -> 6; matrix products, arithmetic and copies ran while one was open for 5% -> 6% of each run, Pallas kernels for 34% -> 40%
where the time goes in v11:
time: 108 us; the launch traced here: 106 us
  Pallas kernels  46.1 us (43%)
  starting transfers between devices  24.6 us (23%)
  waiting for transfers between devices  22.8 us (21%)
  local copies, waits for them, and re-layouts  6.57 us (6%)
  other arithmetic  5.22 us (5%)
  between operations  1.08 us (1%)
    pallas_call x5, Pallas kernels, tiles(): pl.pallas_call(functools.partial(tiles_kernel, heights, len(arrived), n_s...  25.6 us
    ppermute x9, waiting for transfers between devices, shifted(): return lax.ppermute(value, axis, pairs)  17.4 us
    ppermute x9, starting transfers between devices, shifted(): return lax.ppermute(value, axis, pairs)  14.7 us
    ppermute x17, starting transfers between devices, to_strip_target(): return lax.ppermute(value, 'bands', pairs)  9.89 us
    pallas_call x3, Pallas kernels, pick(): pl.pallas_call(functools.partial(pick_kernel, count, blocks, tile, parts)...  7.56 us
    ppermute x17, waiting for transfers between devices, to_strip_target(): return lax.ppermute(value, 'bands', pairs)  5.4 us
    unnamed x24, local copies, waits for them, and re-layouts  5.2 us
    pallas_call x1, Pallas kernels, place_early(): pl.pallas_call(functools.partial(place_early_kernel, chips, sizes, per_co...  4.6 us
  transfers between devices with their start and end apart: 26, of which 6 were waited for; matrix products, arithmetic and copies ran while one was open for 6% of the time, Pallas kernels for 40%

profile of v11, /device:TPU:0, one launch (start us, length us, event | category | flops | bytes accessed | tf_op | source)
XLA Modules:
  0.0 106.3 jit_solution(10847849452197452467)
XLA Ops:
  1.1 2.6 %collective-permute-start.2 = (s32[8,16]{1,0:T(8,128)}, s32[8,16]{1,0:T(8,128)S(1)}, u32[]{:S(2)}, u32[]{:S(2)}) collective-permute-start(s32[8,16]{1,0:T(8,128)} %param.7), channel_id=1, source_target_pairs={{0,8},{4,12},{8,16},{12,20},{16,24},{20,28},{24,0},{28,4},{1,9},{5... | collective-permute-start | bytes 1544 | tf_op jit(solution)/shard_map/ppermute | solution.py:26
  5.3 3.2 %collective-permute-start = (s32[8,16]{1,0:T(8,128)}, s32[8,16]{1,0:T(8,128)S(1)}, u32[]{:S(2)}, u32[]{:S(2)}) collective-permute-start(s32[8,16]{1,0:T(8,128)} %param.7), channel_id=1, source_target_pairs={{0,28},{4,0},{8,4},{12,8},{16,12},{20,16},{24,20},{28,24},{1,29},{... | collective-permute-start | bytes 1544 | tf_op jit(solution)/shard_map/ppermute | solution.py:26
  10.3 2.0 %collective-permute-done.3.refs_0_ = s32[8,16]{1,0:T(8,128)S(1)} collective-permute-done((s32[8,16]{1,0:T(8,128)}, s32[8,16]{1,0:T(8,128)S(1)}, u32[]{:S(2)}, u32[]{:S(2)}) %collective-permute-start.3) | collective-permute-done | bytes 544 | tf_op jit(solution)/shard_map/ppermute | solution.py:26
  12.3 2.0 %pick_blocks.3 = bf16[2,128,2048]{2,1,0:T(8,128)(2,1)S(1)} custom-call(s32[2]{0:T(128)S(1)} %pad_add_fusion.place_ref, s32[8,16]{1,0:T(8,128)S(1)} %collective-permute-done.2.refs_0_, bf16[1024,2048]{1,0:T(8,128)(2,1)} %refs_1_.3, bf16[1024,2048]{1,0:T(8,128)(2,1)} %collective-permute-done.4.refs_2_.refs_3_.sib), custom_call_target="tpu_custom_call" | custom-call | tf_op jit(solution)/shard_map/pick_blocks/pallas_call | solution.py:73
  14.3 2.2 %collective-permute-start.8 = (bf16[2,128,2048]{2,1,0:T(8,128)(2,1)S(1)}, bf16[2,128,2048]{2,1,0:T(8,128)(2,1)S(1)}, u32[]{:S(2)}, u32[]{:S(2)}) collective-permute-start(bf16[2,128,2048]{2,1,0:T(8,128)(2,1)S(1)} %pick_blocks.3), channel_id=1, source_target_pairs={{0,24},{4,28},{8,0},{12,4},{16,8},{20,12},{24,16},{28,20},{1,25},{... | collective-permute-start | bytes 3145736 | tf_op jit(solution)/shard_map/ppermute | solution.py:26
  16.6 3.6 %pick_blocks.4 = (bf16[2,128,2048]{2,1,0:T(8,128)(2,1)}, bf16[2,128,2048]{2,1,0:T(8,128)(2,1)}) custom-call(s32[2]{0:T(128)S(1)} %pad_add_fusion.place_ref, s32[8,16]{1,0:T(8,128)S(1)} %collective-permute-done.refs_0_, s32[8,16]{1,0:T(8,128)S(1)} %collective-permute-done.1.refs_1_, bf16[1024,2048]{1,0:T(8,128)(2,1)} %refs_1_.3, ...), custom_call_target="tpu_custom_call" | custom-call | tf_op jit(solution)/shard_map/pick_blocks/pallas_call | solution.py:73
  21.4 3.6 %collective-permute-start.6 = (bf16[2,128,2048]{2,1,0:T(8,128)(2,1)}, bf16[2,128,2048]{2,1,0:T(8,128)(2,1)}, u32[]{:S(2)}, u32[]{:S(2)}) collective-permute-start(bf16[2,128,2048]{2,1,0:T(8,128)(2,1)} %get-tuple-element.83), channel_id=1, source_target_pairs={{0,28},{4,0},{8,4},{12,8},{16,12},{20,16},{24,20},{28,24},{1,29},{... | collective-permute-start | bytes 3145736 | tf_op jit(solution)/shard_map/ppermute | solution.py:26
  25.0 3.5 %keep.1 = (bf16[1024,2048]{1,0:T(8,128)(2,1)S(1)}, bf16[1024,2048]{1,0:T(8,128)(2,1)S(1)}) custom-call(bf16[1024,2048]{1,0:T(8,128)(2,1)} %refs_1_.3, bf16[1024,2048]{1,0:T(8,128)(2,1)} %collective-permute-done.4.refs_2_.refs_3_.sib), custom_call_target="tpu_custom_call" | custom-call | tf_op jit(solution)/shard_map/keep/pallas_call | solution.py:98
  28.5 10.8 %tiles.5 = (bf16[8,8,32,128]{3,2,1,0:T(8,128)(2,1)S(1)}, bf16[8,8,32,128]{3,2,1,0:T(8,128)(2,1)}, bf16[2,8,8,32,128]{4,3,2,1,0:T(8,128)(2,1)}) custom-call(s32[5]{0:T(128)S(1)} %stack.44.place_ref, bf16[1024,2048]{1,0:T(8,128)(2,1)S(1)} %get-tuple-element.85.refs_0_, bf16[1024,2048]{1,0:T(8,128)(2,1)S(1)} %get-tuple-element.86.refs_1_, ...), custom_call_target="tpu_custom_call" | custom-call | tf_op jit(solution)/shard_map/tiles/pallas_call | solution.py:165
  41.0 2.0 %pick_blocks.5 = (bf16[2,64,2048]{2,1,0:T(8,128)(2,1)S(1)}, bf16[2,64,2048]{2,1,0:T(8,128)(2,1)S(1)}) custom-call(s32[2]{0:T(128)S(1)} %pad_add_fusion.place_ref, s32[8,16]{1,0:T(8,128)S(1)} %collective-permute-done.3.refs_0_, bf16[1024,2048]{1,0:T(8,128)(2,1)} %refs_1_.3, bf16[1024,2048]{1,0:T(8,128)(2,1)} %collective-permute-done.4.refs_2_.refs_3_.sib), custom_call_target="tpu_custom_call" | custom-call | tf_op jit(solution)/shard_map/pick_blocks/pallas_call | solution.py:73
  43.8 3.0 %tiles.6 = (bf16[2,8,32,128]{3,2,1,0:T(8,128)(2,1)S(1)}, bf16[2,8,32,128]{3,2,1,0:T(8,128)(2,1)S(1)}, bf16[2,2,8,32,128]{4,3,2,1,0:T(8,128)(2,1)S(1)}) custom-call(s32[5]{0:T(128)S(1)} %stack.44.place_ref, bf16[1024,2048]{1,0:T(8,128)(2,1)S(1)} %get-tuple-element.85.refs_0_, bf16[1024,2048]{1,0:T(8,128)(2,1)S(1)} %get-tuple-element.86.refs_1_, ...), custom_call_target="tpu_custom_call" | custom-call | tf_op jit(solution)/shard_map/tiles/pallas_call | solution.py:165
  48.0 3.0 %fusion.9.where_ref = s32[8,16]{1,0:T(8,128)} fusion(pred[8,16]{1,0:T(8,128)(4,1)S(1)} %get-tuple-element.161, pred[8,16]{1,0:T(8,128)(4,1)S(1)} %get-tuple-element.160, pred[8,16]{1,0:T(8,128)(4,1)S(1)} %get-tuple-element.159, pred[8,16]{1,0:T(8,128)(4,1)S(1)} %get-tuple-element.158, s32[]{:T(128)} %and.14, s32[]{:T(128)} %get-tuple-element.156, ...), kind=kLoop, calls=%fused_computation.22 | loop fusion | flops 4352 | bytes 1556 | tf_op jit(solution)/shard_map/add | solution.py:403
  51.0 3.0 %list_open.1.later = s32[129]{0:T(256)} custom-call(s32[8,16]{1,0:T(8,128)} %fusion.9.where_ref), custom_call_target="tpu_custom_call" | custom-call | tf_op jit(solution)/shard_map/list_open/pallas_call | solution.py:202
  54.1 15.4 %collective-permute-done.6.refs_5_ = bf16[2,128,2048]{2,1,0:T(8,128)(2,1)} collective-permute-done((bf16[2,128,2048]{2,1,0:T(8,128)(2,1)}, bf16[2,128,2048]{2,1,0:T(8,128)(2,1)}, u32[]{:S(2)}, u32[]{:S(2)}) %collective-permute-start.6) | collective-permute-done | bytes 1048608 | tf_op jit(solution)/shard_map/ppermute | solution.py:26
  72.1 2.2 %copy-done.1 = bf16[1024,2048]{1,0:T(8,128)(2,1)S(1)} copy-done((bf16[1024,2048]{1,0:T(8,128)(2,1)S(1)}, bf16[1024,2048]{1,0:T(8,128)(2,1)}, u32[]{:S(2)}) %copy-start.1) | copy-done | bytes 4194328
  74.3 2.2 %copy-done.3 = bf16[1024,2048]{1,0:T(8,128)(2,1)S(1)} copy-done((bf16[1024,2048]{1,0:T(8,128)(2,1)S(1)}, bf16[1024,2048]{1,0:T(8,128)(2,1)}, u32[]{:S(2)}) %copy-start.3) | copy-done | bytes 4194328
  76.5 6.0 %tiles.7 = (bf16[4,8,32,128]{3,2,1,0:T(8,128)(2,1)S(1)}, bf16[4,8,32,128]{3,2,1,0:T(8,128)(2,1)S(1)}, bf16[4,8,32,128]{3,2,1,0:T(8,128)(2,1)S(1)}, bf16[4,8,32,128]{3,2,1,0:T(8,128)(2,1)S(1)}) custom-call(s32[5]{0:T(128)S(1)} %stack.44.place_ref, bf16[1024,2048]{1,0:T(8,128)(2,1)S(1)} %copy-done.1, bf16[1024,2048]{1,0:T(8,128)(2,1)S(1)} %copy-done.3, ...), custom_call_target="tpu_custom_call" | custom-call | tf_op jit(solution)/shard_map/tiles/pallas_call | solution.py:165
  84.7 2.9 %tiles.8 = (bf16[1,8,32,128]{3,2,1,0:T(8,128)(2,1)S(1)}, bf16[1,8,32,128]{3,2,1,0:T(8,128)(2,1)S(1)}, bf16[1,8,32,128]{3,2,1,0:T(8,128)(2,1)S(1)}, bf16[1,8,32,128]{3,2,1,0:T(8,128)(2,1)S(1)}) custom-call(s32[5]{0:T(128)S(1)} %stack.44.place_ref, bf16[1024,2048]{1,0:T(8,128)(2,1)S(1)} %copy-done.1, bf16[1024,2048]{1,0:T(8,128)(2,1)S(1)} %copy-done.3, ...), custom_call_target="tpu_custom_call" | custom-call | tf_op jit(solution)/shard_map/tiles/pallas_call | solution.py:165
  89.8 2.4 %collective-permute-done.18.refs_7_ = bf16[4,8,32,128]{3,2,1,0:T(8,128)(2,1)S(1)} collective-permute-done((bf16[4,8,32,128]{3,2,1,0:T(8,128)(2,1)S(1)}, bf16[4,8,32,128]{3,2,1,0:T(8,128)(2,1)S(1)}, u32[]{:S(2)}, u32[]{:S(2)}) %collective-permute-start.18) | collective-permute-done | bytes 262176 | tf_op jit(solution)/shard_map/ppermute | solution.py:39
  92.2 2.9 %tiles.9 = (bf16[1,8,32,128]{3,2,1,0:T(8,128)(2,1)S(1)}, bf16[1,8,32,128]{3,2,1,0:T(8,128)(2,1)S(1)}, bf16[1,8,32,128]{3,2,1,0:T(8,128)(2,1)S(1)}, bf16[1,8,32,128]{3,2,1,0:T(8,128)(2,1)S(1)}) custom-call(s32[5]{0:T(128)S(1)} %stack.44.place_ref, bf16[1024,2048]{1,0:T(8,128)(2,1)S(1)} %copy-done.1, bf16[1024,2048]{1,0:T(8,128)(2,1)S(1)} %copy-done.3, ...), custom_call_target="tpu_custom_call" | custom-call | tf_op jit(solution)/shard_map/tiles/pallas_call | solution.py:165
  95.1 1.8 %collective-permute-start.22 = (bf16[1,8,32,128]{3,2,1,0:T(8,128)(2,1)S(1)}, bf16[1,8,32,128]{3,2,1,0:T(8,128)(2,1)S(1)}, u32[]{:S(2)}, u32[]{:S(2)}) collective-permute-start(bf16[1,8,32,128]{3,2,1,0:T(8,128)(2,1)S(1)} %get-tuple-element.137), channel_id=1, source_target_pairs={{0,1},{1,0},{2,3},{3,2},{4,5},{5,4},{6,7},{7,6},{8,9},{9,8},{10,11... | collective-permute-start | bytes 196616 | tf_op jit(solution)/shard_map/ppermute | solution.py:39
  97.3 1.7 %collective-permute-done.20.refs_2_ = bf16[1,8,32,128]{3,2,1,0:T(8,128)(2,1)S(1)} collective-permute-done((bf16[1,8,32,128]{3,2,1,0:T(8,128)(2,1)S(1)}, bf16[1,8,32,128]{3,2,1,0:T(8,128)(2,1)S(1)}, u32[]{:S(2)}, u32[]{:S(2)}) %collective-permute-start.20) | collective-permute-done | bytes 65568 | tf_op jit(solution)/shard_map/ppermute | solution.py:39
  99.7 4.6 %place_early.1 = (f32[8,16,32,128]{3,2,1,0:T(8,128)}, f32[8,16,32,128]{3,2,1,0:T(8,128)}) custom-call(s32[8,16]{1,0:T(8,128)S(1)} %copy-done.6, bf16[8,8,32,128]{3,2,1,0:T(8,128)(2,1)S(1)} %copy-done.5, bf16[4,8,32,128]{3,2,1,0:T(8,128)(2,1)S(1)} %get-tuple-element.141.refs_1_, bf16[2,8,32,128]{3,2,1,0:T(8,128)(2,1)S(1)} %get-tuple-element.142.refs_2_, ...), custom_call_target="tpu_custom_call" | custom-call | tf_op jit(solution)/shard_map/place_early/pallas_call | solution.py:262
  104.3 1.8 %place_late.1 = (f32[8,16,32,128]{3,2,1,0:T(8,128)}, f32[8,16,32,128]{3,2,1,0:T(8,128)}) custom-call(s32[8,16]{1,0:T(8,128)S(1)} %copy-done.6, s32[129]{0:T(256)S(1)} %copy-done.7, bf16[1,8,32,128]{3,2,1,0:T(8,128)(2,1)S(1)} %get-tuple-element.132.refs_0_, ...), custom_call_target="tpu_custom_call", output_to_operand_aliasing={{0}: (10, {}), {1}: (11, {})} | custom-call | tf_op jit(solution)/shard_map/place_late/pallas_call | solution.py:320
  (72 shorter events, 16.9 us)
Async XLA Ops:
  0.6 11.7 %collective-permute-start.4 = (bf16[1024,2048]{1,0:T(8,128)(2,1)}, bf16[1024,2048]{1,0:T(8,128)(2,1)}, u32[]{:S(2)}, u32[]{:S(2)}) collective-permute-start(bf16[1024,2048]{1,0:T(8,128)(2,1)} %refs_1_.3), channel_id=1, source_target_pairs={{0,1},{1,0},{2,3},{3,2},{4,5},{5,4},{6,7},{7,6},{8,9},{9,8},{10,11... | collective-permute-start | bytes 12582920 | tf_op jit(solution)/shard_map/ppermute | solution.py:39
  1.1 9.2 %collective-permute-start.2 = (s32[8,16]{1,0:T(8,128)}, s32[8,16]{1,0:T(8,128)S(1)}, u32[]{:S(2)}, u32[]{:S(2)}) collective-permute-start(s32[8,16]{1,0:T(8,128)} %param.7), channel_id=1, source_target_pairs={{0,8},{4,12},{8,16},{12,20},{16,24},{20,28},{24,0},{28,4},{1,9},{5... | collective-permute-start | bytes 1544 | tf_op jit(solution)/shard_map/ppermute | solution.py:26
  3.8 6.6 %collective-permute-start.1 = (s32[8,16]{1,0:T(8,128)}, s32[8,16]{1,0:T(8,128)S(1)}, u32[]{:S(2)}, u32[]{:S(2)}) collective-permute-start(s32[8,16]{1,0:T(8,128)} %param.7), channel_id=1, source_target_pairs={{0,4},{4,8},{8,12},{12,16},{16,20},{20,24},{24,28},{28,0},{1,5},{5... | collective-permute-start | bytes 1544 | tf_op jit(solution)/shard_map/ppermute | solution.py:26
  5.3 5.1 %collective-permute-start = (s32[8,16]{1,0:T(8,128)}, s32[8,16]{1,0:T(8,128)S(1)}, u32[]{:S(2)}, u32[]{:S(2)}) collective-permute-start(s32[8,16]{1,0:T(8,128)} %param.7), channel_id=1, source_target_pairs={{0,28},{4,0},{8,4},{12,8},{16,12},{20,16},{24,20},{28,24},{1,29},{... | collective-permute-start | bytes 1544 | tf_op jit(solution)/shard_map/ppermute | solution.py:26
  14.3 29.5 %collective-permute-start.8 = (bf16[2,128,2048]{2,1,0:T(8,128)(2,1)S(1)}, bf16[2,128,2048]{2,1,0:T(8,128)(2,1)S(1)}, u32[]{:S(2)}, u32[]{:S(2)}) collective-permute-start(bf16[2,128,2048]{2,1,0:T(8,128)(2,1)S(1)} %pick_blocks.3), channel_id=1, source_target_pairs={{0,24},{4,28},{8,0},{12,4},{16,8},{20,12},{24,16},{28,20},{1,25},{... | collective-permute-start | bytes 3145736 | tf_op jit(solution)/shard_map/ppermute | solution.py:26
  16.5 12.0 %collective-permute-start.7 = (f32[2,2048]{1,0:T(2,128)S(1)}, f32[2,2048]{1,0:T(2,128)S(1)}, u32[]{:S(2)}, u32[]{:S(2)}) collective-permute-start(f32[2,2048]{1,0:T(2,128)S(1)} %pad_maximum_fusion.refs_2_), channel_id=1, source_target_pairs={{0,1},{1,0},{2,3},{3,2},{4,5},{5,4},{6,7},{7,6},{8,9},{9,8},{10,11... | collective-permute-start | bytes 49160 | tf_op jit(solution)/shard_map/ppermute | solution.py:39
  20.2 49.3 %collective-permute-start.5 = (bf16[2,128,2048]{2,1,0:T(8,128)(2,1)}, bf16[2,128,2048]{2,1,0:T(8,128)(2,1)S(1)}, u32[]{:S(2)}, u32[]{:S(2)}) collective-permute-start(bf16[2,128,2048]{2,1,0:T(8,128)(2,1)} %get-tuple-element.82), channel_id=1, source_target_pairs={{0,4},{4,8},{8,12},{12,16},{16,20},{20,24},{24,28},{28,0},{1,5},{5... | collective-permute-start | bytes 3145736 | tf_op jit(solution)/shard_map/ppermute | solution.py:26
  21.4 48.1 %collective-permute-start.6 = (bf16[2,128,2048]{2,1,0:T(8,128)(2,1)}, bf16[2,128,2048]{2,1,0:T(8,128)(2,1)}, u32[]{:S(2)}, u32[]{:S(2)}) collective-permute-start(bf16[2,128,2048]{2,1,0:T(8,128)(2,1)} %get-tuple-element.83), channel_id=1, source_target_pairs={{0,28},{4,0},{8,4},{12,8},{16,12},{20,16},{24,20},{28,24},{1,29},{... | collective-permute-start | bytes 3145736 | tf_op jit(solution)/shard_map/ppermute | solution.py:26
  39.3 30.2 %collective-permute-start.11 = (bf16[2,8,8,32,128]{4,3,2,1,0:T(8,128)(2,1)}, bf16[2,8,8,32,128]{4,3,2,1,0:T(8,128)(2,1)}, u32[]{:S(2)}, u32[]{:S(2)}) collective-permute-start(bf16[2,8,8,32,128]{4,3,2,1,0:T(8,128)(2,1)} %get-tuple-element.102), channel_id=1, source_target_pairs={{0,2},{1,3},{2,0},{3,1},{4,6},{5,7},{6,4},{7,5},{8,10},{9,11},{10,... | collective-permute-start | bytes 3145736 | tf_op jit(solution)/shard_map/ppermute | solution.py:39
  41.0 13.0 %collective-permute-start.10 = (bf16[8,8,32,128]{3,2,1,0:T(8,128)(2,1)}, bf16[8,8,32,128]{3,2,1,0:T(8,128)(2,1)}, u32[]{:S(2)}, u32[]{:S(2)}) collective-permute-start(bf16[8,8,32,128]{3,2,1,0:T(8,128)(2,1)} %get-tuple-element.101), channel_id=1, source_target_pairs={{0,1},{1,0},{2,3},{3,2},{4,5},{5,4},{6,7},{7,6},{8,9},{9,8},{10,11... | collective-permute-start | bytes 1572872 | tf_op jit(solution)/shard_map/ppermute | solution.py:39
  46.8 23.3 %collective-permute-start.9 = (bf16[2,2,8,32,128]{4,3,2,1,0:T(8,128)(2,1)S(1)}, bf16[2,2,8,32,128]{4,3,2,1,0:T(8,128)(2,1)S(1)}, u32[]{:S(2)}, u32[]{:S(2)}) collective-permute-start(bf16[2,2,8,32,128]{4,3,2,1,0:T(8,128)(2,1)S(1)} %get-tuple-element.99), channel_id=1, source_target_pairs={{0,2},{1,3},{2,0},{3,1},{4,6},{5,7},{6,4},{7,5},{8,10},{9,11},{10,... | collective-permute-start | bytes 786440 | tf_op jit(solution)/shard_map/ppermute | solution.py:39
  54.0 30.7 %collective-permute-start.13 = (bf16[2,64,2048]{2,1,0:T(8,128)(2,1)S(1)}, bf16[2,64,2048]{2,1,0:T(8,128)(2,1)S(1)}, u32[]{:S(2)}, u32[]{:S(2)}) collective-permute-start(bf16[2,64,2048]{2,1,0:T(8,128)(2,1)S(1)} %copy-done.10), channel_id=1, source_target_pairs={{0,8},{4,12},{8,16},{12,20},{16,24},{20,28},{24,0},{28,4},{1,9},{5... | collective-permute-start | bytes 1572872 | tf_op jit(solution)/shard_map/ppermute | solution.py:26
  70.2 12.3 %collective-permute-start.16 = (bf16[2,8,32,128]{3,2,1,0:T(8,128)(2,1)S(1)}, bf16[2,8,32,128]{3,2,1,0:T(8,128)(2,1)S(1)}, u32[]{:S(2)}, u32[]{:S(2)}) collective-permute-start(bf16[2,8,32,128]{3,2,1,0:T(8,128)(2,1)S(1)} %get-tuple-element.115), channel_id=1, source_target_pairs={{0,1},{1,0},{2,3},{3,2},{4,5},{5,4},{6,7},{7,6},{8,9},{9,8},{10,11... | collective-permute-start | bytes 393224 | tf_op jit(solution)/shard_map/ppermute | solution.py:39
  70.2 22.0 %collective-permute-start.12 = (bf16[2,64,2048]{2,1,0:T(8,128)(2,1)}, bf16[2,64,2048]{2,1,0:T(8,128)(2,1)S(1)}, u32[]{:S(2)}, u32[]{:S(2)}) collective-permute-start(bf16[2,64,2048]{2,1,0:T(8,128)(2,1)} %copy-done.8), channel_id=1, source_target_pairs={{0,8},{4,12},{8,16},{12,20},{16,24},{20,28},{24,0},{28,4},{1,9},{5... | collective-permute-start | bytes 1572872 | tf_op jit(solution)/shard_map/ppermute | solution.py:26
  71.4 13.3 %collective-permute-start.15 = (bf16[8,8,32,128]{3,2,1,0:T(8,128)(2,1)S(1)}, bf16[8,8,32,128]{3,2,1,0:T(8,128)(2,1)S(1)}, u32[]{:S(2)}, u32[]{:S(2)}) collective-permute-start(bf16[8,8,32,128]{3,2,1,0:T(8,128)(2,1)S(1)} %get-tuple-element.162), channel_id=1, source_target_pairs={{0,1},{1,0},{2,3},{3,2},{4,5},{5,4},{6,7},{7,6},{8,9},{9,8},{10,11... | collective-permute-start | bytes 1572872 | tf_op jit(solution)/shard_map/ppermute | solution.py:39
  72.0 11.0 %collective-permute-start.17 = (bf16[2,8,32,128]{3,2,1,0:T(8,128)(2,1)S(1)}, bf16[2,8,32,128]{3,2,1,0:T(8,128)(2,1)S(1)}, u32[]{:S(2)}, u32[]{:S(2)}) collective-permute-start(bf16[2,8,32,128]{3,2,1,0:T(8,128)(2,1)S(1)} %get-tuple-element.164), channel_id=1, source_target_pairs={{0,1},{1,0},{2,3},{3,2},{4,5},{5,4},{6,7},{7,6},{8,9},{9,8},{10,11... | collective-permute-start | bytes 393224 | tf_op jit(solution)/shard_map/ppermute | solution.py:39
  83.0 9.2 %collective-permute-start.18 = (bf16[4,8,32,128]{3,2,1,0:T(8,128)(2,1)S(1)}, bf16[4,8,32,128]{3,2,1,0:T(8,128)(2,1)S(1)}, u32[]{:S(2)}, u32[]{:S(2)}) collective-permute-start(bf16[4,8,32,128]{3,2,1,0:T(8,128)(2,1)S(1)} %get-tuple-element.121), channel_id=1, source_target_pairs={{0,2},{1,3},{2,0},{3,1},{4,6},{5,7},{6,4},{7,5},{8,10},{9,11},{10,... | collective-permute-start | bytes 786440 | tf_op jit(solution)/shard_map/ppermute | solution.py:39
  84.7 14.9 %collective-permute-start.25 = (bf16[4,8,32,128]{3,2,1,0:T(8,128)(2,1)S(1)}, bf16[4,8,32,128]{3,2,1,0:T(8,128)(2,1)S(1)}, u32[]{:S(2)}, u32[]{:S(2)}) collective-permute-start(bf16[4,8,32,128]{3,2,1,0:T(8,128)(2,1)S(1)} %get-tuple-element.150), channel_id=1, source_target_pairs={{0,3},{1,2},{2,1},{3,0},{4,7},{5,6},{6,5},{7,4},{8,11},{9,10},{10,... | collective-permute-start | bytes 786440 | tf_op jit(solution)/shard_map/ppermute | solution.py:39
  87.6 9.3 %collective-permute-start.19 = (bf16[1,8,32,128]{3,2,1,0:T(8,128)(2,1)S(1)}, bf16[1,8,32,128]{3,2,1,0:T(8,128)(2,1)S(1)}, u32[]{:S(2)}, u32[]{:S(2)}) collective-permute-start(bf16[1,8,32,128]{3,2,1,0:T(8,128)(2,1)S(1)} %get-tuple-element.127), channel_id=1, source_target_pairs={{0,1},{1,0},{2,3},{3,2},{4,5},{5,4},{6,7},{7,6},{8,9},{9,8},{10,11... | collective-permute-start | bytes 196616 | tf_op jit(solution)/shard_map/ppermute | solution.py:39
  88.2 10.9 %collective-permute-start.20 = (bf16[1,8,32,128]{3,2,1,0:T(8,128)(2,1)S(1)}, bf16[1,8,32,128]{3,2,1,0:T(8,128)(2,1)S(1)}, u32[]{:S(2)}, u32[]{:S(2)}) collective-permute-start(bf16[1,8,32,128]{3,2,1,0:T(8,128)(2,1)S(1)} %get-tuple-element.128), channel_id=1, source_target_pairs={{0,2},{1,3},{2,0},{3,1},{4,6},{5,7},{6,4},{7,5},{8,10},{9,11},{10,... | collective-permute-start | bytes 196616 | tf_op jit(solution)/shard_map/ppermute | solution.py:39
  92.2 7.4 %collective-permute-start.21 = (bf16[1,8,32,128]{3,2,1,0:T(8,128)(2,1)S(1)}, bf16[1,8,32,128]{3,2,1,0:T(8,128)(2,1)S(1)}, u32[]{:S(2)}, u32[]{:S(2)}) collective-permute-start(bf16[1,8,32,128]{3,2,1,0:T(8,128)(2,1)S(1)} %get-tuple-element.129), channel_id=1, source_target_pairs={{0,3},{1,2},{2,1},{3,0},{4,7},{5,6},{6,5},{7,4},{8,11},{9,10},{10,... | collective-permute-start | bytes 196616 | tf_op jit(solution)/shard_map/ppermute | solution.py:39
  95.1 9.1 %collective-permute-start.22 = (bf16[1,8,32,128]{3,2,1,0:T(8,128)(2,1)S(1)}, bf16[1,8,32,128]{3,2,1,0:T(8,128)(2,1)S(1)}, u32[]{:S(2)}, u32[]{:S(2)}) collective-permute-start(bf16[1,8,32,128]{3,2,1,0:T(8,128)(2,1)S(1)} %get-tuple-element.137), channel_id=1, source_target_pairs={{0,1},{1,0},{2,3},{3,2},{4,5},{5,4},{6,7},{7,6},{8,9},{9,8},{10,11... | collective-permute-start | bytes 196616 | tf_op jit(solution)/shard_map/ppermute | solution.py:39
  97.0 7.3 %collective-permute-start.23 = (bf16[1,8,32,128]{3,2,1,0:T(8,128)(2,1)S(1)}, bf16[1,8,32,128]{3,2,1,0:T(8,128)(2,1)S(1)}, u32[]{:S(2)}, u32[]{:S(2)}) collective-permute-start(bf16[1,8,32,128]{3,2,1,0:T(8,128)(2,1)S(1)} %get-tuple-element.138), channel_id=1, source_target_pairs={{0,2},{1,3},{2,0},{3,1},{4,6},{5,7},{6,4},{7,5},{8,10},{9,11},{10,... | collective-permute-start | bytes 196616 | tf_op jit(solution)/shard_map/ppermute | solution.py:39
  99.1 5.2 %collective-permute-start.24 = (bf16[1,8,32,128]{3,2,1,0:T(8,128)(2,1)S(1)}, bf16[1,8,32,128]{3,2,1,0:T(8,128)(2,1)S(1)}, u32[]{:S(2)}, u32[]{:S(2)}) collective-permute-start(bf16[1,8,32,128]{3,2,1,0:T(8,128)(2,1)S(1)} %get-tuple-element.139), channel_id=1, source_target_pairs={{0,3},{1,2},{2,1},{3,0},{4,7},{5,6},{6,5},{7,4},{8,11},{9,10},{10,... | collective-permute-start | bytes 196616 | tf_op jit(solution)/shard_map/ppermute | solution.py:39
  (14 other events, 89.2 us)

commit v12 on v11

--- a/solution.py
+++ b/solution.py
@@ -205,6 +205,7 @@
         in_specs=[smem],
         out_specs=smem,
         name="list_open",
+        compiler_params=pltpu.CompilerParams(vmem_limit_bytes=VMEM_LIMIT),
         cost_estimate=SOON,
     )(where)
 
@@ -215,17 +216,14 @@
     density, energy, pool, tiles_out, sems = refs[2 * chips * n_chunks :]
     blocks, slots = density.shape[:2]
 
-    def copies(i, buffer):
+    def copies(i):
         return [
-            pltpu.make_async_copy(
-                tiles_out.at[buffer, kind], out.at[i], sems.at[buffer, kind]
-            )
+            pltpu.make_async_copy(tiles_out.at[i, kind], out.at[i], sems.at[i, kind])
             for kind, out in enumerate((density, energy))
         ]
 
     @pl.loop(0, blocks)
     def _(i):
-        buffer = lax.rem(i, 2)
         for other_core in range(2):
             first = other_core * per_core
             for chunk in range(n_chunks):
@@ -234,22 +232,15 @@
                         ins, chips, n_chunks, other_core, chunk, unit, i
                     )
                 first += sizes[chunk]
-
-        @pl.when(i >= 2)
-        def _():
-            for copy in copies(i - 2, buffer):
-                copy.wait()
-
         for slot in range(slots):
             where = where_ref[i, slot]
             for kind in range(2):
-                tiles_out[buffer, kind, slot] = pool[where, kind]
-
-        for copy in copies(i, buffer):
+                tiles_out[i, kind, slot] = pool[where, kind]
+        for copy in copies(i):
             copy.start()
 
-    for i in range(max(blocks - 2, 0), blocks):
-        for copy in copies(i, i % 2):
+    for i in range(blocks):
+        for copy in copies(i):
             copy.wait()
 
 
@@ -266,8 +257,8 @@
         out_specs=[pl.BlockSpec(memory_space=pl.ANY)] * 2,
         scratch_shapes=[
             pltpu.VMEM((2 * per_core, 2, strip, tile), jnp.float32),
-            pltpu.VMEM((2, 2, slots, strip, tile), jnp.float32),
-            pltpu.SemaphoreType.DMA((2, 2)),
+            pltpu.VMEM((blocks, 2, slots, strip, tile), jnp.float32),
+            pltpu.SemaphoreType.DMA((blocks, 2)),
         ],
         name="place_early",
         compiler_params=pltpu.CompilerParams(vmem_limit_bytes=VMEM_LIMIT),
@@ -361,13 +352,11 @@
 
     asks, own_weights = lax.optimization_barrier((asks, own_weights))
     weights = (own_weights, to_strip_target(own_weights, chips, 0, 1))
-    picked = list(pick(here, asks[2:3], eigvecs, sib, tile, 1))
-    here, picked[0] = lax.optimization_barrier((here, picked[0]))
-    picked = list(pick(here, asks[:2], eigvecs, sib, tile, 1)) + picked
+    picked = list(pick(here, asks[:3], eigvecs, sib, tile, 1))
     arrived = [
         shifted(value, "atoms", -offset) for value, offset in zip(picked, offsets)
     ]
-    kept_eigvecs, picked[0] = lax.optimization_barrier((eigvecs, picked[0]))
+    kept_eigvecs, picked[2] = lax.optimization_barrier((eigvecs, picked[2]))
     own, kept_sib = keep(kept_eigvecs, sib)
 
     def strips_of(arrived, paired):

time: 108 us -> 96.7 us (0.90); the launches traced: 106 us -> 96.2 us
  local copies, waits for them, and re-layouts: 6.57 us -> 0.2 us
  Pallas kernels: 46.1 us -> 40.5 us
  starting transfers between devices: 24.6 us -> 25.8 us
    unnamed x24 -> x2, local copies, waits for them, and re-layouts: 5.2 us -> 0.01 us
    ppermute x9, waiting for transfers between devices: 17.4 us -> 21.2 us  [shifted(): return lax.ppermute(value, axis, pairs)]
    ppermute x17, waiting for transfers between devices: 5.4 us -> 2.67 us  [to_strip_target(): return lax.ppermute(value, 'bands', pairs)]
    pallas_call x3 -> x2, Pallas kernels: 7.56 us -> 5.67 us  [pick(): pl.pallas_call(functools.partial(pick_kernel, count, blocks, tile, parts)...]
    pallas_call x1, Pallas kernels: 4.6 us -> 2.81 us  [place_early(): pl.pallas_call(functools.partial(place_early_kernel, chips, sizes, per_co...]
    pallas_call x5, Pallas kernels: 25.6 us -> 23.8 us  [tiles(): pl.pallas_call(functools.partial(tiles_kernel, heights, len(arrived), n_s...]
    squeeze x2, local copies, waits for them, and re-layouts: 1.29 us -> 0.11 us  [passed_on(): singles += [pair[0], to_strip_target(pair[1], chips, 0, 1)]]
  transfers between devices with their start and end apart: 26 -> 26, of which waited for: 6 -> 9; matrix products, arithmetic and copies ran while one was open for 6% -> 5% of each run, Pallas kernels for 40% -> 36%
where the time goes in v12:
time: 96.7 us; the launch traced here: 96.2 us
  Pallas kernels  40.5 us (42%)
  starting transfers between devices  25.8 us (27%)
  waiting for transfers between devices  23.8 us (25%)
  other arithmetic  4.92 us (5%)
  between operations  1 us (1%)
    pallas_call x5, Pallas kernels, tiles(): pl.pallas_call(functools.partial(tiles_kernel, heights, len(arrived), n_s...  23.8 us
    ppermute x9, waiting for transfers between devices, shifted(): return lax.ppermute(value, axis, pairs)  21.2 us
    ppermute x9, starting transfers between devices, shifted(): return lax.ppermute(value, axis, pairs)  15.2 us
    ppermute x17, starting transfers between devices, to_strip_target(): return lax.ppermute(value, 'bands', pairs)  10.6 us
    pallas_call x2, Pallas kernels, pick(): pl.pallas_call(functools.partial(pick_kernel, count, blocks, tile, parts)...  5.67 us
    pallas_call x1, Pallas kernels, keep(): pl.pallas_call(keep_kernel, out_shape=[pltpu.VMEM(own.shape, own.dtype)]...  3.48 us
    pallas_call x1, Pallas kernels, list_open(): pl.pallas_call(functools.partial(list_kernel, per_core), out_shape=jax.Sh...  2.95 us
    pallas_call x1, Pallas kernels, place_early(): pl.pallas_call(functools.partial(place_early_kernel, chips, sizes, per_co...  2.81 us
  transfers between devices with their start and end apart: 26, of which 9 were waited for; matrix products, arithmetic and copies ran while one was open for 5% of the time, Pallas kernels for 36%

profile of v12, /device:TPU:0, one launch (start us, length us, event | category | flops | bytes accessed | tf_op | source)
XLA Modules:
  0.0 96.2 jit_solution(7222820883662707111)
XLA Ops:
  1.1 2.6 %collective-permute-start.2 = (s32[8,16]{1,0:T(8,128)}, s32[8,16]{1,0:T(8,128)S(1)}, u32[]{:S(2)}, u32[]{:S(2)}) collective-permute-start(s32[8,16]{1,0:T(8,128)} %param.7), channel_id=1, source_target_pairs={{0,8},{4,12},{8,16},{12,20},{16,24},{20,28},{24,0},{28,4},{1,9},{5... | collective-permute-start | bytes 1544 | tf_op jit(solution)/shard_map/ppermute | solution.py:26
  5.3 3.2 %collective-permute-start = (s32[8,16]{1,0:T(8,128)}, s32[8,16]{1,0:T(8,128)S(1)}, u32[]{:S(2)}, u32[]{:S(2)}) collective-permute-start(s32[8,16]{1,0:T(8,128)} %param.7), channel_id=1, source_target_pairs={{0,28},{4,0},{8,4},{12,8},{16,12},{20,16},{24,20},{28,24},{1,29},{... | collective-permute-start | bytes 1544 | tf_op jit(solution)/shard_map/ppermute | solution.py:26
  10.3 2.0 %collective-permute-done.3.refs_0_ = s32[8,16]{1,0:T(8,128)S(1)} collective-permute-done((s32[8,16]{1,0:T(8,128)}, s32[8,16]{1,0:T(8,128)S(1)}, u32[]{:S(2)}, u32[]{:S(2)}) %collective-permute-start.3) | collective-permute-done | bytes 544 | tf_op jit(solution)/shard_map/ppermute | solution.py:26
  12.3 3.7 %pick_blocks.2 = (bf16[2,128,2048]{2,1,0:T(8,128)(2,1)S(1)}, bf16[2,128,2048]{2,1,0:T(8,128)(2,1)S(1)}, bf16[2,128,2048]{2,1,0:T(8,128)(2,1)}) custom-call(s32[2]{0:T(128)S(1)} %pad_add_fusion.place_ref, s32[8,16]{1,0:T(8,128)S(1)} %collective-permute-done.refs_0_, s32[8,16]{1,0:T(8,128)S(1)} %collective-permute-done.1.refs_1_, ...), custom_call_target="tpu_custom_call" | custom-call | tf_op jit(solution)/shard_map/pick_blocks/pallas_call | solution.py:73
  16.0 2.1 %collective-permute-start.8 = (bf16[2,128,2048]{2,1,0:T(8,128)(2,1)}, bf16[2,128,2048]{2,1,0:T(8,128)(2,1)S(1)}, u32[]{:S(2)}, u32[]{:S(2)}) collective-permute-start(bf16[2,128,2048]{2,1,0:T(8,128)(2,1)} %get-tuple-element.82), channel_id=1, source_target_pairs={{0,24},{4,28},{8,0},{12,4},{16,8},{20,12},{24,16},{28,20},{1,25},{... | collective-permute-start | bytes 3145736 | tf_op jit(solution)/shard_map/ppermute | solution.py:26
  19.3 3.6 %collective-permute-start.6 = (bf16[2,128,2048]{2,1,0:T(8,128)(2,1)S(1)}, bf16[2,128,2048]{2,1,0:T(8,128)(2,1)S(1)}, u32[]{:S(2)}, u32[]{:S(2)}) collective-permute-start(bf16[2,128,2048]{2,1,0:T(8,128)(2,1)S(1)} %get-tuple-element.81), channel_id=1, source_target_pairs={{0,28},{4,0},{8,4},{12,8},{16,12},{20,16},{24,20},{28,24},{1,29},{... | collective-permute-start | bytes 3145736 | tf_op jit(solution)/shard_map/ppermute | solution.py:26
  22.9 3.5 %keep.1 = (bf16[1024,2048]{1,0:T(8,128)(2,1)S(1)}, bf16[1024,2048]{1,0:T(8,128)(2,1)S(1)}) custom-call(bf16[1024,2048]{1,0:T(8,128)(2,1)} %refs_1_.1, bf16[1024,2048]{1,0:T(8,128)(2,1)} %collective-permute-done.4.refs_4_.sib.refs_2_), custom_call_target="tpu_custom_call" | custom-call | tf_op jit(solution)/shard_map/keep/pallas_call | solution.py:98
  26.4 9.8 %tiles.5 = (bf16[8,8,32,128]{3,2,1,0:T(8,128)(2,1)S(1)}, bf16[8,8,32,128]{3,2,1,0:T(8,128)(2,1)S(1)}, bf16[2,8,8,32,128]{4,3,2,1,0:T(8,128)(2,1)S(1)}) custom-call(s32[5]{0:T(128)S(1)} %stack.44.place_ref, bf16[1024,2048]{1,0:T(8,128)(2,1)S(1)} %get-tuple-element.84.refs_0_, bf16[1024,2048]{1,0:T(8,128)(2,1)S(1)} %get-tuple-element.85.refs_1_, ...), custom_call_target="tpu_custom_call" | custom-call | tf_op jit(solution)/shard_map/tiles/pallas_call | solution.py:165
  36.2 1.7 %collective-permute-start.11 = (bf16[2,8,8,32,128]{4,3,2,1,0:T(8,128)(2,1)S(1)}, bf16[2,8,8,32,128]{4,3,2,1,0:T(8,128)(2,1)S(1)}, u32[]{:S(2)}, u32[]{:S(2)}) collective-permute-start(bf16[2,8,8,32,128]{4,3,2,1,0:T(8,128)(2,1)S(1)} %get-tuple-element.100), channel_id=1, source_target_pairs={{0,2},{1,3},{2,0},{3,1},{4,6},{5,7},{6,4},{7,5},{8,10},{9,11},{10,... | collective-permute-start | bytes 3145736 | tf_op jit(solution)/shard_map/ppermute | solution.py:39
  37.9 2.0 %pick_blocks.3 = (bf16[2,64,2048]{2,1,0:T(8,128)(2,1)S(1)}, bf16[2,64,2048]{2,1,0:T(8,128)(2,1)S(1)}) custom-call(s32[2]{0:T(128)S(1)} %pad_add_fusion.place_ref, s32[8,16]{1,0:T(8,128)S(1)} %collective-permute-done.3.refs_0_, bf16[1024,2048]{1,0:T(8,128)(2,1)} %refs_1_.1, bf16[1024,2048]{1,0:T(8,128)(2,1)} %collective-permute-done.4.refs_4_.sib.refs_2_), custom_call_target="tpu_custom_call" | custom-call | tf_op jit(solution)/shard_map/pick_blocks/pallas_call | solution.py:73
  39.9 2.5 %collective-permute-done.8.refs_4_ = bf16[2,128,2048]{2,1,0:T(8,128)(2,1)S(1)} collective-permute-done((bf16[2,128,2048]{2,1,0:T(8,128)(2,1)}, bf16[2,128,2048]{2,1,0:T(8,128)(2,1)S(1)}, u32[]{:S(2)}, u32[]{:S(2)}) %collective-permute-start.8) | collective-permute-done | bytes 1048608 | tf_op jit(solution)/shard_map/ppermute | solution.py:26
  42.4 3.0 %tiles.6 = (bf16[2,8,32,128]{3,2,1,0:T(8,128)(2,1)S(1)}, bf16[2,8,32,128]{3,2,1,0:T(8,128)(2,1)S(1)}, bf16[2,2,8,32,128]{4,3,2,1,0:T(8,128)(2,1)S(1)}) custom-call(s32[5]{0:T(128)S(1)} %stack.44.place_ref, bf16[1024,2048]{1,0:T(8,128)(2,1)S(1)} %get-tuple-element.84.refs_0_, bf16[1024,2048]{1,0:T(8,128)(2,1)S(1)} %get-tuple-element.85.refs_1_, ...), custom_call_target="tpu_custom_call" | custom-call | tf_op jit(solution)/shard_map/tiles/pallas_call | solution.py:165
  47.8 2.7 %fusion.9.where_ref = s32[8,16]{1,0:T(8,128)S(1)} fusion(pred[8,16]{1,0:T(8,128)(4,1)S(1)} %get-tuple-element.159, pred[8,16]{1,0:T(8,128)(4,1)S(1)} %get-tuple-element.158, pred[8,16]{1,0:T(8,128)(4,1)S(1)} %get-tuple-element.157, pred[8,16]{1,0:T(8,128)(4,1)S(1)} %get-tuple-element.156, s32[]{:T(128)} %and.14, s32[]{:T(128)} %get-tuple-element.154, ...), kind=kLoop, calls=%fused_computation.22 | loop fusion | flops 4352 | bytes 1556 | tf_op jit(solution)/shard_map/add | solution.py:392
  50.4 3.0 %list_open.1.later = s32[129]{0:T(256)S(1)} custom-call(s32[8,16]{1,0:T(8,128)S(1)} %fusion.9.where_ref), custom_call_target="tpu_custom_call" | custom-call | tf_op jit(solution)/shard_map/list_open/pallas_call | solution.py:202
  53.5 12.0 %collective-permute-done.5.refs_4_ = bf16[2,128,2048]{2,1,0:T(8,128)(2,1)S(1)} collective-permute-done((bf16[2,128,2048]{2,1,0:T(8,128)(2,1)S(1)}, bf16[2,128,2048]{2,1,0:T(8,128)(2,1)S(1)}, u32[]{:S(2)}, u32[]{:S(2)}) %collective-permute-start.5) | collective-permute-done | bytes 1048608 | tf_op jit(solution)/shard_map/ppermute | solution.py:26
  65.4 1.7 %collective-permute-done.6.refs_5_ = bf16[2,128,2048]{2,1,0:T(8,128)(2,1)S(1)} collective-permute-done((bf16[2,128,2048]{2,1,0:T(8,128)(2,1)S(1)}, bf16[2,128,2048]{2,1,0:T(8,128)(2,1)S(1)}, u32[]{:S(2)}, u32[]{:S(2)}) %collective-permute-start.6) | collective-permute-done | bytes 1048608 | tf_op jit(solution)/shard_map/ppermute | solution.py:26
  68.6 5.3 %tiles.7 = (bf16[4,8,32,128]{3,2,1,0:T(8,128)(2,1)S(1)}, bf16[4,8,32,128]{3,2,1,0:T(8,128)(2,1)S(1)}, bf16[4,8,32,128]{3,2,1,0:T(8,128)(2,1)S(1)}, bf16[4,8,32,128]{3,2,1,0:T(8,128)(2,1)S(1)}) custom-call(s32[5]{0:T(128)S(1)} %stack.44.place_ref, bf16[1024,2048]{1,0:T(8,128)(2,1)S(1)} %get-tuple-element.84.refs_0_, ...), custom_call_target="tpu_custom_call" | custom-call | tf_op jit(solution)/shard_map/tiles/pallas_call | solution.py:165
  76.4 2.9 %tiles.8 = (bf16[1,8,32,128]{3,2,1,0:T(8,128)(2,1)S(1)}, bf16[1,8,32,128]{3,2,1,0:T(8,128)(2,1)S(1)}, bf16[1,8,32,128]{3,2,1,0:T(8,128)(2,1)S(1)}, bf16[1,8,32,128]{3,2,1,0:T(8,128)(2,1)S(1)}) custom-call(s32[5]{0:T(128)S(1)} %stack.44.place_ref, bf16[1024,2048]{1,0:T(8,128)(2,1)S(1)} %get-tuple-element.84.refs_0_, ...), custom_call_target="tpu_custom_call" | custom-call | tf_op jit(solution)/shard_map/tiles/pallas_call | solution.py:165
  79.3 1.7 %collective-permute-start.19 = (bf16[1,8,32,128]{3,2,1,0:T(8,128)(2,1)S(1)}, bf16[1,8,32,128]{3,2,1,0:T(8,128)(2,1)S(1)}, u32[]{:S(2)}, u32[]{:S(2)}) collective-permute-start(bf16[1,8,32,128]{3,2,1,0:T(8,128)(2,1)S(1)} %get-tuple-element.125), channel_id=1, source_target_pairs={{0,1},{1,0},{2,3},{3,2},{4,5},{5,4},{6,7},{7,6},{8,9},{9,8},{10,11... | collective-permute-start | bytes 196616 | tf_op jit(solution)/shard_map/ppermute | solution.py:39
  81.5 1.7 %collective-permute-done.18.refs_7_ = bf16[4,8,32,128]{3,2,1,0:T(8,128)(2,1)S(1)} collective-permute-done((bf16[4,8,32,128]{3,2,1,0:T(8,128)(2,1)S(1)}, bf16[4,8,32,128]{3,2,1,0:T(8,128)(2,1)S(1)}, u32[]{:S(2)}, u32[]{:S(2)}) %collective-permute-start.18) | collective-permute-done | bytes 262176 | tf_op jit(solution)/shard_map/ppermute | solution.py:39
  83.5 2.3 %collective-permute-done.12.refs_4_ = bf16[2,64,2048]{2,1,0:T(8,128)(2,1)S(1)} collective-permute-done((bf16[2,64,2048]{2,1,0:T(8,128)(2,1)S(1)}, bf16[2,64,2048]{2,1,0:T(8,128)(2,1)S(1)}, u32[]{:S(2)}, u32[]{:S(2)}) %collective-permute-start.12) | collective-permute-done | bytes 524320 | tf_op jit(solution)/shard_map/ppermute | solution.py:26
  85.7 2.9 %tiles.9 = (bf16[1,8,32,128]{3,2,1,0:T(8,128)(2,1)S(1)}, bf16[1,8,32,128]{3,2,1,0:T(8,128)(2,1)S(1)}, bf16[1,8,32,128]{3,2,1,0:T(8,128)(2,1)S(1)}, bf16[1,8,32,128]{3,2,1,0:T(8,128)(2,1)S(1)}) custom-call(s32[5]{0:T(128)S(1)} %stack.44.place_ref, bf16[1024,2048]{1,0:T(8,128)(2,1)S(1)} %get-tuple-element.84.refs_0_, ...), custom_call_target="tpu_custom_call" | custom-call | tf_op jit(solution)/shard_map/tiles/pallas_call | solution.py:165
  90.7 2.8 %place_early.1 = (f32[8,16,32,128]{3,2,1,0:T(8,128)}, f32[8,16,32,128]{3,2,1,0:T(8,128)}) custom-call(s32[8,16]{1,0:T(8,128)S(1)} %fusion.9.where_ref, bf16[8,8,32,128]{3,2,1,0:T(8,128)(2,1)S(1)} %get-tuple-element.138.refs_0_, bf16[4,8,32,128]{3,2,1,0:T(8,128)(2,1)S(1)} %get-tuple-element.139.refs_1_, ...), custom_call_target="tpu_custom_call" | custom-call | tf_op jit(solution)/shard_map/place_early/pallas_call | solution.py:253
  94.4 1.7 %place_late.1 = (f32[8,16,32,128]{3,2,1,0:T(8,128)}, f32[8,16,32,128]{3,2,1,0:T(8,128)}) custom-call(s32[8,16]{1,0:T(8,128)S(1)} %fusion.9.where_ref, s32[129]{0:T(256)S(1)} %list_open.1.later, bf16[1,8,32,128]{3,2,1,0:T(8,128)(2,1)S(1)} %get-tuple-element.130.refs_0_, ...), custom_call_target="tpu_custom_call", output_to_operand_aliasing={{0}: (10, {}), {1}: (11, {})} | custom-call | tf_op jit(solution)/shard_map/place_late/pallas_call | solution.py:311
  (49 shorter events, 15.1 us)
Async XLA Ops:
  0.6 11.7 %collective-permute-start.4 = (bf16[1024,2048]{1,0:T(8,128)(2,1)}, bf16[1024,2048]{1,0:T(8,128)(2,1)}, u32[]{:S(2)}, u32[]{:S(2)}) collective-permute-start(bf16[1024,2048]{1,0:T(8,128)(2,1)} %refs_1_.1), channel_id=1, source_target_pairs={{0,1},{1,0},{2,3},{3,2},{4,5},{5,4},{6,7},{7,6},{8,9},{9,8},{10,11... | collective-permute-start | bytes 12582920 | tf_op jit(solution)/shard_map/ppermute | solution.py:39
  1.1 9.2 %collective-permute-start.2 = (s32[8,16]{1,0:T(8,128)}, s32[8,16]{1,0:T(8,128)S(1)}, u32[]{:S(2)}, u32[]{:S(2)}) collective-permute-start(s32[8,16]{1,0:T(8,128)} %param.7), channel_id=1, source_target_pairs={{0,8},{4,12},{8,16},{12,20},{16,24},{20,28},{24,0},{28,4},{1,9},{5... | collective-permute-start | bytes 1544 | tf_op jit(solution)/shard_map/ppermute | solution.py:26
  3.8 6.6 %collective-permute-start.1 = (s32[8,16]{1,0:T(8,128)}, s32[8,16]{1,0:T(8,128)S(1)}, u32[]{:S(2)}, u32[]{:S(2)}) collective-permute-start(s32[8,16]{1,0:T(8,128)} %param.7), channel_id=1, source_target_pairs={{0,4},{4,8},{8,12},{12,16},{16,20},{20,24},{24,28},{28,0},{1,5},{5... | collective-permute-start | bytes 1544 | tf_op jit(solution)/shard_map/ppermute | solution.py:26
  5.3 5.1 %collective-permute-start = (s32[8,16]{1,0:T(8,128)}, s32[8,16]{1,0:T(8,128)S(1)}, u32[]{:S(2)}, u32[]{:S(2)}) collective-permute-start(s32[8,16]{1,0:T(8,128)} %param.7), channel_id=1, source_target_pairs={{0,28},{4,0},{8,4},{12,8},{16,12},{20,16},{24,20},{28,24},{1,29},{... | collective-permute-start | bytes 1544 | tf_op jit(solution)/shard_map/ppermute | solution.py:26
  16.0 26.4 %collective-permute-start.8 = (bf16[2,128,2048]{2,1,0:T(8,128)(2,1)}, bf16[2,128,2048]{2,1,0:T(8,128)(2,1)S(1)}, u32[]{:S(2)}, u32[]{:S(2)}) collective-permute-start(bf16[2,128,2048]{2,1,0:T(8,128)(2,1)} %get-tuple-element.82), channel_id=1, source_target_pairs={{0,24},{4,28},{8,0},{12,4},{16,8},{20,12},{24,16},{28,20},{1,25},{... | collective-permute-start | bytes 3145736 | tf_op jit(solution)/shard_map/ppermute | solution.py:26
  18.1 8.3 %collective-permute-start.7 = (f32[2,2048]{1,0:T(2,128)S(1)}, f32[2,2048]{1,0:T(2,128)S(1)}, u32[]{:S(2)}, u32[]{:S(2)}) collective-permute-start(f32[2,2048]{1,0:T(2,128)S(1)} %pad_maximum_fusion.refs_2_), channel_id=1, source_target_pairs={{0,1},{1,0},{2,3},{3,2},{4,5},{5,4},{6,7},{7,6},{8,9},{9,8},{10,11... | collective-permute-start | bytes 49160 | tf_op jit(solution)/shard_map/ppermute | solution.py:39
  18.2 47.2 %collective-permute-start.5 = (bf16[2,128,2048]{2,1,0:T(8,128)(2,1)S(1)}, bf16[2,128,2048]{2,1,0:T(8,128)(2,1)S(1)}, u32[]{:S(2)}, u32[]{:S(2)}) collective-permute-start(bf16[2,128,2048]{2,1,0:T(8,128)(2,1)S(1)} %get-tuple-element.80), channel_id=1, source_target_pairs={{0,4},{4,8},{8,12},{12,16},{16,20},{20,24},{24,28},{28,0},{1,5},{5... | collective-permute-start | bytes 3145736 | tf_op jit(solution)/shard_map/ppermute | solution.py:26
  19.3 47.8 %collective-permute-start.6 = (bf16[2,128,2048]{2,1,0:T(8,128)(2,1)S(1)}, bf16[2,128,2048]{2,1,0:T(8,128)(2,1)S(1)}, u32[]{:S(2)}, u32[]{:S(2)}) collective-permute-start(bf16[2,128,2048]{2,1,0:T(8,128)(2,1)S(1)} %get-tuple-element.81), channel_id=1, source_target_pairs={{0,28},{4,0},{8,4},{12,8},{16,12},{20,16},{24,20},{28,24},{1,29},{... | collective-permute-start | bytes 3145736 | tf_op jit(solution)/shard_map/ppermute | solution.py:26
  36.2 30.9 %collective-permute-start.11 = (bf16[2,8,8,32,128]{4,3,2,1,0:T(8,128)(2,1)S(1)}, bf16[2,8,8,32,128]{4,3,2,1,0:T(8,128)(2,1)S(1)}, u32[]{:S(2)}, u32[]{:S(2)}) collective-permute-start(bf16[2,8,8,32,128]{4,3,2,1,0:T(8,128)(2,1)S(1)} %get-tuple-element.100), channel_id=1, source_target_pairs={{0,2},{1,3},{2,0},{3,1},{4,6},{5,7},{6,4},{7,5},{8,10},{9,11},{10,... | collective-permute-start | bytes 3145736 | tf_op jit(solution)/shard_map/ppermute | solution.py:39
  37.9 15.4 %collective-permute-start.10 = (bf16[8,8,32,128]{3,2,1,0:T(8,128)(2,1)S(1)}, bf16[8,8,32,128]{3,2,1,0:T(8,128)(2,1)S(1)}, u32[]{:S(2)}, u32[]{:S(2)}) collective-permute-start(bf16[8,8,32,128]{3,2,1,0:T(8,128)(2,1)S(1)} %get-tuple-element.99), channel_id=1, source_target_pairs={{0,1},{1,0},{2,3},{3,2},{4,5},{5,4},{6,7},{7,6},{8,9},{9,8},{10,11... | collective-permute-start | bytes 1572872 | tf_op jit(solution)/shard_map/ppermute | solution.py:39
  45.4 21.7 %collective-permute-start.9 = (bf16[2,2,8,32,128]{4,3,2,1,0:T(8,128)(2,1)S(1)}, bf16[2,2,8,32,128]{4,3,2,1,0:T(8,128)(2,1)S(1)}, u32[]{:S(2)}, u32[]{:S(2)}) collective-permute-start(bf16[2,2,8,32,128]{4,3,2,1,0:T(8,128)(2,1)S(1)} %get-tuple-element.97), channel_id=1, source_target_pairs={{0,2},{1,3},{2,0},{3,1},{4,6},{5,7},{6,4},{7,5},{8,10},{9,11},{10,... | collective-permute-start | bytes 786440 | tf_op jit(solution)/shard_map/ppermute | solution.py:39
  53.4 23.0 %collective-permute-start.13 = (bf16[2,64,2048]{2,1,0:T(8,128)(2,1)S(1)}, bf16[2,64,2048]{2,1,0:T(8,128)(2,1)S(1)}, u32[]{:S(2)}, u32[]{:S(2)}) collective-permute-start(bf16[2,64,2048]{2,1,0:T(8,128)(2,1)S(1)} %get-tuple-element.101), channel_id=1, source_target_pairs={{0,8},{4,12},{8,16},{12,20},{16,24},{20,28},{24,0},{28,4},{1,9},{5... | collective-permute-start | bytes 1572872 | tf_op jit(solution)/shard_map/ppermute | solution.py:26
  67.1 6.8 %collective-permute-start.16 = (bf16[2,8,32,128]{3,2,1,0:T(8,128)(2,1)S(1)}, bf16[2,8,32,128]{3,2,1,0:T(8,128)(2,1)S(1)}, u32[]{:S(2)}, u32[]{:S(2)}) collective-permute-start(bf16[2,8,32,128]{3,2,1,0:T(8,128)(2,1)S(1)} %get-tuple-element.113), channel_id=1, source_target_pairs={{0,1},{1,0},{2,3},{3,2},{4,5},{5,4},{6,7},{7,6},{8,9},{9,8},{10,11... | collective-permute-start | bytes 393224 | tf_op jit(solution)/shard_map/ppermute | solution.py:39
  67.1 18.6 %collective-permute-start.12 = (bf16[2,64,2048]{2,1,0:T(8,128)(2,1)S(1)}, bf16[2,64,2048]{2,1,0:T(8,128)(2,1)S(1)}, u32[]{:S(2)}, u32[]{:S(2)}) collective-permute-start(bf16[2,64,2048]{2,1,0:T(8,128)(2,1)S(1)} %get-tuple-element.104), channel_id=1, source_target_pairs={{0,8},{4,12},{8,16},{12,20},{16,24},{20,28},{24,0},{28,4},{1,9},{5... | collective-permute-start | bytes 1572872 | tf_op jit(solution)/shard_map/ppermute | solution.py:26
  67.9 8.4 %collective-permute-start.15 = (bf16[8,8,32,128]{3,2,1,0:T(8,128)(2,1)S(1)}, bf16[8,8,32,128]{3,2,1,0:T(8,128)(2,1)S(1)}, u32[]{:S(2)}, u32[]{:S(2)}) collective-permute-start(bf16[8,8,32,128]{3,2,1,0:T(8,128)(2,1)S(1)} %get-tuple-element.160), channel_id=1, source_target_pairs={{0,1},{1,0},{2,3},{3,2},{4,5},{5,4},{6,7},{7,6},{8,9},{9,8},{10,11... | collective-permute-start | bytes 1572872 | tf_op jit(solution)/shard_map/ppermute | solution.py:39
  68.0 5.9 %collective-permute-start.17 = (bf16[2,8,32,128]{3,2,1,0:T(8,128)(2,1)S(1)}, bf16[2,8,32,128]{3,2,1,0:T(8,128)(2,1)S(1)}, u32[]{:S(2)}, u32[]{:S(2)}) collective-permute-start(bf16[2,8,32,128]{3,2,1,0:T(8,128)(2,1)S(1)} %get-tuple-element.162), channel_id=1, source_target_pairs={{0,1},{1,0},{2,3},{3,2},{4,5},{5,4},{6,7},{7,6},{8,9},{9,8},{10,11... | collective-permute-start | bytes 393224 | tf_op jit(solution)/shard_map/ppermute | solution.py:39
  74.0 9.2 %collective-permute-start.18 = (bf16[4,8,32,128]{3,2,1,0:T(8,128)(2,1)S(1)}, bf16[4,8,32,128]{3,2,1,0:T(8,128)(2,1)S(1)}, u32[]{:S(2)}, u32[]{:S(2)}) collective-permute-start(bf16[4,8,32,128]{3,2,1,0:T(8,128)(2,1)S(1)} %get-tuple-element.119), channel_id=1, source_target_pairs={{0,2},{1,3},{2,0},{3,1},{4,6},{5,7},{6,4},{7,5},{8,10},{9,11},{10,... | collective-permute-start | bytes 786440 | tf_op jit(solution)/shard_map/ppermute | solution.py:39
  76.3 14.3 %collective-permute-start.25 = (bf16[4,8,32,128]{3,2,1,0:T(8,128)(2,1)S(1)}, bf16[4,8,32,128]{3,2,1,0:T(8,128)(2,1)S(1)}, u32[]{:S(2)}, u32[]{:S(2)}) collective-permute-start(bf16[4,8,32,128]{3,2,1,0:T(8,128)(2,1)S(1)} %get-tuple-element.148), channel_id=1, source_target_pairs={{0,3},{1,2},{2,1},{3,0},{4,7},{5,6},{6,5},{7,4},{8,11},{9,10},{10,... | collective-permute-start | bytes 786440 | tf_op jit(solution)/shard_map/ppermute | solution.py:39
  79.3 9.4 %collective-permute-start.19 = (bf16[1,8,32,128]{3,2,1,0:T(8,128)(2,1)S(1)}, bf16[1,8,32,128]{3,2,1,0:T(8,128)(2,1)S(1)}, u32[]{:S(2)}, u32[]{:S(2)}) collective-permute-start(bf16[1,8,32,128]{3,2,1,0:T(8,128)(2,1)S(1)} %get-tuple-element.125), channel_id=1, source_target_pairs={{0,1},{1,0},{2,3},{3,2},{4,5},{5,4},{6,7},{7,6},{8,9},{9,8},{10,11... | collective-permute-start | bytes 196616 | tf_op jit(solution)/shard_map/ppermute | solution.py:39
  81.0 9.3 %collective-permute-start.20 = (bf16[1,8,32,128]{3,2,1,0:T(8,128)(2,1)S(1)}, bf16[1,8,32,128]{3,2,1,0:T(8,128)(2,1)S(1)}, u32[]{:S(2)}, u32[]{:S(2)}) collective-permute-start(bf16[1,8,32,128]{3,2,1,0:T(8,128)(2,1)S(1)} %get-tuple-element.126), channel_id=1, source_target_pairs={{0,2},{1,3},{2,0},{3,1},{4,6},{5,7},{6,4},{7,5},{8,10},{9,11},{10,... | collective-permute-start | bytes 196616 | tf_op jit(solution)/shard_map/ppermute | solution.py:39
  83.2 7.5 %collective-permute-start.21 = (bf16[1,8,32,128]{3,2,1,0:T(8,128)(2,1)S(1)}, bf16[1,8,32,128]{3,2,1,0:T(8,128)(2,1)S(1)}, u32[]{:S(2)}, u32[]{:S(2)}) collective-permute-start(bf16[1,8,32,128]{3,2,1,0:T(8,128)(2,1)S(1)} %get-tuple-element.127), channel_id=1, source_target_pairs={{0,3},{1,2},{2,1},{3,0},{4,7},{5,6},{6,5},{7,4},{8,11},{9,10},{10,... | collective-permute-start | bytes 196616 | tf_op jit(solution)/shard_map/ppermute | solution.py:39
  88.6 4.9 %collective-permute-start.22 = (bf16[1,8,32,128]{3,2,1,0:T(8,128)(2,1)S(1)}, bf16[1,8,32,128]{3,2,1,0:T(8,128)(2,1)S(1)}, u32[]{:S(2)}, u32[]{:S(2)}) collective-permute-start(bf16[1,8,32,128]{3,2,1,0:T(8,128)(2,1)S(1)} %get-tuple-element.135), channel_id=1, source_target_pairs={{0,1},{1,0},{2,3},{3,2},{4,5},{5,4},{6,7},{7,6},{8,9},{9,8},{10,11... | collective-permute-start | bytes 196616 | tf_op jit(solution)/shard_map/ppermute | solution.py:39
  88.7 4.8 %collective-permute-start.23 = (bf16[1,8,32,128]{3,2,1,0:T(8,128)(2,1)S(1)}, bf16[1,8,32,128]{3,2,1,0:T(8,128)(2,1)S(1)}, u32[]{:S(2)}, u32[]{:S(2)}) collective-permute-start(bf16[1,8,32,128]{3,2,1,0:T(8,128)(2,1)S(1)} %get-tuple-element.136), channel_id=1, source_target_pairs={{0,2},{1,3},{2,0},{3,1},{4,6},{5,7},{6,4},{7,5},{8,10},{9,11},{10,... | collective-permute-start | bytes 196616 | tf_op jit(solution)/shard_map/ppermute | solution.py:39
  90.3 4.1 %collective-permute-start.24 = (bf16[1,8,32,128]{3,2,1,0:T(8,128)(2,1)S(1)}, bf16[1,8,32,128]{3,2,1,0:T(8,128)(2,1)S(1)}, u32[]{:S(2)}, u32[]{:S(2)}) collective-permute-start(bf16[1,8,32,128]{3,2,1,0:T(8,128)(2,1)S(1)} %get-tuple-element.137), channel_id=1, source_target_pairs={{0,3},{1,2},{2,1},{3,0},{4,7},{5,6},{6,5},{7,4},{8,11},{9,10},{10,... | collective-permute-start | bytes 196616 | tf_op jit(solution)/shard_map/ppermute | solution.py:39
  (3 other events, 10.9 us)

commit v13 on v12

--- a/solution.py
+++ b/solution.py
@@ -189,19 +189,23 @@
 def list_kernel(per_core, where_ref, later):
     blocks, slots = where_ref.shape
 
-    def step(entry, count):
-        where = where_ref[lax.div(entry, slots), lax.rem(entry, slots)]
-        later[count + 1] = entry
-        return count + (lax.rem(where, per_core) == per_core - 1).astype(jnp.int32)
-
-    later[0] = lax.fori_loop(0, blocks * slots, step, 0)
+    def block(i, count):
+        for slot in range(slots):
+            where = where_ref[i, slot]
+            other_core = (where >= per_core).astype(jnp.int32)
+            later[2 * count + 1] = i * slots + slot
+            later[2 * count + 2] = other_core * blocks + i
+            count += (where - other_core * per_core == per_core - 1).astype(jnp.int32)
+        return count
+
+    later[0] = lax.fori_loop(0, blocks, block, 0)
 
 
 def list_open(where, per_core):
     smem = pl.BlockSpec(memory_space=pltpu.SMEM)
     return pl.pallas_call(
         functools.partial(list_kernel, per_core),
-        out_shape=jax.ShapeDtypeStruct((where.size + 1,), jnp.int32),
+        out_shape=jax.ShapeDtypeStruct((2 * where.size + 1,), jnp.int32),
         in_specs=[smem],
         out_specs=smem,
         name="list_open",
@@ -214,11 +218,13 @@
     n_chunks = len(sizes)
     ins = refs[: 2 * chips * n_chunks]
     density, energy, pool, tiles_out, sems = refs[2 * chips * n_chunks :]
-    blocks, slots = density.shape[:2]
+    blocks, slots = where_ref.shape
 
     def copies(i):
         return [
-            pltpu.make_async_copy(tiles_out.at[i, kind], out.at[i], sems.at[i, kind])
+            pltpu.make_async_copy(
+                tiles_out.at[i, kind], out.at[pl.ds(i * slots, slots)], sems.at[i, kind]
+            )
             for kind, out in enumerate((density, energy))
         ]
 
@@ -247,7 +253,7 @@
 def place_early(where, strips, sizes, chips, per_core):
     _, blocks, strip, tile = strips[0][0].shape
     slots = where.shape[1]
-    out = jax.ShapeDtypeStruct((blocks, slots, strip, tile), jnp.float32)
+    out = jax.ShapeDtypeStruct((blocks * slots, strip, tile), jnp.float32)
     flat = [value for group in strips for value in group]
     smem = pl.BlockSpec(memory_space=pltpu.SMEM)
     return pl.pallas_call(
@@ -266,64 +272,59 @@
     )(where, *flat)
 
 
-def place_late_kernel(chips, per_core, where_ref, later, *refs):
+def place_late_kernel(chips, later, *refs):
     lower, upper = refs[: 2 * chips], refs[2 * chips : 4 * chips]
     density, energy, pool, sems = refs[4 * chips + 2 :]
-    blocks, slots = density.shape[:2]
-    cut = density.shape[3] // 2
-    unit = lower[0].shape[0] - 1
+    blocks = pool.shape[0] // 2
+    cut = density.shape[2] // 2
     for other_core in range(2):
         for i in range(blocks):
-            low = strip_sum(lower, chips, 1, other_core, 0, unit, i)
+            low = strip_sum(lower, chips, 1, other_core, 0, 0, i)
             high = strip_sum(upper, chips, 1, other_core, 0, 0, i)
-            pool[other_core, i, 0] = jnp.concatenate([low[:, :cut], high[:, :cut]], 1)
-            pool[other_core, i, 1] = jnp.concatenate([low[:, cut:], high[:, cut:]], 1)
+            spot = other_core * blocks + i
+            pool[spot, 0] = jnp.concatenate([low[:, :cut], high[:, :cut]], 1)
+            pool[spot, 1] = jnp.concatenate([low[:, cut:], high[:, cut:]], 1)
     count = later[0]
 
-    def copies(n):
-        entry = jnp.clip(later[n + 1], 0, blocks * slots - 1)
-        i, slot = lax.div(entry, slots), lax.rem(entry, slots)
-        other_core = jnp.clip(lax.div(where_ref[i, slot], per_core), 0, 1)
+    def copies(source, target):
         return [
-            pltpu.make_async_copy(
-                pool.at[other_core, i, kind], out.at[i, slot], sems.at[kind]
-            )
+            pltpu.make_async_copy(pool.at[source, kind], out.at[target], sems.at[kind])
             for kind, out in enumerate((density, energy))
         ]
 
     @pl.loop(0, count)
     def _(n):
-        for copy in copies(n):
+        for copy in copies(later[2 * n + 2], later[2 * n + 1]):
             copy.start()
 
     @pl.loop(0, count)
     def _(n):
-        for copy in copies(n):
+        for copy in copies(0, 0):
             copy.wait()
 
 
-def place_late(where, later, lower, upper, density, energy, chips, per_core):
-    blocks, _, strip, tile = density.shape
+def place_late(later, lower, upper, density, energy, chips):
+    _, blocks, strip, tile = upper[0].shape
     smem = pl.BlockSpec(memory_space=pltpu.SMEM)
     anywhere = pl.BlockSpec(memory_space=pl.ANY)
     out = jax.ShapeDtypeStruct(density.shape, density.dtype)
     strips = [*lower, *upper]
     return pl.pallas_call(
-        functools.partial(place_late_kernel, chips, per_core),
+        functools.partial(place_late_kernel, chips),
         out_shape=[out, out],
-        in_specs=[smem, smem]
+        in_specs=[smem]
         + [pl.BlockSpec(memory_space=pltpu.VMEM)] * len(strips)
         + [anywhere] * 2,
         out_specs=[anywhere] * 2,
         scratch_shapes=[
-            pltpu.VMEM((2, blocks, 2, strip, tile), jnp.float32),
+            pltpu.VMEM((2 * blocks, 2, strip, tile), jnp.float32),
             pltpu.SemaphoreType.DMA((2,)),
         ],
-        input_output_aliases={2 + len(strips): 0, 3 + len(strips): 1},
+        input_output_aliases={1 + len(strips): 0, 2 + len(strips): 1},
         name="place_late",
         compiler_params=pltpu.CompilerParams(vmem_limit_bytes=VMEM_LIMIT),
         cost_estimate=SOON,
-    )(where, later, *strips, density, energy)
+    )(later, *strips, density, energy)
 
 
 def body(eigvecs, occupations, energies, neighbours):
@@ -352,11 +353,13 @@
 
     asks, own_weights = lax.optimization_barrier((asks, own_weights))
     weights = (own_weights, to_strip_target(own_weights, chips, 0, 1))
-    picked = list(pick(here, asks[:3], eigvecs, sib, tile, 1))
+    picked = list(pick(here, asks[2:3], eigvecs, sib, tile, 1))
+    here, picked[0] = lax.optimization_barrier((here, picked[0]))
+    picked = list(pick(here, asks[:2], eigvecs, sib, tile, 1)) + picked
     arrived = [
         shifted(value, "atoms", -offset) for value, offset in zip(picked, offsets)
     ]
-    kept_eigvecs, picked[2] = lax.optimization_barrier((eigvecs, picked[2]))
+    kept_eigvecs, picked[0] = lax.optimization_barrier((eigvecs, picked[0]))
     own, kept_sib = keep(kept_eigvecs, sib)
 
     def strips_of(arrived, paired):
@@ -423,7 +426,8 @@
     strips = list(zip(local, direct, far))
     sizes = [half_blocks, 2, 1]
     density, energy = place_early(where, strips, sizes, chips, per_core)
-    return place_late(where, later, lower, last, density, energy, chips, per_core)
+    outs = place_late(later, lower, last, density, energy, chips)
+    return tuple(out.reshape(*where.shape, *out.shape[1:]) for out in outs)
 
 
 def solution(mesh):

time: 96.7 us -> 97.1 us (level)
  waiting for transfers between devices: 23.8 us -> 25.7 us
    ppermute x17, waiting for transfers between devices: 2.67 us -> 5.89 us  [to_strip_target(): return lax.ppermute(value, 'bands', pairs)]
    ppermute x9, waiting for transfers between devices: 21.2 us -> 19.8 us  [shifted(): return lax.ppermute(value, axis, pairs)]
    pallas_call x1, Pallas kernels: 2.95 us -> 1.89 us  [list_open(): pl.pallas_call(functools.partial(list_kernel, per_core), out_shape=jax.Sh...]
    pallas_call x2 -> x3, Pallas kernels: 5.67 us -> 6.23 us  [pick(): pl.pallas_call(functools.partial(pick_kernel, count, blocks, tile, parts)...]
  transfers between devices with their start and end apart: 26 -> 26, of which waited for: 9 -> 7; matrix products, arithmetic and copies ran while one was open for 5% -> 5% of each run, Pallas kernels for 36% -> 38%
where the time goes in v13:
time: 97.1 us; the launch traced here: 96.7 us
  Pallas kernels  39.8 us (41%)
  waiting for transfers between devices  25.7 us (26%)
  starting transfers between devices  25.2 us (26%)
  other arithmetic  4.83 us (5%)
  between operations  1 us (1%)
    pallas_call x5, Pallas kernels, tiles(): pl.pallas_call(functools.partial(tiles_kernel, heights, len(arrived), n_s...  23.8 us
    ppermute x9, waiting for transfers between devices, shifted(): return lax.ppermute(value, axis, pairs)  19.8 us
    ppermute x9, starting transfers between devices, shifted(): return lax.ppermute(value, axis, pairs)  14.9 us
    ppermute x17, starting transfers between devices, to_strip_target(): return lax.ppermute(value, 'bands', pairs)  10.3 us
    pallas_call x3, Pallas kernels, pick(): pl.pallas_call(functools.partial(pick_kernel, count, blocks, tile, parts)...  6.23 us
    ppermute x17, waiting for transfers between devices, to_strip_target(): return lax.ppermute(value, 'bands', pairs)  5.89 us
    pallas_call x1, Pallas kernels, keep(): pl.pallas_call(keep_kernel, out_shape=[pltpu.VMEM(own.shape, own.dtype)]...  3.48 us
    pallas_call x1, Pallas kernels, place_early(): pl.pallas_call(functools.partial(place_early_kernel, chips, sizes, per_co...  2.81 us
  transfers between devices with their start and end apart: 26, of which 7 were waited for; matrix products, arithmetic and copies ran while one was open for 5% of the time, Pallas kernels for 38%

profile of v13, /device:TPU:0, one launch (start us, length us, event | category | flops | bytes accessed | tf_op | source)
XLA Modules:
  0.0 96.7 jit_solution(6077335573791708629)
XLA Ops:
  1.1 2.6 %collective-permute-start.2 = (s32[8,16]{1,0:T(8,128)}, s32[8,16]{1,0:T(8,128)S(1)}, u32[]{:S(2)}, u32[]{:S(2)}) collective-permute-start(s32[8,16]{1,0:T(8,128)} %param.7), channel_id=1, source_target_pairs={{0,8},{4,12},{8,16},{12,20},{16,24},{20,28},{24,0},{28,4},{1,9},{5... | collective-permute-start | bytes 1544 | tf_op jit(solution)/shard_map/ppermute | solution.py:26
  5.3 3.2 %collective-permute-start = (s32[8,16]{1,0:T(8,128)}, s32[8,16]{1,0:T(8,128)S(1)}, u32[]{:S(2)}, u32[]{:S(2)}) collective-permute-start(s32[8,16]{1,0:T(8,128)} %param.7), channel_id=1, source_target_pairs={{0,28},{4,0},{8,4},{12,8},{16,12},{20,16},{24,20},{28,24},{1,29},{... | collective-permute-start | bytes 1544 | tf_op jit(solution)/shard_map/ppermute | solution.py:26
  10.3 2.0 %collective-permute-done.3.refs_0_ = s32[8,16]{1,0:T(8,128)S(1)} collective-permute-done((s32[8,16]{1,0:T(8,128)}, s32[8,16]{1,0:T(8,128)S(1)}, u32[]{:S(2)}, u32[]{:S(2)}) %collective-permute-start.3) | collective-permute-done | bytes 544 | tf_op jit(solution)/shard_map/ppermute | solution.py:26
  12.3 2.0 %pick_blocks.3 = bf16[2,128,2048]{2,1,0:T(8,128)(2,1)S(1)} custom-call(s32[2]{0:T(128)S(1)} %pad_add_fusion.place_ref, s32[8,16]{1,0:T(8,128)S(1)} %collective-permute-done.2.refs_0_, bf16[1024,2048]{1,0:T(8,128)(2,1)} %refs_1_.3, bf16[1024,2048]{1,0:T(8,128)(2,1)} %collective-permute-done.4.refs_2_.refs_3_.sib), custom_call_target="tpu_custom_call" | custom-call | tf_op jit(solution)/shard_map/pick_blocks/pallas_call | solution.py:73
  14.3 2.2 %collective-permute-start.8 = (bf16[2,128,2048]{2,1,0:T(8,128)(2,1)S(1)}, bf16[2,128,2048]{2,1,0:T(8,128)(2,1)S(1)}, u32[]{:S(2)}, u32[]{:S(2)}) collective-permute-start(bf16[2,128,2048]{2,1,0:T(8,128)(2,1)S(1)} %pick_blocks.3), channel_id=1, source_target_pairs={{0,24},{4,28},{8,0},{12,4},{16,8},{20,12},{24,16},{28,20},{1,25},{... | collective-permute-start | bytes 3145736 | tf_op jit(solution)/shard_map/ppermute | solution.py:26
  16.6 2.3 %pick_blocks.4 = (bf16[2,128,2048]{2,1,0:T(8,128)(2,1)S(1)}, bf16[2,128,2048]{2,1,0:T(8,128)(2,1)S(1)}) custom-call(s32[2]{0:T(128)S(1)} %pad_add_fusion.place_ref, s32[8,16]{1,0:T(8,128)S(1)} %collective-permute-done.refs_0_, s32[8,16]{1,0:T(8,128)S(1)} %collective-permute-done.1.refs_1_, bf16[1024,2048]{1,0:T(8,128)(2,1)} %refs_1_.3, ...), custom_call_target="tpu_custom_call" | custom-call | tf_op jit(solution)/shard_map/pick_blocks/pallas_call | solution.py:73
  20.1 3.6 %collective-permute-start.6 = (bf16[2,128,2048]{2,1,0:T(8,128)(2,1)S(1)}, bf16[2,128,2048]{2,1,0:T(8,128)(2,1)S(1)}, u32[]{:S(2)}, u32[]{:S(2)}) collective-permute-start(bf16[2,128,2048]{2,1,0:T(8,128)(2,1)S(1)} %get-tuple-element.85), channel_id=1, source_target_pairs={{0,28},{4,0},{8,4},{12,8},{16,12},{20,16},{24,20},{28,24},{1,29},{... | collective-permute-start | bytes 3145736 | tf_op jit(solution)/shard_map/ppermute | solution.py:26
  23.6 3.5 %keep.1 = (bf16[1024,2048]{1,0:T(8,128)(2,1)S(1)}, bf16[1024,2048]{1,0:T(8,128)(2,1)S(1)}) custom-call(bf16[1024,2048]{1,0:T(8,128)(2,1)} %refs_1_.3, bf16[1024,2048]{1,0:T(8,128)(2,1)} %collective-permute-done.4.refs_2_.refs_3_.sib), custom_call_target="tpu_custom_call" | custom-call | tf_op jit(solution)/shard_map/keep/pallas_call | solution.py:98
  27.1 9.8 %tiles.5 = (bf16[8,8,32,128]{3,2,1,0:T(8,128)(2,1)S(1)}, bf16[8,8,32,128]{3,2,1,0:T(8,128)(2,1)S(1)}, bf16[2,8,8,32,128]{4,3,2,1,0:T(8,128)(2,1)S(1)}) custom-call(s32[5]{0:T(128)S(1)} %stack.44.place_ref, bf16[1024,2048]{1,0:T(8,128)(2,1)S(1)} %get-tuple-element.87.refs_0_, bf16[1024,2048]{1,0:T(8,128)(2,1)S(1)} %get-tuple-element.88.refs_1_, ...), custom_call_target="tpu_custom_call" | custom-call | tf_op jit(solution)/shard_map/tiles/pallas_call | solution.py:165
  36.9 1.7 %collective-permute-start.11 = (bf16[2,8,8,32,128]{4,3,2,1,0:T(8,128)(2,1)S(1)}, bf16[2,8,8,32,128]{4,3,2,1,0:T(8,128)(2,1)S(1)}, u32[]{:S(2)}, u32[]{:S(2)}) collective-permute-start(bf16[2,8,8,32,128]{4,3,2,1,0:T(8,128)(2,1)S(1)} %get-tuple-element.104), channel_id=1, source_target_pairs={{0,2},{1,3},{2,0},{3,1},{4,6},{5,7},{6,4},{7,5},{8,10},{9,11},{10,... | collective-permute-start | bytes 3145736 | tf_op jit(solution)/shard_map/ppermute | solution.py:39
  38.7 2.0 %pick_blocks.5 = (bf16[2,64,2048]{2,1,0:T(8,128)(2,1)S(1)}, bf16[2,64,2048]{2,1,0:T(8,128)(2,1)S(1)}) custom-call(s32[2]{0:T(128)S(1)} %pad_add_fusion.place_ref, s32[8,16]{1,0:T(8,128)S(1)} %collective-permute-done.3.refs_0_, bf16[1024,2048]{1,0:T(8,128)(2,1)} %refs_1_.3, bf16[1024,2048]{1,0:T(8,128)(2,1)} %collective-permute-done.4.refs_2_.refs_3_.sib), custom_call_target="tpu_custom_call" | custom-call | tf_op jit(solution)/shard_map/pick_blocks/pallas_call | solution.py:73
  40.7 3.0 %tiles.6 = (bf16[2,8,32,128]{3,2,1,0:T(8,128)(2,1)S(1)}, bf16[2,8,32,128]{3,2,1,0:T(8,128)(2,1)S(1)}, bf16[2,2,8,32,128]{4,3,2,1,0:T(8,128)(2,1)S(1)}) custom-call(s32[5]{0:T(128)S(1)} %stack.44.place_ref, bf16[1024,2048]{1,0:T(8,128)(2,1)S(1)} %get-tuple-element.87.refs_0_, bf16[1024,2048]{1,0:T(8,128)(2,1)S(1)} %get-tuple-element.88.refs_1_, ...), custom_call_target="tpu_custom_call" | custom-call | tf_op jit(solution)/shard_map/tiles/pallas_call | solution.py:165
  45.8 2.6 %fusion.9.where_ref = s32[8,16]{1,0:T(8,128)S(1)} fusion(pred[8,16]{1,0:T(8,128)(4,1)S(1)} %get-tuple-element.165, pred[8,16]{1,0:T(8,128)(4,1)S(1)} %get-tuple-element.164, pred[8,16]{1,0:T(8,128)(4,1)S(1)} %get-tuple-element.163, pred[8,16]{1,0:T(8,128)(4,1)S(1)} %get-tuple-element.162, s32[]{:T(128)} %and.14, s32[]{:T(128)} %get-tuple-element.160, ...), kind=kLoop, calls=%fused_computation.22 | loop fusion | flops 4352 | bytes 1556 | tf_op jit(solution)/shard_map/add | solution.py:395
  48.4 1.9 %list_open.1.later = s32[257]{0:T(512)S(1)} custom-call(s32[8,16]{1,0:T(8,128)S(1)} %fusion.9.where_ref), custom_call_target="tpu_custom_call" | custom-call | tf_op jit(solution)/shard_map/list_open/pallas_call | solution.py:206
  50.4 17.5 %collective-permute-done.6.refs_5_ = bf16[2,128,2048]{2,1,0:T(8,128)(2,1)S(1)} collective-permute-done((bf16[2,128,2048]{2,1,0:T(8,128)(2,1)S(1)}, bf16[2,128,2048]{2,1,0:T(8,128)(2,1)S(1)}, u32[]{:S(2)}, u32[]{:S(2)}) %collective-permute-start.6) | collective-permute-done | bytes 1048608 | tf_op jit(solution)/shard_map/ppermute | solution.py:26
  68.9 5.3 %tiles.7 = (bf16[4,8,32,128]{3,2,1,0:T(8,128)(2,1)S(1)}, bf16[4,8,32,128]{3,2,1,0:T(8,128)(2,1)S(1)}, bf16[4,8,32,128]{3,2,1,0:T(8,128)(2,1)S(1)}, bf16[4,8,32,128]{3,2,1,0:T(8,128)(2,1)S(1)}) custom-call(s32[5]{0:T(128)S(1)} %stack.44.place_ref, bf16[1024,2048]{1,0:T(8,128)(2,1)S(1)} %get-tuple-element.87.refs_0_, ...), custom_call_target="tpu_custom_call" | custom-call | tf_op jit(solution)/shard_map/tiles/pallas_call | solution.py:165
  74.5 1.5 %collective-permute-start.18 = (bf16[4,8,32,128]{3,2,1,0:T(8,128)(2,1)S(1)}, bf16[4,8,32,128]{3,2,1,0:T(8,128)(2,1)S(1)}, u32[]{:S(2)}, u32[]{:S(2)}) collective-permute-start(bf16[4,8,32,128]{3,2,1,0:T(8,128)(2,1)S(1)} %get-tuple-element.124), channel_id=1, source_target_pairs={{0,2},{1,3},{2,0},{3,1},{4,6},{5,7},{6,4},{7,5},{8,10},{9,11},{10,... | collective-permute-start | bytes 786440 | tf_op jit(solution)/shard_map/ppermute | solution.py:39
  76.2 2.9 %tiles.8 = (bf16[1,8,32,128]{3,2,1,0:T(8,128)(2,1)S(1)}, bf16[1,8,32,128]{3,2,1,0:T(8,128)(2,1)S(1)}, bf16[1,8,32,128]{3,2,1,0:T(8,128)(2,1)S(1)}, bf16[1,8,32,128]{3,2,1,0:T(8,128)(2,1)S(1)}) custom-call(s32[5]{0:T(128)S(1)} %stack.44.place_ref, bf16[1024,2048]{1,0:T(8,128)(2,1)S(1)} %get-tuple-element.87.refs_0_, ...), custom_call_target="tpu_custom_call" | custom-call | tf_op jit(solution)/shard_map/tiles/pallas_call | solution.py:165
  79.7 1.5 %collective-permute-start.20 = (bf16[1,8,32,128]{3,2,1,0:T(8,128)(2,1)S(1)}, bf16[1,8,32,128]{3,2,1,0:T(8,128)(2,1)S(1)}, u32[]{:S(2)}, u32[]{:S(2)}) collective-permute-start(bf16[1,8,32,128]{3,2,1,0:T(8,128)(2,1)S(1)} %get-tuple-element.131), channel_id=1, source_target_pairs={{0,2},{1,3},{2,0},{3,1},{4,6},{5,7},{6,4},{7,5},{8,10},{9,11},{10,... | collective-permute-start | bytes 196616 | tf_op jit(solution)/shard_map/ppermute | solution.py:39
  81.2 2.5 %collective-permute-done.18.refs_7_ = bf16[4,8,32,128]{3,2,1,0:T(8,128)(2,1)S(1)} collective-permute-done((bf16[4,8,32,128]{3,2,1,0:T(8,128)(2,1)S(1)}, bf16[4,8,32,128]{3,2,1,0:T(8,128)(2,1)S(1)}, u32[]{:S(2)}, u32[]{:S(2)}) %collective-permute-start.18) | collective-permute-done | bytes 262176 | tf_op jit(solution)/shard_map/ppermute | solution.py:39
  84.0 2.9 %tiles.9 = (bf16[1,8,32,128]{3,2,1,0:T(8,128)(2,1)S(1)}, bf16[1,8,32,128]{3,2,1,0:T(8,128)(2,1)S(1)}, bf16[1,8,32,128]{3,2,1,0:T(8,128)(2,1)S(1)}, bf16[1,8,32,128]{3,2,1,0:T(8,128)(2,1)S(1)}) custom-call(s32[5]{0:T(128)S(1)} %stack.44.place_ref, bf16[1024,2048]{1,0:T(8,128)(2,1)S(1)} %get-tuple-element.87.refs_0_, ...), custom_call_target="tpu_custom_call" | custom-call | tf_op jit(solution)/shard_map/tiles/pallas_call | solution.py:165
  88.8 1.9 %collective-permute-done.20.refs_2_ = bf16[1,8,32,128]{3,2,1,0:T(8,128)(2,1)S(1)} collective-permute-done((bf16[1,8,32,128]{3,2,1,0:T(8,128)(2,1)S(1)}, bf16[1,8,32,128]{3,2,1,0:T(8,128)(2,1)S(1)}, u32[]{:S(2)}, u32[]{:S(2)}) %collective-permute-start.20) | collective-permute-done | bytes 65568 | tf_op jit(solution)/shard_map/ppermute | solution.py:39
  91.1 2.8 %place_early.1 = (f32[128,32,128]{2,1,0:T(8,128)}, f32[128,32,128]{2,1,0:T(8,128)}) custom-call(s32[8,16]{1,0:T(8,128)S(1)} %fusion.9.where_ref, bf16[8,8,32,128]{3,2,1,0:T(8,128)(2,1)S(1)} %get-tuple-element.142.refs_0_, bf16[4,8,32,128]{3,2,1,0:T(8,128)(2,1)S(1)} %get-tuple-element.143.refs_1_, bf16[2,8,32,128]{3,2,1,0:T(8,128)(2,1)S(1)} %get-tuple-element.144.refs_2_, ...), custom_call_target="tpu_custom_call" | custom-call | tf_op jit(solution)/shard_map/place_early/pallas_call | solution.py:259
  95.0 1.6 %place_late.1 = (f32[128,32,128]{2,1,0:T(8,128)}, f32[128,32,128]{2,1,0:T(8,128)}) custom-call(s32[257]{0:T(512)S(1)} %list_open.1.later, bf16[1,8,32,128]{3,2,1,0:T(8,128)(2,1)S(1)} %get-tuple-element.133.refs_0_, bf16[1,8,32,128]{3,2,1,0:T(8,128)(2,1)S(1)} %collective-permute-done.19.refs_1_, ...), custom_call_target="tpu_custom_call", output_to_operand_aliasing={{0}: (9, {}), {1}: (10, {})} | custom-call | tf_op jit(solution)/shard_map/place_late/pallas_call | solution.py:312
  (50 shorter events, 13.1 us)
Async XLA Ops:
  0.6 11.7 %collective-permute-start.4 = (bf16[1024,2048]{1,0:T(8,128)(2,1)}, bf16[1024,2048]{1,0:T(8,128)(2,1)}, u32[]{:S(2)}, u32[]{:S(2)}) collective-permute-start(bf16[1024,2048]{1,0:T(8,128)(2,1)} %refs_1_.3), channel_id=1, source_target_pairs={{0,1},{1,0},{2,3},{3,2},{4,5},{5,4},{6,7},{7,6},{8,9},{9,8},{10,11... | collective-permute-start | bytes 12582920 | tf_op jit(solution)/shard_map/ppermute | solution.py:39
  1.1 9.2 %collective-permute-start.2 = (s32[8,16]{1,0:T(8,128)}, s32[8,16]{1,0:T(8,128)S(1)}, u32[]{:S(2)}, u32[]{:S(2)}) collective-permute-start(s32[8,16]{1,0:T(8,128)} %param.7), channel_id=1, source_target_pairs={{0,8},{4,12},{8,16},{12,20},{16,24},{20,28},{24,0},{28,4},{1,9},{5... | collective-permute-start | bytes 1544 | tf_op jit(solution)/shard_map/ppermute | solution.py:26
  3.8 6.6 %collective-permute-start.1 = (s32[8,16]{1,0:T(8,128)}, s32[8,16]{1,0:T(8,128)S(1)}, u32[]{:S(2)}, u32[]{:S(2)}) collective-permute-start(s32[8,16]{1,0:T(8,128)} %param.7), channel_id=1, source_target_pairs={{0,4},{4,8},{8,12},{12,16},{16,20},{20,24},{24,28},{28,0},{1,5},{5... | collective-permute-start | bytes 1544 | tf_op jit(solution)/shard_map/ppermute | solution.py:26
  5.3 5.1 %collective-permute-start = (s32[8,16]{1,0:T(8,128)}, s32[8,16]{1,0:T(8,128)S(1)}, u32[]{:S(2)}, u32[]{:S(2)}) collective-permute-start(s32[8,16]{1,0:T(8,128)} %param.7), channel_id=1, source_target_pairs={{0,28},{4,0},{8,4},{12,8},{16,12},{20,16},{24,20},{28,24},{1,29},{... | collective-permute-start | bytes 1544 | tf_op jit(solution)/shard_map/ppermute | solution.py:26
  14.3 26.3 %collective-permute-start.8 = (bf16[2,128,2048]{2,1,0:T(8,128)(2,1)S(1)}, bf16[2,128,2048]{2,1,0:T(8,128)(2,1)S(1)}, u32[]{:S(2)}, u32[]{:S(2)}) collective-permute-start(bf16[2,128,2048]{2,1,0:T(8,128)(2,1)S(1)} %pick_blocks.3), channel_id=1, source_target_pairs={{0,24},{4,28},{8,0},{12,4},{16,8},{20,12},{24,16},{28,20},{1,25},{... | collective-permute-start | bytes 3145736 | tf_op jit(solution)/shard_map/ppermute | solution.py:26
  16.5 10.7 %collective-permute-start.7 = (f32[2,2048]{1,0:T(2,128)S(1)}, f32[2,2048]{1,0:T(2,128)S(1)}, u32[]{:S(2)}, u32[]{:S(2)}) collective-permute-start(f32[2,2048]{1,0:T(2,128)S(1)} %pad_maximum_fusion.refs_2_), channel_id=1, source_target_pairs={{0,1},{1,0},{2,3},{3,2},{4,5},{5,4},{6,7},{7,6},{8,9},{9,8},{10,11... | collective-permute-start | bytes 49160 | tf_op jit(solution)/shard_map/ppermute | solution.py:39
  18.9 49.0 %collective-permute-start.5 = (bf16[2,128,2048]{2,1,0:T(8,128)(2,1)S(1)}, bf16[2,128,2048]{2,1,0:T(8,128)(2,1)S(1)}, u32[]{:S(2)}, u32[]{:S(2)}) collective-permute-start(bf16[2,128,2048]{2,1,0:T(8,128)(2,1)S(1)} %get-tuple-element.84), channel_id=1, source_target_pairs={{0,4},{4,8},{8,12},{12,16},{16,20},{20,24},{24,28},{28,0},{1,5},{5... | collective-permute-start | bytes 3145736 | tf_op jit(solution)/shard_map/ppermute | solution.py:26
  20.1 47.8 %collective-permute-start.6 = (bf16[2,128,2048]{2,1,0:T(8,128)(2,1)S(1)}, bf16[2,128,2048]{2,1,0:T(8,128)(2,1)S(1)}, u32[]{:S(2)}, u32[]{:S(2)}) collective-permute-start(bf16[2,128,2048]{2,1,0:T(8,128)(2,1)S(1)} %get-tuple-element.85), channel_id=1, source_target_pairs={{0,28},{4,0},{8,4},{12,8},{16,12},{20,16},{24,20},{28,24},{1,29},{... | collective-permute-start | bytes 3145736 | tf_op jit(solution)/shard_map/ppermute | solution.py:26
  36.9 30.9 %collective-permute-start.11 = (bf16[2,8,8,32,128]{4,3,2,1,0:T(8,128)(2,1)S(1)}, bf16[2,8,8,32,128]{4,3,2,1,0:T(8,128)(2,1)S(1)}, u32[]{:S(2)}, u32[]{:S(2)}) collective-permute-start(bf16[2,8,8,32,128]{4,3,2,1,0:T(8,128)(2,1)S(1)} %get-tuple-element.104), channel_id=1, source_target_pairs={{0,2},{1,3},{2,0},{3,1},{4,6},{5,7},{6,4},{7,5},{8,10},{9,11},{10,... | collective-permute-start | bytes 3145736 | tf_op jit(solution)/shard_map/ppermute | solution.py:39
  38.7 11.6 %collective-permute-start.10 = (bf16[8,8,32,128]{3,2,1,0:T(8,128)(2,1)S(1)}, bf16[8,8,32,128]{3,2,1,0:T(8,128)(2,1)S(1)}, u32[]{:S(2)}, u32[]{:S(2)}) collective-permute-start(bf16[8,8,32,128]{3,2,1,0:T(8,128)(2,1)S(1)} %get-tuple-element.103), channel_id=1, source_target_pairs={{0,1},{1,0},{2,3},{3,2},{4,5},{5,4},{6,7},{7,6},{8,9},{9,8},{10,11... | collective-permute-start | bytes 1572872 | tf_op jit(solution)/shard_map/ppermute | solution.py:39
  43.7 24.2 %collective-permute-start.9 = (bf16[2,2,8,32,128]{4,3,2,1,0:T(8,128)(2,1)S(1)}, bf16[2,2,8,32,128]{4,3,2,1,0:T(8,128)(2,1)S(1)}, u32[]{:S(2)}, u32[]{:S(2)}) collective-permute-start(bf16[2,2,8,32,128]{4,3,2,1,0:T(8,128)(2,1)S(1)} %get-tuple-element.101), channel_id=1, source_target_pairs={{0,2},{1,3},{2,0},{3,1},{4,6},{5,7},{6,4},{7,5},{8,10},{9,11},{10,... | collective-permute-start | bytes 786440 | tf_op jit(solution)/shard_map/ppermute | solution.py:39
  50.3 25.8 %collective-permute-start.13 = (bf16[2,64,2048]{2,1,0:T(8,128)(2,1)S(1)}, bf16[2,64,2048]{2,1,0:T(8,128)(2,1)S(1)}, u32[]{:S(2)}, u32[]{:S(2)}) collective-permute-start(bf16[2,64,2048]{2,1,0:T(8,128)(2,1)S(1)} %get-tuple-element.105), channel_id=1, source_target_pairs={{0,8},{4,12},{8,16},{12,20},{16,24},{20,28},{24,0},{28,4},{1,9},{5... | collective-permute-start | bytes 1572872 | tf_op jit(solution)/shard_map/ppermute | solution.py:26
  67.8 6.4 %collective-permute-start.16 = (bf16[2,8,32,128]{3,2,1,0:T(8,128)(2,1)S(1)}, bf16[2,8,32,128]{3,2,1,0:T(8,128)(2,1)S(1)}, u32[]{:S(2)}, u32[]{:S(2)}) collective-permute-start(bf16[2,8,32,128]{3,2,1,0:T(8,128)(2,1)S(1)} %get-tuple-element.118), channel_id=1, source_target_pairs={{0,1},{1,0},{2,3},{3,2},{4,5},{5,4},{6,7},{7,6},{8,9},{9,8},{10,11... | collective-permute-start | bytes 393224 | tf_op jit(solution)/shard_map/ppermute | solution.py:39
  67.9 16.1 %collective-permute-start.12 = (bf16[2,64,2048]{2,1,0:T(8,128)(2,1)S(1)}, bf16[2,64,2048]{2,1,0:T(8,128)(2,1)S(1)}, u32[]{:S(2)}, u32[]{:S(2)}) collective-permute-start(bf16[2,64,2048]{2,1,0:T(8,128)(2,1)S(1)} %get-tuple-element.109), channel_id=1, source_target_pairs={{0,8},{4,12},{8,16},{12,20},{16,24},{20,28},{24,0},{28,4},{1,9},{5... | collective-permute-start | bytes 1572872 | tf_op jit(solution)/shard_map/ppermute | solution.py:26
  68.3 7.9 %collective-permute-start.15 = (bf16[8,8,32,128]{3,2,1,0:T(8,128)(2,1)S(1)}, bf16[8,8,32,128]{3,2,1,0:T(8,128)(2,1)S(1)}, u32[]{:S(2)}, u32[]{:S(2)}) collective-permute-start(bf16[8,8,32,128]{3,2,1,0:T(8,128)(2,1)S(1)} %get-tuple-element.166), channel_id=1, source_target_pairs={{0,1},{1,0},{2,3},{3,2},{4,5},{5,4},{6,7},{7,6},{8,9},{9,8},{10,11... | collective-permute-start | bytes 1572872 | tf_op jit(solution)/shard_map/ppermute | solution.py:39
  68.6 5.9 %collective-permute-start.17 = (bf16[2,8,32,128]{3,2,1,0:T(8,128)(2,1)S(1)}, bf16[2,8,32,128]{3,2,1,0:T(8,128)(2,1)S(1)}, u32[]{:S(2)}, u32[]{:S(2)}) collective-permute-start(bf16[2,8,32,128]{3,2,1,0:T(8,128)(2,1)S(1)} %get-tuple-element.168), channel_id=1, source_target_pairs={{0,1},{1,0},{2,3},{3,2},{4,5},{5,4},{6,7},{7,6},{8,9},{9,8},{10,11... | collective-permute-start | bytes 393224 | tf_op jit(solution)/shard_map/ppermute | solution.py:39
  74.5 9.1 %collective-permute-start.18 = (bf16[4,8,32,128]{3,2,1,0:T(8,128)(2,1)S(1)}, bf16[4,8,32,128]{3,2,1,0:T(8,128)(2,1)S(1)}, u32[]{:S(2)}, u32[]{:S(2)}) collective-permute-start(bf16[4,8,32,128]{3,2,1,0:T(8,128)(2,1)S(1)} %get-tuple-element.124), channel_id=1, source_target_pairs={{0,2},{1,3},{2,0},{3,1},{4,6},{5,7},{6,4},{7,5},{8,10},{9,11},{10,... | collective-permute-start | bytes 786440 | tf_op jit(solution)/shard_map/ppermute | solution.py:39
  76.1 15.1 %collective-permute-start.25 = (bf16[4,8,32,128]{3,2,1,0:T(8,128)(2,1)S(1)}, bf16[4,8,32,128]{3,2,1,0:T(8,128)(2,1)S(1)}, u32[]{:S(2)}, u32[]{:S(2)}) collective-permute-start(bf16[4,8,32,128]{3,2,1,0:T(8,128)(2,1)S(1)} %get-tuple-element.152), channel_id=1, source_target_pairs={{0,3},{1,2},{2,1},{3,0},{4,7},{5,6},{6,5},{7,4},{8,11},{9,10},{10,... | collective-permute-start | bytes 786440 | tf_op jit(solution)/shard_map/ppermute | solution.py:39
  79.1 9.2 %collective-permute-start.19 = (bf16[1,8,32,128]{3,2,1,0:T(8,128)(2,1)S(1)}, bf16[1,8,32,128]{3,2,1,0:T(8,128)(2,1)S(1)}, u32[]{:S(2)}, u32[]{:S(2)}) collective-permute-start(bf16[1,8,32,128]{3,2,1,0:T(8,128)(2,1)S(1)} %get-tuple-element.130), channel_id=1, source_target_pairs={{0,1},{1,0},{2,3},{3,2},{4,5},{5,4},{6,7},{7,6},{8,9},{9,8},{10,11... | collective-permute-start | bytes 196616 | tf_op jit(solution)/shard_map/ppermute | solution.py:39
  79.7 11.0 %collective-permute-start.20 = (bf16[1,8,32,128]{3,2,1,0:T(8,128)(2,1)S(1)}, bf16[1,8,32,128]{3,2,1,0:T(8,128)(2,1)S(1)}, u32[]{:S(2)}, u32[]{:S(2)}) collective-permute-start(bf16[1,8,32,128]{3,2,1,0:T(8,128)(2,1)S(1)} %get-tuple-element.131), channel_id=1, source_target_pairs={{0,2},{1,3},{2,0},{3,1},{4,6},{5,7},{6,4},{7,5},{8,10},{9,11},{10,... | collective-permute-start | bytes 196616 | tf_op jit(solution)/shard_map/ppermute | solution.py:39
  83.7 7.5 %collective-permute-start.21 = (bf16[1,8,32,128]{3,2,1,0:T(8,128)(2,1)S(1)}, bf16[1,8,32,128]{3,2,1,0:T(8,128)(2,1)S(1)}, u32[]{:S(2)}, u32[]{:S(2)}) collective-permute-start(bf16[1,8,32,128]{3,2,1,0:T(8,128)(2,1)S(1)} %get-tuple-element.132), channel_id=1, source_target_pairs={{0,3},{1,2},{2,1},{3,0},{4,7},{5,6},{6,5},{7,4},{8,11},{9,10},{10,... | collective-permute-start | bytes 196616 | tf_op jit(solution)/shard_map/ppermute | solution.py:39
  86.9 7.0 %collective-permute-start.22 = (bf16[1,8,32,128]{3,2,1,0:T(8,128)(2,1)S(1)}, bf16[1,8,32,128]{3,2,1,0:T(8,128)(2,1)S(1)}, u32[]{:S(2)}, u32[]{:S(2)}) collective-permute-start(bf16[1,8,32,128]{3,2,1,0:T(8,128)(2,1)S(1)} %get-tuple-element.138), channel_id=1, source_target_pairs={{0,1},{1,0},{2,3},{3,2},{4,5},{5,4},{6,7},{7,6},{8,9},{9,8},{10,11... | collective-permute-start | bytes 196616 | tf_op jit(solution)/shard_map/ppermute | solution.py:39
  88.3 5.7 %collective-permute-start.23 = (bf16[1,8,32,128]{3,2,1,0:T(8,128)(2,1)S(1)}, bf16[1,8,32,128]{3,2,1,0:T(8,128)(2,1)S(1)}, u32[]{:S(2)}, u32[]{:S(2)}) collective-permute-start(bf16[1,8,32,128]{3,2,1,0:T(8,128)(2,1)S(1)} %get-tuple-element.139), channel_id=1, source_target_pairs={{0,2},{1,3},{2,0},{3,1},{4,6},{5,7},{6,4},{7,5},{8,10},{9,11},{10,... | collective-permute-start | bytes 196616 | tf_op jit(solution)/shard_map/ppermute | solution.py:39
  90.7 4.3 %collective-permute-start.24 = (bf16[1,8,32,128]{3,2,1,0:T(8,128)(2,1)S(1)}, bf16[1,8,32,128]{3,2,1,0:T(8,128)(2,1)S(1)}, u32[]{:S(2)}, u32[]{:S(2)}) collective-permute-start(bf16[1,8,32,128]{3,2,1,0:T(8,128)(2,1)S(1)} %get-tuple-element.140), channel_id=1, source_target_pairs={{0,3},{1,2},{2,1},{3,0},{4,7},{5,6},{6,5},{7,4},{8,11},{9,10},{10,... | collective-permute-start | bytes 196616 | tf_op jit(solution)/shard_map/ppermute | solution.py:39
  (3 other events, 10.2 us)

commit v14 on v13

--- a/solution.py
+++ b/solution.py
@@ -408,23 +408,27 @@
     upper = shifted(halves[1], "atoms", -offsets[3])
     chunks.append([parts[0], to_strip_target(parts[1], chips, 0, 1)] + pairs)
     chunks = [passed_on(chunk) for chunk in chunks]
-    direct = strips_of(near, False)
-    lower, direct[:2], chunks = lax.optimization_barrier((lower, direct[:2], chunks))
+    before = strips_of(near[:1], False)
+    near[1], before[:1] = lax.optimization_barrier((near[1], before[:1]))
+    after = strips_of(near[1:], False)
+    lower, before, after[:2], chunks = lax.optimization_barrier(
+        (lower, before, after[:2], chunks)
+    )
     lower = list(tiles(place, own, kept_sib, [lower], weights, n_bands, tile, False))
     lower_sib = lower[1]
     for index in range(2, n_bands):
         lower[index] = to_strip_target(lower[index], chips, index // 2, index % 2)
-    where, upper, lower[0], direct[:3] = lax.optimization_barrier(
-        (where, upper, lower[0], direct[:3])
+    where, upper, lower[0], after[:3] = lax.optimization_barrier(
+        (where, upper, lower[0], after[:3])
     )
-    chunks.append(direct)
+    chunks += [before, after]
     last = strips_of([upper], False)
     where, last[0] = lax.optimization_barrier((where, last[0]))
     lower[1] = to_strip_target(lower_sib, chips, 0, 1)
     where, lower = lax.optimization_barrier((where, lower))
-    local, far, direct = chunks
-    strips = list(zip(local, direct, far))
-    sizes = [half_blocks, 2, 1]
+    local, far, before, after = chunks
+    strips = list(zip(local, before, after, far))
+    sizes = [half_blocks, 1, 1, 1]
     density, energy = place_early(where, strips, sizes, chips, per_core)
     outs = place_late(later, lower, last, density, energy, chips)
     return tuple(out.reshape(*where.shape, *out.shape[1:]) for out in outs)

time: 97.1 us -> 98.4 us (1.013)
  starting transfers between devices: 25.2 us -> 28.6 us
  waiting for transfers between devices: 25.7 us -> 22.9 us
    ppermute x17 -> x20, starting transfers between devices: 10.3 us -> 13.6 us  [to_strip_target(): return lax.ppermute(value, 'bands', pairs)]
    ppermute x17 -> x20, waiting for transfers between devices: 5.89 us -> 3.36 us  [to_strip_target(): return lax.ppermute(value, 'bands', pairs)]
    pallas_call x5 -> x6, Pallas kernels: 23.8 us -> 24.5 us  [tiles(): pl.pallas_call(functools.partial(tiles_kernel, heights, len(arrived), n_s...]
  transfers between devices with their start and end apart: 26 -> 29, of which waited for: 7 -> 6; matrix products, arithmetic and copies ran while one was open for 5% -> 5% of each run, Pallas kernels for 38% -> 38%
where the time goes in v14:
time: 98.4 us; the launch traced here: 98 us
  Pallas kernels  40.6 us (41%)
  starting transfers between devices  28.6 us (29%)
  waiting for transfers between devices  22.9 us (23%)
  other arithmetic  4.73 us (5%)
  between operations  1.02 us (1%)
    pallas_call x6, Pallas kernels, tiles(): pl.pallas_call(functools.partial(tiles_kernel, heights, len(arrived), n_s...  24.5 us
    ppermute x9, waiting for transfers between devices, shifted(): return lax.ppermute(value, axis, pairs)  19.6 us
    ppermute x9, starting transfers between devices, shifted(): return lax.ppermute(value, axis, pairs)  14.9 us
    ppermute x20, starting transfers between devices, to_strip_target(): return lax.ppermute(value, 'bands', pairs)  13.6 us
    pallas_call x3, Pallas kernels, pick(): pl.pallas_call(functools.partial(pick_kernel, count, blocks, tile, parts)...  6.3 us
    pallas_call x1, Pallas kernels, keep(): pl.pallas_call(keep_kernel, out_shape=[pltpu.VMEM(own.shape, own.dtype)]...  3.48 us
    ppermute x20, waiting for transfers between devices, to_strip_target(): return lax.ppermute(value, 'bands', pairs)  3.36 us
    pallas_call x1, Pallas kernels, place_early(): pl.pallas_call(functools.partial(place_early_kernel, chips, sizes, per_co...  2.81 us
  transfers between devices with their start and end apart: 29, of which 6 were waited for; matrix products, arithmetic and copies ran while one was open for 5% of the time, Pallas kernels for 38%

profile of v14, /device:TPU:0, one launch (start us, length us, event | category | flops | bytes accessed | tf_op | source)
XLA Modules:
  0.0 98.0 jit_solution(2735846575044235361)
XLA Ops:
  1.1 2.6 %collective-permute-start.2 = (s32[8,16]{1,0:T(8,128)}, s32[8,16]{1,0:T(8,128)S(1)}, u32[]{:S(2)}, u32[]{:S(2)}) collective-permute-start(s32[8,16]{1,0:T(8,128)} %param.7), channel_id=1, source_target_pairs={{0,8},{4,12},{8,16},{12,20},{16,24},{20,28},{24,0},{28,4},{1,9},{5... | collective-permute-start | bytes 1544 | tf_op jit(solution)/shard_map/ppermute | solution.py:26
  5.3 3.2 %collective-permute-start = (s32[8,16]{1,0:T(8,128)}, s32[8,16]{1,0:T(8,128)S(1)}, u32[]{:S(2)}, u32[]{:S(2)}) collective-permute-start(s32[8,16]{1,0:T(8,128)} %param.7), channel_id=1, source_target_pairs={{0,28},{4,0},{8,4},{12,8},{16,12},{20,16},{24,20},{28,24},{1,29},{... | collective-permute-start | bytes 1544 | tf_op jit(solution)/shard_map/ppermute | solution.py:26
  10.3 2.0 %collective-permute-done.3.refs_0_ = s32[8,16]{1,0:T(8,128)S(1)} collective-permute-done((s32[8,16]{1,0:T(8,128)}, s32[8,16]{1,0:T(8,128)S(1)}, u32[]{:S(2)}, u32[]{:S(2)}) %collective-permute-start.3) | collective-permute-done | bytes 544 | tf_op jit(solution)/shard_map/ppermute | solution.py:26
  12.3 2.0 %pick_blocks.3 = bf16[2,128,2048]{2,1,0:T(8,128)(2,1)S(1)} custom-call(s32[2]{0:T(128)S(1)} %pad_add_fusion.place_ref, s32[8,16]{1,0:T(8,128)S(1)} %collective-permute-done.2.refs_0_, bf16[1024,2048]{1,0:T(8,128)(2,1)} %refs_1_.3, bf16[1024,2048]{1,0:T(8,128)(2,1)} %collective-permute-done.4.refs_2_.refs_3_.sib), custom_call_target="tpu_custom_call" | custom-call | tf_op jit(solution)/shard_map/pick_blocks/pallas_call | solution.py:73
  14.3 2.2 %collective-permute-start.8 = (bf16[2,128,2048]{2,1,0:T(8,128)(2,1)S(1)}, bf16[2,128,2048]{2,1,0:T(8,128)(2,1)S(1)}, u32[]{:S(2)}, u32[]{:S(2)}) collective-permute-start(bf16[2,128,2048]{2,1,0:T(8,128)(2,1)S(1)} %pick_blocks.3), channel_id=1, source_target_pairs={{0,24},{4,28},{8,0},{12,4},{16,8},{20,12},{24,16},{28,20},{1,25},{... | collective-permute-start | bytes 3145736 | tf_op jit(solution)/shard_map/ppermute | solution.py:26
  16.6 2.4 %pick_blocks.4 = (bf16[2,128,2048]{2,1,0:T(8,128)(2,1)S(1)}, bf16[2,128,2048]{2,1,0:T(8,128)(2,1)S(1)}) custom-call(s32[2]{0:T(128)S(1)} %pad_add_fusion.place_ref, s32[8,16]{1,0:T(8,128)S(1)} %collective-permute-done.refs_0_, s32[8,16]{1,0:T(8,128)S(1)} %collective-permute-done.1.refs_1_, bf16[1024,2048]{1,0:T(8,128)(2,1)} %refs_1_.3, ...), custom_call_target="tpu_custom_call" | custom-call | tf_op jit(solution)/shard_map/pick_blocks/pallas_call | solution.py:73
  20.1 3.6 %collective-permute-start.6 = (bf16[2,128,2048]{2,1,0:T(8,128)(2,1)S(1)}, bf16[2,128,2048]{2,1,0:T(8,128)(2,1)S(1)}, u32[]{:S(2)}, u32[]{:S(2)}) collective-permute-start(bf16[2,128,2048]{2,1,0:T(8,128)(2,1)S(1)} %get-tuple-element.95), channel_id=1, source_target_pairs={{0,28},{4,0},{8,4},{12,8},{16,12},{20,16},{24,20},{28,24},{1,29},{... | collective-permute-start | bytes 3145736 | tf_op jit(solution)/shard_map/ppermute | solution.py:26
  23.7 3.5 %keep.1 = (bf16[1024,2048]{1,0:T(8,128)(2,1)S(1)}, bf16[1024,2048]{1,0:T(8,128)(2,1)S(1)}) custom-call(bf16[1024,2048]{1,0:T(8,128)(2,1)} %refs_1_.3, bf16[1024,2048]{1,0:T(8,128)(2,1)} %collective-permute-done.4.refs_2_.refs_3_.sib), custom_call_target="tpu_custom_call" | custom-call | tf_op jit(solution)/shard_map/keep/pallas_call | solution.py:98
  27.2 9.8 %tiles.6 = (bf16[8,8,32,128]{3,2,1,0:T(8,128)(2,1)S(1)}, bf16[8,8,32,128]{3,2,1,0:T(8,128)(2,1)S(1)}, bf16[2,8,8,32,128]{4,3,2,1,0:T(8,128)(2,1)S(1)}) custom-call(s32[5]{0:T(128)S(1)} %stack.44.place_ref, bf16[1024,2048]{1,0:T(8,128)(2,1)S(1)} %get-tuple-element.97.refs_0_, bf16[1024,2048]{1,0:T(8,128)(2,1)S(1)} %get-tuple-element.98.refs_1_, ...), custom_call_target="tpu_custom_call" | custom-call | tf_op jit(solution)/shard_map/tiles/pallas_call | solution.py:165
  37.0 1.7 %collective-permute-start.11 = (bf16[2,8,8,32,128]{4,3,2,1,0:T(8,128)(2,1)S(1)}, bf16[2,8,8,32,128]{4,3,2,1,0:T(8,128)(2,1)S(1)}, u32[]{:S(2)}, u32[]{:S(2)}) collective-permute-start(bf16[2,8,8,32,128]{4,3,2,1,0:T(8,128)(2,1)S(1)} %get-tuple-element.114), channel_id=1, source_target_pairs={{0,2},{1,3},{2,0},{3,1},{4,6},{5,7},{6,4},{7,5},{8,10},{9,11},{10,... | collective-permute-start | bytes 3145736 | tf_op jit(solution)/shard_map/ppermute | solution.py:39
  38.7 2.0 %pick_blocks.5 = (bf16[2,64,2048]{2,1,0:T(8,128)(2,1)S(1)}, bf16[2,64,2048]{2,1,0:T(8,128)(2,1)S(1)}) custom-call(s32[2]{0:T(128)S(1)} %pad_add_fusion.place_ref, s32[8,16]{1,0:T(8,128)S(1)} %collective-permute-done.3.refs_0_, bf16[1024,2048]{1,0:T(8,128)(2,1)} %refs_1_.3, bf16[1024,2048]{1,0:T(8,128)(2,1)} %collective-permute-done.4.refs_2_.refs_3_.sib), custom_call_target="tpu_custom_call" | custom-call | tf_op jit(solution)/shard_map/pick_blocks/pallas_call | solution.py:73
  40.7 3.0 %tiles.7 = (bf16[2,8,32,128]{3,2,1,0:T(8,128)(2,1)S(1)}, bf16[2,8,32,128]{3,2,1,0:T(8,128)(2,1)S(1)}, bf16[2,2,8,32,128]{4,3,2,1,0:T(8,128)(2,1)S(1)}) custom-call(s32[5]{0:T(128)S(1)} %stack.44.place_ref, bf16[1024,2048]{1,0:T(8,128)(2,1)S(1)} %get-tuple-element.97.refs_0_, bf16[1024,2048]{1,0:T(8,128)(2,1)S(1)} %get-tuple-element.98.refs_1_, ...), custom_call_target="tpu_custom_call" | custom-call | tf_op jit(solution)/shard_map/tiles/pallas_call | solution.py:165
  45.8 2.5 %fusion.9.where_ref = s32[8,16]{1,0:T(8,128)S(1)} fusion(pred[8,16]{1,0:T(8,128)(4,1)S(1)} %get-tuple-element.185, pred[8,16]{1,0:T(8,128)(4,1)S(1)} %get-tuple-element.184, pred[8,16]{1,0:T(8,128)(4,1)S(1)} %get-tuple-element.183, pred[8,16]{1,0:T(8,128)(4,1)S(1)} %get-tuple-element.182, s32[]{:T(128)} %and.14, s32[]{:T(128)} %get-tuple-element.180, ...), kind=kLoop, calls=%fused_computation.22 | loop fusion | flops 4352 | bytes 1556 | tf_op jit(solution)/shard_map/add | solution.py:395
  48.3 1.9 %list_open.1.later = s32[257]{0:T(512)S(1)} custom-call(s32[8,16]{1,0:T(8,128)S(1)} %fusion.9.where_ref), custom_call_target="tpu_custom_call" | custom-call | tf_op jit(solution)/shard_map/list_open/pallas_call | solution.py:206
  50.3 17.6 %collective-permute-done.6.refs_4_ = bf16[2,128,2048]{2,1,0:T(8,128)(2,1)S(1)} collective-permute-done((bf16[2,128,2048]{2,1,0:T(8,128)(2,1)S(1)}, bf16[2,128,2048]{2,1,0:T(8,128)(2,1)S(1)}, u32[]{:S(2)}, u32[]{:S(2)}) %collective-permute-start.6) | collective-permute-done | bytes 1048608 | tf_op jit(solution)/shard_map/ppermute | solution.py:26
  68.9 3.0 %tiles.8 = (bf16[2,8,32,128]{3,2,1,0:T(8,128)(2,1)S(1)}, bf16[2,8,32,128]{3,2,1,0:T(8,128)(2,1)S(1)}, bf16[2,8,32,128]{3,2,1,0:T(8,128)(2,1)S(1)}, bf16[2,8,32,128]{3,2,1,0:T(8,128)(2,1)S(1)}) custom-call(s32[5]{0:T(128)S(1)} %stack.44.place_ref, bf16[1024,2048]{1,0:T(8,128)(2,1)S(1)} %get-tuple-element.97.refs_0_, ...), custom_call_target="tpu_custom_call" | custom-call | tf_op jit(solution)/shard_map/tiles/pallas_call | solution.py:165
  72.2 1.5 %collective-permute-start.15 = (bf16[2,8,32,128]{3,2,1,0:T(8,128)(2,1)S(1)}, bf16[2,8,32,128]{3,2,1,0:T(8,128)(2,1)S(1)}, u32[]{:S(2)}, u32[]{:S(2)}) collective-permute-start(bf16[2,8,32,128]{3,2,1,0:T(8,128)(2,1)S(1)} %get-tuple-element.125), channel_id=1, source_target_pairs={{0,2},{1,3},{2,0},{3,1},{4,6},{5,7},{6,4},{7,5},{8,10},{9,11},{10,... | collective-permute-start | bytes 393224 | tf_op jit(solution)/shard_map/ppermute | solution.py:39
  74.7 3.0 %tiles.9 = (bf16[2,8,32,128]{3,2,1,0:T(8,128)(2,1)S(1)}, bf16[2,8,32,128]{3,2,1,0:T(8,128)(2,1)S(1)}, bf16[2,8,32,128]{3,2,1,0:T(8,128)(2,1)S(1)}, bf16[2,8,32,128]{3,2,1,0:T(8,128)(2,1)S(1)}) custom-call(s32[5]{0:T(128)S(1)} %stack.44.place_ref, bf16[1024,2048]{1,0:T(8,128)(2,1)S(1)} %get-tuple-element.97.refs_0_, ...), custom_call_target="tpu_custom_call" | custom-call | tf_op jit(solution)/shard_map/tiles/pallas_call | solution.py:165
  80.0 1.5 %collective-permute-start.21 = (bf16[2,8,32,128]{3,2,1,0:T(8,128)(2,1)S(1)}, bf16[2,8,32,128]{3,2,1,0:T(8,128)(2,1)S(1)}, u32[]{:S(2)}, u32[]{:S(2)}) collective-permute-start(bf16[2,8,32,128]{3,2,1,0:T(8,128)(2,1)S(1)} %get-tuple-element.140), channel_id=1, source_target_pairs={{0,2},{1,3},{2,0},{3,1},{4,6},{5,7},{6,4},{7,5},{8,10},{9,11},{10,... | collective-permute-start | bytes 393224 | tf_op jit(solution)/shard_map/ppermute | solution.py:39
  82.2 2.9 %tiles.10 = (bf16[1,8,32,128]{3,2,1,0:T(8,128)(2,1)S(1)}, bf16[1,8,32,128]{3,2,1,0:T(8,128)(2,1)S(1)}, bf16[1,8,32,128]{3,2,1,0:T(8,128)(2,1)S(1)}, bf16[1,8,32,128]{3,2,1,0:T(8,128)(2,1)S(1)}) custom-call(s32[5]{0:T(128)S(1)} %stack.44.place_ref, bf16[1024,2048]{1,0:T(8,128)(2,1)S(1)} %get-tuple-element.97.refs_0_, ...), custom_call_target="tpu_custom_call" | custom-call | tf_op jit(solution)/shard_map/tiles/pallas_call | solution.py:165
  85.2 1.6 %collective-permute-start.23 = (bf16[1,8,32,128]{3,2,1,0:T(8,128)(2,1)S(1)}, bf16[1,8,32,128]{3,2,1,0:T(8,128)(2,1)S(1)}, u32[]{:S(2)}, u32[]{:S(2)}) collective-permute-start(bf16[1,8,32,128]{3,2,1,0:T(8,128)(2,1)S(1)} %get-tuple-element.147), channel_id=1, source_target_pairs={{0,2},{1,3},{2,0},{3,1},{4,6},{5,7},{6,4},{7,5},{8,10},{9,11},{10,... | collective-permute-start | bytes 196616 | tf_op jit(solution)/shard_map/ppermute | solution.py:39
  87.3 2.9 %tiles.11 = (bf16[1,8,32,128]{3,2,1,0:T(8,128)(2,1)S(1)}, bf16[1,8,32,128]{3,2,1,0:T(8,128)(2,1)S(1)}, bf16[1,8,32,128]{3,2,1,0:T(8,128)(2,1)S(1)}, bf16[1,8,32,128]{3,2,1,0:T(8,128)(2,1)S(1)}) custom-call(s32[5]{0:T(128)S(1)} %stack.44.place_ref, bf16[1024,2048]{1,0:T(8,128)(2,1)S(1)} %get-tuple-element.97.refs_0_, ...), custom_call_target="tpu_custom_call" | custom-call | tf_op jit(solution)/shard_map/tiles/pallas_call | solution.py:165
  92.5 2.8 %place_early.1 = (f32[128,32,128]{2,1,0:T(8,128)}, f32[128,32,128]{2,1,0:T(8,128)}) custom-call(s32[8,16]{1,0:T(8,128)S(1)} %fusion.9.where_ref, bf16[8,8,32,128]{3,2,1,0:T(8,128)(2,1)S(1)} %get-tuple-element.158.refs_0_, bf16[2,8,32,128]{3,2,1,0:T(8,128)(2,1)S(1)} %get-tuple-element.159.refs_1_, bf16[2,8,32,128]{3,2,1,0:T(8,128)(2,1)S(1)} %get-tuple-element.160.refs_2_, ...), custom_call_target="tpu_custom_call" | custom-call | tf_op jit(solution)/shard_map/place_early/pallas_call | solution.py:259
  96.3 1.5 %place_late.1 = (f32[128,32,128]{2,1,0:T(8,128)}, f32[128,32,128]{2,1,0:T(8,128)}) custom-call(s32[257]{0:T(512)S(1)} %list_open.1.later, bf16[1,8,32,128]{3,2,1,0:T(8,128)(2,1)S(1)} %get-tuple-element.149.refs_0_, bf16[1,8,32,128]{3,2,1,0:T(8,128)(2,1)S(1)} %collective-permute-done.22.refs_1_, ...), custom_call_target="tpu_custom_call", output_to_operand_aliasing={{0}: (9, {}), {1}: (10, {})} | custom-call | tf_op jit(solution)/shard_map/place_late/pallas_call | solution.py:312
  (57 shorter events, 16.4 us)
Async XLA Ops:
  0.6 11.7 %collective-permute-start.4 = (bf16[1024,2048]{1,0:T(8,128)(2,1)}, bf16[1024,2048]{1,0:T(8,128)(2,1)}, u32[]{:S(2)}, u32[]{:S(2)}) collective-permute-start(bf16[1024,2048]{1,0:T(8,128)(2,1)} %refs_1_.3), channel_id=1, source_target_pairs={{0,1},{1,0},{2,3},{3,2},{4,5},{5,4},{6,7},{7,6},{8,9},{9,8},{10,11... | collective-permute-start | bytes 12582920 | tf_op jit(solution)/shard_map/ppermute | solution.py:39
  1.1 9.2 %collective-permute-start.2 = (s32[8,16]{1,0:T(8,128)}, s32[8,16]{1,0:T(8,128)S(1)}, u32[]{:S(2)}, u32[]{:S(2)}) collective-permute-start(s32[8,16]{1,0:T(8,128)} %param.7), channel_id=1, source_target_pairs={{0,8},{4,12},{8,16},{12,20},{16,24},{20,28},{24,0},{28,4},{1,9},{5... | collective-permute-start | bytes 1544 | tf_op jit(solution)/shard_map/ppermute | solution.py:26
  3.8 6.6 %collective-permute-start.1 = (s32[8,16]{1,0:T(8,128)}, s32[8,16]{1,0:T(8,128)S(1)}, u32[]{:S(2)}, u32[]{:S(2)}) collective-permute-start(s32[8,16]{1,0:T(8,128)} %param.7), channel_id=1, source_target_pairs={{0,4},{4,8},{8,12},{12,16},{16,20},{20,24},{24,28},{28,0},{1,5},{5... | collective-permute-start | bytes 1544 | tf_op jit(solution)/shard_map/ppermute | solution.py:26
  5.3 5.1 %collective-permute-start = (s32[8,16]{1,0:T(8,128)}, s32[8,16]{1,0:T(8,128)S(1)}, u32[]{:S(2)}, u32[]{:S(2)}) collective-permute-start(s32[8,16]{1,0:T(8,128)} %param.7), channel_id=1, source_target_pairs={{0,28},{4,0},{8,4},{12,8},{16,12},{20,16},{24,20},{28,24},{1,29},{... | collective-permute-start | bytes 1544 | tf_op jit(solution)/shard_map/ppermute | solution.py:26
  14.3 26.4 %collective-permute-start.8 = (bf16[2,128,2048]{2,1,0:T(8,128)(2,1)S(1)}, bf16[2,128,2048]{2,1,0:T(8,128)(2,1)S(1)}, u32[]{:S(2)}, u32[]{:S(2)}) collective-permute-start(bf16[2,128,2048]{2,1,0:T(8,128)(2,1)S(1)} %pick_blocks.3), channel_id=1, source_target_pairs={{0,24},{4,28},{8,0},{12,4},{16,8},{20,12},{24,16},{28,20},{1,25},{... | collective-permute-start | bytes 3145736 | tf_op jit(solution)/shard_map/ppermute | solution.py:26
  16.5 10.7 %collective-permute-start.7 = (f32[2,2048]{1,0:T(2,128)S(1)}, f32[2,2048]{1,0:T(2,128)S(1)}, u32[]{:S(2)}, u32[]{:S(2)}) collective-permute-start(f32[2,2048]{1,0:T(2,128)S(1)} %pad_maximum_fusion.refs_2_), channel_id=1, source_target_pairs={{0,1},{1,0},{2,3},{3,2},{4,5},{5,4},{6,7},{7,6},{8,9},{9,8},{10,11... | collective-permute-start | bytes 49160 | tf_op jit(solution)/shard_map/ppermute | solution.py:39
  18.9 48.9 %collective-permute-start.5 = (bf16[2,128,2048]{2,1,0:T(8,128)(2,1)S(1)}, bf16[2,128,2048]{2,1,0:T(8,128)(2,1)S(1)}, u32[]{:S(2)}, u32[]{:S(2)}) collective-permute-start(bf16[2,128,2048]{2,1,0:T(8,128)(2,1)S(1)} %get-tuple-element.94), channel_id=1, source_target_pairs={{0,4},{4,8},{8,12},{12,16},{16,20},{20,24},{24,28},{28,0},{1,5},{5... | collective-permute-start | bytes 3145736 | tf_op jit(solution)/shard_map/ppermute | solution.py:26
  20.1 47.7 %collective-permute-start.6 = (bf16[2,128,2048]{2,1,0:T(8,128)(2,1)S(1)}, bf16[2,128,2048]{2,1,0:T(8,128)(2,1)S(1)}, u32[]{:S(2)}, u32[]{:S(2)}) collective-permute-start(bf16[2,128,2048]{2,1,0:T(8,128)(2,1)S(1)} %get-tuple-element.95), channel_id=1, source_target_pairs={{0,28},{4,0},{8,4},{12,8},{16,12},{20,16},{24,20},{28,24},{1,29},{... | collective-permute-start | bytes 3145736 | tf_op jit(solution)/shard_map/ppermute | solution.py:26
  37.0 30.8 %collective-permute-start.11 = (bf16[2,8,8,32,128]{4,3,2,1,0:T(8,128)(2,1)S(1)}, bf16[2,8,8,32,128]{4,3,2,1,0:T(8,128)(2,1)S(1)}, u32[]{:S(2)}, u32[]{:S(2)}) collective-permute-start(bf16[2,8,8,32,128]{4,3,2,1,0:T(8,128)(2,1)S(1)} %get-tuple-element.114), channel_id=1, source_target_pairs={{0,2},{1,3},{2,0},{3,1},{4,6},{5,7},{6,4},{7,5},{8,10},{9,11},{10,... | collective-permute-start | bytes 3145736 | tf_op jit(solution)/shard_map/ppermute | solution.py:39
  38.7 11.5 %collective-permute-start.10 = (bf16[8,8,32,128]{3,2,1,0:T(8,128)(2,1)S(1)}, bf16[8,8,32,128]{3,2,1,0:T(8,128)(2,1)S(1)}, u32[]{:S(2)}, u32[]{:S(2)}) collective-permute-start(bf16[8,8,32,128]{3,2,1,0:T(8,128)(2,1)S(1)} %get-tuple-element.113), channel_id=1, source_target_pairs={{0,1},{1,0},{2,3},{3,2},{4,5},{5,4},{6,7},{7,6},{8,9},{9,8},{10,11... | collective-permute-start | bytes 1572872 | tf_op jit(solution)/shard_map/ppermute | solution.py:39
  43.7 24.1 %collective-permute-start.9 = (bf16[2,2,8,32,128]{4,3,2,1,0:T(8,128)(2,1)S(1)}, bf16[2,2,8,32,128]{4,3,2,1,0:T(8,128)(2,1)S(1)}, u32[]{:S(2)}, u32[]{:S(2)}) collective-permute-start(bf16[2,2,8,32,128]{4,3,2,1,0:T(8,128)(2,1)S(1)} %get-tuple-element.111), channel_id=1, source_target_pairs={{0,2},{1,3},{2,0},{3,1},{4,6},{5,7},{6,4},{7,5},{8,10},{9,11},{10,... | collective-permute-start | bytes 786440 | tf_op jit(solution)/shard_map/ppermute | solution.py:39
  50.2 32.0 %collective-permute-start.13 = (bf16[2,64,2048]{2,1,0:T(8,128)(2,1)S(1)}, bf16[2,64,2048]{2,1,0:T(8,128)(2,1)S(1)}, u32[]{:S(2)}, u32[]{:S(2)}) collective-permute-start(bf16[2,64,2048]{2,1,0:T(8,128)(2,1)S(1)} %get-tuple-element.115), channel_id=1, source_target_pairs={{0,8},{4,12},{8,16},{12,20},{16,24},{20,28},{24,0},{28,4},{1,9},{5... | collective-permute-start | bytes 1572872 | tf_op jit(solution)/shard_map/ppermute | solution.py:26
  67.9 19.4 %collective-permute-start.12 = (bf16[2,64,2048]{2,1,0:T(8,128)(2,1)S(1)}, bf16[2,64,2048]{2,1,0:T(8,128)(2,1)S(1)}, u32[]{:S(2)}, u32[]{:S(2)}) collective-permute-start(bf16[2,64,2048]{2,1,0:T(8,128)(2,1)S(1)} %get-tuple-element.119), channel_id=1, source_target_pairs={{0,8},{4,12},{8,16},{12,20},{16,24},{20,28},{24,0},{28,4},{1,9},{5... | collective-permute-start | bytes 1572872 | tf_op jit(solution)/shard_map/ppermute | solution.py:26
  68.3 13.9 %collective-permute-start.18 = (bf16[8,8,32,128]{3,2,1,0:T(8,128)(2,1)S(1)}, bf16[8,8,32,128]{3,2,1,0:T(8,128)(2,1)S(1)}, u32[]{:S(2)}, u32[]{:S(2)}) collective-permute-start(bf16[8,8,32,128]{3,2,1,0:T(8,128)(2,1)S(1)} %get-tuple-element.186), channel_id=1, source_target_pairs={{0,1},{1,0},{2,3},{3,2},{4,5},{5,4},{6,7},{7,6},{8,9},{9,8},{10,11... | collective-permute-start | bytes 1572872 | tf_op jit(solution)/shard_map/ppermute | solution.py:39
  72.2 6.3 %collective-permute-start.15 = (bf16[2,8,32,128]{3,2,1,0:T(8,128)(2,1)S(1)}, bf16[2,8,32,128]{3,2,1,0:T(8,128)(2,1)S(1)}, u32[]{:S(2)}, u32[]{:S(2)}) collective-permute-start(bf16[2,8,32,128]{3,2,1,0:T(8,128)(2,1)S(1)} %get-tuple-element.125), channel_id=1, source_target_pairs={{0,2},{1,3},{2,0},{3,1},{4,6},{5,7},{6,4},{7,5},{8,10},{9,11},{10,... | collective-permute-start | bytes 393224 | tf_op jit(solution)/shard_map/ppermute | solution.py:39
  73.8 6.3 %collective-permute-start.16 = (bf16[2,8,32,128]{3,2,1,0:T(8,128)(2,1)S(1)}, bf16[2,8,32,128]{3,2,1,0:T(8,128)(2,1)S(1)}, u32[]{:S(2)}, u32[]{:S(2)}) collective-permute-start(bf16[2,8,32,128]{3,2,1,0:T(8,128)(2,1)S(1)} %get-tuple-element.126), channel_id=1, source_target_pairs={{0,3},{1,2},{2,1},{3,0},{4,7},{5,6},{6,5},{7,4},{8,11},{9,10},{10,... | collective-permute-start | bytes 393224 | tf_op jit(solution)/shard_map/ppermute | solution.py:39
  80.0 6.7 %collective-permute-start.21 = (bf16[2,8,32,128]{3,2,1,0:T(8,128)(2,1)S(1)}, bf16[2,8,32,128]{3,2,1,0:T(8,128)(2,1)S(1)}, u32[]{:S(2)}, u32[]{:S(2)}) collective-permute-start(bf16[2,8,32,128]{3,2,1,0:T(8,128)(2,1)S(1)} %get-tuple-element.140), channel_id=1, source_target_pairs={{0,2},{1,3},{2,0},{3,1},{4,6},{5,7},{6,4},{7,5},{8,10},{9,11},{10,... | collective-permute-start | bytes 393224 | tf_op jit(solution)/shard_map/ppermute | solution.py:39
  81.6 10.9 %collective-permute-start.28 = (bf16[2,8,32,128]{3,2,1,0:T(8,128)(2,1)S(1)}, bf16[2,8,32,128]{3,2,1,0:T(8,128)(2,1)S(1)}, u32[]{:S(2)}, u32[]{:S(2)}) collective-permute-start(bf16[2,8,32,128]{3,2,1,0:T(8,128)(2,1)S(1)} %get-tuple-element.172), channel_id=1, source_target_pairs={{0,3},{1,2},{2,1},{3,0},{4,7},{5,6},{6,5},{7,4},{8,11},{9,10},{10,... | collective-permute-start | bytes 393224 | tf_op jit(solution)/shard_map/ppermute | solution.py:39
  85.1 5.9 %collective-permute-start.22 = (bf16[1,8,32,128]{3,2,1,0:T(8,128)(2,1)S(1)}, bf16[1,8,32,128]{3,2,1,0:T(8,128)(2,1)S(1)}, u32[]{:S(2)}, u32[]{:S(2)}) collective-permute-start(bf16[1,8,32,128]{3,2,1,0:T(8,128)(2,1)S(1)} %get-tuple-element.146), channel_id=1, source_target_pairs={{0,1},{1,0},{2,3},{3,2},{4,5},{5,4},{6,7},{7,6},{8,9},{9,8},{10,11... | collective-permute-start | bytes 196616 | tf_op jit(solution)/shard_map/ppermute | solution.py:39
  85.2 6.7 %collective-permute-start.23 = (bf16[1,8,32,128]{3,2,1,0:T(8,128)(2,1)S(1)}, bf16[1,8,32,128]{3,2,1,0:T(8,128)(2,1)S(1)}, u32[]{:S(2)}, u32[]{:S(2)}) collective-permute-start(bf16[1,8,32,128]{3,2,1,0:T(8,128)(2,1)S(1)} %get-tuple-element.147), channel_id=1, source_target_pairs={{0,2},{1,3},{2,0},{3,1},{4,6},{5,7},{6,4},{7,5},{8,10},{9,11},{10,... | collective-permute-start | bytes 196616 | tf_op jit(solution)/shard_map/ppermute | solution.py:39
  86.8 5.7 %collective-permute-start.24 = (bf16[1,8,32,128]{3,2,1,0:T(8,128)(2,1)S(1)}, bf16[1,8,32,128]{3,2,1,0:T(8,128)(2,1)S(1)}, u32[]{:S(2)}, u32[]{:S(2)}) collective-permute-start(bf16[1,8,32,128]{3,2,1,0:T(8,128)(2,1)S(1)} %get-tuple-element.148), channel_id=1, source_target_pairs={{0,3},{1,2},{2,1},{3,0},{4,7},{5,6},{6,5},{7,4},{8,11},{9,10},{10,... | collective-permute-start | bytes 196616 | tf_op jit(solution)/shard_map/ppermute | solution.py:39
  90.2 5.1 %collective-permute-start.25 = (bf16[1,8,32,128]{3,2,1,0:T(8,128)(2,1)S(1)}, bf16[1,8,32,128]{3,2,1,0:T(8,128)(2,1)S(1)}, u32[]{:S(2)}, u32[]{:S(2)}) collective-permute-start(bf16[1,8,32,128]{3,2,1,0:T(8,128)(2,1)S(1)} %get-tuple-element.154), channel_id=1, source_target_pairs={{0,1},{1,0},{2,3},{3,2},{4,5},{5,4},{6,7},{7,6},{8,9},{9,8},{10,11... | collective-permute-start | bytes 196616 | tf_op jit(solution)/shard_map/ppermute | solution.py:39
  91.0 4.7 %collective-permute-start.26 = (bf16[1,8,32,128]{3,2,1,0:T(8,128)(2,1)S(1)}, bf16[1,8,32,128]{3,2,1,0:T(8,128)(2,1)S(1)}, u32[]{:S(2)}, u32[]{:S(2)}) collective-permute-start(bf16[1,8,32,128]{3,2,1,0:T(8,128)(2,1)S(1)} %get-tuple-element.155), channel_id=1, source_target_pairs={{0,2},{1,3},{2,0},{3,1},{4,6},{5,7},{6,4},{7,5},{8,10},{9,11},{10,... | collective-permute-start | bytes 196616 | tf_op jit(solution)/shard_map/ppermute | solution.py:39
  91.9 4.4 %collective-permute-start.27 = (bf16[1,8,32,128]{3,2,1,0:T(8,128)(2,1)S(1)}, bf16[1,8,32,128]{3,2,1,0:T(8,128)(2,1)S(1)}, u32[]{:S(2)}, u32[]{:S(2)}) collective-permute-start(bf16[1,8,32,128]{3,2,1,0:T(8,128)(2,1)S(1)} %get-tuple-element.156), channel_id=1, source_target_pairs={{0,3},{1,2},{2,1},{3,0},{4,7},{5,6},{6,5},{7,4},{8,11},{9,10},{10,... | collective-permute-start | bytes 196616 | tf_op jit(solution)/shard_map/ppermute | solution.py:39
  (6 other events, 20.7 us)

commit v15 on v13

--- a/solution.py
+++ b/solution.py
@@ -353,9 +353,7 @@
 
     asks, own_weights = lax.optimization_barrier((asks, own_weights))
     weights = (own_weights, to_strip_target(own_weights, chips, 0, 1))
-    picked = list(pick(here, asks[2:3], eigvecs, sib, tile, 1))
-    here, picked[0] = lax.optimization_barrier((here, picked[0]))
-    picked = list(pick(here, asks[:2], eigvecs, sib, tile, 1)) + picked
+    picked = list(pick(here, asks[:3], eigvecs, sib, tile, 1))
     arrived = [
         shifted(value, "atoms", -offset) for value, offset in zip(picked, offsets)
     ]

time: 97.1 us -> 96.4 us (level)
    ppermute x17, waiting for transfers between devices: 5.89 us -> 2.66 us  [to_strip_target(): return lax.ppermute(value, 'bands', pairs)]
    ppermute x9, waiting for transfers between devices: 19.8 us -> 22.4 us  [shifted(): return lax.ppermute(value, axis, pairs)]
    pallas_call x3 -> x2, Pallas kernels: 6.23 us -> 5.7 us  [pick(): pl.pallas_call(functools.partial(pick_kernel, count, blocks, tile, parts)...]
  transfers between devices with their start and end apart: 26 -> 26, of which waited for: 7 -> 7; matrix products, arithmetic and copies ran while one was open for 5% -> 5% of each run, Pallas kernels for 38% -> 35%
where the time goes in v15:
time: 96.4 us; the launch traced here: 96 us
  Pallas kernels  39.3 us (41%)
  starting transfers between devices  25.7 us (27%)
  waiting for transfers between devices  25.1 us (26%)
  other arithmetic  4.83 us (5%)
  between operations  1.01 us (1%)
    pallas_call x5, Pallas kernels, tiles(): pl.pallas_call(functools.partial(tiles_kernel, heights, len(arrived), n_s...  23.8 us
    ppermute x9, waiting for transfers between devices, shifted(): return lax.ppermute(value, axis, pairs)  22.4 us
    ppermute x9, starting transfers between devices, shifted(): return lax.ppermute(value, axis, pairs)  15.1 us
    ppermute x17, starting transfers between devices, to_strip_target(): return lax.ppermute(value, 'bands', pairs)  10.6 us
    pallas_call x2, Pallas kernels, pick(): pl.pallas_call(functools.partial(pick_kernel, count, blocks, tile, parts)...  5.7 us
    pallas_call x1, Pallas kernels, keep(): pl.pallas_call(keep_kernel, out_shape=[pltpu.VMEM(own.shape, own.dtype)]...  3.48 us
    pallas_call x1, Pallas kernels, place_early(): pl.pallas_call(functools.partial(place_early_kernel, chips, sizes, per_co...  2.81 us
    ppermute x17, waiting for transfers between devices, to_strip_target(): return lax.ppermute(value, 'bands', pairs)  2.66 us
  transfers between devices with their start and end apart: 26, of which 7 were waited for; matrix products, arithmetic and copies ran while one was open for 5% of the time, Pallas kernels for 35%

profile of v15, /device:TPU:0, one launch (start us, length us, event | category | flops | bytes accessed | tf_op | source)
XLA Modules:
  0.0 96.0 jit_solution(8528419069308707162)
XLA Ops:
  1.1 2.6 %collective-permute-start.2 = (s32[8,16]{1,0:T(8,128)}, s32[8,16]{1,0:T(8,128)S(1)}, u32[]{:S(2)}, u32[]{:S(2)}) collective-permute-start(s32[8,16]{1,0:T(8,128)} %param.7), channel_id=1, source_target_pairs={{0,8},{4,12},{8,16},{12,20},{16,24},{20,28},{24,0},{28,4},{1,9},{5... | collective-permute-start | bytes 1544 | tf_op jit(solution)/shard_map/ppermute | solution.py:26
  5.3 3.2 %collective-permute-start = (s32[8,16]{1,0:T(8,128)}, s32[8,16]{1,0:T(8,128)S(1)}, u32[]{:S(2)}, u32[]{:S(2)}) collective-permute-start(s32[8,16]{1,0:T(8,128)} %param.7), channel_id=1, source_target_pairs={{0,28},{4,0},{8,4},{12,8},{16,12},{20,16},{24,20},{28,24},{1,29},{... | collective-permute-start | bytes 1544 | tf_op jit(solution)/shard_map/ppermute | solution.py:26
  10.3 2.0 %collective-permute-done.3.refs_0_ = s32[8,16]{1,0:T(8,128)S(1)} collective-permute-done((s32[8,16]{1,0:T(8,128)}, s32[8,16]{1,0:T(8,128)S(1)}, u32[]{:S(2)}, u32[]{:S(2)}) %collective-permute-start.3) | collective-permute-done | bytes 544 | tf_op jit(solution)/shard_map/ppermute | solution.py:26
  12.3 3.7 %pick_blocks.2 = (bf16[2,128,2048]{2,1,0:T(8,128)(2,1)S(1)}, bf16[2,128,2048]{2,1,0:T(8,128)(2,1)S(1)}, bf16[2,128,2048]{2,1,0:T(8,128)(2,1)}) custom-call(s32[2]{0:T(128)S(1)} %pad_add_fusion.place_ref, s32[8,16]{1,0:T(8,128)S(1)} %collective-permute-done.refs_0_, s32[8,16]{1,0:T(8,128)S(1)} %collective-permute-done.1.refs_1_, ...), custom_call_target="tpu_custom_call" | custom-call | tf_op jit(solution)/shard_map/pick_blocks/pallas_call | solution.py:73
  16.1 2.1 %collective-permute-start.8 = (bf16[2,128,2048]{2,1,0:T(8,128)(2,1)}, bf16[2,128,2048]{2,1,0:T(8,128)(2,1)S(1)}, u32[]{:S(2)}, u32[]{:S(2)}) collective-permute-start(bf16[2,128,2048]{2,1,0:T(8,128)(2,1)} %get-tuple-element.90), channel_id=1, source_target_pairs={{0,24},{4,28},{8,0},{12,4},{16,8},{20,12},{24,16},{28,20},{1,25},{... | collective-permute-start | bytes 3145736 | tf_op jit(solution)/shard_map/ppermute | solution.py:26
  19.3 3.6 %collective-permute-start.6 = (bf16[2,128,2048]{2,1,0:T(8,128)(2,1)S(1)}, bf16[2,128,2048]{2,1,0:T(8,128)(2,1)S(1)}, u32[]{:S(2)}, u32[]{:S(2)}) collective-permute-start(bf16[2,128,2048]{2,1,0:T(8,128)(2,1)S(1)} %get-tuple-element.83), channel_id=1, source_target_pairs={{0,28},{4,0},{8,4},{12,8},{16,12},{20,16},{24,20},{28,24},{1,29},{... | collective-permute-start | bytes 3145736 | tf_op jit(solution)/shard_map/ppermute | solution.py:26
  22.9 3.5 %keep.1 = (bf16[1024,2048]{1,0:T(8,128)(2,1)S(1)}, bf16[1024,2048]{1,0:T(8,128)(2,1)S(1)}) custom-call(bf16[1024,2048]{1,0:T(8,128)(2,1)} %refs_1_.1, bf16[1024,2048]{1,0:T(8,128)(2,1)} %collective-permute-done.4.refs_4_.sib.refs_2_), custom_call_target="tpu_custom_call" | custom-call | tf_op jit(solution)/shard_map/keep/pallas_call | solution.py:98
  26.4 9.8 %tiles.5 = (bf16[8,8,32,128]{3,2,1,0:T(8,128)(2,1)S(1)}, bf16[8,8,32,128]{3,2,1,0:T(8,128)(2,1)S(1)}, bf16[2,8,8,32,128]{4,3,2,1,0:T(8,128)(2,1)S(1)}) custom-call(s32[5]{0:T(128)S(1)} %stack.44.place_ref, bf16[1024,2048]{1,0:T(8,128)(2,1)S(1)} %get-tuple-element.85.refs_0_, bf16[1024,2048]{1,0:T(8,128)(2,1)S(1)} %get-tuple-element.86.refs_1_, ...), custom_call_target="tpu_custom_call" | custom-call | tf_op jit(solution)/shard_map/tiles/pallas_call | solution.py:165
  36.2 1.7 %collective-permute-start.11 = (bf16[2,8,8,32,128]{4,3,2,1,0:T(8,128)(2,1)S(1)}, bf16[2,8,8,32,128]{4,3,2,1,0:T(8,128)(2,1)S(1)}, u32[]{:S(2)}, u32[]{:S(2)}) collective-permute-start(bf16[2,8,8,32,128]{4,3,2,1,0:T(8,128)(2,1)S(1)} %get-tuple-element.102), channel_id=1, source_target_pairs={{0,2},{1,3},{2,0},{3,1},{4,6},{5,7},{6,4},{7,5},{8,10},{9,11},{10,... | collective-permute-start | bytes 3145736 | tf_op jit(solution)/shard_map/ppermute | solution.py:39
  38.0 2.0 %pick_blocks.3 = (bf16[2,64,2048]{2,1,0:T(8,128)(2,1)S(1)}, bf16[2,64,2048]{2,1,0:T(8,128)(2,1)S(1)}) custom-call(s32[2]{0:T(128)S(1)} %pad_add_fusion.place_ref, s32[8,16]{1,0:T(8,128)S(1)} %collective-permute-done.3.refs_0_, bf16[1024,2048]{1,0:T(8,128)(2,1)} %refs_1_.1, bf16[1024,2048]{1,0:T(8,128)(2,1)} %collective-permute-done.4.refs_4_.sib.refs_2_), custom_call_target="tpu_custom_call" | custom-call | tf_op jit(solution)/shard_map/pick_blocks/pallas_call | solution.py:73
  39.9 2.5 %collective-permute-done.8.refs_4_ = bf16[2,128,2048]{2,1,0:T(8,128)(2,1)S(1)} collective-permute-done((bf16[2,128,2048]{2,1,0:T(8,128)(2,1)}, bf16[2,128,2048]{2,1,0:T(8,128)(2,1)S(1)}, u32[]{:S(2)}, u32[]{:S(2)}) %collective-permute-start.8) | collective-permute-done | bytes 1048608 | tf_op jit(solution)/shard_map/ppermute | solution.py:26
  42.4 3.0 %tiles.6 = (bf16[2,8,32,128]{3,2,1,0:T(8,128)(2,1)S(1)}, bf16[2,8,32,128]{3,2,1,0:T(8,128)(2,1)S(1)}, bf16[2,2,8,32,128]{4,3,2,1,0:T(8,128)(2,1)S(1)}) custom-call(s32[5]{0:T(128)S(1)} %stack.44.place_ref, bf16[1024,2048]{1,0:T(8,128)(2,1)S(1)} %get-tuple-element.85.refs_0_, bf16[1024,2048]{1,0:T(8,128)(2,1)S(1)} %get-tuple-element.86.refs_1_, ...), custom_call_target="tpu_custom_call" | custom-call | tf_op jit(solution)/shard_map/tiles/pallas_call | solution.py:165
  47.8 2.6 %fusion.9.where_ref = s32[8,16]{1,0:T(8,128)S(1)} fusion(pred[8,16]{1,0:T(8,128)(4,1)S(1)} %get-tuple-element.163, pred[8,16]{1,0:T(8,128)(4,1)S(1)} %get-tuple-element.162, pred[8,16]{1,0:T(8,128)(4,1)S(1)} %get-tuple-element.161, pred[8,16]{1,0:T(8,128)(4,1)S(1)} %get-tuple-element.160, s32[]{:T(128)} %and.14, s32[]{:T(128)} %get-tuple-element.158, ...), kind=kLoop, calls=%fused_computation.22 | loop fusion | flops 4352 | bytes 1556 | tf_op jit(solution)/shard_map/add | solution.py:393
  50.3 1.9 %list_open.1.later = s32[257]{0:T(512)S(1)} custom-call(s32[8,16]{1,0:T(8,128)S(1)} %fusion.9.where_ref), custom_call_target="tpu_custom_call" | custom-call | tf_op jit(solution)/shard_map/list_open/pallas_call | solution.py:206
  52.3 14.8 %collective-permute-done.6.refs_5_ = bf16[2,128,2048]{2,1,0:T(8,128)(2,1)S(1)} collective-permute-done((bf16[2,128,2048]{2,1,0:T(8,128)(2,1)S(1)}, bf16[2,128,2048]{2,1,0:T(8,128)(2,1)S(1)}, u32[]{:S(2)}, u32[]{:S(2)}) %collective-permute-start.6) | collective-permute-done | bytes 1048608 | tf_op jit(solution)/shard_map/ppermute | solution.py:26
  68.5 5.3 %tiles.7 = (bf16[4,8,32,128]{3,2,1,0:T(8,128)(2,1)S(1)}, bf16[4,8,32,128]{3,2,1,0:T(8,128)(2,1)S(1)}, bf16[4,8,32,128]{3,2,1,0:T(8,128)(2,1)S(1)}, bf16[4,8,32,128]{3,2,1,0:T(8,128)(2,1)S(1)}) custom-call(s32[5]{0:T(128)S(1)} %stack.44.place_ref, bf16[1024,2048]{1,0:T(8,128)(2,1)S(1)} %get-tuple-element.85.refs_0_, ...), custom_call_target="tpu_custom_call" | custom-call | tf_op jit(solution)/shard_map/tiles/pallas_call | solution.py:165
  73.9 1.6 %collective-permute-start.18 = (bf16[4,8,32,128]{3,2,1,0:T(8,128)(2,1)S(1)}, bf16[4,8,32,128]{3,2,1,0:T(8,128)(2,1)S(1)}, u32[]{:S(2)}, u32[]{:S(2)}) collective-permute-start(bf16[4,8,32,128]{3,2,1,0:T(8,128)(2,1)S(1)} %get-tuple-element.122), channel_id=1, source_target_pairs={{0,2},{1,3},{2,0},{3,1},{4,6},{5,7},{6,4},{7,5},{8,10},{9,11},{10,... | collective-permute-start | bytes 786440 | tf_op jit(solution)/shard_map/ppermute | solution.py:39
  76.3 2.9 %tiles.8 = (bf16[1,8,32,128]{3,2,1,0:T(8,128)(2,1)S(1)}, bf16[1,8,32,128]{3,2,1,0:T(8,128)(2,1)S(1)}, bf16[1,8,32,128]{3,2,1,0:T(8,128)(2,1)S(1)}, bf16[1,8,32,128]{3,2,1,0:T(8,128)(2,1)S(1)}) custom-call(s32[5]{0:T(128)S(1)} %stack.44.place_ref, bf16[1024,2048]{1,0:T(8,128)(2,1)S(1)} %get-tuple-element.85.refs_0_, ...), custom_call_target="tpu_custom_call" | custom-call | tf_op jit(solution)/shard_map/tiles/pallas_call | solution.py:165
  79.2 1.7 %collective-permute-start.19 = (bf16[1,8,32,128]{3,2,1,0:T(8,128)(2,1)S(1)}, bf16[1,8,32,128]{3,2,1,0:T(8,128)(2,1)S(1)}, u32[]{:S(2)}, u32[]{:S(2)}) collective-permute-start(bf16[1,8,32,128]{3,2,1,0:T(8,128)(2,1)S(1)} %get-tuple-element.128), channel_id=1, source_target_pairs={{0,1},{1,0},{2,3},{3,2},{4,5},{5,4},{6,7},{7,6},{8,9},{9,8},{10,11... | collective-permute-start | bytes 196616 | tf_op jit(solution)/shard_map/ppermute | solution.py:39
  81.4 1.7 %collective-permute-done.18.refs_7_ = bf16[4,8,32,128]{3,2,1,0:T(8,128)(2,1)S(1)} collective-permute-done((bf16[4,8,32,128]{3,2,1,0:T(8,128)(2,1)S(1)}, bf16[4,8,32,128]{3,2,1,0:T(8,128)(2,1)S(1)}, u32[]{:S(2)}, u32[]{:S(2)}) %collective-permute-start.18) | collective-permute-done | bytes 262176 | tf_op jit(solution)/shard_map/ppermute | solution.py:39
  83.4 2.3 %collective-permute-done.12.refs_4_ = bf16[2,64,2048]{2,1,0:T(8,128)(2,1)S(1)} collective-permute-done((bf16[2,64,2048]{2,1,0:T(8,128)(2,1)S(1)}, bf16[2,64,2048]{2,1,0:T(8,128)(2,1)S(1)}, u32[]{:S(2)}, u32[]{:S(2)}) %collective-permute-start.12) | collective-permute-done | bytes 524320 | tf_op jit(solution)/shard_map/ppermute | solution.py:26
  85.7 2.9 %tiles.9 = (bf16[1,8,32,128]{3,2,1,0:T(8,128)(2,1)S(1)}, bf16[1,8,32,128]{3,2,1,0:T(8,128)(2,1)S(1)}, bf16[1,8,32,128]{3,2,1,0:T(8,128)(2,1)S(1)}, bf16[1,8,32,128]{3,2,1,0:T(8,128)(2,1)S(1)}) custom-call(s32[5]{0:T(128)S(1)} %stack.44.place_ref, bf16[1024,2048]{1,0:T(8,128)(2,1)S(1)} %get-tuple-element.85.refs_0_, ...), custom_call_target="tpu_custom_call" | custom-call | tf_op jit(solution)/shard_map/tiles/pallas_call | solution.py:165
  88.7 1.6 %collective-permute-start.23 = (bf16[1,8,32,128]{3,2,1,0:T(8,128)(2,1)S(1)}, bf16[1,8,32,128]{3,2,1,0:T(8,128)(2,1)S(1)}, u32[]{:S(2)}, u32[]{:S(2)}) collective-permute-start(bf16[1,8,32,128]{3,2,1,0:T(8,128)(2,1)S(1)} %get-tuple-element.137), channel_id=1, source_target_pairs={{0,2},{1,3},{2,0},{3,1},{4,6},{5,7},{6,4},{7,5},{8,10},{9,11},{10,... | collective-permute-start | bytes 196616 | tf_op jit(solution)/shard_map/ppermute | solution.py:39
  90.6 2.8 %place_early.1 = (f32[128,32,128]{2,1,0:T(8,128)}, f32[128,32,128]{2,1,0:T(8,128)}) custom-call(s32[8,16]{1,0:T(8,128)S(1)} %fusion.9.where_ref, bf16[8,8,32,128]{3,2,1,0:T(8,128)(2,1)S(1)} %get-tuple-element.140.refs_0_, bf16[4,8,32,128]{3,2,1,0:T(8,128)(2,1)S(1)} %get-tuple-element.141.refs_1_, bf16[2,8,32,128]{3,2,1,0:T(8,128)(2,1)S(1)} %get-tuple-element.142.refs_2_, ...), custom_call_target="tpu_custom_call" | custom-call | tf_op jit(solution)/shard_map/place_early/pallas_call | solution.py:259
  (49 shorter events, 13.3 us)
Async XLA Ops:
  0.6 11.7 %collective-permute-start.4 = (bf16[1024,2048]{1,0:T(8,128)(2,1)}, bf16[1024,2048]{1,0:T(8,128)(2,1)}, u32[]{:S(2)}, u32[]{:S(2)}) collective-permute-start(bf16[1024,2048]{1,0:T(8,128)(2,1)} %refs_1_.1), channel_id=1, source_target_pairs={{0,1},{1,0},{2,3},{3,2},{4,5},{5,4},{6,7},{7,6},{8,9},{9,8},{10,11... | collective-permute-start | bytes 12582920 | tf_op jit(solution)/shard_map/ppermute | solution.py:39
  1.1 9.2 %collective-permute-start.2 = (s32[8,16]{1,0:T(8,128)}, s32[8,16]{1,0:T(8,128)S(1)}, u32[]{:S(2)}, u32[]{:S(2)}) collective-permute-start(s32[8,16]{1,0:T(8,128)} %param.7), channel_id=1, source_target_pairs={{0,8},{4,12},{8,16},{12,20},{16,24},{20,28},{24,0},{28,4},{1,9},{5... | collective-permute-start | bytes 1544 | tf_op jit(solution)/shard_map/ppermute | solution.py:26
  3.8 6.6 %collective-permute-start.1 = (s32[8,16]{1,0:T(8,128)}, s32[8,16]{1,0:T(8,128)S(1)}, u32[]{:S(2)}, u32[]{:S(2)}) collective-permute-start(s32[8,16]{1,0:T(8,128)} %param.7), channel_id=1, source_target_pairs={{0,4},{4,8},{8,12},{12,16},{16,20},{20,24},{24,28},{28,0},{1,5},{5... | collective-permute-start | bytes 1544 | tf_op jit(solution)/shard_map/ppermute | solution.py:26
  5.3 5.1 %collective-permute-start = (s32[8,16]{1,0:T(8,128)}, s32[8,16]{1,0:T(8,128)S(1)}, u32[]{:S(2)}, u32[]{:S(2)}) collective-permute-start(s32[8,16]{1,0:T(8,128)} %param.7), channel_id=1, source_target_pairs={{0,28},{4,0},{8,4},{12,8},{16,12},{20,16},{24,20},{28,24},{1,29},{... | collective-permute-start | bytes 1544 | tf_op jit(solution)/shard_map/ppermute | solution.py:26
  16.1 26.4 %collective-permute-start.8 = (bf16[2,128,2048]{2,1,0:T(8,128)(2,1)}, bf16[2,128,2048]{2,1,0:T(8,128)(2,1)S(1)}, u32[]{:S(2)}, u32[]{:S(2)}) collective-permute-start(bf16[2,128,2048]{2,1,0:T(8,128)(2,1)} %get-tuple-element.90), channel_id=1, source_target_pairs={{0,24},{4,28},{8,0},{12,4},{16,8},{20,12},{24,16},{28,20},{1,25},{... | collective-permute-start | bytes 3145736 | tf_op jit(solution)/shard_map/ppermute | solution.py:26
  18.1 8.3 %collective-permute-start.7 = (f32[2,2048]{1,0:T(2,128)S(1)}, f32[2,2048]{1,0:T(2,128)S(1)}, u32[]{:S(2)}, u32[]{:S(2)}) collective-permute-start(f32[2,2048]{1,0:T(2,128)S(1)} %pad_maximum_fusion.refs_2_), channel_id=1, source_target_pairs={{0,1},{1,0},{2,3},{3,2},{4,5},{5,4},{6,7},{7,6},{8,9},{9,8},{10,11... | collective-permute-start | bytes 49160 | tf_op jit(solution)/shard_map/ppermute | solution.py:39
  18.2 48.9 %collective-permute-start.5 = (bf16[2,128,2048]{2,1,0:T(8,128)(2,1)S(1)}, bf16[2,128,2048]{2,1,0:T(8,128)(2,1)S(1)}, u32[]{:S(2)}, u32[]{:S(2)}) collective-permute-start(bf16[2,128,2048]{2,1,0:T(8,128)(2,1)S(1)} %get-tuple-element.82), channel_id=1, source_target_pairs={{0,4},{4,8},{8,12},{12,16},{16,20},{20,24},{24,28},{28,0},{1,5},{5... | collective-permute-start | bytes 3145736 | tf_op jit(solution)/shard_map/ppermute | solution.py:26
  19.3 47.8 %collective-permute-start.6 = (bf16[2,128,2048]{2,1,0:T(8,128)(2,1)S(1)}, bf16[2,128,2048]{2,1,0:T(8,128)(2,1)S(1)}, u32[]{:S(2)}, u32[]{:S(2)}) collective-permute-start(bf16[2,128,2048]{2,1,0:T(8,128)(2,1)S(1)} %get-tuple-element.83), channel_id=1, source_target_pairs={{0,28},{4,0},{8,4},{12,8},{16,12},{20,16},{24,20},{28,24},{1,29},{... | collective-permute-start | bytes 3145736 | tf_op jit(solution)/shard_map/ppermute | solution.py:26
  36.2 30.9 %collective-permute-start.11 = (bf16[2,8,8,32,128]{4,3,2,1,0:T(8,128)(2,1)S(1)}, bf16[2,8,8,32,128]{4,3,2,1,0:T(8,128)(2,1)S(1)}, u32[]{:S(2)}, u32[]{:S(2)}) collective-permute-start(bf16[2,8,8,32,128]{4,3,2,1,0:T(8,128)(2,1)S(1)} %get-tuple-element.102), channel_id=1, source_target_pairs={{0,2},{1,3},{2,0},{3,1},{4,6},{5,7},{6,4},{7,5},{8,10},{9,11},{10,... | collective-permute-start | bytes 3145736 | tf_op jit(solution)/shard_map/ppermute | solution.py:39
  38.0 14.3 %collective-permute-start.10 = (bf16[8,8,32,128]{3,2,1,0:T(8,128)(2,1)S(1)}, bf16[8,8,32,128]{3,2,1,0:T(8,128)(2,1)S(1)}, u32[]{:S(2)}, u32[]{:S(2)}) collective-permute-start(bf16[8,8,32,128]{3,2,1,0:T(8,128)(2,1)S(1)} %get-tuple-element.101), channel_id=1, source_target_pairs={{0,1},{1,0},{2,3},{3,2},{4,5},{5,4},{6,7},{7,6},{8,9},{9,8},{10,11... | collective-permute-start | bytes 1572872 | tf_op jit(solution)/shard_map/ppermute | solution.py:39
  45.4 21.7 %collective-permute-start.9 = (bf16[2,2,8,32,128]{4,3,2,1,0:T(8,128)(2,1)S(1)}, bf16[2,2,8,32,128]{4,3,2,1,0:T(8,128)(2,1)S(1)}, u32[]{:S(2)}, u32[]{:S(2)}) collective-permute-start(bf16[2,2,8,32,128]{4,3,2,1,0:T(8,128)(2,1)S(1)} %get-tuple-element.99), channel_id=1, source_target_pairs={{0,2},{1,3},{2,0},{3,1},{4,6},{5,7},{6,4},{7,5},{8,10},{9,11},{10,... | collective-permute-start | bytes 786440 | tf_op jit(solution)/shard_map/ppermute | solution.py:39
  52.3 24.0 %collective-permute-start.13 = (bf16[2,64,2048]{2,1,0:T(8,128)(2,1)S(1)}, bf16[2,64,2048]{2,1,0:T(8,128)(2,1)S(1)}, u32[]{:S(2)}, u32[]{:S(2)}) collective-permute-start(bf16[2,64,2048]{2,1,0:T(8,128)(2,1)S(1)} %get-tuple-element.103), channel_id=1, source_target_pairs={{0,8},{4,12},{8,16},{12,20},{16,24},{20,28},{24,0},{28,4},{1,9},{5... | collective-permute-start | bytes 1572872 | tf_op jit(solution)/shard_map/ppermute | solution.py:26
  67.1 6.7 %collective-permute-start.16 = (bf16[2,8,32,128]{3,2,1,0:T(8,128)(2,1)S(1)}, bf16[2,8,32,128]{3,2,1,0:T(8,128)(2,1)S(1)}, u32[]{:S(2)}, u32[]{:S(2)}) collective-permute-start(bf16[2,8,32,128]{3,2,1,0:T(8,128)(2,1)S(1)} %get-tuple-element.116), channel_id=1, source_target_pairs={{0,1},{1,0},{2,3},{3,2},{4,5},{5,4},{6,7},{7,6},{8,9},{9,8},{10,11... | collective-permute-start | bytes 393224 | tf_op jit(solution)/shard_map/ppermute | solution.py:39
  67.2 18.5 %collective-permute-start.12 = (bf16[2,64,2048]{2,1,0:T(8,128)(2,1)S(1)}, bf16[2,64,2048]{2,1,0:T(8,128)(2,1)S(1)}, u32[]{:S(2)}, u32[]{:S(2)}) collective-permute-start(bf16[2,64,2048]{2,1,0:T(8,128)(2,1)S(1)} %get-tuple-element.107), channel_id=1, source_target_pairs={{0,8},{4,12},{8,16},{12,20},{16,24},{20,28},{24,0},{28,4},{1,9},{5... | collective-permute-start | bytes 1572872 | tf_op jit(solution)/shard_map/ppermute | solution.py:26
  67.9 8.4 %collective-permute-start.15 = (bf16[8,8,32,128]{3,2,1,0:T(8,128)(2,1)S(1)}, bf16[8,8,32,128]{3,2,1,0:T(8,128)(2,1)S(1)}, u32[]{:S(2)}, u32[]{:S(2)}) collective-permute-start(bf16[8,8,32,128]{3,2,1,0:T(8,128)(2,1)S(1)} %get-tuple-element.164), channel_id=1, source_target_pairs={{0,1},{1,0},{2,3},{3,2},{4,5},{5,4},{6,7},{7,6},{8,9},{9,8},{10,11... | collective-permute-start | bytes 1572872 | tf_op jit(solution)/shard_map/ppermute | solution.py:39
  68.0 5.9 %collective-permute-start.17 = (bf16[2,8,32,128]{3,2,1,0:T(8,128)(2,1)S(1)}, bf16[2,8,32,128]{3,2,1,0:T(8,128)(2,1)S(1)}, u32[]{:S(2)}, u32[]{:S(2)}) collective-permute-start(bf16[2,8,32,128]{3,2,1,0:T(8,128)(2,1)S(1)} %get-tuple-element.166), channel_id=1, source_target_pairs={{0,1},{1,0},{2,3},{3,2},{4,5},{5,4},{6,7},{7,6},{8,9},{9,8},{10,11... | collective-permute-start | bytes 393224 | tf_op jit(solution)/shard_map/ppermute | solution.py:39
  73.9 9.2 %collective-permute-start.18 = (bf16[4,8,32,128]{3,2,1,0:T(8,128)(2,1)S(1)}, bf16[4,8,32,128]{3,2,1,0:T(8,128)(2,1)S(1)}, u32[]{:S(2)}, u32[]{:S(2)}) collective-permute-start(bf16[4,8,32,128]{3,2,1,0:T(8,128)(2,1)S(1)} %get-tuple-element.122), channel_id=1, source_target_pairs={{0,2},{1,3},{2,0},{3,1},{4,6},{5,7},{6,4},{7,5},{8,10},{9,11},{10,... | collective-permute-start | bytes 786440 | tf_op jit(solution)/shard_map/ppermute | solution.py:39
  76.3 14.3 %collective-permute-start.25 = (bf16[4,8,32,128]{3,2,1,0:T(8,128)(2,1)S(1)}, bf16[4,8,32,128]{3,2,1,0:T(8,128)(2,1)S(1)}, u32[]{:S(2)}, u32[]{:S(2)}) collective-permute-start(bf16[4,8,32,128]{3,2,1,0:T(8,128)(2,1)S(1)} %get-tuple-element.150), channel_id=1, source_target_pairs={{0,3},{1,2},{2,1},{3,0},{4,7},{5,6},{6,5},{7,4},{8,11},{9,10},{10,... | collective-permute-start | bytes 786440 | tf_op jit(solution)/shard_map/ppermute | solution.py:39
  79.2 9.5 %collective-permute-start.19 = (bf16[1,8,32,128]{3,2,1,0:T(8,128)(2,1)S(1)}, bf16[1,8,32,128]{3,2,1,0:T(8,128)(2,1)S(1)}, u32[]{:S(2)}, u32[]{:S(2)}) collective-permute-start(bf16[1,8,32,128]{3,2,1,0:T(8,128)(2,1)S(1)} %get-tuple-element.128), channel_id=1, source_target_pairs={{0,1},{1,0},{2,3},{3,2},{4,5},{5,4},{6,7},{7,6},{8,9},{9,8},{10,11... | collective-permute-start | bytes 196616 | tf_op jit(solution)/shard_map/ppermute | solution.py:39
  80.9 9.4 %collective-permute-start.20 = (bf16[1,8,32,128]{3,2,1,0:T(8,128)(2,1)S(1)}, bf16[1,8,32,128]{3,2,1,0:T(8,128)(2,1)S(1)}, u32[]{:S(2)}, u32[]{:S(2)}) collective-permute-start(bf16[1,8,32,128]{3,2,1,0:T(8,128)(2,1)S(1)} %get-tuple-element.129), channel_id=1, source_target_pairs={{0,2},{1,3},{2,0},{3,1},{4,6},{5,7},{6,4},{7,5},{8,10},{9,11},{10,... | collective-permute-start | bytes 196616 | tf_op jit(solution)/shard_map/ppermute | solution.py:39
  83.1 7.5 %collective-permute-start.21 = (bf16[1,8,32,128]{3,2,1,0:T(8,128)(2,1)S(1)}, bf16[1,8,32,128]{3,2,1,0:T(8,128)(2,1)S(1)}, u32[]{:S(2)}, u32[]{:S(2)}) collective-permute-start(bf16[1,8,32,128]{3,2,1,0:T(8,128)(2,1)S(1)} %get-tuple-element.130), channel_id=1, source_target_pairs={{0,3},{1,2},{2,1},{3,0},{4,7},{5,6},{6,5},{7,4},{8,11},{9,10},{10,... | collective-permute-start | bytes 196616 | tf_op jit(solution)/shard_map/ppermute | solution.py:39
  88.6 4.8 %collective-permute-start.22 = (bf16[1,8,32,128]{3,2,1,0:T(8,128)(2,1)S(1)}, bf16[1,8,32,128]{3,2,1,0:T(8,128)(2,1)S(1)}, u32[]{:S(2)}, u32[]{:S(2)}) collective-permute-start(bf16[1,8,32,128]{3,2,1,0:T(8,128)(2,1)S(1)} %get-tuple-element.136), channel_id=1, source_target_pairs={{0,1},{1,0},{2,3},{3,2},{4,5},{5,4},{6,7},{7,6},{8,9},{9,8},{10,11... | collective-permute-start | bytes 196616 | tf_op jit(solution)/shard_map/ppermute | solution.py:39
  88.7 4.7 %collective-permute-start.23 = (bf16[1,8,32,128]{3,2,1,0:T(8,128)(2,1)S(1)}, bf16[1,8,32,128]{3,2,1,0:T(8,128)(2,1)S(1)}, u32[]{:S(2)}, u32[]{:S(2)}) collective-permute-start(bf16[1,8,32,128]{3,2,1,0:T(8,128)(2,1)S(1)} %get-tuple-element.137), channel_id=1, source_target_pairs={{0,2},{1,3},{2,0},{3,1},{4,6},{5,7},{6,4},{7,5},{8,10},{9,11},{10,... | collective-permute-start | bytes 196616 | tf_op jit(solution)/shard_map/ppermute | solution.py:39
  90.3 4.1 %collective-permute-start.24 = (bf16[1,8,32,128]{3,2,1,0:T(8,128)(2,1)S(1)}, bf16[1,8,32,128]{3,2,1,0:T(8,128)(2,1)S(1)}, u32[]{:S(2)}, u32[]{:S(2)}) collective-permute-start(bf16[1,8,32,128]{3,2,1,0:T(8,128)(2,1)S(1)} %get-tuple-element.138), channel_id=1, source_target_pairs={{0,3},{1,2},{2,1},{3,0},{4,7},{5,6},{6,5},{7,4},{8,11},{9,10},{10,... | collective-permute-start | bytes 196616 | tf_op jit(solution)/shard_map/ppermute | solution.py:39
  (3 other events, 10.9 us)
